TPU v7x, 32 devices: a whole 2x2x4 slice. The times are simulated.
32 devices in a mesh: dp: 8 (over z, x), mp: 4 (over y, core).
Axes of the slice: x: 2, y: 2, z: 4, core: 2. Of those that a mesh axis runs over, the one named last changes fastest.
Arguments:
- tokens: bfloat16 [2, 40960, 1024], P(None, ('dp', 'mp')), may hold values from -6 to 6
- cotangent: bfloat16 [2, 40960, 1024], P(None, ('dp', 'mp')), may hold values from -6 to 6
- qkv_weight: bfloat16 [3, 1024, 1024], P(None, None, 'mp'), may hold values from -0.1875 to 0.1875
- out_weight: bfloat16 [1024, 1024], P('mp'), may hold values from -0.75 to 0.75
- up_weight: bfloat16 [1024, 4096], P(None, 'mp'), may hold values from -0.1875 to 0.1875
- down_weight: bfloat16 [4096, 1024], P('mp'), may hold values from -0.09375 to 0.09375
- rel_bias: float32 [16, 2025], P('mp'), may hold values from -4 to 4
- ada_weight: bfloat16 [1024, 6144], P('mp'), may hold values from -0.1875 to 0.1875
- ada_bias: float32 [6144], replicated, may hold values from -3 to 3
- class_embed: float32 [1000, 1024], P(None, 'mp'), may hold values from -5 to 5
- window_clip: int32 [2, 128], P(None, 'dp'), may hold values from 0 to 7, as said below
- timesteps: int32 [2, 8], replicated, may hold values from 0 to 999
- class_ids: int32 [2, 8], replicated, may hold values from 0 to 999
Outputs:
- block_out: bfloat16 [2, 40960, 1024], P(None, ('dp', 'mp'))
- token_grad: bfloat16 [2, 40960, 1024], P(None, ('dp', 'mp'))
- qkv_grad: float32 [3, 1024, 1024], P(None, None, 'mp')
- out_grad: float32 [1024, 1024], P('mp')
- up_grad: float32 [1024, 4096], P(None, 'mp')
- down_grad: float32 [4096, 1024], P('mp')
- rel_grad: float32 [16, 2025], P('mp')
- ada_weight_grad: float32 [1024, 6144], P('mp')
- ada_bias_grad: float32 [6144], replicated
- class_grad: float32 [1000, 1024], P(None, 'mp')
Inputs may be any that keep to these rules, and one draw needn't show every extreme that they name: `window_clip`: in each micro-batch, one clip drawn from the seed holds the first window of every index of dp.
All inputs are finite; a program needn't handle non-finite values.
Results may differ from a plain program's by a relative error of at most 0.02.
The roundings to bfloat16 on the way count: a program that leaves them out, or rounds other values in their place, can miss the bound.
Values may be sent and summed in bfloat16 or wider, within the bound.
No kernel may reach another device: no remote copies, remote signals or barrier semaphores. Data moves between devices by JAX's collectives and lax.ppermute only.
A program may use at most 640 MiB of HBM per device.

v0:
```python
import math

import jax
import jax.numpy as jnp
from jax import lax
from jax.sharding import PartitionSpec as P

D = 1024
WIN_T = 5
WIN_H = 8
WIN_W = 8


epsilon = 1e-06
highest = lax.Precision.HIGHEST


def layer_norm(values):
    centred = values - jnp.mean(values, axis=-1, keepdims=True)
    inverse = lax.rsqrt(jnp.mean(centred * centred, axis=-1, keepdims=True) + epsilon)
    return (centred * inverse, inverse)


def layer_norm_back(normed, inverse, grad_in):
    return inverse * (
        grad_in
        - jnp.mean(grad_in, axis=-1, keepdims=True)
        - normed * jnp.mean(grad_in * normed, axis=-1, keepdims=True)
    )


def gelu_tanh(values):
    return (
        0.5
        * values
        * (1.0 + jnp.tanh(0.7978845608028654 * (values + 0.044715 * values * values * values)))
    )


def offset_hot(extent):
    places = jnp.arange(extent)
    offsets = places[:, None] - places[None, :] + extent - 1
    return (offsets[:, :, None] == jnp.arange(2 * extent - 1)[None, None, :]).astype(jnp.float32)


def spread_bias(rel_table):
    head_count = rel_table.shape[0]
    window_len = WIN_T * WIN_H * WIN_W
    cube = rel_table.reshape(head_count, 2 * WIN_T - 1, 2 * WIN_H - 1, 2 * WIN_W - 1)
    spread = jnp.einsum(
        "htuv,pqt,rsu,xyv->hprxqsy",
        cube,
        offset_hot(WIN_T),
        offset_hot(WIN_H),
        offset_hot(WIN_W),
        precision=highest,
    )
    return spread.reshape(head_count, window_len, window_len)


def collect_bias(grad_table):
    head_count = grad_table.shape[0]
    split = grad_table.reshape(head_count, WIN_T, WIN_H, WIN_W, WIN_T, WIN_H, WIN_W)
    cube = jnp.einsum(
        "hprxqsy,pqt,rsu,xyv->htuv",
        split,
        offset_hot(WIN_T),
        offset_hot(WIN_H),
        offset_hot(WIN_W),
        precision=highest,
    )
    return cube.reshape(head_count, -1)


def contract_rows(left, right, precision=None):
    return lax.dot_general(
        left,
        right,
        (((0,), (0,)), ((), ())),
        precision=precision,
        preferred_element_type=jnp.float32,
    )


def contract_cols(left, right):
    return lax.dot_general(
        left, right, (((1,), (1,)), ((), ())), preferred_element_type=jnp.float32
    )


def window_scores(queries, keys_in, bias_table, score_scale):
    scores = jnp.einsum("wihd,wjhd->whij", queries, keys_in, preferred_element_type=jnp.float32)
    return scores * score_scale + bias_table[None]


def attend_forward(inputs_block, bias_table, score_scale):
    queries, keys_in, values_in = inputs_block
    scores = window_scores(queries, keys_in, bias_table, score_scale)
    row_max = jnp.max(scores, axis=-1, keepdims=True)
    exponent = jnp.exp(scores - row_max)
    row_total = jnp.sum(exponent, axis=-1, keepdims=True)
    probs = exponent / row_total
    mixed = jnp.einsum(
        "whij,wjhd->wihd", probs.astype(jnp.bfloat16), values_in, preferred_element_type=jnp.float32
    )
    return (mixed.astype(jnp.bfloat16), row_max + jnp.log(row_total))


def attend_backward(inputs_block, bias_table, score_scale):
    queries, keys_in, values_in, grad_mixed, log_total = inputs_block
    scores = window_scores(queries, keys_in, bias_table, score_scale)
    probs = jnp.exp(scores - log_total)
    grad_probs = jnp.einsum(
        "wihd,wjhd->whij", grad_mixed, values_in, preferred_element_type=jnp.float32
    )
    inner = jnp.sum(grad_probs * probs, axis=-1, keepdims=True)
    grad_scores = (probs * (grad_probs - inner)).astype(jnp.bfloat16)
    grad_queries = (
        jnp.einsum("whij,wjhd->wihd", grad_scores, keys_in, preferred_element_type=jnp.float32)
        * score_scale
    ).astype(jnp.bfloat16)
    grad_keys = (
        jnp.einsum("whij,wihd->wjhd", grad_scores, queries, preferred_element_type=jnp.float32)
        * score_scale
    ).astype(jnp.bfloat16)
    grad_values = jnp.einsum(
        "whij,wihd->wjhd",
        probs.astype(jnp.bfloat16),
        grad_mixed,
        preferred_element_type=jnp.float32,
    ).astype(jnp.bfloat16)
    grad_bias = jnp.sum(grad_scores.astype(jnp.float32), axis=0)
    return (grad_queries, grad_keys, grad_values, grad_bias)


def body(
    tokens,
    cotangent,
    qkv_weight,
    out_weight,
    up_weight,
    down_weight,
    rel_bias,
    ada_weight,
    ada_bias,
    class_embed,
    window_clip,
    timesteps,
    class_ids,
):
    mp_index = lax.axis_index("mp")
    local_rows = tokens.shape[1]
    local_cols = class_embed.shape[1]
    clip_count = timesteps.shape[1]
    window_len = WIN_T * WIN_H * WIN_W
    qkv_w, out_w, up_w, down_w = (qkv_weight, out_weight, up_weight, down_weight)
    per_block = 4
    head_width = qkv_w.shape[2]
    local_heads = rel_bias.shape[0]
    head_size = head_width // local_heads
    score_scale = 1.0 / math.sqrt(head_size)
    bias_table = spread_bias(rel_bias)
    columns = mp_index * local_cols + jnp.arange(local_cols)
    half_width = D // 2
    freq_index = (columns % half_width).astype(jnp.float32)
    frequency = jnp.exp(-math.log(10000.0) * freq_index / half_width)
    angle = timesteps.astype(jnp.float32)[..., None] * frequency
    step_embed = jnp.where(columns < half_width, jnp.sin(angle), jnp.cos(angle))
    class_hot = (class_ids[..., None] == jnp.arange(class_embed.shape[0])).astype(jnp.float32)
    condition = step_embed + jnp.einsum("mck,kd->mcd", class_hot, class_embed, precision=highest)
    lowered = jax.nn.silu(condition).astype(jnp.bfloat16)
    mod_terms = jnp.einsum("mcd,de->mce", lowered, ada_weight, preferred_element_type=jnp.float32)
    modulation = lax.psum(mod_terms, "mp") + ada_bias
    row_window = (mp_index * local_rows + jnp.arange(local_rows)) // window_len
    window_hot = (row_window[:, None] == jnp.arange(window_clip.shape[1])).astype(jnp.int32)
    acc_qkv = jnp.zeros(qkv_w.shape, jnp.float32)
    acc_out = jnp.zeros(out_w.shape, jnp.float32)
    acc_up = jnp.zeros(up_w.shape, jnp.float32)
    acc_down = jnp.zeros(down_w.shape, jnp.float32)
    acc_bias = jnp.zeros(bias_table.shape, jnp.float32)
    block_outs = []
    token_grads = []
    mod_grads = []
    for micro in range(tokens.shape[0]):
        clip_row = jnp.sum(window_hot * window_clip[micro][None, :], axis=1)
        row_hot = (clip_row[:, None] == jnp.arange(clip_count)).astype(jnp.float32)
        token_mod = jnp.dot(row_hot, modulation[micro], precision=highest)
        shift_one, scale_one, gate_one, shift_two, scale_two, gate_two = jnp.split(
            token_mod, 6, axis=1
        )
        inputs_f = tokens[micro].astype(jnp.float32)
        normed_one, inverse_one = layer_norm(inputs_f)
        attn_in = (normed_one * (1.0 + scale_one) + shift_one).astype(jnp.bfloat16)
        attn_full = lax.all_gather(attn_in, "mp", axis=0, tiled=True)
        projected = jnp.einsum(
            "rd,sde->sre", attn_full, qkv_w, preferred_element_type=jnp.float32
        ).astype(jnp.bfloat16)
        group_rows = attn_full.shape[0]
        block_count = group_rows // (per_block * window_len)
        split_heads = projected.reshape(
            3, block_count, per_block, window_len, local_heads, head_size
        )
        mixed, log_total = lax.map(
            lambda item_in: attend_forward(item_in, bias_table, score_scale),
            (split_heads[0], split_heads[1], split_heads[2]),
        )
        mixed_rows = mixed.reshape(group_rows, head_width)
        attn_out = lax.psum_scatter(
            jnp.dot(mixed_rows, out_w, preferred_element_type=jnp.float32).astype(jnp.bfloat16),
            "mp",
            scatter_dimension=0,
            tiled=True,
        ).astype(jnp.float32)
        resid = inputs_f + gate_one * attn_out
        normed_two, inverse_two = layer_norm(resid)
        mlp_in = (normed_two * (1.0 + scale_two) + shift_two).astype(jnp.bfloat16)
        mlp_full = lax.all_gather(mlp_in, "mp", axis=0, tiled=True)
        hidden = jnp.dot(mlp_full, up_w, preferred_element_type=jnp.float32)
        activated = gelu_tanh(hidden).astype(jnp.bfloat16)
        mlp_out = lax.psum_scatter(
            jnp.dot(activated, down_w, preferred_element_type=jnp.float32).astype(jnp.bfloat16),
            "mp",
            scatter_dimension=0,
            tiled=True,
        ).astype(jnp.float32)
        block_outs.append((resid + gate_two * mlp_out).astype(jnp.bfloat16))
        grad_out = cotangent[micro].astype(jnp.float32)
        grad_gate_two = grad_out * mlp_out
        grad_mlp = (gate_two * grad_out).astype(jnp.bfloat16)
        grad_mlp_full = lax.all_gather(grad_mlp, "mp", axis=0, tiled=True)
        acc_down = acc_down + contract_rows(activated, grad_mlp_full)
        grad_act = contract_cols(grad_mlp_full, down_w)
        grad_hidden = jax.vjp(gelu_tanh, hidden)[1](grad_act)[0].astype(jnp.bfloat16)
        acc_up = acc_up + contract_rows(mlp_full, grad_hidden)
        grad_mlp_in = lax.psum_scatter(
            contract_cols(grad_hidden, up_w).astype(jnp.bfloat16),
            "mp",
            scatter_dimension=0,
            tiled=True,
        ).astype(jnp.float32)
        grad_scale_two = grad_mlp_in * normed_two
        grad_resid = grad_out + layer_norm_back(
            normed_two, inverse_two, grad_mlp_in * (1.0 + scale_two)
        )
        grad_gate_one = grad_resid * attn_out
        grad_attn = (gate_one * grad_resid).astype(jnp.bfloat16)
        grad_attn_full = lax.all_gather(grad_attn, "mp", axis=0, tiled=True)
        acc_out = acc_out + contract_rows(mixed_rows, grad_attn_full)
        grad_mixed = contract_cols(grad_attn_full, out_w).astype(jnp.bfloat16)
        grad_blocks = grad_mixed.reshape(block_count, per_block, window_len, local_heads, head_size)
        grad_queries, grad_keys, grad_values, grad_bias = lax.map(
            lambda item_in: attend_backward(item_in, bias_table, score_scale),
            (split_heads[0], split_heads[1], split_heads[2], grad_blocks, log_total),
        )
        acc_bias = acc_bias + jnp.sum(grad_bias, axis=0)
        grad_proj = jnp.stack(
            [
                grad_queries.reshape(group_rows, head_width),
                grad_keys.reshape(group_rows, head_width),
                grad_values.reshape(group_rows, head_width),
            ]
        )
        acc_qkv = acc_qkv + jnp.einsum(
            "rd,sre->sde", attn_full, grad_proj, preferred_element_type=jnp.float32
        )
        grad_attn_in = lax.psum_scatter(
            jnp.einsum("sre,sde->rd", grad_proj, qkv_w, preferred_element_type=jnp.float32).astype(
                jnp.bfloat16
            ),
            "mp",
            scatter_dimension=0,
            tiled=True,
        ).astype(jnp.float32)
        grad_tokens = grad_resid + layer_norm_back(
            normed_one, inverse_one, grad_attn_in * (1.0 + scale_one)
        )
        token_grads.append(grad_tokens.astype(jnp.bfloat16))
        grad_token_mod = jnp.concatenate(
            [
                grad_attn_in,
                grad_attn_in * normed_one,
                grad_gate_one,
                grad_mlp_in,
                grad_scale_two,
                grad_gate_two,
            ],
            axis=1,
        )
        mod_grads.append(contract_rows(row_hot, grad_token_mod, precision=highest))
    mod_grad = jnp.stack(mod_grads)
    mod_total = lax.psum(mod_grad.astype(jnp.bfloat16), "mp").astype(jnp.float32)
    grad_ada_bias = jnp.sum(mod_total, axis=(0, 1))
    grad_ada = jnp.einsum("mcd,mce->de", lowered.astype(jnp.float32), mod_total, precision=highest)
    grad_lowered = jnp.einsum(
        "mce,de->mcd", mod_total, ada_weight.astype(jnp.float32), precision=highest
    )
    grad_condition = jax.vjp(jax.nn.silu, condition)[1](grad_lowered)[0]
    grad_class = jnp.einsum("mck,mcd->kd", class_hot, grad_condition, precision=highest)
    grad_rel = collect_bias(acc_bias)
    totals = (
        lax.psum(acc_qkv.astype(jnp.bfloat16), "dp").astype(jnp.float32),
        lax.psum(acc_out.astype(jnp.bfloat16), "dp").astype(jnp.float32),
        lax.psum(acc_up.astype(jnp.bfloat16), "dp").astype(jnp.float32),
        lax.psum(acc_down.astype(jnp.bfloat16), "dp").astype(jnp.float32),
        lax.psum(grad_rel.astype(jnp.bfloat16), "dp").astype(jnp.float32),
        lax.psum(grad_ada.astype(jnp.bfloat16), "dp").astype(jnp.float32),
        lax.psum(grad_ada_bias.astype(jnp.bfloat16), "dp").astype(jnp.float32),
        lax.psum(grad_class.astype(jnp.bfloat16), "dp").astype(jnp.float32),
    )
    summed = totals[:5]
    cond_grads = totals[5:]
    return (
        jnp.stack(block_outs),
        jnp.stack(token_grads),
        summed[0],
        summed[1],
        summed[2],
        summed[3],
        summed[4],
        cond_grads[0],
        cond_grads[1],
        cond_grads[2],
    )


def solution(mesh):
    in_specs = (
        P(None, ("dp", "mp"), None),
        P(None, ("dp", "mp"), None),
        P(None, None, "mp"),
        P("mp", None),
        P(None, "mp"),
        P("mp", None),
        P("mp", None),
        P("mp", None),
        P(),
        P(None, "mp"),
        P(None, "dp"),
        P(),
        P(),
    )
    out_specs = (
        P(None, ("dp", "mp"), None),
        P(None, ("dp", "mp"), None),
        P(None, None, "mp"),
        P("mp", None),
        P(None, "mp"),
        P("mp", None),
        P("mp", None),
        P("mp", None),
        P(),
        P(None, "mp"),
    )
    return jax.shard_map(body, mesh=mesh, in_specs=in_specs, out_specs=out_specs, check_vma=False)
```

profile of v0, /device:TPU:0, one launch (start us, length us, event | category | flops | bytes accessed | tf_op | source)
XLA Modules:
  0.0 2721.6 jit_solution(10095336250827898646)
XLA Ops:
  18.3 28.9 %all-reduce.6.cloned.1.call-done = f32[2,8,6144]{2,1,0:T(8,128)} async-done(((f32[2,8,6144]{2,1,0:T(8,128)}), f32[2,8,6144]{2,1,0:T(8,128)}) %all-reduce.6.cloned.1.call-update) | async-done | bytes 393232 | tf_op jit(solution)/shard_map/psum | solution.py:173
  49.0 12.8 fusion.212
  61.9 10.4 copy-done.5
  86.6 21.5 convolution_bitcast_fusion
  108.0 86.7 %copy.290 = f32[4,5,8,8,5,8,8]{3,2,1,6,5,4,0:T(8,128)} copy(f32[4,5,8,8,5,8,8]{4,6,1,3,0,5,2:T(8,128)} %convolution_bitcast_fusion) | data formatting | bytes 3276800 | tf_op jit(solution)/shard_map/while | solution.py:203
  194.7 16.5 add.628
  211.2 11.5 fusion.134
  282.3 39.5 %while.61 = (s32[]{:T(128)}, bf16[4,4,320,4,64]{2,1,0,4,3:T(4,128)(2,1)}, f32[4,4,4,320,1]{3,2,1,4,0:T(4,128)S(1)}, bf16[4,4,320,4,64]{2,4,3,1,0:T(8,128)(2,1)},...) while((s32[]{:T(128)}, ...), condition=%wide.wide.region_18.19_spmd, body=%wide.wide.region_15.18_spmd.sunk | while | flops 439413760 | bytes 36091020 | solution.py:203
  337.6 85.4 %reduce-scatter.13.cloned.1.call-done = bf16[1280,1024]{1,0:T(8,128)(2,1)} async-done(((bf16[5120,1024]{1,0:T(8,128)(2,1)}), bf16[1280,1024]{1,0:T(8,128)(2,1)}) %reduce-scatter.13.cloned.1.call-update) | async-done | bytes 2621456 | tf_op jit(solution)/shard_map/reduce_scatter | solution.py:208
  428.7 10.6 fusion.184
  440.0 69.7 %all-gather.21.cloned.1.call-done = bf16[5120,1024]{1,0:T(8,128)(2,1)} async-done(((bf16[1280,1024]{1,0:T(8,128)(2,1)}), bf16[5120,1024]{1,0:T(8,128)(2,1)}) %all-gather.21.cloned.1.call-update) | async-done | bytes 10485776 | tf_op jit(solution)/shard_map/all_gather | solution.py:230
  509.7 18.6 fusion.258
  528.4 53.7 %all-gather.15.cloned.1.call-done = bf16[5120,1024]{1,0:T(8,128)(2,1)} async-done(((bf16[1280,1024]{1,0:T(8,128)(2,1)}), bf16[5120,1024]{1,0:T(8,128)(2,1)}) %all-gather.15.cloned.1.call-update) | async-done | bytes 10485776 | tf_op jit(solution)/shard_map/all_gather | solution.py:217
  582.0 38.0 %fusion.113 = (bf16[5120,1024]{1,0:T(8,128)(2,1)}, f32[5120,1024]{1,0:T(8,128)}) fusion(f32[5120,1024]{1,0:T(8,128)} %fusion.258, bf16[5120,1024]{1,0:T(8,128)(2,1)} %all-gather.15.cloned.1.call-done, bf16[1024,1024]{1,0:T(8,128)(2,1)} %param.25), kind=kOutput, calls=%fused_computation.133 | convolution fusion | flops 10863247360 | bytes 65011712 | tf_op jit(solution)/shard_map/dot_general | solution.py:218
  620.1 17.5 convolution_convert_fusion.2
  637.6 20.9 convolution_convert_fusion.4
  658.6 64.5 %reduce-scatter.21.cloned.1.call-done = bf16[1280,1024]{1,0:T(8,128)(2,1)} async-done(((bf16[5120,1024]{1,0:T(8,128)(2,1)}), bf16[1280,1024]{1,0:T(8,128)(2,1)}) %reduce-scatter.21.cloned.1.call-update) | async-done | bytes 2621456 | tf_op jit(solution)/shard_map/reduce_scatter | solution.py:235
  728.9 82.3 %reduce-scatter.15.cloned.1.call-done = bf16[1280,1024]{1,0:T(8,128)(2,1)} async-done(((bf16[5120,1024]{1,0:T(8,128)(2,1)}), bf16[1280,1024]{1,0:T(8,128)(2,1)}) %reduce-scatter.15.cloned.1.call-update) | async-done | bytes 2621456 | tf_op jit(solution)/shard_map/reduce_scatter | solution.py:220
  811.2 14.8 multiply_convert_fusion.8
  826.1 17.6 add.645
  843.7 52.7 %all-gather.23.cloned.1.call-done = bf16[5120,1024]{1,0:T(8,128)(2,1)} async-done(((bf16[1280,1024]{1,0:T(8,128)(2,1)}), bf16[5120,1024]{1,0:T(8,128)(2,1)}) %all-gather.23.cloned.1.call-update) | async-done | bytes 10485776 | tf_op jit(solution)/shard_map/all_gather | solution.py:247
  933.2 80.6 %while.63 = (s32[]{:T(128)}, bf16[4,4,320,4,64]{2,4,3,1,0:T(8,128)(2,1)}, bf16[4,4,320,4,64]{2,4,3,1,0:T(8,128)(2,1)}, bf16[4,4,320,4,64]{2,4,3,1,0:T(8,128)(2,1...) while((s32[]{:T(128)}, ...), condition=%wide.wide.region_39.40_spmd, body=%wide.wide.region_36.39_spmd.sunk | while | flops 1077652480 | bytes 87647424 | solution.py:251
  1013.8 9.6 copy.359
  1076.4 14.4 bitcast_convert_fusion
  1091.9 18.9 fusion.213
  1110.8 65.5 %reduce-scatter.23.cloned.1.call-done = bf16[1280,1024]{1,0:T(8,128)(2,1)} async-done(((bf16[5120,1024]{1,0:T(8,128)(2,1)}), bf16[1280,1024]{1,0:T(8,128)(2,1)}) %reduce-scatter.23.cloned.1.call-update) | async-done | bytes 2621456 | tf_op jit(solution)/shard_map/reduce_scatter | solution.py:266
  1186.1 14.3 fusion.181
  1200.5 17.8 add.618
  1218.3 52.5 %all-gather.9.cloned.1.call-done = bf16[5120,1024]{1,0:T(8,128)(2,1)} async-done(((bf16[1280,1024]{1,0:T(8,128)(2,1)}), bf16[5120,1024]{1,0:T(8,128)(2,1)}) %all-gather.9.cloned.1.call-update) | async-done | bytes 10485776 | tf_op jit(solution)/shard_map/all_gather | solution.py:194
  1270.8 11.5 fusion.137
  1341.4 39.9 %while.60 = (s32[]{:T(128)}, bf16[4,4,320,4,64]{2,1,0,4,3:T(4,128)(2,1)}, f32[4,4,4,320,1]{3,2,1,4,0:T(4,128)S(1)}, bf16[4,4,320,4,64]{2,4,3,1,0:T(8,128)(2,1)},...) while((s32[]{:T(128)}, ...), condition=%wide.wide.region_7.8_spmd, body=%wide.wide.region_4.7_spmd.sunk | while | flops 439413760 | bytes 36091020 | solution.py:203
  1397.0 85.4 %reduce-scatter.9.cloned.1.call-done = bf16[1280,1024]{1,0:T(8,128)(2,1)} async-done(((bf16[5120,1024]{1,0:T(8,128)(2,1)}), bf16[1280,1024]{1,0:T(8,128)(2,1)}) %reduce-scatter.9.cloned.1.call-update) | async-done | bytes 2621456 | tf_op jit(solution)/shard_map/reduce_scatter | solution.py:208
  1488.1 10.6 fusion.182
  1499.5 69.6 %all-gather.17.cloned.1.call-done = bf16[5120,1024]{1,0:T(8,128)(2,1)} async-done(((bf16[1280,1024]{1,0:T(8,128)(2,1)}), bf16[5120,1024]{1,0:T(8,128)(2,1)}) %all-gather.17.cloned.1.call-update) | async-done | bytes 10485776 | tf_op jit(solution)/shard_map/all_gather | solution.py:230
  1569.1 18.5 fusion.257
  1587.5 53.4 %all-gather.11.cloned.1.call-done = bf16[5120,1024]{1,0:T(8,128)(2,1)} async-done(((bf16[1280,1024]{1,0:T(8,128)(2,1)}), bf16[5120,1024]{1,0:T(8,128)(2,1)}) %all-gather.11.cloned.1.call-update) | async-done | bytes 10485776 | tf_op jit(solution)/shard_map/all_gather | solution.py:217
  1640.9 37.7 %fusion.109 = (bf16[5120,1024]{1,0:T(8,128)(2,1)}, f32[5120,1024]{1,0:T(8,128)}) fusion(f32[5120,1024]{1,0:T(8,128)} %fusion.257, bf16[5120,1024]{1,0:T(8,128)(2,1)} %all-gather.11.cloned.1.call-done, bf16[1024,1024]{1,0:T(8,128)(2,1)} %param.25), kind=kOutput, calls=%fused_computation.129 | convolution fusion | flops 10863247360 | bytes 65011712 | tf_op jit(solution)/shard_map/dot_general | solution.py:218
  1678.7 17.4 convolution_convert_fusion.3
  1696.1 21.1 convolution_convert_fusion.5
  1717.2 64.3 %reduce-scatter.17.cloned.1.call-done = bf16[1280,1024]{1,0:T(8,128)(2,1)} async-done(((bf16[5120,1024]{1,0:T(8,128)(2,1)}), bf16[1280,1024]{1,0:T(8,128)(2,1)}) %reduce-scatter.17.cloned.1.call-update) | async-done | bytes 2621456 | tf_op jit(solution)/shard_map/reduce_scatter | solution.py:235
  1787.4 82.1 %reduce-scatter.11.cloned.1.call-done = bf16[1280,1024]{1,0:T(8,128)(2,1)} async-done(((bf16[5120,1024]{1,0:T(8,128)(2,1)}), bf16[1280,1024]{1,0:T(8,128)(2,1)}) %reduce-scatter.11.cloned.1.call-update) | async-done | bytes 2621456 | tf_op jit(solution)/shard_map/reduce_scatter | solution.py:220
  1869.5 14.8 multiply_convert_fusion.9
  1884.4 17.6 add.638
  1902.0 52.7 %all-gather.19.cloned.1.call-done = bf16[5120,1024]{1,0:T(8,128)(2,1)} async-done(((bf16[1280,1024]{1,0:T(8,128)(2,1)}), bf16[5120,1024]{1,0:T(8,128)(2,1)}) %all-gather.19.cloned.1.call-update) | async-done | bytes 10485776 | tf_op jit(solution)/shard_map/all_gather | solution.py:247
  1991.5 80.3 %while.62 = (s32[]{:T(128)}, bf16[4,4,320,4,64]{2,4,3,1,0:T(8,128)(2,1)}, bf16[4,4,320,4,64]{2,4,3,1,0:T(8,128)(2,1)}, bf16[4,4,320,4,64]{2,4,3,1,0:T(8,128)(2,1...) while((s32[]{:T(128)}, ...), condition=%wide.wide.region_29.30_spmd, body=%wide.wide.region_26.29_spmd.sunk | while | flops 1077652480 | bytes 87647424 | solution.py:251
  2071.9 9.6 copy.354
  2093.3 9.6 copy.355
  2111.3 9.6 copy.356
  2134.4 14.4 bitcast_convert_fusion.1
  2148.9 14.6 fusion.118
  2180.2 15.3 fusion.260
  2195.5 15.9 add_convert_fusion.1
  2211.3 19.9 fusion.250
  2231.2 20.5 add_convert_fusion
  2259.7 14.3 fusion.200
  2309.3 15.1 fusion.140
  2324.4 15.0 fusion.141
  2349.3 23.4 all-reduce.8.cloned.1.call-done
  2400.0 15.1 reshape.287
  2415.1 71.3 %copy.327 = f32[4,5,8,8,5,8,8]{4,6,1,5,3,2,0:T(8,128)} copy(f32[4,5,8,8,5,8,8]{3,2,1,6,5,4,0:T(8,128)} %reshape.287) | data formatting | bytes 3276800 | tf_op jit(solution)/shard_map/add | solution.py:255
  2486.3 32.1 %convolution_bitcast_fusion.2 = f32[9,4,8,8,8,8]{0,5,4,3,2,1:T(8,128)} fusion(f32[4,5,8,8,5,8,8]{4,6,1,5,3,2,0:T(8,128)} %copy.327, s32[5,5]{1,0:T(8,128)S(1)} %copy-done.54), kind=kOutput, calls=%fused_computation.262 | convolution fusion | flops 44237024 | bytes 2228324 | tf_op jit(solution)/shard_map/hprxqsy,pqt,rsu,xyv->htuv/dot_general | solution.py:64
  2518.4 15.5 copy.328
  2549.2 38.2 %all-reduce = (bf16[4,2025]{1,0:T(4,128)(2,1)S(1)}, bf16[6144]{0:T(1024)(128)(2,1)S(1)}) all-reduce(bf16[4,2025]{1,0:T(4,128)(2,1)S(1)} %convert_element_type.352, bf16[6144]{0:T(1024)(128)(2,1)S(1)} %reduce_sum.266), channel_id=1, replica_groups=mesh['dp'=8,'mp'=4] {'dp'}, use_global_device_ids=true, to_apply=%region_49.50 | all-reduce | flops 14244 | bytes 56976 | tf_op jit(solution)/shard_map/psum | solution.py:305
  2588.7 108.7 %all-reduce.10.cloned.1.call-done = (bf16[3,1024,256]{1,2,0:T(8,128)(2,1)}, bf16[256,1024]{1,0:T(8,128)(2,1)}, bf16[1024,1024]{1,0:T(8,128)(2,1)}, bf16[1024,102...) async-done(((bf16[3,1024,256]{1,2,0:T(8,128)(2,1)}, bf16[256,1024]{1,0:T(8,128)(2,1)}, bf16[1024,1024]{1,0:T(8,128)(2,1)}, ...) | async-done | bytes 9949200 | tf_op jit(solution)/shard_map/psum | solution.py:301
  (458 shorter events, 742.8 us)
Async XLA Ops:
  7.2 40.0 %all-reduce.6.cloned.1.call-start = ((), (), s32[]{:S(2)}) async-start(), calls=%async_computation.8 | async-start | bytes 786432 | tf_op jit(solution)/shard_map/psum | solution.py:173
  10.4 36.8 %copy-start.56 = (f32[6144]{0:T(1024)S(1)}, f32[6144]{0:T(1024)}, u32[]{:S(2)}) copy-start(f32[6144]{0:T(1024)} %param.29) | copy-start | bytes 73732
  11.7 199.5 %all-gather.13.cloned.1.call-start = ((), (), s32[]{:S(2)}) async-start(), calls=%async_computation.13 | async-start | bytes 13107200 | tf_op jit(solution)/shard_map/all_gather | solution.py:194
  16.7 45.1 %copy-start.43 = (f32[1280]{0:T(1024)}, f32[1280]{0:T(1024)S(1)}, u32[]{:S(2)}) copy-start(f32[1280]{0:T(1024)S(1)} %broadcast_multiply_fusion.9) | copy-start | bytes 15364
  18.3 43.6 %copy-start.29 = (s32[1280]{0:T(1024)}, s32[1280]{0:T(1024)S(1)}, u32[]{:S(2)}) copy-start(s32[1280]{0:T(1024)S(1)} %get-tuple-element.506) | copy-start | bytes 15364
  18.3 43.6 %copy-start.49 = (f32[1280]{0:T(1024)}, f32[1280]{0:T(1024)S(1)}, u32[]{:S(2)}) copy-start(f32[1280]{0:T(1024)S(1)} %add_rsqrt_fusion.1) | copy-start | bytes 15364
  61.9 10.4 copy-start.5
  76.0 347.0 %reduce-scatter.13.cloned.1.call-start = ((), (), s32[]{:S(2)}) async-start(), calls=%async_computation.14 | async-start | bytes 13107200 | tf_op jit(solution)/shard_map/reduce_scatter | solution.py:208
  76.5 10.0 copy-start.53
  321.8 15.7 copy-start.27
  337.6 172.2 %all-gather.21.cloned.1.call-start = ((), (), s32[]{:S(2)}) async-start(), calls=%async_computation.21 | async-start | bytes 13107200 | tf_op jit(solution)/shard_map/all_gather | solution.py:230
  428.0 11.3 copy-start.6
  428.0 383.1 %copy-start.33 = (f32[1280]{0:T(1024)}, f32[1280]{0:T(1024)S(1)}, u32[]{:S(2)}) copy-start(f32[1280]{0:T(1024)S(1)} %broadcast_multiply_fusion.8) | copy-start | bytes 15364
  428.7 382.4 %copy-start.39 = (f32[1280]{0:T(1024)}, f32[1280]{0:T(1024)S(1)}, u32[]{:S(2)}) copy-start(f32[1280]{0:T(1024)S(1)} %add_rsqrt_fusion) | copy-start | bytes 15364
  439.4 142.6 %all-gather.15.cloned.1.call-start = ((), (), s32[]{:S(2)}) async-start(), calls=%async_computation.15 | async-start | bytes 13107200 | tf_op jit(solution)/shard_map/all_gather | solution.py:217
  440.0 283.1 %reduce-scatter.21.cloned.1.call-start = ((), (), s32[]{:S(2)}) async-start(), calls=%async_computation.22 | async-start | bytes 13107200 | tf_op jit(solution)/shard_map/reduce_scatter | solution.py:235
  582.0 38.0 %copy-start.58 = (bf16[1024,1024]{1,0:T(8,128)(2,1)S(1)}, bf16[1024,1024]{1,0:T(8,128)(2,1)}, u32[]{:S(2)}) copy-start(bf16[1024,1024]{1,0:T(8,128)(2,1)} %param.25) | copy-start | bytes 6291460
  637.6 173.6 %reduce-scatter.15.cloned.1.call-start = ((), (), s32[]{:S(2)}) async-start(), calls=%async_computation.16 | async-start | bytes 13107200 | tf_op jit(solution)/shard_map/reduce_scatter | solution.py:220
  658.5 237.8 %all-gather.23.cloned.1.call-start = ((), (), s32[]{:S(2)}) async-start(), calls=%async_computation.23 | async-start | bytes 13107200 | tf_op jit(solution)/shard_map/all_gather | solution.py:247
  826.0 350.4 %reduce-scatter.23.cloned.1.call-start = ((), (), s32[]{:S(2)}) async-start(), calls=%async_computation.24 | async-start | bytes 13107200 | tf_op jit(solution)/shard_map/reduce_scatter | solution.py:266
  1090.9 179.9 %all-gather.9.cloned.1.call-start = ((), (), s32[]{:S(2)}) async-start(), calls=%async_computation.9 | async-start | bytes 13107200 | tf_op jit(solution)/shard_map/all_gather | solution.py:194
  1091.7 94.4 %copy-start.41 = (f32[1280]{0:T(1024)}, f32[1280]{0:T(1024)S(1)}, u32[]{:S(2)}) copy-start(f32[1280]{0:T(1024)S(1)} %broadcast_multiply_fusion.11) | copy-start | bytes 15364
  1176.4 6.6 copy-start.14
  1183.0 17.5 copy-start.47
  1200.5 281.9 %reduce-scatter.9.cloned.1.call-start = ((), (), s32[]{:S(2)}) async-start(), calls=%async_computation.10 | async-start | bytes 13107200 | tf_op jit(solution)/shard_map/reduce_scatter | solution.py:208
  1381.4 15.5 copy-start.28
  1396.9 172.2 %all-gather.17.cloned.1.call-start = ((), (), s32[]{:S(2)}) async-start(), calls=%async_computation.17 | async-start | bytes 13107200 | tf_op jit(solution)/shard_map/all_gather | solution.py:230
  1487.3 11.3 copy-start.7
  1487.4 382.1 %copy-start.35 = (f32[1280]{0:T(1024)}, f32[1280]{0:T(1024)S(1)}, u32[]{:S(2)}) copy-start(f32[1280]{0:T(1024)S(1)} %broadcast_multiply_fusion.10) | copy-start | bytes 15364
  1488.1 381.4 %copy-start.45 = (f32[1280]{0:T(1024)}, f32[1280]{0:T(1024)S(1)}, u32[]{:S(2)}) copy-start(f32[1280]{0:T(1024)S(1)} %add_rsqrt_fusion.2) | copy-start | bytes 15364
  1498.7 142.2 %all-gather.11.cloned.1.call-start = ((), (), s32[]{:S(2)}) async-start(), calls=%async_computation.11 | async-start | bytes 13107200 | tf_op jit(solution)/shard_map/all_gather | solution.py:217
  1499.5 282.1 %reduce-scatter.17.cloned.1.call-start = ((), (), s32[]{:S(2)}) async-start(), calls=%async_computation.18 | async-start | bytes 13107200 | tf_op jit(solution)/shard_map/reduce_scatter | solution.py:235
  1640.9 37.7 %copy-start.59 = (bf16[1024,1024]{1,0:T(8,128)(2,1)S(1)}, bf16[1024,1024]{1,0:T(8,128)(2,1)}, u32[]{:S(2)}) copy-start(bf16[1024,1024]{1,0:T(8,128)(2,1)} %param.25) | copy-start | bytes 6291460
  1696.1 173.4 %reduce-scatter.11.cloned.1.call-start = ((), (), s32[]{:S(2)}) async-start(), calls=%async_computation.12 | async-start | bytes 13107200 | tf_op jit(solution)/shard_map/reduce_scatter | solution.py:220
  1717.2 237.5 %all-gather.19.cloned.1.call-start = ((), (), s32[]{:S(2)}) async-start(), calls=%async_computation.19 | async-start | bytes 13107200 | tf_op jit(solution)/shard_map/all_gather | solution.py:247
  1884.4 389.6 %reduce-scatter.19.cloned.1.call-start = ((), (), s32[]{:S(2)}) async-start(), calls=%async_computation.20 | async-start | bytes 13107200 | tf_op jit(solution)/shard_map/reduce_scatter | solution.py:266
  2148.8 223.9 %all-reduce.8.cloned.1.call-start = ((), (), s32[]{:S(2)}) async-start(), calls=%async_computation.25 | async-start | bytes 393216 | tf_op jit(solution)/shard_map/psum | solution.py:291
  2148.9 14.6 copy-start.18
  2163.5 7.2 copy-start.9
  2163.5 16.7 slice-start.9
  2163.5 16.7 slice-start.10
  2173.7 6.5 slice-start.11
  2173.7 21.8 slice-start.6
  2180.2 15.3 slice-start.7
  2180.2 15.3 slice-start.8
  2231.2 20.5 copy-start.15
  2251.7 8.0 copy-start.62
  2259.7 14.3 copy-start.42
  2259.7 14.3 copy-start.48
  2279.3 12.3 slice-start.4
  2279.3 18.7 slice-start
  2282.7 9.0 slice-start.5
  2282.7 9.0 copy-start.19
  2282.7 15.3 slice-start.1
  2294.9 6.7 slice-start.2
  2302.9 6.5 copy-start.32
  2309.3 15.1 copy-start.30
  2340.2 34.4 %copy-start.38 = (f32[2,8,256]{2,1,0:T(8,128)S(1)}, f32[2,8,256]{2,1,0:T(8,128)}, u32[]{:S(2)}) copy-start(f32[2,8,256]{2,1,0:T(8,128)} %copy-done.37) | copy-start | bytes 49156
  2340.2 34.4 %copy-start.57 = (s32[2,8]{1,0:T(2,128)S(1)}, s32[2,8]{1,0:T(2,128)}, u32[]{:S(2)}) copy-start(s32[2,8]{1,0:T(2,128)} %param.33) | copy-start | bytes 196
  2340.2 357.2 %all-reduce.10.cloned.1.call-start = ((), (), s32[]{:S(2)}) async-start(), calls=%async_computation.26 | async-start | bytes 19898368 | tf_op jit(solution)/shard_map/psum | solution.py:301
  2415.1 71.3 %copy-start.54 = (s32[5,5]{1,0:T(8,128)S(1)}, s32[5,5]{1,0:T(8,128)}, u32[]{:S(2)}) copy-start(s32[5,5]{1,0:T(8,128)} %copy-done.53) | copy-start | bytes 304
  2518.4 15.5 copy-start.52
  2543.0 6.1 copy-start.24
  2704.7 6.7 copy-start.22
  (48 other events, 149.8 us)
Sparse Core Ops, SparseCore 0:
  11.9 35.3 all-reduce.5
  76.1 70.1 all-gather.12
  337.7 85.2 reduce-scatter.12
  439.5 70.1 all-gather.20
  511.8 70.1 all-gather.14
  637.7 85.2 reduce-scatter.20
  725.8 85.2 reduce-scatter.14
  826.1 70.1 all-gather.22
  1091.0 85.2 reduce-scatter.22
  1200.6 70.1 all-gather.8
  1397.0 85.2 reduce-scatter.8
  1498.8 70.1 all-gather.16
  1570.7 70.1 all-gather.10
  1696.2 85.2 reduce-scatter.16
  1784.1 85.2 reduce-scatter.10
  1884.5 70.1 all-gather.18
  2148.9 85.2 reduce-scatter.18
  2340.3 32.3 all-reduce.7
  2379.8 317.5 all-reduce.9
where the time goes:
time: 2740 us; the launch traced here: 2720 us
  waiting for transfers between devices  1100 us (40%)
  matrix products  710 us (26%)
  local copies, waits for them, and re-layouts  621 us (23%)
  other arithmetic  239 us (9%)
  blocking collectives  38.2 us (1%)
    reduce_scatter x2, waiting for transfers between devices, body(): lax.psum_scatter(jnp.dot(mixed_rows, out_w, preferred_element_type=jnp.fl...  171 us
    reduce_scatter x2, waiting for transfers between devices, body(): lax.psum_scatter(jnp.dot(activated, down_w, preferred_element_type=jnp.fl...  164 us
    while x7, local copies, waits for them, and re-layouts, body(): lax.map(lambda item_in: attend_forward(item_in, bias_table, score_scale),...  142 us
    all_gather x2, waiting for transfers between devices, body(): grad_mlp_full = lax.all_gather(grad_mlp, 'mp', axis=0, tiled=True)  139 us
    reduce_scatter x2, waiting for transfers between devices, body(): lax.psum_scatter(contract_cols(grad_hidden, up_w).astype(jnp.bfloat16), '...  129 us
    dot_general x8, matrix products, contract_rows(): lax.dot_general(left, right, (((0,), (0,)), ((), ())), precision=precisio...  118 us
    another operation x14, local copies, waits for them, and re-layouts, body(): jnp.stack([grad_queries.reshape(group_rows, head_width), grad_keys.reshap...  111 us
    psum x1, waiting for transfers between devices, body(): lax.psum(acc_qkv.astype(jnp.bfloat16), 'dp').astype(jnp.float32)  109 us
  transfers between devices with their start and end apart: 19, of which 17 were waited for; matrix products, arithmetic and copies ran while one was open for 22% of the time, Pallas kernels for 0%

commit v1 on v0

v1 whole, which is shorter than its diff:
```python
import functools
import math

import jax
import jax.numpy as jnp
from jax import lax
from jax.experimental import pallas as pl
from jax.experimental.pallas import tpu as pltpu
from jax.sharding import PartitionSpec as P

WIN_T = 5
WIN_H = 8
WIN_W = 8
WIN_TOK = WIN_T * WIN_H * WIN_W
FRAME = WIN_H * WIN_W
PAD_TOK = 384
HEAD_DIM = 64
N_TIME, N_ROW, N_COL = 2 * WIN_T - 1, 2 * WIN_H - 1, 2 * WIN_W - 1

BF = jnp.bfloat16
F32 = jnp.float32
epsilon = 1e-06
highest = lax.Precision.HIGHEST
GELU_A = 0.7978845608028654
GELU_B = GELU_A * 0.044715
VMEM_LIMIT = 60 * 1024 * 1024


def dot(left, right, left_dim=1, right_dim=0):
    return lax.dot_general(
        left, right, (((left_dim,), (right_dim,)), ((), ())), preferred_element_type=F32
    )


def params():
    return pltpu.CompilerParams(vmem_limit_bytes=VMEM_LIMIT)


def shaped(shape, dtype):
    return jax.ShapeDtypeStruct(shape, dtype)


def row_spec(rows, cols):
    return pl.BlockSpec((rows, cols), lambda i: (i, 0))


def part_spec(rows, cols):
    return pl.BlockSpec((3, rows, cols), lambda i: (0, i, 0))


def whole_spec(shape):
    return pl.BlockSpec(shape, lambda i: (0,) * len(shape))


def mod_spec(count, cols):
    return pl.BlockSpec((None, count, cols), lambda i: (i, 0, 0))


def cost(flops, nbytes, transcendentals=0):
    return pl.CostEstimate(
        flops=int(flops), bytes_accessed=int(nbytes), transcendentals=int(transcendentals)
    )


def normalise(values):
    centred = values - jnp.mean(values, axis=-1, keepdims=True)
    inverse = lax.rsqrt(jnp.mean(centred * centred, axis=-1, keepdims=True) + epsilon)
    return centred * inverse, inverse


def normalise_back(normed, inverse, grad_in):
    return inverse * (
        grad_in
        - jnp.mean(grad_in, axis=-1, keepdims=True)
        - normed * jnp.mean(grad_in * normed, axis=-1, keepdims=True)
    )


def swap(value, axis, size, bit):
    return lax.ppermute(value, axis, [(i, i ^ bit) for i in range(size)])


def bits_of(size):
    return [1 << b for b in range(size.bit_length() - 1)]


def add_low(left, right):
    return (left.astype(F32) + right.astype(F32)).astype(left.dtype)


def gather_shards(own, axis, size):
    shards = {0: own}
    for bit in bits_of(size):
        for mask in list(shards):
            shards[mask ^ bit] = swap(shards[mask], axis, size, bit)
    return shards


def reduce_shards(terms, axis, size):
    terms = dict(terms)
    for bit in bits_of(size):
        for mask in [m for m in terms if m & bit]:
            terms[mask ^ bit] = add_low(terms[mask ^ bit], swap(terms.pop(mask), axis, size, bit))
    return terms[0]


def reduce_all(value, axis, size):
    for bit in bits_of(size):
        value = add_low(value, swap(value, axis, size, bit))
    return value


def reduce_split(value, axis, size):
    index = lax.axis_index(axis)
    for bit in bits_of(size):
        half = value.shape[0] // 2
        mine = (index // bit) % 2
        keep = lax.dynamic_slice_in_dim(value, mine * half, half, 0)
        send = lax.dynamic_slice_in_dim(value, (1 - mine) * half, half, 0)
        value = add_low(keep, swap(send, axis, size, bit))
    for bit in reversed(bits_of(size)):
        other = swap(value, axis, size, bit)
        first = (index // bit) % 2 == 0
        value = jnp.where(
            first,
            jnp.concatenate([value, other], axis=0),
            jnp.concatenate([other, value], axis=0),
        )
    return value


def place_hot():
    place = jnp.arange(FRAME)
    row, col = place // WIN_W, place % WIN_W
    offset = (row[:, None] - row[None, :] + WIN_H - 1) * N_COL + (
        col[:, None] - col[None, :] + WIN_W - 1
    )
    return (offset.reshape(1, -1) == jnp.arange(N_ROW * N_COL)[:, None]).astype(F32)


def bias_strips(rel_table):
    heads = rel_table.shape[0]

    def strip(cube):
        blocks = lax.dot(cube.reshape(heads * N_TIME, N_ROW * N_COL), place_hot(), precision=highest)
        blocks = blocks.reshape(heads, N_TIME, FRAME, FRAME)[:, ::-1]
        blocks = blocks.transpose(0, 2, 1, 3).reshape(heads, FRAME, N_TIME * FRAME)
        return jnp.pad(blocks, ((0, 0), (0, 0), (0, FRAME)))

    cube = rel_table.reshape(heads, N_TIME, N_ROW * N_COL)
    return strip(cube), strip(cube[:, ::-1, ::-1])


def collect_strips(strip_grad):
    heads = strip_grad.shape[0]
    blocks = strip_grad[:, :, : N_TIME * FRAME].reshape(heads, FRAME, N_TIME, FRAME)
    blocks = blocks.transpose(0, 2, 1, 3).reshape(heads * N_TIME, FRAME * FRAME)
    cube = lax.dot_general(blocks, place_hot(), (((1,), (1,)), ((), ())), precision=highest)
    return cube.reshape(heads, N_TIME, N_ROW * N_COL)[:, :, ::-1].reshape(heads, -1)


def strip_column(frame):
    return (WIN_T - 1 - frame) * FRAME


def spread_strips(strip_ref, table, fill):
    for head in range(table.shape[0]):
        strip = strip_ref[head]
        for frame in range(WIN_T):
            column = strip_column(frame)
            table[head, frame * FRAME : (frame + 1) * FRAME, :WIN_TOK] = strip[
                :, column : column + WIN_TOK
            ]
        table[head, :, WIN_TOK:] = jnp.full((WIN_TOK, PAD_TOK - WIN_TOK), fill, F32)


def norm_kernel(tokens_ref, mod_ref, attn_in_ref):
    normed, _ = normalise(tokens_ref[...].astype(F32))
    attn_in_ref[...] = (normed * (1.0 + mod_ref[1:2]) + mod_ref[0:1]).astype(BF)


def norm_call(tokens, mods):
    rows, width = tokens.shape
    return pl.pallas_call(
        norm_kernel,
        grid=(rows // WIN_TOK,),
        in_specs=[row_spec(WIN_TOK, width), mod_spec(mods.shape[1], width)],
        out_specs=row_spec(WIN_TOK, width),
        out_shape=shaped((rows, width), BF),
        compiler_params=params(),
        cost_estimate=cost(10 * rows * width, 4 * rows * width),
        name="norm_in",
    )(tokens, mods)


def head_copies(value, heads):
    if heads == 1:
        return [value]
    lane = lax.broadcasted_iota(jnp.int32, value.shape, 1) // HEAD_DIM
    return [jnp.where(lane == head, value, jnp.zeros_like(value)) for head in range(heads)]


def pad_rows(value):
    return jnp.concatenate(
        [value, jnp.zeros((PAD_TOK - WIN_TOK, value.shape[1]), value.dtype)], axis=0
    )


def attend_kernel(x_ref, w_ref, strip_ref, qkv_ref, mixed_ref, lse_ref, table, columns):
    heads = strip_ref.shape[0]

    @pl.when(pl.program_id(0) == 0)
    def _():
        spread_strips(strip_ref, table, -1e30)
        columns[...] = jnp.zeros_like(columns)

    x = x_ref[...]
    query = dot(x, w_ref[0]).astype(BF)
    key = dot(x, w_ref[1]).astype(BF)
    value = dot(x, w_ref[2]).astype(BF)
    qkv_ref[0] = query
    qkv_ref[1] = key
    qkv_ref[2] = value
    scaled = query * jnp.asarray(HEAD_DIM**-0.5, BF)
    scores = dot(jnp.concatenate(head_copies(scaled, heads), axis=0), pad_rows(key), 1, 1)
    probs = []
    for head in range(heads):
        score = scores[head * WIN_TOK : (head + 1) * WIN_TOK] + table[head]
        top = jnp.max(score, axis=1, keepdims=True)
        exponent = jnp.exp(score - top)
        total = jnp.sum(exponent, axis=1, keepdims=True)
        probs.append((exponent * (1.0 / total)).astype(BF))
        columns[:WIN_TOK, head : head + 1] = top + jnp.log(total)
    values = jnp.concatenate([pad_rows(part) for part in head_copies(value, heads)], axis=0)
    mixed_ref[...] = dot(jnp.concatenate(probs, axis=1), values).astype(BF)
    lse_ref[...] = columns[...].T[: lse_ref.shape[0]]


def attend_call(attn_in, weight, strip):
    rows, width = attn_in.shape
    cols = weight.shape[2]
    heads = strip.shape[0]
    windows = rows // WIN_TOK
    stat_rows = -(-heads // 8) * 8
    return pl.pallas_call(
        attend_kernel,
        grid=(windows,),
        in_specs=[row_spec(WIN_TOK, width), whole_spec(weight.shape), whole_spec(strip.shape)],
        out_specs=[
            part_spec(WIN_TOK, cols),
            row_spec(WIN_TOK, cols),
            mod_spec(stat_rows, PAD_TOK),
        ],
        out_shape=[
            shaped((3, rows, cols), BF),
            shaped((rows, cols), BF),
            shaped((windows, stat_rows, PAD_TOK), F32),
        ],
        scratch_shapes=[
            pltpu.VMEM((heads, WIN_TOK, PAD_TOK), F32),
            pltpu.VMEM((PAD_TOK, 128), F32),
        ],
        compiler_params=params(),
        cost_estimate=cost(
            6 * rows * width * cols + 16 * rows * PAD_TOK * cols, 2 * rows * width + 8 * rows * cols
        ),
        name="attend",
    )(attn_in, weight, strip)


def attend_back_kernel(
    grad_ref, out_w_ref, qkv_ref, mixed_ref, lse_ref, strip_ref, dqkv_ref, dstrip_ref, table, total
):
    heads = strip_ref.shape[0]
    cols = out_w_ref.shape[0]
    step = pl.program_id(0)

    @pl.when(step == 0)
    def _():
        spread_strips(strip_ref, table, 0.0)
        total[...] = jnp.zeros_like(total)

    grad_mixed = dot(grad_ref[...], out_w_ref[...], 1, 1).astype(BF)
    query = qkv_ref[0]
    key = qkv_ref[1]
    value = qkv_ref[2]
    scale = jnp.asarray(HEAD_DIM**-0.5, BF)
    product = grad_mixed.astype(F32) * mixed_ref[...].astype(F32)
    upper = product.astype(BF)
    lower = (product - upper.astype(F32)).astype(BF)
    head_rows = (lse_ref.shape[0], cols)
    head_hot = (
        lax.broadcasted_iota(jnp.int32, head_rows, 1) // HEAD_DIM
        == lax.broadcasted_iota(jnp.int32, head_rows, 0)
    ).astype(BF)
    inner = dot(head_hot, pad_rows(upper), 1, 1) + dot(head_hot, pad_rows(lower), 1, 1)
    keys = jnp.concatenate(head_copies(key * scale, heads), axis=0)
    values = jnp.concatenate(head_copies(value, heads), axis=0)
    query_pad = pad_rows(query)
    grad_pad = pad_rows(grad_mixed)
    scores = dot(keys, query_pad, 1, 1)
    grad_probs = dot(values, grad_pad, 1, 1)
    probs = []
    grad_scores = []
    for head in range(heads):
        span = slice(head * WIN_TOK, (head + 1) * WIN_TOK)
        prob = jnp.exp(scores[span] + table[head] - lse_ref[head : head + 1, :])
        grad_score = (prob * (grad_probs[span] - inner[head : head + 1, :])).astype(BF)
        probs.append(prob.astype(BF))
        grad_scores.append(grad_score)
        total[head] += grad_score.astype(F32)
    wide = jnp.concatenate(grad_scores, axis=1)
    grad_value = dot(
        jnp.concatenate(probs, axis=1), jnp.concatenate(head_copies(grad_pad, heads), axis=0)
    )
    grad_key = dot(wide, jnp.concatenate(head_copies(query_pad * scale, heads), axis=0))
    grad_query = dot(jnp.concatenate(grad_scores, axis=0), keys, 0, 0)[:WIN_TOK]
    dqkv_ref[0] = grad_query.astype(BF)
    dqkv_ref[1] = grad_key.astype(BF)
    dqkv_ref[2] = grad_value.astype(BF)

    @pl.when(step == pl.num_programs(0) - 1)
    def _():
        dstrip_ref[...] = jnp.zeros_like(dstrip_ref)
        for head in range(heads):
            for frame in range(WIN_T):
                column = strip_column(frame)
                dstrip_ref[head, :, column : column + WIN_TOK] += total[
                    head, frame * FRAME : (frame + 1) * FRAME, :WIN_TOK
                ]


def attend_back_call(grad_attn, out_weight, qkv, mixed, lse, strip):
    rows, width = grad_attn.shape
    cols = out_weight.shape[0]
    heads = strip.shape[0]
    return pl.pallas_call(
        attend_back_kernel,
        grid=(rows // WIN_TOK,),
        in_specs=[
            row_spec(WIN_TOK, width),
            whole_spec(out_weight.shape),
            part_spec(WIN_TOK, cols),
            row_spec(WIN_TOK, cols),
            mod_spec(lse.shape[1], PAD_TOK),
            whole_spec(strip.shape),
        ],
        out_specs=[part_spec(WIN_TOK, cols), whole_spec(strip.shape)],
        out_shape=[shaped((3, rows, cols), BF), shaped(strip.shape, F32)],
        scratch_shapes=[pltpu.VMEM((heads, WIN_TOK, PAD_TOK), F32)] * 2,
        compiler_params=params(),
        cost_estimate=cost(
            2 * rows * width * cols + 40 * rows * PAD_TOK * cols, 2 * rows * width + 14 * rows * cols
        ),
        name="attend_back",
    )(grad_attn, out_weight, qkv, mixed, lse, strip)


def middle_kernel(*refs, count):
    mixed_refs = refs[:count]
    weight_refs = refs[count : 2 * count]
    tokens_ref, cot_ref, mod_ref, attn_out_ref, mlp_in_ref, grad_mlp_ref = refs[2 * count :]
    attn_out = dot(mixed_refs[0][...], weight_refs[0][...])
    for mixed_ref, weight_ref in zip(mixed_refs[1:], weight_refs[1:]):
        attn_out = attn_out + dot(mixed_ref[...], weight_ref[...])
    attn_out_ref[...] = attn_out
    resid = tokens_ref[...].astype(F32) + mod_ref[2:3] * attn_out
    normed, _ = normalise(resid)
    mlp_in_ref[...] = (normed * (1.0 + mod_ref[4:5]) + mod_ref[3:4]).astype(BF)
    grad_mlp_ref[...] = (mod_ref[5:6] * cot_ref[...].astype(F32)).astype(BF)


def middle_call(mixed, weights, tokens, cotangent, mods):
    rows, width = tokens.shape
    count = len(mixed)
    row = row_spec(WIN_TOK, width)
    return pl.pallas_call(
        functools.partial(middle_kernel, count=count),
        grid=(rows // WIN_TOK,),
        in_specs=[row_spec(WIN_TOK, part.shape[1]) for part in mixed]
        + [whole_spec(part.shape) for part in weights]
        + [row, row, mod_spec(mods.shape[1], width)],
        out_specs=[row, row, row],
        out_shape=[
            shaped((rows, width), F32),
            shaped((rows, width), BF),
            shaped((rows, width), BF),
        ],
        compiler_params=params(),
        cost_estimate=cost(2 * rows * width * width, 16 * rows * width),
        name="middle",
    )(*mixed, *weights, tokens, cotangent, mods)


def mlp_kernel(*refs, chunk, first):
    if first:
        x_ref, g_ref, up_ref, down_ref, out_ref, gin_ref, ddown_ref, dup_ref = refs[:8]
    else:
        x_ref, g_ref, up_ref, down_ref, out_in, gin_in, out_ref, gin_ref, ddown_ref, dup_ref = refs[
            :10
        ]
    act, ghid, down_total, up_total = refs[-4:]
    step = pl.program_id(0)
    hidden_width = up_ref.shape[1]
    x = x_ref[...]
    g = g_ref[...]
    for start in range(0, hidden_width, chunk):
        span = slice(start, start + chunk)
        hidden = dot(x, up_ref[:, span])
        grad_act = dot(g, down_ref[span, :], 1, 1)
        square = hidden * hidden
        tanh = jnp.tanh(hidden * (GELU_A + GELU_B * square))
        half = 0.5 * hidden
        act[:, span] = (half + half * tanh).astype(BF)
        slope = 0.5 + 0.5 * tanh + half * (1.0 - tanh * tanh) * (GELU_A + 3.0 * GELU_B * square)
        ghid[:, span] = (grad_act * slope).astype(BF)
    out = dot(act[...], down_ref[...])
    gin = dot(ghid[...], up_ref[...], 1, 1)
    if first:
        out_ref[...] = out
        gin_ref[...] = gin
    else:
        out_ref[...] = out_in[...] + out
        gin_ref[...] = gin_in[...] + gin

    @pl.when(step == 0)
    def _():
        down_total[...] = dot(act[...], g, 0, 0)
        up_total[...] = dot(x, ghid[...], 0, 0)

    @pl.when(step > 0)
    def _():
        down_total[...] += dot(act[...], g, 0, 0)
        up_total[...] += dot(x, ghid[...], 0, 0)

    @pl.when(step == pl.num_programs(0) - 1)
    def _():
        ddown_ref[...] = down_total[...].astype(BF)
        dup_ref[...] = up_total[...].astype(BF)


def mlp_call(x, g, up, down, sums):
    rows, width = x.shape
    hidden = up.shape[1]
    block = 512 if rows % 512 == 0 else WIN_TOK
    row = row_spec(block, width)
    first = sums is None
    extra = () if first else tuple(sums)
    return pl.pallas_call(
        functools.partial(mlp_kernel, chunk=min(512, hidden), first=first),
        grid=(rows // block,),
        in_specs=[row, row, whole_spec(up.shape), whole_spec(down.shape)] + [row] * len(extra),
        out_specs=[row, row, whole_spec(down.shape), whole_spec(up.shape)],
        out_shape=[
            shaped((rows, width), F32),
            shaped((rows, width), F32),
            shaped(down.shape, BF),
            shaped(up.shape, BF),
        ],
        scratch_shapes=[
            pltpu.VMEM((block, hidden), BF),
            pltpu.VMEM((block, hidden), BF),
            pltpu.VMEM(down.shape, F32),
            pltpu.VMEM(up.shape, F32),
        ],
        input_output_aliases={} if first else {4: 0, 5: 1},
        compiler_params=params(),
        cost_estimate=cost(
            12 * rows * width * hidden, 20 * rows * width + 8 * width * hidden, rows * hidden
        ),
        name="mlp",
    )(x, g, up, down, *extra)


def middle_back_kernel(
    tokens_ref, cot_ref, attn_out_ref, mlp_out_ref, gin_ref, mod_ref, out_ref, gres_ref, gattn_ref, sums_ref
):
    cot = cot_ref[...].astype(F32)
    attn_out = attn_out_ref[...]
    mlp_out = mlp_out_ref[...]
    gin = gin_ref[...]
    resid = tokens_ref[...].astype(F32) + mod_ref[2:3] * attn_out
    out_ref[...] = (resid + mod_ref[5:6] * mlp_out).astype(BF)
    normed, inverse = normalise(resid)
    gres = cot + normalise_back(normed, inverse, gin * (1.0 + mod_ref[4:5]))
    gres_ref[...] = gres
    gattn_ref[...] = (mod_ref[2:3] * gres).astype(BF)
    sums_ref[0:1] = jnp.sum(gres * attn_out, axis=0, keepdims=True)
    sums_ref[1:2] = jnp.sum(gin, axis=0, keepdims=True)
    sums_ref[2:3] = jnp.sum(gin * normed, axis=0, keepdims=True)
    sums_ref[3:4] = jnp.sum(cot * mlp_out, axis=0, keepdims=True)


def middle_back_call(tokens, cotangent, attn_out, mlp_out, gin, mods):
    rows, width = tokens.shape
    row = row_spec(WIN_TOK, width)
    windows = rows // WIN_TOK
    return pl.pallas_call(
        middle_back_kernel,
        grid=(windows,),
        in_specs=[row] * 5 + [mod_spec(mods.shape[1], width)],
        out_specs=[row, row, row, mod_spec(4, width)],
        out_shape=[
            shaped((rows, width), BF),
            shaped((rows, width), F32),
            shaped((rows, width), BF),
            shaped((windows, 4, width), F32),
        ],
        compiler_params=params(),
        cost_estimate=cost(40 * rows * width, 24 * rows * width),
        name="middle_back",
    )(tokens, cotangent, attn_out, mlp_out, gin, mods)


def last_kernel(*refs, count):
    dqkv_refs = refs[:count]
    weight_refs = refs[count : 2 * count]
    tokens_ref, gres_ref, mod_ref, out_ref, sums_ref = refs[2 * count :]
    gin = None
    for dqkv_ref, weight_ref in zip(dqkv_refs, weight_refs):
        for part in range(3):
            term = dot(dqkv_ref[part], weight_ref[part], 1, 1)
            gin = term if gin is None else gin + term
    normed, inverse = normalise(tokens_ref[...].astype(F32))
    out_ref[...] = (
        gres_ref[...] + normalise_back(normed, inverse, gin * (1.0 + mod_ref[1:2]))
    ).astype(BF)
    sums_ref[0:1] = jnp.sum(gin, axis=0, keepdims=True)
    sums_ref[1:2] = jnp.sum(gin * normed, axis=0, keepdims=True)


def last_call(dqkv, weights, tokens, gres, mods):
    rows, width = tokens.shape
    count = len(dqkv)
    row = row_spec(WIN_TOK, width)
    windows = rows // WIN_TOK
    return pl.pallas_call(
        functools.partial(last_kernel, count=count),
        grid=(windows,),
        in_specs=[part_spec(WIN_TOK, part.shape[2]) for part in dqkv]
        + [whole_spec(part.shape) for part in weights]
        + [row, row, mod_spec(mods.shape[1], width)],
        out_specs=[row, mod_spec(2, width)],
        out_shape=[shaped((rows, width), BF), shaped((windows, 2, width), F32)],
        compiler_params=params(),
        cost_estimate=cost(6 * rows * width * width, 16 * rows * width),
        name="last",
    )(*dqkv, *weights, tokens, gres, mods)


def body(
    n_dp,
    n_mp,
    tokens,
    cotangent,
    qkv_weight,
    out_weight,
    up_weight,
    down_weight,
    rel_bias,
    ada_weight,
    ada_bias,
    class_embed,
    window_clip,
    timesteps,
    class_ids,
):
    mp_index = lax.axis_index("mp")
    micro, local_rows, width = tokens.shape
    local_cols = class_embed.shape[1]
    clips = timesteps.shape[1]
    own_windows = local_rows // WIN_TOK
    rows = micro * local_rows
    tokens_flat = tokens.reshape(rows, width)
    cot_flat = cotangent.reshape(rows, width)
    masks = range(n_mp)
    order = sorted(masks, key=lambda m: int(format(m, "010b")[::-1], 2), reverse=True)

    columns = mp_index * local_cols + jnp.arange(local_cols)
    half_width = width // 2
    freq_index = (columns % half_width).astype(F32)
    frequency = jnp.exp(-math.log(10000.0) * freq_index / half_width)
    angle = timesteps.astype(F32)[..., None] * frequency
    step_embed = jnp.where(columns < half_width, jnp.sin(angle), jnp.cos(angle))
    class_hot = (class_ids[..., None] == jnp.arange(class_embed.shape[0])).astype(F32)
    condition = step_embed + jnp.einsum("mck,kd->mcd", class_hot, class_embed, precision=highest)
    lowered = jax.nn.silu(condition).astype(BF)
    mod_terms = jnp.einsum("mcd,de->mce", lowered, ada_weight, preferred_element_type=F32)
    modulation = reduce_all(mod_terms, "mp", n_mp) + ada_bias
    own_clip = lax.dynamic_slice_in_dim(window_clip, mp_index * own_windows, own_windows, 1)
    clip_hot = (own_clip[..., None] == jnp.arange(clips)).astype(F32)
    mods = jnp.einsum("mwc,mce->mwe", clip_hot, modulation, precision=highest)
    mods = mods.reshape(micro * own_windows, 6, width)

    qkv_w = gather_shards(qkv_weight, "mp", n_mp)
    rel_tables = gather_shards(rel_bias, "mp", n_mp)
    out_w = gather_shards(out_weight, "mp", n_mp)
    up_w = gather_shards(up_weight, "mp", n_mp)
    down_w = gather_shards(down_weight, "mp", n_mp)
    heads = rel_bias.shape[0]
    strips, strips_back = bias_strips(jnp.concatenate([rel_tables[m] for m in masks], axis=0))

    attn_in = norm_call(tokens_flat, mods)
    qkv, mixed, lse = {}, {}, {}
    for m in masks:
        qkv[m], mixed[m], lse[m] = attend_call(
            attn_in, qkv_w[m], strips[m * heads : (m + 1) * heads]
        )
    attn_out, mlp_in, grad_mlp = middle_call(
        [mixed[m] for m in masks], [out_w[m] for m in masks], tokens_flat, cot_flat, mods
    )
    sums = None
    down_terms, up_terms = {}, {}
    for m in order:
        mlp_out, gin, down_terms[m], up_terms[m] = mlp_call(
            mlp_in, grad_mlp, up_w[m], down_w[m], sums
        )
        sums = (mlp_out, gin)
    block_out, grad_resid, grad_attn, late_sums = middle_back_call(
        tokens_flat, cot_flat, attn_out, mlp_out, gin, mods
    )

    dqkv, qkv_terms, out_terms, rel_terms = {}, {}, {}, {}
    for m in order:
        out_terms[m] = dot(mixed[m], grad_attn, 0, 0).astype(BF)
        dqkv[m], strip_grad = attend_back_call(
            grad_attn, out_w[m], qkv[m], mixed[m], lse[m], strips_back[m * heads : (m + 1) * heads]
        )
        rel_terms[m] = collect_strips(strip_grad).astype(BF)
        qkv_terms[m] = jnp.einsum(
            "rd,sre->sde", attn_in, dqkv[m], preferred_element_type=F32
        ).astype(BF)
    token_grad, early_sums = last_call(
        [dqkv[m] for m in masks], [qkv_w[m] for m in masks], tokens_flat, grad_resid, mods
    )

    def total(terms):
        shard = reduce_shards(terms, "mp", n_mp)
        flat = shard.reshape(-1, shard.shape[-1])
        return reduce_split(flat, "dp", n_dp).reshape(shard.shape).astype(F32)

    down_grad = total(down_terms)
    up_grad = total(up_terms)
    out_grad = total(out_terms)
    qkv_grad = total(qkv_terms)
    rel_grad = reduce_all(reduce_shards(rel_terms, "mp", n_mp), "dp", n_dp).astype(F32)

    def clip_sums(window_sums):
        count = window_sums.shape[1]
        grouped = window_sums.reshape(micro, own_windows, count * width)
        part = jnp.einsum("mwc,mwe->mce", clip_hot, grouped, precision=highest).astype(BF)
        part = reduce_all(reduce_all(part, "mp", n_mp), "dp", n_dp)
        return part.astype(F32).reshape(micro, clips, count, width)

    late = clip_sums(late_sums)
    early = clip_sums(early_sums)
    mod_total = jnp.concatenate(
        [early, late[:, :, 0:1], late[:, :, 1:4]], axis=2
    ).reshape(micro, clips, 6 * width)
    ada_bias_grad = jnp.sum(mod_total, axis=(0, 1))
    ada_weight_grad = jnp.einsum(
        "mcd,mce->de", lowered.astype(F32), mod_total, precision=highest
    )
    grad_lowered = jnp.einsum(
        "mce,de->mcd", mod_total, ada_weight.astype(F32), precision=highest
    )
    grad_condition = jax.vjp(jax.nn.silu, condition)[1](grad_lowered)[0]
    class_grad = jnp.einsum("mck,mcd->kd", class_hot, grad_condition, precision=highest)
    return (
        block_out.reshape(tokens.shape),
        token_grad.reshape(tokens.shape),
        qkv_grad,
        out_grad,
        up_grad,
        down_grad,
        rel_grad,
        ada_weight_grad,
        ada_bias_grad,
        class_grad,
    )


def solution(mesh):
    rows = P(None, ("dp", "mp"), None)
    in_specs = (
        rows,
        rows,
        P(None, None, "mp"),
        P("mp", None),
        P(None, "mp"),
        P("mp", None),
        P("mp", None),
        P("mp", None),
        P(),
        P(None, "mp"),
        P(None, "dp"),
        P(),
        P(),
    )
    out_specs = (
        rows,
        rows,
        P(None, None, "mp"),
        P("mp", None),
        P(None, "mp"),
        P("mp", None),
        P("mp", None),
        P("mp", None),
        P(),
        P(None, "mp"),
    )
    step = functools.partial(body, mesh.shape["dp"], mesh.shape["mp"])
    return jax.shard_map(step, mesh=mesh, in_specs=in_specs, out_specs=out_specs, check_vma=False)
```

time: 2740 us -> 1110 us (0.41)
  waiting for transfers between devices: 1100 us -> 391 us
  matrix products: 710 us -> 87 us
  local copies, waits for them, and re-layouts: 621 us -> 82.3 us
  Pallas kernels: 0 us -> 426 us
  other arithmetic: 239 us -> 37 us
  starting transfers between devices: 1.4 us -> 73.1 us
  blocking collectives: 38.2 us -> 0 us
    dot_general x93 -> x20, matrix products: 706 us -> 83.6 us  [the longest x4 36.7 us: body(): jnp.einsum('rd,sre->sde', attn_in, dqkv[m], preferred_element_type=F32)]
    reduce_scatter x8 -> x0, waiting for transfers between devices: 530 us -> none  [the longest x2 171 us: body(): lax.psum_scatter(jnp.dot(mixed_rows, out_w, preferred_element_type=jnp.fl...]
    pallas_call x0 -> x16, Pallas kernels: none -> 426 us  [the longest x4 181 us: mlp_call(): pl.pallas_call(functools.partial(mlp_kernel, chunk=min(512, hidden), firs...]
    all_gather x8 -> x0, waiting for transfers between devices: 404 us -> none  [the longest x2 139 us: body(): grad_mlp_full = lax.all_gather(grad_mlp, 'mp', axis=0, tiled=True)]
    ppermute x0 -> x69, waiting for transfers between devices: none -> 391 us  [swap(): return lax.ppermute(value, axis, [(i, i ^ bit) for i in range(size)])]
    while x57 -> x0, local copies, waits for them, and re-layouts: 163 us -> none  [the longest x7 142 us: body(): lax.map(lambda item_in: attend_forward(item_in, bias_table, score_scale),...]
    psum x3 -> x0, waiting for transfers between devices: 161 us -> none  [the longest x1 109 us: body(): lax.psum(acc_qkv.astype(jnp.bfloat16), 'dp').astype(jnp.float32)]
    add x6 -> x1, local copies, waits for them, and re-layouts: 156 us -> 0.68 us  [place_hot(): (row[:, None] - row[None, :] + WIN_H - 1) * N_COL]
  transfers between devices with their start and end apart: 19 -> 69, of which waited for: 17 -> 31; matrix products, arithmetic and copies ran while one was open for 22% -> 16% of each run, Pallas kernels for 0% -> 24%
where the time goes in v1:
time: 1110 us; the launch traced here: 1100 us
  Pallas kernels  426 us (38%)
  waiting for transfers between devices  391 us (35%)
  matrix products  87 us (8%)
  local copies, waits for them, and re-layouts  82.3 us (7%)
  starting transfers between devices  73.1 us (7%)
  other arithmetic  37 us (3%)
    ppermute x69, waiting for transfers between devices, swap(): return lax.ppermute(value, axis, [(i, i ^ bit) for i in range(size)])  391 us
    pallas_call x4, Pallas kernels, mlp_call(): pl.pallas_call(functools.partial(mlp_kernel, chunk=min(512, hidden), firs...  181 us
    pallas_call x4, Pallas kernels, attend_back_call(): pl.pallas_call(attend_back_kernel, grid=(rows // WIN_TOK,), in_specs=[row...  91.8 us
    pallas_call x4, Pallas kernels, attend_call(): pl.pallas_call(attend_kernel, grid=(windows,), in_specs=[row_spec(WIN_TOK...  76 us
    ppermute x69, starting transfers between devices, swap(): return lax.ppermute(value, axis, [(i, i ^ bit) for i in range(size)])  73.1 us
    dot_general x4, matrix products, body(): jnp.einsum('rd,sre->sde', attn_in, dqkv[m], preferred_element_type=F32)  36.7 us
    pallas_call x1, Pallas kernels, last_call(): pl.pallas_call(functools.partial(last_kernel, count=count), grid=(windows...  27.8 us
    pallas_call x1, Pallas kernels, middle_back_call(): pl.pallas_call(middle_back_kernel, grid=(windows,), in_specs=[row] * 5 +...  24.4 us
  transfers between devices with their start and end apart: 69, of which 31 were waited for; matrix products, arithmetic and copies ran while one was open for 16% of the time, Pallas kernels for 24%

profile of v1, /device:TPU:0, one launch (start us, length us, event | category | flops | bytes accessed | tf_op | source)
XLA Modules:
  0.0 1098.8 jit_solution(15101459149894421368)
XLA Ops:
  10.9 30.6 %collective-permute-done.4 = f32[4,2025]{1,0:T(4,128)S(1)} collective-permute-done((f32[4,2025]{1,0:T(4,128)S(1)}, f32[4,2025]{1,0:T(4,128)S(1)}, u32[]{:S(2)}, u32[]{:S(2)}) %collective-permute-start.4) | collective-permute-done | bytes 32432 | tf_op jit(solution)/shard_map/ppermute | solution.py:80
  43.3 5.1 fusion.9
  50.5 4.8 reverse_bitcast_fusion.1
  55.3 3.4 fusion.12
  63.0 6.4 copy.40
  69.4 5.4 copy.41
  74.8 6.4 copy.43
  81.2 5.4 copy.44
  86.6 3.4 pad_slice_fusion.4
  95.6 8.5 norm_in.1.x_ref
  105.5 18.9 %attend.4 = (bf16[3,2560,256]{2,1,0:T(8,128)(2,1)}, bf16[2560,256]{1,0:T(8,128)(2,1)}, f32[8,8,384]{2,1,0:T(8,128)}) custom-call(bf16[2560,1024]{1,0:T(8,128)(2,1)} %norm_in.1.x_ref, bf16[3,1024,256]{2,1,0:T(8,128)(2,1)} %refs_4_.3, f32[4,64,640]{2,1,0:T(8,128)} %get-tuple-element.107.strip_ref), custom_call_target="tpu_custom_call" | custom-call | flops 8053063680 | bytes 10485760 | tf_op jit(solution)/shard_map/attend/pallas_call | solution.py:245
  126.5 19.1 %attend.5 = (bf16[3,2560,256]{2,1,0:T(8,128)(2,1)}, bf16[2560,256]{1,0:T(8,128)(2,1)}, f32[8,8,384]{2,1,0:T(8,128)}) custom-call(bf16[2560,1024]{1,0:T(8,128)(2,1)} %norm_in.1.x_ref, bf16[3,1024,256]{2,1,0:T(8,128)(2,1)} %collective-permute-done.5.w_ref.refs_5_, f32[4,64,640]{2,1,0:T(8,128)} %get-tuple-element.105.strip_ref), custom_call_target="tpu_custom_call" | custom-call | flops 8053063680 | bytes 10485760 | tf_op jit(solution)/shard_map/attend/pallas_call | solution.py:245
  146.4 19.0 %attend.6 = (bf16[3,2560,256]{2,1,0:T(8,128)(2,1)}, bf16[2560,256]{1,0:T(8,128)(2,1)}, f32[8,8,384]{2,1,0:T(8,128)}) custom-call(bf16[2560,1024]{1,0:T(8,128)(2,1)} %norm_in.1.x_ref, bf16[3,1024,256]{2,1,0:T(8,128)(2,1)} %collective-permute-done.6.w_ref.refs_6_, f32[4,64,640]{2,1,0:T(8,128)} %get-tuple-element.106.strip_ref), custom_call_target="tpu_custom_call" | custom-call | flops 8053063680 | bytes 10485760 | tf_op jit(solution)/shard_map/attend/pallas_call | solution.py:245
  167.4 19.0 %attend.7 = (bf16[3,2560,256]{2,1,0:T(8,128)(2,1)}, bf16[2560,256]{1,0:T(8,128)(2,1)}, f32[8,8,384]{2,1,0:T(8,128)}) custom-call(bf16[2560,1024]{1,0:T(8,128)(2,1)} %norm_in.1.x_ref, bf16[3,1024,256]{2,1,0:T(8,128)(2,1)} %collective-permute-done.7.w_ref.refs_7_, f32[4,64,640]{2,1,0:T(8,128)} %get-tuple-element.104.strip_ref), custom_call_target="tpu_custom_call" | custom-call | flops 8053063680 | bytes 10485760 | tf_op jit(solution)/shard_map/attend/pallas_call | solution.py:245
  186.4 56.3 %collective-permute-done.9.refs_6_.out_w_ref = bf16[256,1024]{1,0:T(8,128)(2,1)S(1)} collective-permute-done((bf16[256,1024]{1,0:T(8,128)(2,1)}, bf16[256,1024]{1,0:T(8,128)(2,1)S(1)}, u32[]{:S(2)}, u32[]{:S(2)}) %collective-permute-start.9) | collective-permute-done | bytes 524320 | tf_op jit(solution)/shard_map/ppermute | solution.py:80
  244.0 54.9 %collective-permute-done.10.refs_7_.out_w_ref = bf16[256,1024]{1,0:T(8,128)(2,1)} collective-permute-done((bf16[256,1024]{1,0:T(8,128)(2,1)}, bf16[256,1024]{1,0:T(8,128)(2,1)}, u32[]{:S(2)}, u32[]{:S(2)}) %collective-permute-start.10) | collective-permute-done | bytes 524320 | tf_op jit(solution)/shard_map/ppermute | solution.py:80
  298.9 16.6 %middle.1 = (f32[2560,1024]{1,0:T(8,128)}, bf16[2560,1024]{1,0:T(8,128)(2,1)}, bf16[2560,1024]{1,0:T(8,128)(2,1)}) custom-call(bf16[2560,256]{1,0:T(8,128)(2,1)} %get-tuple-element.55.refs_0_.mixed_ref, bf16[2560,256]{1,0:T(8,128)(2,1)} %get-tuple-element.56.refs_1_.mixed_ref, bf16[2560,256]{1,0:T(8,128)(2,1)} %get-tuple-element.57.refs_2_.mixed_ref, ...), custom_call_target="tpu_custom_call" | custom-call | flops 5368709120 | bytes 41943040 | tf_op jit(solution)/shard_map/middle/pallas_call | solution.py:377
  315.5 44.0 %mlp.4 = (f32[2560,1024]{1,0:T(8,128)}, f32[2560,1024]{1,0:T(8,128)}, bf16[1024,1024]{1,0:T(8,128)(2,1)}, bf16[1024,1024]{1,0:T(8,128)(2,1)}) custom-call(bf16[2560,1024]{1,0:T(8,128)(2,1)} %get-tuple-element.60.refs_0_, bf16[2560,1024]{1,0:T(8,128)(2,1)} %get-tuple-element.61.refs_1_, bf16[1024,1024]{1,0:T(8,128)(2,1)} %collective-permute-done.15.refs_2_, ...), custom_call_target="tpu_custom_call" | custom-call | flops 32212254720 | bytes 60817408 | tf_op jit(solution)/shard_map/mlp/pallas_call | solution.py:449
  359.5 45.7 %mlp.5 = (f32[2560,1024]{1,0:T(8,128)}, f32[2560,1024]{1,0:T(8,128)}, bf16[1024,1024]{1,0:T(8,128)(2,1)}, bf16[1024,1024]{1,0:T(8,128)(2,1)}) custom-call(bf16[2560,1024]{1,0:T(8,128)(2,1)} %get-tuple-element.60.refs_0_, bf16[2560,1024]{1,0:T(8,128)(2,1)} %get-tuple-element.61.refs_1_, ...), custom_call_target="tpu_custom_call", output_to_operand_aliasing={{0}: (4, {}), {1}: (5, {})} | custom-call | flops 32212254720 | bytes 60817408 | tf_op jit(solution)/shard_map/mlp/pallas_call | solution.py:449
  405.2 45.6 %mlp.6 = (f32[2560,1024]{1,0:T(8,128)}, f32[2560,1024]{1,0:T(8,128)}, bf16[1024,1024]{1,0:T(8,128)(2,1)}, bf16[1024,1024]{1,0:T(8,128)(2,1)}) custom-call(bf16[2560,1024]{1,0:T(8,128)(2,1)} %get-tuple-element.60.refs_0_, bf16[2560,1024]{1,0:T(8,128)(2,1)} %get-tuple-element.61.refs_1_, ...), custom_call_target="tpu_custom_call", output_to_operand_aliasing={{0}: (4, {}), {1}: (5, {})} | custom-call | flops 32212254720 | bytes 60817408 | tf_op jit(solution)/shard_map/mlp/pallas_call | solution.py:449
  450.8 45.9 %mlp.7 = (f32[2560,1024]{1,0:T(8,128)}, f32[2560,1024]{1,0:T(8,128)}, bf16[1024,1024]{1,0:T(8,128)(2,1)}, bf16[1024,1024]{1,0:T(8,128)(2,1)}) custom-call(bf16[2560,1024]{1,0:T(8,128)(2,1)} %get-tuple-element.60.refs_0_, bf16[2560,1024]{1,0:T(8,128)(2,1)} %get-tuple-element.61.refs_1_, ...), custom_call_target="tpu_custom_call", output_to_operand_aliasing={{0}: (4, {}), {1}: (5, {})} | custom-call | flops 32212254720 | bytes 60817408 | tf_op jit(solution)/shard_map/mlp/pallas_call | solution.py:449
  496.7 24.4 %middle_back.1 = (bf16[2560,1024]{1,0:T(8,128)(2,1)}, f32[2560,1024]{1,0:T(8,128)}, bf16[2560,1024]{1,0:T(8,128)(2,1)}, f32[8,4,1024]{2,1,0:T(4,128)}) custom-call(bf16[2560,1024]{1,0:T(8,128)(2,1)} %bitcast.130, bf16[2560,1024]{1,0:T(8,128)(2,1)} %bitcast.138, f32[2560,1024]{1,0:T(8,128)} %get-tuple-element.59.attn_out_ref, ...), custom_call_target="tpu_custom_call" | custom-call | flops 104857600 | bytes 62914560 | tf_op jit(solution)/shard_map/middle_back/pallas_call | solution.py:498
  521.2 5.4 convolution_convert_fusion.2
  528.9 22.8 %attend_back.6 = (bf16[3,2560,256]{2,1,0:T(8,128)(2,1)}, f32[4,64,640]{2,1,0:T(8,128)}) custom-call(bf16[2560,1024]{1,0:T(8,128)(2,1)} %get-tuple-element.71.grad_ref, bf16[256,1024]{1,0:T(8,128)(2,1)} %copy-done.24, bf16[3,2560,256]{2,1,0:T(8,128)(2,1)} %get-tuple-element.78.qkv_ref, bf16[2560,256]{1,0:T(8,128)(2,1)} %get-tuple-element.57.refs_2_.mixed_ref, ...), custom_call_target="tpu_custom_call" | custom-call | flops 11408506880 | bytes 14417920 | tf_op jit(solution)/shard_map/attend_back/pallas_call | solution.py:337
  551.7 9.1 fusion.43
  560.8 23.0 %attend_back.7 = (bf16[3,2560,256]{2,1,0:T(8,128)(2,1)}, f32[4,64,640]{2,1,0:T(8,128)}) custom-call(bf16[2560,1024]{1,0:T(8,128)(2,1)} %get-tuple-element.71.grad_ref, bf16[256,1024]{1,0:T(8,128)(2,1)} %collective-permute-done.10.refs_7_.out_w_ref, bf16[3,2560,256]{2,1,0:T(8,128)(2,1)} %get-tuple-element.81.qkv_ref, ...), custom_call_target="tpu_custom_call" | custom-call | flops 11408506880 | bytes 14417920 | tf_op jit(solution)/shard_map/attend_back/pallas_call | solution.py:337
  583.8 9.2 fusion.49
  593.0 22.8 %attend_back.5 = (bf16[3,2560,256]{2,1,0:T(8,128)(2,1)}, f32[4,64,640]{2,1,0:T(8,128)}) custom-call(bf16[2560,1024]{1,0:T(8,128)(2,1)} %get-tuple-element.71.grad_ref, bf16[256,1024]{1,0:T(8,128)(2,1)} %collective-permute-done.8.refs_5_.out_w_ref, bf16[3,2560,256]{2,1,0:T(8,128)(2,1)} %get-tuple-element.75.qkv_ref, ...), custom_call_target="tpu_custom_call" | custom-call | flops 11408506880 | bytes 14417920 | tf_op jit(solution)/shard_map/attend_back/pallas_call | solution.py:337
  615.9 9.2 fusion.52
  625.6 23.2 %attend_back.4 = (bf16[3,2560,256]{2,1,0:T(8,128)(2,1)}, f32[4,64,640]{2,1,0:T(8,128)}) custom-call(bf16[2560,1024]{1,0:T(8,128)(2,1)} %get-tuple-element.71.grad_ref, bf16[256,1024]{1,0:T(8,128)(2,1)} %out_w_ref.1, bf16[3,2560,256]{2,1,0:T(8,128)(2,1)} %get-tuple-element.72.qkv_ref, bf16[2560,256]{1,0:T(8,128)(2,1)} %get-tuple-element.55.refs_0_.mixed_ref, ...), custom_call_target="tpu_custom_call" | custom-call | flops 11408506880 | bytes 14417920 | tf_op jit(solution)/shard_map/attend_back/pallas_call | solution.py:337
  648.7 9.2 fusion.37
  673.5 3.3 fusion.15
  685.7 3.3 fusion.21
  696.9 3.3 fusion.19
  700.7 27.8 %last.1 = (bf16[2560,1024]{1,0:T(8,128)(2,1)}, f32[8,2,1024]{2,1,0:T(2,128)}) custom-call(bf16[3,2560,256]{2,1,0:T(8,128)(2,1)} %get-tuple-element.74.refs_0_, bf16[3,2560,256]{2,1,0:T(8,128)(2,1)} %get-tuple-element.77.refs_1_, bf16[3,2560,256]{2,1,0:T(8,128)(2,1)} %get-tuple-element.80.refs_2_, bf16[3,2560,256]{2,1,0:T(8,128)(2,1)} %get-tuple-element.83.refs_3_, ...), custom_call_target="tpu_custom_call" | custom-call | flops 16106127360 | bytes 41943040 | tf_op jit(solution)/shard_map/last/pallas_call | solution.py:537
  728.5 3.3 fusion.17
  747.1 2.9 collective-permute-done.60
  765.9 3.6 collective-permute-done.65
  769.5 2.8 collective-permute-start.63
  776.2 3.4 collective-permute-done.66
  781.5 4.5 fusion.57
  786.4 3.2 collective-permute-start.68
  792.9 3.5 collective-permute-done.68
  797.5 9.1 collective-permute-done.28
  806.6 4.2 fusion.63
  819.3 21.0 %collective-permute-done.19 = bf16[3,1024,256]{1,2,0:T(8,128)(2,1)S(1)} collective-permute-done((bf16[3,1024,256]{1,2,0:T(8,128)(2,1)S(1)}, bf16[3,1024,256]{1,2,0:T(8,128)(2,1)S(1)}, u32[]{:S(2)}, u32[]{:S(2)}) %collective-permute-start.19) | collective-permute-done | bytes 1572896 | tf_op jit(solution)/shard_map/ppermute | solution.py:80
  841.4 3.6 add_convert_fusion.6
  845.0 2.8 copy.49
  854.4 13.2 %collective-permute-done.20 = bf16[1536,256]{1,0:T(8,128)(2,1)} collective-permute-done((bf16[1536,256]{1,0:T(8,128)(2,1)}, bf16[1536,256]{1,0:T(8,128)(2,1)}, u32[]{:S(2)}, u32[]{:S(2)}) %collective-permute-start.20) | collective-permute-done | bytes 786464 | tf_op jit(solution)/shard_map/ppermute | solution.py:80
  871.1 14.3 %collective-permute-done.37 = bf16[1024,1024]{1,0:T(8,128)(2,1)} collective-permute-done((bf16[1024,1024]{1,0:T(8,128)(2,1)}, bf16[1024,1024]{1,0:T(8,128)(2,1)}, u32[]{:S(2)}, u32[]{:S(2)}) %collective-permute-start.37) | collective-permute-done | bytes 2097184 | tf_op jit(solution)/shard_map/ppermute | solution.py:80
  885.3 3.7 add_convert_fusion.3
  890.7 38.6 %collective-permute-done.46 = bf16[1024,1024]{1,0:T(8,128)(2,1)} collective-permute-done((bf16[1024,1024]{1,0:T(8,128)(2,1)}, bf16[1024,1024]{1,0:T(8,128)(2,1)}, u32[]{:S(2)}, u32[]{:S(2)}) %collective-permute-start.46) | collective-permute-done | bytes 2097184 | tf_op jit(solution)/shard_map/ppermute | solution.py:80
  929.3 3.7 add_convert_fusion
  939.8 17.6 %collective-permute-done.47 = bf16[512,1024]{1,0:T(8,128)(2,1)S(1)} collective-permute-done((bf16[512,1024]{1,0:T(8,128)(2,1)S(1)}, bf16[512,1024]{1,0:T(8,128)(2,1)S(1)}, u32[]{:S(2)}, u32[]{:S(2)}) %collective-permute-start.47) | collective-permute-done | bytes 1048608 | tf_op jit(solution)/shard_map/ppermute | solution.py:80
  962.9 16.5 %collective-permute-done.48 = bf16[256,1024]{1,0:T(8,128)(2,1)S(1)} collective-permute-done((bf16[256,1024]{1,0:T(8,128)(2,1)S(1)}, bf16[256,1024]{1,0:T(8,128)(2,1)S(1)}, u32[]{:S(2)}, u32[]{:S(2)}) %collective-permute-start.48) | collective-permute-done | bytes 524320 | tf_op jit(solution)/shard_map/ppermute | solution.py:80
  983.4 15.8 %collective-permute-done.49 = bf16[128,1024]{1,0:T(8,128)(2,1)S(1)} collective-permute-done((bf16[128,1024]{1,0:T(8,128)(2,1)S(1)}, bf16[128,1024]{1,0:T(8,128)(2,1)S(1)}, u32[]{:S(2)}, u32[]{:S(2)}) %collective-permute-start.49) | collective-permute-done | bytes 262176 | tf_op jit(solution)/shard_map/ppermute | solution.py:80
  999.3 11.1 %collective-permute-done.41 = bf16[128,1024]{1,0:T(8,128)(2,1)S(1)} collective-permute-done((bf16[128,1024]{1,0:T(8,128)(2,1)S(1)}, bf16[128,1024]{1,0:T(8,128)(2,1)S(1)}, u32[]{:S(2)}, u32[]{:S(2)}) %collective-permute-start.41) | collective-permute-done | bytes 262176 | tf_op jit(solution)/shard_map/ppermute | solution.py:80
  1015.8 8.7 collective-permute-done.32
  1030.0 11.5 %collective-permute-done.33 = bf16[64,1024]{1,0:T(8,128)(2,1)S(1)} collective-permute-done((bf16[64,1024]{1,0:T(8,128)(2,1)S(1)}, bf16[64,1024]{1,0:T(8,128)(2,1)S(1)}, u32[]{:S(2)}, u32[]{:S(2)}) %collective-permute-start.33) | collective-permute-done | bytes 131104 | tf_op jit(solution)/shard_map/ppermute | solution.py:80
  1045.8 3.7 convolution_bitcast_fusion
  1049.5 26.5 %collective-permute-done.34 = bf16[128,1024]{1,0:T(8,128)(2,1)S(1)} collective-permute-done((bf16[128,1024]{1,0:T(8,128)(2,1)S(1)}, bf16[128,1024]{1,0:T(8,128)(2,1)S(1)}, u32[]{:S(2)}, u32[]{:S(2)}) %collective-permute-start.34) | collective-permute-done | bytes 262176 | tf_op jit(solution)/shard_map/ppermute | solution.py:80
  1079.4 2.9 fusion.29
  1082.3 13.2 %collective-permute-done.52 = bf16[512,1024]{1,0:T(8,128)(2,1)S(1)} collective-permute-done((bf16[512,1024]{1,0:T(8,128)(2,1)S(1)}, bf16[512,1024]{1,0:T(8,128)(2,1)S(1)}, u32[]{:S(2)}, u32[]{:S(2)}) %collective-permute-start.52) | collective-permute-done | bytes 1048608 | tf_op jit(solution)/shard_map/ppermute | solution.py:80
  1095.5 2.9 fusion.30
  (273 shorter events, 165.0 us)
Async XLA Ops:
  0.7 7.4 collective-permute-start.2
  1.2 9.5 collective-permute-start.3
  3.8 100.3 %collective-permute-start.5 = (bf16[3,1024,256]{2,1,0:T(8,128)(2,1)}, bf16[3,1024,256]{2,1,0:T(8,128)(2,1)}, u32[]{:S(2)}, u32[]{:S(2)}) collective-permute-start(bf16[3,1024,256]{2,1,0:T(8,128)(2,1)} %refs_4_.3), channel_id=1, source_target_pairs={{0,1},{1,0},{2,3},{3,2},{4,5},{5,4},{6,7},{7,6},{8,9},{9,8},{10,11... | collective-permute-start | bytes 4718600 | tf_op jit(solution)/shard_map/ppermute | solution.py:80
  4.0 141.7 %collective-permute-start.6 = (bf16[3,1024,256]{2,1,0:T(8,128)(2,1)}, bf16[3,1024,256]{2,1,0:T(8,128)(2,1)}, u32[]{:S(2)}, u32[]{:S(2)}) collective-permute-start(bf16[3,1024,256]{2,1,0:T(8,128)(2,1)} %refs_4_.3), channel_id=1, source_target_pairs={{0,2},{1,3},{2,0},{3,1},{4,6},{5,7},{6,4},{7,5},{8,10},{9,11},{10,... | collective-permute-start | bytes 4718600 | tf_op jit(solution)/shard_map/ppermute | solution.py:80
  7.9 50.8 %collective-permute-start = (f32[2,8,6144]{2,1,0:T(8,128)}, f32[2,8,6144]{2,1,0:T(8,128)}, u32[]{:S(2)}, u32[]{:S(2)}) collective-permute-start(f32[2,8,6144]{2,1,0:T(8,128)} %fusion.27), channel_id=1, source_target_pairs={{0,1},{1,0},{2,3},{3,2},{4,5},{5,4},{6,7},{7,6},{8,9},{9,8},{10,11... | collective-permute-start | bytes 1179656 | tf_op jit(solution)/shard_map/ppermute | solution.py:80
  8.1 33.4 %collective-permute-start.4 = (f32[4,2025]{1,0:T(4,128)S(1)}, f32[4,2025]{1,0:T(4,128)S(1)}, u32[]{:S(2)}, u32[]{:S(2)}) collective-permute-start(f32[4,2025]{1,0:T(4,128)S(1)} %collective-permute-done.2), channel_id=1, source_target_pairs={{0,2},{1,3},{2,0},{3,1},{4,6},{5,7},{6,4},{7,5},{8,10},{9,11},{10,... | collective-permute-start | bytes 97208 | tf_op jit(solution)/shard_map/ppermute | solution.py:80
  10.7 113.7 %collective-permute-start.13 = (bf16[1024,1024]{1,0:T(8,128)(2,1)}, bf16[1024,1024]{1,0:T(8,128)(2,1)}, u32[]{:S(2)}, u32[]{:S(2)}) collective-permute-start(bf16[1024,1024]{1,0:T(8,128)(2,1)} %refs_2_.1), channel_id=1, source_target_pairs={{0,1},{1,0},{2,3},{3,2},{4,5},{5,4},{6,7},{7,6},{8,9},{9,8},{10,11... | collective-permute-start | bytes 6291464 | tf_op jit(solution)/shard_map/ppermute | solution.py:80
  41.5 83.6 %collective-permute-start.14 = (bf16[1024,1024]{1,0:T(8,128)(2,1)}, bf16[1024,1024]{1,0:T(8,128)(2,1)}, u32[]{:S(2)}, u32[]{:S(2)}) collective-permute-start(bf16[1024,1024]{1,0:T(8,128)(2,1)} %refs_3_.1), channel_id=1, source_target_pairs={{0,1},{1,0},{2,3},{3,2},{4,5},{5,4},{6,7},{7,6},{8,9},{9,8},{10,11... | collective-permute-start | bytes 6291464 | tf_op jit(solution)/shard_map/ppermute | solution.py:80
  59.8 31.7 %collective-permute-start.1 = (f32[2,8,6144]{2,1,0:T(8,128)S(1)}, f32[2,8,6144]{2,1,0:T(8,128)}, u32[]{:S(2)}, u32[]{:S(2)}) collective-permute-start(f32[2,8,6144]{2,1,0:T(8,128)S(1)} %add.377), channel_id=1, source_target_pairs={{0,2},{1,3},{2,0},{3,1},{4,6},{5,7},{6,4},{7,5},{8,10},{9,11},{10,... | collective-permute-start | bytes 1179656 | tf_op jit(solution)/shard_map/ppermute | solution.py:80
  91.5 73.8 %collective-permute-start.8 = (bf16[256,1024]{1,0:T(8,128)(2,1)}, bf16[256,1024]{1,0:T(8,128)(2,1)}, u32[]{:S(2)}, u32[]{:S(2)}) collective-permute-start(bf16[256,1024]{1,0:T(8,128)(2,1)} %out_w_ref.1), channel_id=1, source_target_pairs={{0,1},{1,0},{2,3},{3,2},{4,5},{5,4},{6,7},{7,6},{8,9},{9,8},{10,11... | collective-permute-start | bytes 1572872 | tf_op jit(solution)/shard_map/ppermute | solution.py:80
  104.1 62.7 %collective-permute-start.7 = (bf16[3,1024,256]{2,1,0:T(8,128)(2,1)}, bf16[3,1024,256]{2,1,0:T(8,128)(2,1)}, u32[]{:S(2)}, u32[]{:S(2)}) collective-permute-start(bf16[3,1024,256]{2,1,0:T(8,128)(2,1)} %collective-permute-done.5.w_ref.refs_5_), channel_id=1, source_target_pairs={{0,2},{1,3},{2,0},{3,1},{4,6},{5,7},{6,4},{7,5},{8,10},{9,11},{10,... | collective-permute-start | bytes 4718600 | tf_op jit(solution)/shard_map/ppermute | solution.py:80
  124.4 191.1 %collective-permute-start.15 = (bf16[1024,1024]{1,0:T(8,128)(2,1)}, bf16[1024,1024]{1,0:T(8,128)(2,1)}, u32[]{:S(2)}, u32[]{:S(2)}) collective-permute-start(bf16[1024,1024]{1,0:T(8,128)(2,1)} %collective-permute-done.13.refs_2_), channel_id=1, source_target_pairs={{0,2},{1,3},{2,0},{3,1},{4,6},{5,7},{6,4},{7,5},{8,10},{9,11},{10,... | collective-permute-start | bytes 6291464 | tf_op jit(solution)/shard_map/ppermute | solution.py:80
  125.1 190.4 %collective-permute-start.16 = (bf16[1024,1024]{1,0:T(8,128)(2,1)}, bf16[1024,1024]{1,0:T(8,128)(2,1)}, u32[]{:S(2)}, u32[]{:S(2)}) collective-permute-start(bf16[1024,1024]{1,0:T(8,128)(2,1)} %collective-permute-done.14.refs_3_), channel_id=1, source_target_pairs={{0,2},{1,3},{2,0},{3,1},{4,6},{5,7},{6,4},{7,5},{8,10},{9,11},{10,... | collective-permute-start | bytes 6291464 | tf_op jit(solution)/shard_map/ppermute | solution.py:80
  145.7 97.0 %collective-permute-start.9 = (bf16[256,1024]{1,0:T(8,128)(2,1)}, bf16[256,1024]{1,0:T(8,128)(2,1)S(1)}, u32[]{:S(2)}, u32[]{:S(2)}) collective-permute-start(bf16[256,1024]{1,0:T(8,128)(2,1)} %out_w_ref.1), channel_id=1, source_target_pairs={{0,2},{1,3},{2,0},{3,1},{4,6},{5,7},{6,4},{7,5},{8,10},{9,11},{10,... | collective-permute-start | bytes 1572872 | tf_op jit(solution)/shard_map/ppermute | solution.py:80
  165.3 239.9 %collective-permute-start.11 = (bf16[1024,1024]{1,0:T(8,128)(2,1)}, bf16[1024,1024]{1,0:T(8,128)(2,1)}, u32[]{:S(2)}, u32[]{:S(2)}) collective-permute-start(bf16[1024,1024]{1,0:T(8,128)(2,1)} %refs_2_.1), channel_id=1, source_target_pairs={{0,2},{1,3},{2,0},{3,1},{4,6},{5,7},{6,4},{7,5},{8,10},{9,11},{10,... | collective-permute-start | bytes 6291464 | tf_op jit(solution)/shard_map/ppermute | solution.py:80
  166.8 132.1 %collective-permute-start.10 = (bf16[256,1024]{1,0:T(8,128)(2,1)}, bf16[256,1024]{1,0:T(8,128)(2,1)}, u32[]{:S(2)}, u32[]{:S(2)}) collective-permute-start(bf16[256,1024]{1,0:T(8,128)(2,1)} %collective-permute-done.8.refs_5_.out_w_ref), channel_id=1, source_target_pairs={{0,2},{1,3},{2,0},{3,1},{4,6},{5,7},{6,4},{7,5},{8,10},{9,11},{10,... | collective-permute-start | bytes 1572872 | tf_op jit(solution)/shard_map/ppermute | solution.py:80
  242.6 162.6 %collective-permute-start.12 = (bf16[1024,1024]{1,0:T(8,128)(2,1)}, bf16[1024,1024]{1,0:T(8,128)(2,1)}, u32[]{:S(2)}, u32[]{:S(2)}) collective-permute-start(bf16[1024,1024]{1,0:T(8,128)(2,1)} %refs_3_.1), channel_id=1, source_target_pairs={{0,2},{1,3},{2,0},{3,1},{4,6},{5,7},{6,4},{7,5},{8,10},{9,11},{10,... | collective-permute-start | bytes 6291464 | tf_op jit(solution)/shard_map/ppermute | solution.py:80
  593.0 193.4 %collective-permute-start.18 = (bf16[3,1024,256]{1,2,0:T(8,128)(2,1)}, bf16[3,1024,256]{1,2,0:T(8,128)(2,1)}, u32[]{:S(2)}, u32[]{:S(2)}) collective-permute-start(bf16[3,1024,256]{1,2,0:T(8,128)(2,1)} %fusion.49), channel_id=1, source_target_pairs={{0,1},{1,0},{2,3},{3,2},{4,5},{5,4},{6,7},{7,6},{8,9},{9,8},{10,11... | collective-permute-start | bytes 4718600 | tf_op jit(solution)/shard_map/ppermute | solution.py:80
  625.1 192.6 %collective-permute-start.17 = (bf16[3,1024,256]{1,2,0:T(8,128)(2,1)}, bf16[3,1024,256]{1,2,0:T(8,128)(2,1)}, u32[]{:S(2)}, u32[]{:S(2)}) collective-permute-start(bf16[3,1024,256]{1,2,0:T(8,128)(2,1)} %fusion.52), channel_id=1, source_target_pairs={{0,1},{1,0},{2,3},{3,2},{4,5},{5,4},{6,7},{7,6},{8,9},{9,8},{10,11... | collective-permute-start | bytes 4718600 | tf_op jit(solution)/shard_map/ppermute | solution.py:80
  657.9 121.8 %collective-permute-start.27 = (bf16[256,1024]{1,0:T(8,128)(2,1)}, bf16[256,1024]{1,0:T(8,128)(2,1)}, u32[]{:S(2)}, u32[]{:S(2)}) collective-permute-start(bf16[256,1024]{1,0:T(8,128)(2,1)} %convolution_convert_fusion.2), channel_id=1, source_target_pairs={{0,1},{1,0},{2,3},{3,2},{4,5},{5,4},{6,7},{7,6},{8,9},{9,8},{10,11... | collective-permute-start | bytes 1572872 | tf_op jit(solution)/shard_map/ppermute | solution.py:80
  677.4 54.9 %collective-permute-start.54 = (bf16[4,2025]{1,0:T(4,128)(2,1)S(1)}, bf16[4,2025]{1,0:T(4,128)(2,1)S(1)}, u32[]{:S(2)}, u32[]{:S(2)}) collective-permute-start(bf16[4,2025]{1,0:T(4,128)(2,1)S(1)} %convert_element_type.580), channel_id=1, source_target_pairs={{0,1},{1,0},{2,3},{3,2},{4,5},{5,4},{6,7},{7,6},{8,9},{9,8},{10,11... | collective-permute-start | bytes 48608 | tf_op jit(solution)/shard_map/ppermute | solution.py:80
  700.6 35.6 %collective-permute-start.53 = (bf16[4,2025]{1,0:T(4,128)(2,1)S(1)}, bf16[4,2025]{1,0:T(4,128)(2,1)S(1)}, u32[]{:S(2)}, u32[]{:S(2)}) collective-permute-start(bf16[4,2025]{1,0:T(4,128)(2,1)S(1)} %convert_element_type.572), channel_id=1, source_target_pairs={{0,1},{1,0},{2,3},{3,2},{4,5},{5,4},{6,7},{7,6},{8,9},{9,8},{10,11... | collective-permute-start | bytes 48608 | tf_op jit(solution)/shard_map/ppermute | solution.py:80
  736.2 55.5 %collective-permute-start.26 = (bf16[256,1024]{1,0:T(8,128)(2,1)}, bf16[256,1024]{1,0:T(8,128)(2,1)S(1)}, u32[]{:S(2)}, u32[]{:S(2)}) collective-permute-start(bf16[256,1024]{1,0:T(8,128)(2,1)} %convolution_convert_fusion.4), channel_id=1, source_target_pairs={{0,1},{1,0},{2,3},{3,2},{4,5},{5,4},{6,7},{7,6},{8,9},{9,8},{10,11... | collective-permute-start | bytes 1572872 | tf_op jit(solution)/shard_map/ppermute | solution.py:80
  745.7 4.3 collective-permute-start.60
  750.0 4.6 collective-permute-start.58
  754.6 4.3 collective-permute-start.61
  760.2 4.3 collective-permute-start.62
  764.5 5.0 collective-permute-start.65
  769.5 5.2 collective-permute-start.63
  774.6 5.0 collective-permute-start.66
  779.6 32.0 %collective-permute-start.36 = (bf16[1024,1024]{1,0:T(8,128)(2,1)}, bf16[1024,1024]{1,0:T(8,128)(2,1)S(1)}, u32[]{:S(2)}, u32[]{:S(2)}) collective-permute-start(bf16[1024,1024]{1,0:T(8,128)(2,1)} %get-tuple-element.89), channel_id=1, source_target_pairs={{0,1},{1,0},{2,3},{3,2},{4,5},{5,4},{6,7},{7,6},{8,9},{9,8},{10,11... | collective-permute-start | bytes 6291464 | tf_op jit(solution)/shard_map/ppermute | solution.py:80
  779.7 6.3 collective-permute-start.67
  786.0 28.3 %collective-permute-start.45 = (bf16[1024,1024]{1,0:T(8,128)(2,1)S(1)}, bf16[1024,1024]{1,0:T(8,128)(2,1)S(1)}, u32[]{:S(2)}, u32[]{:S(2)}) collective-permute-start(bf16[1024,1024]{1,0:T(8,128)(2,1)S(1)} %copy-done.23), channel_id=1, source_target_pairs={{0,1},{1,0},{2,3},{3,2},{4,5},{5,4},{6,7},{7,6},{8,9},{9,8},{10,11... | collective-permute-start | bytes 6291464 | tf_op jit(solution)/shard_map/ppermute | solution.py:80
  786.4 10.0 collective-permute-start.68
  791.7 14.9 %collective-permute-start.28 = (bf16[256,1024]{1,0:T(8,128)(2,1)S(1)}, bf16[256,1024]{1,0:T(8,128)(2,1)S(1)}, u32[]{:S(2)}, u32[]{:S(2)}) collective-permute-start(bf16[256,1024]{1,0:T(8,128)(2,1)S(1)} %fusion.57), channel_id=1, source_target_pairs={{0,2},{1,3},{2,0},{3,1},{4,6},{5,7},{6,4},{7,5},{8,10},{9,11},{10,... | collective-permute-start | bytes 1572872 | tf_op jit(solution)/shard_map/ppermute | solution.py:80
  796.4 43.9 %collective-permute-start.19 = (bf16[3,1024,256]{1,2,0:T(8,128)(2,1)S(1)}, bf16[3,1024,256]{1,2,0:T(8,128)(2,1)S(1)}, u32[]{:S(2)}, u32[]{:S(2)}) collective-permute-start(bf16[3,1024,256]{1,2,0:T(8,128)(2,1)S(1)} %fusion.23), channel_id=1, source_target_pairs={{0,2},{1,3},{2,0},{3,1},{4,6},{5,7},{6,4},{7,5},{8,10},{9,11},{10,... | collective-permute-start | bytes 4718600 | tf_op jit(solution)/shard_map/ppermute | solution.py:80
  806.6 63.9 %collective-permute-start.35 = (bf16[1024,1024]{1,0:T(8,128)(2,1)}, bf16[1024,1024]{1,0:T(8,128)(2,1)}, u32[]{:S(2)}, u32[]{:S(2)}) collective-permute-start(bf16[1024,1024]{1,0:T(8,128)(2,1)} %get-tuple-element.87), channel_id=1, source_target_pairs={{0,1},{1,0},{2,3},{3,2},{4,5},{5,4},{6,7},{7,6},{8,9},{9,8},{10,11... | collective-permute-start | bytes 6291464 | tf_op jit(solution)/shard_map/ppermute | solution.py:80
  811.6 79.1 %collective-permute-start.44 = (bf16[1024,1024]{1,0:T(8,128)(2,1)}, bf16[1024,1024]{1,0:T(8,128)(2,1)}, u32[]{:S(2)}, u32[]{:S(2)}) collective-permute-start(bf16[1024,1024]{1,0:T(8,128)(2,1)} %get-tuple-element.91), channel_id=1, source_target_pairs={{0,1},{1,0},{2,3},{3,2},{4,5},{5,4},{6,7},{7,6},{8,9},{9,8},{10,11... | collective-permute-start | bytes 6291464 | tf_op jit(solution)/shard_map/ppermute | solution.py:80
  814.3 71.1 %collective-permute-start.37 = (bf16[1024,1024]{1,0:T(8,128)(2,1)}, bf16[1024,1024]{1,0:T(8,128)(2,1)}, u32[]{:S(2)}, u32[]{:S(2)}) collective-permute-start(bf16[1024,1024]{1,0:T(8,128)(2,1)} %add_convert_fusion.4), channel_id=1, source_target_pairs={{0,2},{1,3},{2,0},{3,1},{4,6},{5,7},{6,4},{7,5},{8,10},{9,11},{10,... | collective-permute-start | bytes 6291464 | tf_op jit(solution)/shard_map/ppermute | solution.py:80
  817.7 32.2 %collective-permute-start.29 = (bf16[128,1024]{1,0:T(8,128)(2,1)}, bf16[128,1024]{1,0:T(8,128)(2,1)}, u32[]{:S(2)}, u32[]{:S(2)}) collective-permute-start(bf16[128,1024]{1,0:T(8,128)(2,1)} %constant_dynamic-slice_fusion.8), channel_id=1, source_target_pairs={{0,4},{4,0},{8,12},{12,8},{16,20},{20,16},{24,28},{28,24},{1,5},{5... | collective-permute-start | bytes 786440 | tf_op jit(solution)/shard_map/ppermute | solution.py:80
  840.3 89.0 %collective-permute-start.46 = (bf16[1024,1024]{1,0:T(8,128)(2,1)}, bf16[1024,1024]{1,0:T(8,128)(2,1)}, u32[]{:S(2)}, u32[]{:S(2)}) collective-permute-start(bf16[1024,1024]{1,0:T(8,128)(2,1)} %add_convert_fusion.1), channel_id=1, source_target_pairs={{0,2},{1,3},{2,0},{3,1},{4,6},{5,7},{6,4},{7,5},{8,10},{9,11},{10,... | collective-permute-start | bytes 6291464 | tf_op jit(solution)/shard_map/ppermute | solution.py:80
  849.9 17.7 %collective-permute-start.20 = (bf16[1536,256]{1,0:T(8,128)(2,1)}, bf16[1536,256]{1,0:T(8,128)(2,1)}, u32[]{:S(2)}, u32[]{:S(2)}) collective-permute-start(bf16[1536,256]{1,0:T(8,128)(2,1)} %constant_dynamic-slice_fusion.11), channel_id=1, source_target_pairs={{0,4},{4,0},{8,12},{12,8},{16,20},{20,16},{24,28},{28,24},{1,5},{5... | collective-permute-start | bytes 2359304 | tf_op jit(solution)/shard_map/ppermute | solution.py:80
  867.6 67.1 %collective-permute-start.30 = (bf16[64,1024]{1,0:T(8,128)(2,1)S(1)}, bf16[64,1024]{1,0:T(8,128)(2,1)S(1)}, u32[]{:S(2)}, u32[]{:S(2)}) collective-permute-start(bf16[64,1024]{1,0:T(8,128)(2,1)S(1)} %constant_dynamic-slice_fusion.7), channel_id=1, source_target_pairs={{0,8},{4,12},{8,0},{12,4},{16,24},{20,28},{24,16},{28,20},{1,9},{5... | collective-permute-start | bytes 393224 | tf_op jit(solution)/shard_map/ppermute | solution.py:80
  870.5 64.6 %collective-permute-start.21 = (bf16[768,256]{1,0:T(8,128)(2,1)S(1)}, bf16[768,256]{1,0:T(8,128)(2,1)S(1)}, u32[]{:S(2)}, u32[]{:S(2)}) collective-permute-start(bf16[768,256]{1,0:T(8,128)(2,1)S(1)} %constant_dynamic-slice_fusion.10), channel_id=1, source_target_pairs={{0,8},{4,12},{8,0},{12,4},{16,24},{20,28},{24,16},{28,20},{1,9},{5... | collective-permute-start | bytes 1179656 | tf_op jit(solution)/shard_map/ppermute | solution.py:80
  889.1 48.8 %collective-permute-start.38 = (bf16[512,1024]{1,0:T(8,128)(2,1)S(1)}, bf16[512,1024]{1,0:T(8,128)(2,1)S(1)}, u32[]{:S(2)}, u32[]{:S(2)}) collective-permute-start(bf16[512,1024]{1,0:T(8,128)(2,1)S(1)} %constant_dynamic-slice_fusion.5), channel_id=1, source_target_pairs={{0,4},{4,0},{8,12},{12,8},{16,20},{20,16},{24,28},{28,24},{1,5},{5... | collective-permute-start | bytes 3145736 | tf_op jit(solution)/shard_map/ppermute | solution.py:80
  933.1 24.3 %collective-permute-start.47 = (bf16[512,1024]{1,0:T(8,128)(2,1)S(1)}, bf16[512,1024]{1,0:T(8,128)(2,1)S(1)}, u32[]{:S(2)}, u32[]{:S(2)}) collective-permute-start(bf16[512,1024]{1,0:T(8,128)(2,1)S(1)} %constant_dynamic-slice_fusion.2), channel_id=1, source_target_pairs={{0,4},{4,0},{8,12},{12,8},{16,20},{20,16},{24,28},{28,24},{1,5},{5... | collective-permute-start | bytes 3145736 | tf_op jit(solution)/shard_map/ppermute | solution.py:80
  934.7 75.9 %collective-permute-start.31 = (bf16[32,1024]{1,0:T(8,128)(2,1)S(1)}, bf16[32,1024]{1,0:T(8,128)(2,1)S(1)}, u32[]{:S(2)}, u32[]{:S(2)}) collective-permute-start(bf16[32,1024]{1,0:T(8,128)(2,1)S(1)} %constant_dynamic-slice_fusion.6), channel_id=1, source_target_pairs={{0,16},{4,20},{8,24},{12,28},{16,0},{20,4},{24,8},{28,12},{1,17},{... | collective-permute-start | bytes 196616 | tf_op jit(solution)/shard_map/ppermute | solution.py:80
  935.3 24.2 %collective-permute-start.22 = (bf16[384,256]{1,0:T(8,128)(2,1)S(1)}, bf16[384,256]{1,0:T(8,128)(2,1)S(1)}, u32[]{:S(2)}, u32[]{:S(2)}) collective-permute-start(bf16[384,256]{1,0:T(8,128)(2,1)S(1)} %constant_dynamic-slice_fusion.9), channel_id=1, source_target_pairs={{0,16},{4,20},{8,24},{12,28},{16,0},{20,4},{24,8},{28,12},{1,17},{... | collective-permute-start | bytes 589832 | tf_op jit(solution)/shard_map/ppermute | solution.py:80
  938.4 21.9 %collective-permute-start.39 = (bf16[256,1024]{1,0:T(8,128)(2,1)S(1)}, bf16[256,1024]{1,0:T(8,128)(2,1)S(1)}, u32[]{:S(2)}, u32[]{:S(2)}) collective-permute-start(bf16[256,1024]{1,0:T(8,128)(2,1)S(1)} %constant_dynamic-slice_fusion.4), channel_id=1, source_target_pairs={{0,8},{4,12},{8,0},{12,4},{16,24},{20,28},{24,16},{28,20},{1,9},{5... | collective-permute-start | bytes 1572872 | tf_op jit(solution)/shard_map/ppermute | solution.py:80
  957.9 21.5 %collective-permute-start.48 = (bf16[256,1024]{1,0:T(8,128)(2,1)S(1)}, bf16[256,1024]{1,0:T(8,128)(2,1)S(1)}, u32[]{:S(2)}, u32[]{:S(2)}) collective-permute-start(bf16[256,1024]{1,0:T(8,128)(2,1)S(1)} %constant_dynamic-slice_fusion.1), channel_id=1, source_target_pairs={{0,8},{4,12},{8,0},{12,4},{16,24},{20,28},{24,16},{28,20},{1,9},{5... | collective-permute-start | bytes 1572872 | tf_op jit(solution)/shard_map/ppermute | solution.py:80
  959.6 23.2 %collective-permute-start.23 = (bf16[384,256]{1,0:T(8,128)(2,1)S(1)}, bf16[384,256]{1,0:T(8,128)(2,1)S(1)}, u32[]{:S(2)}, u32[]{:S(2)}) collective-permute-start(bf16[384,256]{1,0:T(8,128)(2,1)S(1)} %add_convert_fusion.16), channel_id=1, source_target_pairs={{0,16},{4,20},{8,24},{12,28},{16,0},{20,4},{24,8},{28,12},{1,17},{... | collective-permute-start | bytes 589832 | tf_op jit(solution)/shard_map/ppermute | solution.py:80
  960.6 20.8 %collective-permute-start.40 = (bf16[128,1024]{1,0:T(8,128)(2,1)S(1)}, bf16[128,1024]{1,0:T(8,128)(2,1)S(1)}, u32[]{:S(2)}, u32[]{:S(2)}) collective-permute-start(bf16[128,1024]{1,0:T(8,128)(2,1)S(1)} %constant_dynamic-slice_fusion.3), channel_id=1, source_target_pairs={{0,16},{4,20},{8,24},{12,28},{16,0},{20,4},{24,8},{28,12},{1,17},{... | collective-permute-start | bytes 786440 | tf_op jit(solution)/shard_map/ppermute | solution.py:80
  979.6 19.6 %collective-permute-start.49 = (bf16[128,1024]{1,0:T(8,128)(2,1)S(1)}, bf16[128,1024]{1,0:T(8,128)(2,1)S(1)}, u32[]{:S(2)}, u32[]{:S(2)}) collective-permute-start(bf16[128,1024]{1,0:T(8,128)(2,1)S(1)} %constant_dynamic-slice_fusion), channel_id=1, source_target_pairs={{0,16},{4,20},{8,24},{12,28},{16,0},{20,4},{24,8},{28,12},{1,17},{... | collective-permute-start | bytes 786440 | tf_op jit(solution)/shard_map/ppermute | solution.py:80
  981.5 28.9 %collective-permute-start.41 = (bf16[128,1024]{1,0:T(8,128)(2,1)S(1)}, bf16[128,1024]{1,0:T(8,128)(2,1)S(1)}, u32[]{:S(2)}, u32[]{:S(2)}) collective-permute-start(bf16[128,1024]{1,0:T(8,128)(2,1)S(1)} %add_convert_fusion.14), channel_id=1, source_target_pairs={{0,16},{4,20},{8,24},{12,28},{16,0},{20,4},{24,8},{28,12},{1,17},{... | collective-permute-start | bytes 786440 | tf_op jit(solution)/shard_map/ppermute | solution.py:80
  982.9 44.1 %collective-permute-start.24 = (bf16[768,256]{1,0:T(8,128)(2,1)S(1)}, bf16[768,256]{1,0:T(8,128)(2,1)S(1)}, u32[]{:S(2)}, u32[]{:S(2)}) collective-permute-start(bf16[768,256]{1,0:T(8,128)(2,1)S(1)} %maximum_select_fusion.9), channel_id=1, source_target_pairs={{0,8},{4,12},{8,0},{12,4},{16,24},{20,28},{24,16},{28,20},{1,9},{5... | collective-permute-start | bytes 1179656 | tf_op jit(solution)/shard_map/ppermute | solution.py:80
  999.3 16.3 %collective-permute-start.50 = (bf16[128,1024]{1,0:T(8,128)(2,1)S(1)}, bf16[128,1024]{1,0:T(8,128)(2,1)S(1)}, u32[]{:S(2)}, u32[]{:S(2)}) collective-permute-start(bf16[128,1024]{1,0:T(8,128)(2,1)S(1)} %add_convert_fusion.13), channel_id=1, source_target_pairs={{0,16},{4,20},{8,24},{12,28},{16,0},{20,4},{24,8},{28,12},{1,17},{... | collective-permute-start | bytes 786440 | tf_op jit(solution)/shard_map/ppermute | solution.py:80
  1010.6 18.3 %collective-permute-start.42 = (bf16[256,1024]{1,0:T(8,128)(2,1)S(1)}, bf16[256,1024]{1,0:T(8,128)(2,1)S(1)}, u32[]{:S(2)}, u32[]{:S(2)}) collective-permute-start(bf16[256,1024]{1,0:T(8,128)(2,1)S(1)} %maximum_select_fusion.7), channel_id=1, source_target_pairs={{0,8},{4,12},{8,0},{12,4},{16,24},{20,28},{24,16},{28,20},{1,9},{5... | collective-permute-start | bytes 1572872 | tf_op jit(solution)/shard_map/ppermute | solution.py:80
  1010.7 13.7 %collective-permute-start.32 = (bf16[32,1024]{1,0:T(8,128)(2,1)S(1)}, bf16[32,1024]{1,0:T(8,128)(2,1)S(1)}, u32[]{:S(2)}, u32[]{:S(2)}) collective-permute-start(bf16[32,1024]{1,0:T(8,128)(2,1)S(1)} %add_convert_fusion.28), channel_id=1, source_target_pairs={{0,16},{4,20},{8,24},{12,28},{16,0},{20,4},{24,8},{28,12},{1,17},{... | collective-permute-start | bytes 196616 | tf_op jit(solution)/shard_map/ppermute | solution.py:80
  1015.7 27.4 %collective-permute-start.51 = (bf16[256,1024]{1,0:T(8,128)(2,1)S(1)}, bf16[256,1024]{1,0:T(8,128)(2,1)S(1)}, u32[]{:S(2)}, u32[]{:S(2)}) collective-permute-start(bf16[256,1024]{1,0:T(8,128)(2,1)S(1)} %maximum_select_fusion.8), channel_id=1, source_target_pairs={{0,8},{4,12},{8,0},{12,4},{16,24},{20,28},{24,16},{28,20},{1,9},{5... | collective-permute-start | bytes 1572872 | tf_op jit(solution)/shard_map/ppermute | solution.py:80
  1024.4 17.0 %collective-permute-start.33 = (bf16[64,1024]{1,0:T(8,128)(2,1)S(1)}, bf16[64,1024]{1,0:T(8,128)(2,1)S(1)}, u32[]{:S(2)}, u32[]{:S(2)}) collective-permute-start(bf16[64,1024]{1,0:T(8,128)(2,1)S(1)} %maximum_select_fusion.11), channel_id=1, source_target_pairs={{0,8},{4,12},{8,0},{12,4},{16,24},{20,28},{24,16},{28,20},{1,9},{5... | collective-permute-start | bytes 393224 | tf_op jit(solution)/shard_map/ppermute | solution.py:80
  1027.3 49.7 %collective-permute-start.25 = (bf16[1536,256]{1,0:T(8,128)(2,1)S(1)}, bf16[1536,256]{1,0:T(8,128)(2,1)S(1)}, u32[]{:S(2)}, u32[]{:S(2)}) collective-permute-start(bf16[1536,256]{1,0:T(8,128)(2,1)S(1)} %maximum_select_fusion.5), channel_id=1, source_target_pairs={{0,4},{4,0},{8,12},{12,8},{16,20},{20,16},{24,28},{28,24},{1,5},{5... | collective-permute-start | bytes 2359304 | tf_op jit(solution)/shard_map/ppermute | solution.py:80
  1029.4 50.1 %collective-permute-start.43 = (bf16[512,1024]{1,0:T(8,128)(2,1)S(1)}, bf16[512,1024]{1,0:T(8,128)(2,1)S(1)}, u32[]{:S(2)}, u32[]{:S(2)}) collective-permute-start(bf16[512,1024]{1,0:T(8,128)(2,1)S(1)} %maximum_select_fusion.3), channel_id=1, source_target_pairs={{0,4},{4,0},{8,12},{12,8},{16,20},{20,16},{24,28},{28,24},{1,5},{5... | collective-permute-start | bytes 3145736 | tf_op jit(solution)/shard_map/ppermute | solution.py:80
  1041.5 34.5 %collective-permute-start.34 = (bf16[128,1024]{1,0:T(8,128)(2,1)S(1)}, bf16[128,1024]{1,0:T(8,128)(2,1)S(1)}, u32[]{:S(2)}, u32[]{:S(2)}) collective-permute-start(bf16[128,1024]{1,0:T(8,128)(2,1)S(1)} %maximum_select_fusion.10), channel_id=1, source_target_pairs={{0,4},{4,0},{8,12},{12,8},{16,20},{20,16},{24,28},{28,24},{1,5},{5... | collective-permute-start | bytes 786440 | tf_op jit(solution)/shard_map/ppermute | solution.py:80
  1043.5 51.9 %collective-permute-start.52 = (bf16[512,1024]{1,0:T(8,128)(2,1)S(1)}, bf16[512,1024]{1,0:T(8,128)(2,1)S(1)}, u32[]{:S(2)}, u32[]{:S(2)}) collective-permute-start(bf16[512,1024]{1,0:T(8,128)(2,1)S(1)} %maximum_select_fusion.4), channel_id=1, source_target_pairs={{0,4},{4,0},{8,12},{12,8},{16,20},{20,16},{24,28},{28,24},{1,5},{5... | collective-permute-start | bytes 3145736 | tf_op jit(solution)/shard_map/ppermute | solution.py:80
  (31 other events, 492.6 us)

commit v2 on v1

--- a/solution.py
+++ b/solution.py
@@ -56,10 +56,27 @@
     return pl.BlockSpec((None, count, cols), lambda i: (i, 0, 0))
 
 
-def cost(flops, nbytes, transcendentals=0):
+def cost(micros, scale=1.0):
     return pl.CostEstimate(
-        flops=int(flops), bytes_accessed=int(nbytes), transcendentals=int(transcendentals)
-    )
+        flops=int(micros * scale * 1e9), bytes_accessed=int(micros * scale * 3.5e6), transcendentals=0
+    )
+
+
+def call_after(kernel, deps, *, in_specs, **rest):
+    deps = tuple(deps)
+    count = len(in_specs)
+
+    def run(*refs):
+        kernel(*refs[:count], *refs[count + len(deps) :])
+
+    call = pl.pallas_call(
+        run, in_specs=list(in_specs) + [pl.BlockSpec(memory_space=pl.ANY)] * len(deps), **rest
+    )
+    return lambda *args: call(*args, *deps)
+
+
+def after(value, *deps):
+    return lax.optimization_barrier((value, *deps))[0]
 
 
 def normalise(values):
@@ -90,10 +107,16 @@
 
 def gather_shards(own, axis, size):
     shards = {0: own}
-    for bit in bits_of(size):
+    for bit in reversed(bits_of(size)):
         for mask in list(shards):
             shards[mask ^ bit] = swap(shards[mask], axis, size, bit)
     return shards
+
+
+def reduce_all(value, axis, size):
+    for bit in bits_of(size):
+        value = add_low(value, swap(value, axis, size, bit))
+    return value
 
 
 def reduce_shards(terms, axis, size):
@@ -104,29 +127,190 @@
     return terms[0]
 
 
-def reduce_all(value, axis, size):
-    for bit in bits_of(size):
-        value = add_low(value, swap(value, axis, size, bit))
-    return value
-
-
-def reduce_split(value, axis, size):
-    index = lax.axis_index(axis)
-    for bit in bits_of(size):
-        half = value.shape[0] // 2
-        mine = (index // bit) % 2
-        keep = lax.dynamic_slice_in_dim(value, mine * half, half, 0)
-        send = lax.dynamic_slice_in_dim(value, (1 - mine) * half, half, 0)
-        value = add_low(keep, swap(send, axis, size, bit))
-    for bit in reversed(bits_of(size)):
-        other = swap(value, axis, size, bit)
-        first = (index // bit) % 2 == 0
-        value = jnp.where(
-            first,
-            jnp.concatenate([value, other], axis=0),
-            jnp.concatenate([other, value], axis=0),
-        )
-    return value
+def add_parts(parts):
+    if len(parts) == 1:
+        return parts[0]
+    total = parts[0].astype(F32)
+    for part in parts[1:]:
+        total = total + part.astype(F32)
+    return total.astype(BF)
+
+
+def split_kernel(index_ref, *refs, count, terms):
+    ins, outs = refs[:terms], refs[terms:]
+    size = outs[0].shape[0]
+    for k in range(count):
+        start = pl.multiple_of((index_ref[0] ^ k) * size, size)
+        total = ins[0][pl.ds(start, size), :].astype(F32)
+        for ref in ins[1:]:
+            total = total + ref[pl.ds(start, size), :].astype(F32)
+        outs[k][...] = total.astype(BF)
+
+
+def split_call(parts, index, count):
+    rows, cols = parts[0].shape
+    piece = (rows // count, cols)
+    spec = pltpu.PrefetchScalarGridSpec(
+        num_scalar_prefetch=1,
+        grid=(1,),
+        in_specs=[pl.BlockSpec((rows, cols), lambda i, f: (0, 0))] * len(parts),
+        out_specs=[pl.BlockSpec(piece, lambda i, f: (0, 0))] * count,
+    )
+    return pl.pallas_call(
+        functools.partial(split_kernel, count=count, terms=len(parts)),
+        grid_spec=spec,
+        out_shape=[shaped(piece, BF)] * count,
+        compiler_params=params(),
+        cost_estimate=cost(3),
+        name="split",
+    )(jnp.reshape(index, (1,)).astype(jnp.int32), *parts)
+
+
+def assemble_kernel(index_ref, *refs):
+    for k, ref in enumerate(refs[:-1]):
+
+        @pl.when(pl.program_id(0) == k)
+        def _():
+            refs[-1][...] = ref[...].astype(F32)
+
+
+def assemble_call(pieces, index):
+    count = len(pieces)
+    rows, cols = pieces[0].shape
+    far = count // 2
+
+    def place(k, f):
+        device = f[0] ^ k
+        return ((device % 2) * far + device // 2, 0)
+
+    spec = pltpu.PrefetchScalarGridSpec(
+        num_scalar_prefetch=1,
+        grid=(count,),
+        in_specs=[pl.BlockSpec((rows, cols), lambda k, f: (0, 0))] * count,
+        out_specs=pl.BlockSpec((rows, cols), place),
+    )
+    return pl.pallas_call(
+        assemble_kernel,
+        grid_spec=spec,
+        out_shape=shaped((rows * count, cols), F32),
+        compiler_params=params(),
+        cost_estimate=cost(4),
+        name="assemble",
+    )(jnp.reshape(index, (1,)).astype(jnp.int32), *pieces)
+
+
+class Steps:
+    def __init__(self):
+        self.jobs, self.token = [], None
+
+    def swap(self, value, axis, size, bit):
+        if self.token is not None:
+            value = after(value, self.token)
+        return swap(value, axis, size, bit)
+
+    def arrive(self, value):
+        return value if self.token is None else after(value, self.token)
+
+    def step(self, token=None):
+        self.token = token
+        ties, jobs = [], []
+        for job in self.jobs:
+            try:
+                ties += next(job)
+            except StopIteration:
+                continue
+            jobs.append(job)
+        self.jobs = jobs
+        return ties if token is None else ties + [token]
+
+    def finish(self):
+        while self.jobs:
+            self.step()
+
+
+def gather_job(steps, own, shards, axis, size, hold):
+    shards[0] = own
+    even = {0: own}
+    shards[1] = steps.swap(own, axis, size, 1)
+    for bit in reversed(bits_of(size)[1:]):
+        new = {mask ^ bit: steps.swap(part, axis, size, bit) for mask, part in even.items()}
+        for _ in range(hold):
+            yield []
+        new = {mask: steps.arrive(part) for mask, part in new.items()}
+        even.update(new)
+        for mask, part in new.items():
+            shards[mask] = part
+            shards[mask ^ 1] = steps.swap(part, axis, size, 1)
+        yield list(new.values())
+
+
+class Sums:
+    def __init__(self, steps, size, lag, hold):
+        self.steps, self.size, self.lag, self.hold = steps, size, lag, hold
+        self.parts = {mask: [] for mask in range(size)}
+        nearest_first = sorted(range(1, size), key=lambda mask: (mask & -mask, mask))
+        steps.jobs += [self.send(mask) for mask in nearest_first]
+
+    def full(self, mask):
+        low = mask & -mask if mask else self.size
+        return len(self.parts[mask]) == low.bit_length()
+
+    def add(self, mask, term):
+        self.parts[mask].append(term)
+
+    def send(self, mask):
+        while not self.full(mask):
+            yield []
+        bit = mask & -mask
+        for _ in range(self.lag if bit > 1 else 0):
+            yield []
+        other = self.steps.swap(add_parts(self.parts[mask]), "mp", self.size, bit)
+        for _ in range(self.hold if bit > 1 else 1):
+            yield []
+        other = self.steps.arrive(other)
+        self.add(mask ^ bit, other)
+        yield [other]
+
+
+def psum_job(sums, n_dp, turn, out, name):
+    while not all(part.full(0) for part in sums):
+        yield []
+    values = [add_parts(part.parts[0]) for part in sums]
+    group = [(place + turn) % n_dp for place in range(n_dp)]
+    totals = lax.psum(values, "dp", axis_index_groups=[group])
+    out[name] = totals
+    yield values
+
+
+def all_job(steps, value, n_mp, n_dp, out, name):
+    ready = []
+    for axis, size in (("mp", n_mp), ("dp", n_dp)):
+        for bit in bits_of(size):
+            other = steps.swap(value, axis, size, bit)
+            yield ready
+            value = add_low(value, steps.arrive(other))
+            ready = [value]
+    out[name] = value
+    yield ready
+
+
+def spread_job(steps, sums, n_dp, out, name):
+    while not sums.full(0):
+        yield []
+    index = lax.axis_index("dp")
+    keep, send = split_call(sums.parts[0], index % 2, 2)
+    other = steps.swap(send, "dp", n_dp, 1)
+    yield [send]
+    other = steps.arrive(other)
+    pieces = split_call([keep, other], index // 2, n_dp // 2)
+    others = [steps.swap(pieces[k], "dp", n_dp, 2 * k) for k in range(1, n_dp // 2)]
+    yield [other]
+    total = add_parts([pieces[0]] + others)
+    whole = [total] + [steps.swap(total, "dp", n_dp, k) for k in range(1, n_dp)]
+    yield others
+    yield []
+    out[name] = assemble_call(whole, index)
+    yield whole
 
 
 def place_hot():
@@ -138,39 +322,34 @@
     return (offset.reshape(1, -1) == jnp.arange(N_ROW * N_COL)[:, None]).astype(F32)
 
 
-def bias_strips(rel_table):
+def bias_blocks(rel_table):
     heads = rel_table.shape[0]
-
-    def strip(cube):
-        blocks = lax.dot(cube.reshape(heads * N_TIME, N_ROW * N_COL), place_hot(), precision=highest)
-        blocks = blocks.reshape(heads, N_TIME, FRAME, FRAME)[:, ::-1]
-        blocks = blocks.transpose(0, 2, 1, 3).reshape(heads, FRAME, N_TIME * FRAME)
-        return jnp.pad(blocks, ((0, 0), (0, 0), (0, FRAME)))
-
-    cube = rel_table.reshape(heads, N_TIME, N_ROW * N_COL)
-    return strip(cube), strip(cube[:, ::-1, ::-1])
-
-
-def collect_strips(strip_grad):
-    heads = strip_grad.shape[0]
-    blocks = strip_grad[:, :, : N_TIME * FRAME].reshape(heads, FRAME, N_TIME, FRAME)
-    blocks = blocks.transpose(0, 2, 1, 3).reshape(heads * N_TIME, FRAME * FRAME)
-    cube = lax.dot_general(blocks, place_hot(), (((1,), (1,)), ((), ())), precision=highest)
-    return cube.reshape(heads, N_TIME, N_ROW * N_COL)[:, :, ::-1].reshape(heads, -1)
-
-
-def strip_column(frame):
-    return (WIN_T - 1 - frame) * FRAME
-
-
-def spread_strips(strip_ref, table, fill):
+    cube = rel_table.reshape(heads * N_TIME, N_ROW * N_COL)
+    return lax.dot(cube, place_hot(), precision=highest).reshape(heads, N_TIME, FRAME, FRAME)
+
+
+def collect_blocks(block_grad):
+    heads = block_grad.shape[0]
+    flat = block_grad.reshape(heads * N_TIME, FRAME * FRAME)
+    cube = lax.dot_general(flat, place_hot(), (((1,), (1,)), ((), ())), precision=highest)
+    return cube[:, ::-1].reshape(heads, -1)
+
+
+def frame_span(frame):
+    return slice(frame * FRAME, (frame + 1) * FRAME)
+
+
+def spread_blocks(blocks_ref, table, fill, transposed):
     for head in range(table.shape[0]):
-        strip = strip_ref[head]
-        for frame in range(WIN_T):
-            column = strip_column(frame)
-            table[head, frame * FRAME : (frame + 1) * FRAME, :WIN_TOK] = strip[
-                :, column : column + WIN_TOK
-            ]
+        for offset in range(N_TIME):
+            block = blocks_ref[head, offset]
+            if transposed:
+                block = block.T
+            for query in range(WIN_T):
+                key = query - (offset - WIN_T + 1)
+                if 0 <= key < WIN_T:
+                    row, col = (key, query) if transposed else (query, key)
+                    table[head, frame_span(row), frame_span(col)] = block
         table[head, :, WIN_TOK:] = jnp.full((WIN_TOK, PAD_TOK - WIN_TOK), fill, F32)
 
 
@@ -179,16 +358,17 @@
     attn_in_ref[...] = (normed * (1.0 + mod_ref[1:2]) + mod_ref[0:1]).astype(BF)
 
 
-def norm_call(tokens, mods):
+def norm_call(tokens, mods, deps=()):
     rows, width = tokens.shape
-    return pl.pallas_call(
+    return call_after(
         norm_kernel,
+        deps,
         grid=(rows // WIN_TOK,),
         in_specs=[row_spec(WIN_TOK, width), mod_spec(mods.shape[1], width)],
         out_specs=row_spec(WIN_TOK, width),
         out_shape=shaped((rows, width), BF),
         compiler_params=params(),
-        cost_estimate=cost(10 * rows * width, 4 * rows * width),
+        cost_estimate=cost(8),
         name="norm_in",
     )(tokens, mods)
 
@@ -206,12 +386,12 @@
     )
 
 
-def attend_kernel(x_ref, w_ref, strip_ref, qkv_ref, mixed_ref, lse_ref, table, columns):
-    heads = strip_ref.shape[0]
+def attend_kernel(x_ref, w_ref, blocks_ref, qkv_ref, mixed_ref, lse_ref, table, columns):
+    heads = blocks_ref.shape[0]
 
     @pl.when(pl.program_id(0) == 0)
     def _():
-        spread_strips(strip_ref, table, -1e30)
+        spread_blocks(blocks_ref, table, -1e30, False)
         columns[...] = jnp.zeros_like(columns)
 
     x = x_ref[...]
@@ -236,16 +416,17 @@
     lse_ref[...] = columns[...].T[: lse_ref.shape[0]]
 
 
-def attend_call(attn_in, weight, strip):
+def attend_call(attn_in, weight, blocks, deps=()):
     rows, width = attn_in.shape
     cols = weight.shape[2]
-    heads = strip.shape[0]
+    heads = blocks.shape[0]
     windows = rows // WIN_TOK
     stat_rows = -(-heads // 8) * 8
-    return pl.pallas_call(
+    return call_after(
         attend_kernel,
+        deps,
         grid=(windows,),
-        in_specs=[row_spec(WIN_TOK, width), whole_spec(weight.shape), whole_spec(strip.shape)],
+        in_specs=[row_spec(WIN_TOK, width), whole_spec(weight.shape), whole_spec(blocks.shape)],
         out_specs=[
             part_spec(WIN_TOK, cols),
             row_spec(WIN_TOK, cols),
@@ -261,23 +442,21 @@
             pltpu.VMEM((PAD_TOK, 128), F32),
         ],
         compiler_params=params(),
-        cost_estimate=cost(
-            6 * rows * width * cols + 16 * rows * PAD_TOK * cols, 2 * rows * width + 8 * rows * cols
-        ),
+        cost_estimate=cost(19),
         name="attend",
-    )(attn_in, weight, strip)
+    )(attn_in, weight, blocks)
 
 
 def attend_back_kernel(
-    grad_ref, out_w_ref, qkv_ref, mixed_ref, lse_ref, strip_ref, dqkv_ref, dstrip_ref, table, total
+    grad_ref, out_w_ref, qkv_ref, mixed_ref, lse_ref, blocks_ref, x_ref, dqkv_ref, dblocks_ref, dw_ref, table, total, x_all, d_all
 ):
-    heads = strip_ref.shape[0]
+    heads = blocks_ref.shape[0]
     cols = out_w_ref.shape[0]
     step = pl.program_id(0)
 
     @pl.when(step == 0)
     def _():
-        spread_strips(strip_ref, table, 0.0)
+        spread_blocks(blocks_ref, table, 0.0, True)
         total[...] = jnp.zeros_like(total)
 
     grad_mixed = dot(grad_ref[...], out_w_ref[...], 1, 1).astype(BF)
@@ -315,27 +494,35 @@
     )
     grad_key = dot(wide, jnp.concatenate(head_copies(query_pad * scale, heads), axis=0))
     grad_query = dot(jnp.concatenate(grad_scores, axis=0), keys, 0, 0)[:WIN_TOK]
-    dqkv_ref[0] = grad_query.astype(BF)
-    dqkv_ref[1] = grad_key.astype(BF)
-    dqkv_ref[2] = grad_value.astype(BF)
+    rows = pl.ds(pl.multiple_of(step * WIN_TOK, WIN_TOK), WIN_TOK)
+    x_all[rows, :] = x_ref[...]
+    for part, grad in enumerate((grad_query, grad_key, grad_value)):
+        grad = grad.astype(BF)
+        dqkv_ref[part] = grad
+        d_all[part, rows, :] = grad
 
     @pl.when(step == pl.num_programs(0) - 1)
     def _():
-        dstrip_ref[...] = jnp.zeros_like(dstrip_ref)
+        for part in range(3):
+            dw_ref[part] = dot(x_all[...], d_all[part], 0, 0).astype(BF)
         for head in range(heads):
-            for frame in range(WIN_T):
-                column = strip_column(frame)
-                dstrip_ref[head, :, column : column + WIN_TOK] += total[
-                    head, frame * FRAME : (frame + 1) * FRAME, :WIN_TOK
-                ]
-
-
-def attend_back_call(grad_attn, out_weight, qkv, mixed, lse, strip):
+            for offset in range(N_TIME):
+                block = None
+                for query in range(WIN_T):
+                    key = query - (offset - WIN_T + 1)
+                    if 0 <= key < WIN_T:
+                        part = total[head, frame_span(key), frame_span(query)]
+                        block = part if block is None else block + part
+                dblocks_ref[head, offset] = block
+
+
+def attend_back_call(grad_attn, out_weight, qkv, mixed, lse, blocks, attn_in, deps=()):
     rows, width = grad_attn.shape
     cols = out_weight.shape[0]
-    heads = strip.shape[0]
-    return pl.pallas_call(
+    heads = blocks.shape[0]
+    return call_after(
         attend_back_kernel,
+        deps,
         grid=(rows // WIN_TOK,),
         in_specs=[
             row_spec(WIN_TOK, width),
@@ -343,17 +530,25 @@
             part_spec(WIN_TOK, cols),
             row_spec(WIN_TOK, cols),
             mod_spec(lse.shape[1], PAD_TOK),
-            whole_spec(strip.shape),
+            whole_spec(blocks.shape),
+            row_spec(WIN_TOK, width),
         ],
-        out_specs=[part_spec(WIN_TOK, cols), whole_spec(strip.shape)],
-        out_shape=[shaped((3, rows, cols), BF), shaped(strip.shape, F32)],
-        scratch_shapes=[pltpu.VMEM((heads, WIN_TOK, PAD_TOK), F32)] * 2,
+        out_specs=[
+            part_spec(WIN_TOK, cols),
+            whole_spec(blocks.shape),
+            whole_spec((3, width, cols)),
+        ],
+        out_shape=[
+            shaped((3, rows, cols), BF),
+            shaped(blocks.shape, F32),
+            shaped((3, width, cols), BF),
+        ],
+        scratch_shapes=[pltpu.VMEM((heads, WIN_TOK, PAD_TOK), F32)] * 2
+        + [pltpu.VMEM((rows, width), BF), pltpu.VMEM((3, rows, cols), BF)],
         compiler_params=params(),
-        cost_estimate=cost(
-            2 * rows * width * cols + 40 * rows * PAD_TOK * cols, 2 * rows * width + 14 * rows * cols
-        ),
+        cost_estimate=cost(30),
         name="attend_back",
-    )(grad_attn, out_weight, qkv, mixed, lse, strip)
+    )(grad_attn, out_weight, qkv, mixed, lse, blocks, attn_in)
 
 
 def middle_kernel(*refs, count):
@@ -370,12 +565,13 @@
     grad_mlp_ref[...] = (mod_ref[5:6] * cot_ref[...].astype(F32)).astype(BF)
 
 
-def middle_call(mixed, weights, tokens, cotangent, mods):
+def middle_call(mixed, weights, tokens, cotangent, mods, deps=()):
     rows, width = tokens.shape
     count = len(mixed)
     row = row_spec(WIN_TOK, width)
-    return pl.pallas_call(
+    return call_after(
         functools.partial(middle_kernel, count=count),
+        deps,
         grid=(rows // WIN_TOK,),
         in_specs=[row_spec(WIN_TOK, part.shape[1]) for part in mixed]
         + [whole_spec(part.shape) for part in weights]
@@ -387,19 +583,17 @@
             shaped((rows, width), BF),
         ],
         compiler_params=params(),
-        cost_estimate=cost(2 * rows * width * width, 16 * rows * width),
+        cost_estimate=cost(16),
         name="middle",
     )(*mixed, *weights, tokens, cotangent, mods)
 
 
 def mlp_kernel(*refs, chunk, first):
-    if first:
-        x_ref, g_ref, up_ref, down_ref, out_ref, gin_ref, ddown_ref, dup_ref = refs[:8]
-    else:
-        x_ref, g_ref, up_ref, down_ref, out_in, gin_in, out_ref, gin_ref, ddown_ref, dup_ref = refs[
-            :10
-        ]
-    act, ghid, down_total, up_total = refs[-4:]
+    x_ref, g_ref, up_ref, down_ref = refs[:4]
+    rest = refs[4:] if first else refs[6:]
+    out_ref, gin_ref = rest[:2]
+    ddown_refs, dup_refs = rest[2:4], rest[4:6]
+    down_total, up_total, act, ghid = rest[6:]
     step = pl.program_id(0)
     hidden_width = up_ref.shape[1]
     x = x_ref[...]
@@ -420,8 +614,8 @@
         out_ref[...] = out
         gin_ref[...] = gin
     else:
-        out_ref[...] = out_in[...] + out
-        gin_ref[...] = gin_in[...] + gin
+        out_ref[...] = refs[4][...] + out
+        gin_ref[...] = refs[5][...] + gin
 
     @pl.when(step == 0)
     def _():
@@ -435,41 +629,39 @@
 
     @pl.when(step == pl.num_programs(0) - 1)
     def _():
-        ddown_ref[...] = down_total[...].astype(BF)
-        dup_ref[...] = up_total[...].astype(BF)
-
-
-def mlp_call(x, g, up, down, sums):
+        for total, halves in ((down_total, ddown_refs), (up_total, dup_refs)):
+            size = halves[0].shape[0]
+            halves[0][...] = total[:size].astype(BF)
+            halves[1][...] = total[size:].astype(BF)
+
+
+def mlp_call(x, g, up, down, sums, deps=()):
     rows, width = x.shape
     hidden = up.shape[1]
     block = 512 if rows % 512 == 0 else WIN_TOK
     row = row_spec(block, width)
     first = sums is None
     extra = () if first else tuple(sums)
-    return pl.pallas_call(
+    halves = [(hidden // 2, width)] * 2 + [(width // 2, hidden)] * 2
+    out = call_after(
         functools.partial(mlp_kernel, chunk=min(512, hidden), first=first),
+        deps,
         grid=(rows // block,),
         in_specs=[row, row, whole_spec(up.shape), whole_spec(down.shape)] + [row] * len(extra),
-        out_specs=[row, row, whole_spec(down.shape), whole_spec(up.shape)],
-        out_shape=[
-            shaped((rows, width), F32),
-            shaped((rows, width), F32),
-            shaped(down.shape, BF),
-            shaped(up.shape, BF),
-        ],
+        out_specs=[row, row] + [whole_spec(shape) for shape in halves],
+        out_shape=[shaped((rows, width), F32)] * 2 + [shaped(shape, BF) for shape in halves],
         scratch_shapes=[
+            pltpu.VMEM(down.shape, F32),
+            pltpu.VMEM(up.shape, F32),
             pltpu.VMEM((block, hidden), BF),
             pltpu.VMEM((block, hidden), BF),
-            pltpu.VMEM(down.shape, F32),
-            pltpu.VMEM(up.shape, F32),
         ],
         input_output_aliases={} if first else {4: 0, 5: 1},
         compiler_params=params(),
-        cost_estimate=cost(
-            12 * rows * width * hidden, 20 * rows * width + 8 * width * hidden, rows * hidden
-        ),
+        cost_estimate=cost(46),
         name="mlp",
     )(x, g, up, down, *extra)
+    return out[0], out[1], out[2:]
 
 
 def middle_back_kernel(
@@ -491,12 +683,13 @@
     sums_ref[3:4] = jnp.sum(cot * mlp_out, axis=0, keepdims=True)
 
 
-def middle_back_call(tokens, cotangent, attn_out, mlp_out, gin, mods):
+def middle_back_call(tokens, cotangent, attn_out, mlp_out, gin, mods, deps=()):
     rows, width = tokens.shape
     row = row_spec(WIN_TOK, width)
     windows = rows // WIN_TOK
-    return pl.pallas_call(
+    return call_after(
         middle_back_kernel,
+        deps,
         grid=(windows,),
         in_specs=[row] * 5 + [mod_spec(mods.shape[1], width)],
         out_specs=[row, row, row, mod_spec(4, width)],
@@ -507,7 +700,7 @@
             shaped((windows, 4, width), F32),
         ],
         compiler_params=params(),
-        cost_estimate=cost(40 * rows * width, 24 * rows * width),
+        cost_estimate=cost(24),
         name="middle_back",
     )(tokens, cotangent, attn_out, mlp_out, gin, mods)
 
@@ -529,13 +722,14 @@
     sums_ref[1:2] = jnp.sum(gin * normed, axis=0, keepdims=True)
 
 
-def last_call(dqkv, weights, tokens, gres, mods):
+def last_call(dqkv, weights, tokens, gres, mods, deps=()):
     rows, width = tokens.shape
     count = len(dqkv)
     row = row_spec(WIN_TOK, width)
     windows = rows // WIN_TOK
-    return pl.pallas_call(
+    return call_after(
         functools.partial(last_kernel, count=count),
+        deps,
         grid=(windows,),
         in_specs=[part_spec(WIN_TOK, part.shape[2]) for part in dqkv]
         + [whole_spec(part.shape) for part in weights]
@@ -543,7 +737,7 @@
         out_specs=[row, mod_spec(2, width)],
         out_shape=[shaped((rows, width), BF), shaped((windows, 2, width), F32)],
         compiler_params=params(),
-        cost_estimate=cost(6 * rows * width * width, 16 * rows * width),
+        cost_estimate=cost(28),
         name="last",
     )(*dqkv, *weights, tokens, gres, mods)
 
@@ -574,7 +768,6 @@
     tokens_flat = tokens.reshape(rows, width)
     cot_flat = cotangent.reshape(rows, width)
     masks = range(n_mp)
-    order = sorted(masks, key=lambda m: int(format(m, "010b")[::-1], 2), reverse=True)
 
     columns = mp_index * local_cols + jnp.arange(local_cols)
     half_width = width // 2
@@ -586,74 +779,105 @@
     condition = step_embed + jnp.einsum("mck,kd->mcd", class_hot, class_embed, precision=highest)
     lowered = jax.nn.silu(condition).astype(BF)
     mod_terms = jnp.einsum("mcd,de->mce", lowered, ada_weight, preferred_element_type=F32)
-    modulation = reduce_all(mod_terms, "mp", n_mp) + ada_bias
+    near_terms = add_low(mod_terms, swap(mod_terms, "mp", n_mp, 1))
+    modulation = near_terms
+    for bit in bits_of(n_mp)[1:]:
+        modulation = add_low(modulation, swap(modulation, "mp", n_mp, bit))
+    modulation = modulation + ada_bias
     own_clip = lax.dynamic_slice_in_dim(window_clip, mp_index * own_windows, own_windows, 1)
     clip_hot = (own_clip[..., None] == jnp.arange(clips)).astype(F32)
     mods = jnp.einsum("mwc,mce->mwe", clip_hot, modulation, precision=highest)
     mods = mods.reshape(micro * own_windows, 6, width)
 
-    qkv_w = gather_shards(qkv_weight, "mp", n_mp)
+    steps = Steps()
     rel_tables = gather_shards(rel_bias, "mp", n_mp)
-    out_w = gather_shards(out_weight, "mp", n_mp)
-    up_w = gather_shards(up_weight, "mp", n_mp)
-    down_w = gather_shards(down_weight, "mp", n_mp)
+    blocks = bias_blocks(jnp.concatenate([rel_tables[m] for m in masks], axis=0))
     heads = rel_bias.shape[0]
-    strips, strips_back = bias_strips(jnp.concatenate([rel_tables[m] for m in masks], axis=0))
-
+    blocks = {m: blocks[m * heads : (m + 1) * heads] for m in masks}
+
+    def gather(own, hold):
+        shards = {}
+        steps.jobs.append(gather_job(steps, own, shards, "mp", n_mp, hold))
+        return shards
+
+    def need(shards, mask, ties, token):
+        while mask not in shards:
+            ties = ties + steps.step(token)
+        return ties
+
+    qkv_w = gather(qkv_weight, 3)
+    steps.step(modulation)
     attn_in = norm_call(tokens_flat, mods)
+    out_w = gather(out_weight, 3)
+    ties = steps.step(attn_in)
     qkv, mixed, lse = {}, {}, {}
     for m in masks:
-        qkv[m], mixed[m], lse[m] = attend_call(
-            attn_in, qkv_w[m], strips[m * heads : (m + 1) * heads]
+        ties = need(qkv_w, m, ties, attn_in)
+        qkv[m], mixed[m], lse[m] = attend_call(attn_in, qkv_w[m], blocks[m], ties)
+        if m == 0:
+            down_w = gather(down_weight, 4)
+        elif m == 2 or m == n_mp - 1 == 1:
+            up_w = gather(up_weight, 3)
+        ties = steps.step(mixed[m])
+    for m in masks:
+        ties = need(out_w, m, ties, mixed[0])
+    attn_out, mlp_in, grad_mlp = middle_call(
+        [mixed[m] for m in masks], [out_w[m] for m in masks], tokens_flat, cot_flat, mods, ties
+    )
+    ties = steps.step(mlp_in)
+    wide_sums = [Sums(steps, n_mp, lag, 1) for lag in (0, 0, 1, 2)]
+    grads = {}
+    steps.jobs.append(psum_job(wide_sums[:2], n_dp, 0, grads, "down"))
+    steps.jobs.append(psum_job(wide_sums[2:], n_dp, 2, grads, "up"))
+    sums = None
+    for m in [m for m in masks if m % 2] + [m for m in reversed(masks) if m % 2 == 0]:
+        ties = need(down_w, m, need(up_w, m, ties, mlp_in), mlp_in)
+        mlp_out, gin, wide_terms = mlp_call(mlp_in, grad_mlp, up_w[m], down_w[m], sums, ties)
+        sums = (mlp_out, gin)
+        for wide_sum, term in zip(wide_sums, wide_terms):
+            wide_sum.add(m, term)
+        ties = steps.step(wide_terms[0])
+    block_out, grad_resid, grad_attn, late_sums = middle_back_call(
+        tokens_flat, cot_flat, attn_out, mlp_out, gin, mods, ties
+    )
+
+    def clip_sums(window_sums):
+        grouped = window_sums.reshape(micro, own_windows, -1)
+        return jnp.einsum("mwc,mwe->mce", clip_hot, grouped, precision=highest).astype(BF)
+
+    steps.jobs.append(all_job(steps, clip_sums(late_sums), n_mp, n_dp, grads, "late"))
+
+    out_sum = Sums(steps, n_mp, 0, 1)
+    qkv_sum = Sums(steps, n_mp, 0, 1)
+    steps.jobs.append(psum_job([out_sum], n_dp, 4, grads, "out"))
+    steps.jobs.append(spread_job(steps, qkv_sum, n_dp, grads, "qkv"))
+    dqkv, block_grads = {}, {}
+    for m in masks:
+        out_sum.add(m, dot(mixed[m], grad_attn, 0, 0).astype(BF))
+    ties = steps.step(grad_attn)
+    for m in reversed(masks):
+        dqkv[m], block_grads[m], qkv_term = attend_back_call(
+            grad_attn, out_w[m], qkv[m], mixed[m], lse[m], blocks[m], attn_in, ties
         )
-    attn_out, mlp_in, grad_mlp = middle_call(
-        [mixed[m] for m in masks], [out_w[m] for m in masks], tokens_flat, cot_flat, mods
-    )
-    sums = None
-    down_terms, up_terms = {}, {}
-    for m in order:
-        mlp_out, gin, down_terms[m], up_terms[m] = mlp_call(
-            mlp_in, grad_mlp, up_w[m], down_w[m], sums
-        )
-        sums = (mlp_out, gin)
-    block_out, grad_resid, grad_attn, late_sums = middle_back_call(
-        tokens_flat, cot_flat, attn_out, mlp_out, gin, mods
-    )
-
-    dqkv, qkv_terms, out_terms, rel_terms = {}, {}, {}, {}
-    for m in order:
-        out_terms[m] = dot(mixed[m], grad_attn, 0, 0).astype(BF)
-        dqkv[m], strip_grad = attend_back_call(
-            grad_attn, out_w[m], qkv[m], mixed[m], lse[m], strips_back[m * heads : (m + 1) * heads]
-        )
-        rel_terms[m] = collect_strips(strip_grad).astype(BF)
-        qkv_terms[m] = jnp.einsum(
-            "rd,sre->sde", attn_in, dqkv[m], preferred_element_type=F32
-        ).astype(BF)
+        qkv_sum.add(m, qkv_term.reshape(-1, qkv_term.shape[2]))
+        ties = steps.step(qkv_term)
     token_grad, early_sums = last_call(
-        [dqkv[m] for m in masks], [qkv_w[m] for m in masks], tokens_flat, grad_resid, mods
-    )
-
-    def total(terms):
-        shard = reduce_shards(terms, "mp", n_mp)
-        flat = shard.reshape(-1, shard.shape[-1])
-        return reduce_split(flat, "dp", n_dp).reshape(shard.shape).astype(F32)
-
-    down_grad = total(down_terms)
-    up_grad = total(up_terms)
-    out_grad = total(out_terms)
-    qkv_grad = total(qkv_terms)
+        [dqkv[m] for m in masks], [qkv_w[m] for m in masks], tokens_flat, grad_resid, mods, ties
+    )
+    steps.jobs.append(all_job(steps, clip_sums(early_sums), n_mp, n_dp, grads, "early"))
+    steps.step(token_grad)
+    steps.finish()
+    down_grad, up_grad, out_grad = [
+        jnp.concatenate([after(part, token_grad) for part in grads[name]], axis=0).astype(F32)
+        for name in ("down", "up", "out")
+    ]
+    qkv_grad = grads["qkv"].reshape(qkv_weight.shape)
+    rel_grads = collect_blocks(jnp.concatenate([block_grads[m] for m in masks], axis=0)).astype(BF)
+    rel_terms = {m: rel_grads[m * heads : (m + 1) * heads] for m in masks}
     rel_grad = reduce_all(reduce_shards(rel_terms, "mp", n_mp), "dp", n_dp).astype(F32)
 
-    def clip_sums(window_sums):
-        count = window_sums.shape[1]
-        grouped = window_sums.reshape(micro, own_windows, count * width)
-        part = jnp.einsum("mwc,mwe->mce", clip_hot, grouped, precision=highest).astype(BF)
-        part = reduce_all(reduce_all(part, "mp", n_mp), "dp", n_dp)
-        return part.astype(F32).reshape(micro, clips, count, width)
-
-    late = clip_sums(late_sums)
-    early = clip_sums(early_sums)
+    late = grads["late"].astype(F32).reshape(micro, clips, -1, width)
+    early = grads["early"].astype(F32).reshape(micro, clips, -1, width)
     mod_total = jnp.concatenate(
         [early, late[:, :, 0:1], late[:, :, 1:4]], axis=2
     ).reshape(micro, clips, 6 * width)

time: 1110 us -> 847 us (0.76)
  waiting for transfers between devices: 391 us -> 191 us
  local copies, waits for them, and re-layouts: 82.3 us -> 27.7 us
  matrix products: 87 us -> 32.6 us
  Pallas kernels: 426 us -> 464 us
  starting transfers between devices: 73.1 us -> 52.3 us
  other arithmetic: 37 us -> 54.7 us
  between operations: 1.97 us -> 14.6 us
    ppermute x69 -> x62, waiting for transfers between devices: 391 us -> 57.1 us  [swap(): return lax.ppermute(value, axis, [(i, i ^ bit) for i in range(size)])]
    psum x0 -> x3, waiting for transfers between devices: none -> 133 us  [psum_job(): totals = lax.psum(values, 'dp', axis_index_groups=[group])]
    dot_general x10 -> x2, matrix products: 58.6 us -> 6.59 us  [the longest x1 4.09 us: collect_blocks(): lax.dot_general(flat, place_hot(), (((1,), (1,)), ((), ())), precision=hi...]
    pallas_call x16 -> x19, Pallas kernels: 426 us -> 464 us  [the longest x16 452 us: call_after(): return lambda *args: call(*args, *deps)]
    convert_element_type x4 -> x13, other arithmetic: 8.79 us -> 38.9 us  [the longest x10 28.8 us: add_parts(): return total.astype(BF)]
    dot_general x9 -> x0, local copies, waits for them, and re-layouts: 22.4 us -> none  [the longest x8 21.3 us: collect_strips(): lax.dot_general(blocks, place_hot(), (((1,), (1,)), ((), ())), precision=...]
    ppermute x69 -> x62, starting transfers between devices: 73.1 us -> 52.1 us  [swap(): return lax.ppermute(value, axis, [(i, i ^ bit) for i in range(size)])]
    transpose x4 -> x0, local copies, waits for them, and re-layouts: 20.1 us -> none  [strip(): blocks = blocks.transpose(0, 2, 1, 3).reshape(heads, FRAME, N_TIME * FRAME)]
  transfers between devices with their start and end apart: 69 -> 65, of which waited for: 31 -> 18; matrix products, arithmetic and copies ran while one was open for 16% -> 12% of each run, Pallas kernels for 24% -> 51%
where the time goes in v2:
time: 847 us; the launch traced here: 837 us
  Pallas kernels  464 us (55%)
  waiting for transfers between devices  191 us (23%)
  other arithmetic  54.7 us (6%)
  starting transfers between devices  52.3 us (6%)
  matrix products  32.6 us (4%)
  local copies, waits for them, and re-layouts  27.7 us (3%)
  between operations  14.6 us (2%)
    pallas_call x16, Pallas kernels, call_after(): return lambda *args: call(*args, *deps)  452 us
    psum x3, waiting for transfers between devices, psum_job(): totals = lax.psum(values, 'dp', axis_index_groups=[group])  133 us
    ppermute x62, waiting for transfers between devices, swap(): return lax.ppermute(value, axis, [(i, i ^ bit) for i in range(size)])  57.1 us
    ppermute x62, starting transfers between devices, swap(): return lax.ppermute(value, axis, [(i, i ^ bit) for i in range(size)])  52.1 us
    convert_element_type x10, other arithmetic, add_parts(): return total.astype(BF)  28.8 us
  transfers between devices with their start and end apart: 65, of which 18 were waited for; matrix products, arithmetic and copies ran while one was open for 12% of the time, Pallas kernels for 51%

profile of v2, /device:TPU:0, one launch (start us, length us, event | category | flops | bytes accessed | tf_op | source)
XLA Modules:
  0.0 836.9 jit_solution(17084157494075948353)
XLA Ops:
  7.2 3.0 collective-permute-start.3
  19.8 2.5 fusion.1
  22.3 1.8 add.236
  25.8 2.6 slice.48.refs_2_.refs_5_
  28.4 2.6 slice.50.refs_2_.refs_5_
  31.0 2.6 slice.52.refs_2_.refs_5_
  33.6 2.6 slice.54.refs_2_.refs_5_
  40.4 8.7 %norm_in.1.refs_0_.refs_3_.refs_6_ = bf16[2560,1024]{1,0:T(8,128)(2,1)} custom-call(bf16[2560,1024]{1,0:T(8,128)(2,1)} %bitcast.58, f32[8,6,1024]{2,1,0:T(8,128)} %reshape.207.refs_1_.refs_10_.refs_5_), custom_call_target="tpu_custom_call" | custom-call | flops 8000000000 | bytes 28000000 | tf_op jit(solution)/shard_map/norm_in/pallas_call | solution.py:75
  49.4 19.3 %attend.4 = (bf16[3,2560,256]{2,1,0:T(8,128)(2,1)}, bf16[2560,256]{1,0:T(8,128)(2,1)}, f32[8,8,384]{2,1,0:T(8,128)}) custom-call(bf16[2560,1024]{1,0:T(8,128)(2,1)} %norm_in.1.refs_0_.refs_3_.refs_6_, bf16[3,1024,256]{2,1,0:T(8,128)(2,1)} %refs_4_.3, f32[4,9,64,64]{3,2,1,0:T(8,128)} %slice.48.refs_2_.refs_5_, bf16[2560,1024]{1,0:T(8,128)(2,1)} %norm_in.1.refs_0_.refs_3_.refs_6_), custom_call_target="tpu_custom_call" | custom-call | flops 19000000512 | bytes 66500000 | tf_op jit(solution)/shard_map/attend/pallas_call | solution.py:75
  70.9 19.2 %attend.5 = (bf16[3,2560,256]{2,1,0:T(8,128)(2,1)}, bf16[2560,256]{1,0:T(8,128)(2,1)}, f32[8,8,384]{2,1,0:T(8,128)}) custom-call(bf16[2560,1024]{1,0:T(8,128)(2,1)} %norm_in.1.refs_0_.refs_3_.refs_6_, bf16[3,1024,256]{2,1,0:T(8,128)(2,1)} %collective-permute-done.5.refs_1_.refs_5_, f32[4,9,64,64]{3,2,1,0:T(8,128)} %slice.50.refs_2_.refs_5_, ...), custom_call_target="tpu_custom_call" | custom-call | flops 19000000512 | bytes 66500000 | tf_op jit(solution)/shard_map/attend/pallas_call | solution.py:75
  90.3 19.3 %attend.6 = (bf16[3,2560,256]{2,1,0:T(8,128)(2,1)}, bf16[2560,256]{1,0:T(8,128)(2,1)}, f32[8,8,384]{2,1,0:T(8,128)}) custom-call(bf16[2560,1024]{1,0:T(8,128)(2,1)} %norm_in.1.refs_0_.refs_3_.refs_6_, bf16[3,1024,256]{2,1,0:T(8,128)(2,1)} %collective-permute-done.6.refs_1_.refs_3_.refs_6_, f32[4,9,64,64]{3,2,1,0:T(8,128)} %slice.52.refs_2_.refs_5_, ...), custom_call_target="tpu_custom_call" | custom-call | flops 19000000512 | bytes 66500000 | tf_op jit(solution)/shard_map/attend/pallas_call | solution.py:75
  110.1 19.3 %attend.7 = (bf16[3,2560,256]{2,1,0:T(8,128)(2,1)}, bf16[2560,256]{1,0:T(8,128)(2,1)}, f32[8,8,384]{2,1,0:T(8,128)}) custom-call(bf16[2560,1024]{1,0:T(8,128)(2,1)} %norm_in.1.refs_0_.refs_3_.refs_6_, bf16[3,1024,256]{2,1,0:T(8,128)(2,1)} %collective-permute-done.7.refs_1_.refs_7_, f32[4,9,64,64]{3,2,1,0:T(8,128)} %slice.54.refs_2_.refs_5_, ...), custom_call_target="tpu_custom_call" | custom-call | flops 19000000512 | bytes 66500000 | tf_op jit(solution)/shard_map/attend/pallas_call | solution.py:75
  129.8 16.6 %middle.1 = (f32[2560,1024]{1,0:T(8,128)}, bf16[2560,1024]{1,0:T(8,128)(2,1)}, bf16[2560,1024]{1,0:T(8,128)(2,1)}) custom-call(bf16[2560,256]{1,0:T(8,128)(2,1)} %get-tuple-element.142.refs_3_.refs_0_, bf16[2560,256]{1,0:T(8,128)(2,1)} %get-tuple-element.144.refs_4_.refs_1_.refs_3_, bf16[2560,256]{1,0:T(8,128)(2,1)} %get-tuple-element.146.refs_4_.refs_2_.refs_3_, ...), custom_call_target="tpu_custom_call" | custom-call | flops 16000000000 | bytes 56000000 | tf_op jit(solution)/shard_map/middle/pallas_call | solution.py:75
  146.6 43.8 %mlp.4 = (f32[2560,1024]{1,0:T(8,128)}, f32[2560,1024]{1,0:T(8,128)}, bf16[512,1024]{1,0:T(8,128)(2,1)}, bf16[512,1024]{1,0:T(8,128)(2,1)}, bf16[512,1024]{1,0:T(8,128)(2,1)}, /*index=5*/bf16[512,1024]{1,0:T(8,128)(2,1)}) custom-call(bf16[2560,1024]{1,0:T(8,128)(2,1)} %get-tuple-element.153.refs_0_.refs_5_, bf16[2560,1024]{1,0:T(8,128)(2,1)} %get-tuple-element.154.refs_1_, ...), custom_call_target="tpu_custom_call" | custom-call | flops 46000001024 | bytes 161000000 | tf_op jit(solution)/shard_map/mlp/pallas_call | solution.py:75
  191.9 3.1 collective-permute-done.15.refs_2_
  195.0 45.8 %mlp.5 = (f32[2560,1024]{1,0:T(8,128)}, f32[2560,1024]{1,0:T(8,128)}, bf16[512,1024]{1,0:T(8,128)(2,1)}, bf16[512,1024]{1,0:T(8,128)(2,1)}, bf16[512,1024]{1,0:T(8,128)(2,1)}, /*index=5*/bf16[512,1024]{1,0:T(8,128)(2,1)}) custom-call(bf16[2560,1024]{1,0:T(8,128)(2,1)} %get-tuple-element.153.refs_0_.refs_5_, ...), custom_call_target="tpu_custom_call", output_to_operand_aliasing={{0}: (4, {}), {1}: (5, {})} | custom-call | flops 46000001024 | bytes 161000000 | tf_op jit(solution)/shard_map/mlp/pallas_call | solution.py:75
  242.0 45.6 %mlp.6 = (f32[2560,1024]{1,0:T(8,128)}, f32[2560,1024]{1,0:T(8,128)}, bf16[512,1024]{1,0:T(8,128)(2,1)}, bf16[512,1024]{1,0:T(8,128)(2,1)}, bf16[512,1024]{1,0:T(8,128)(2,1)}, /*index=5*/bf16[512,1024]{1,0:T(8,128)(2,1)}) custom-call(bf16[2560,1024]{1,0:T(8,128)(2,1)} %get-tuple-element.153.refs_0_.refs_5_, ...), custom_call_target="tpu_custom_call", output_to_operand_aliasing={{0}: (4, {}), {1}: (5, {})} | custom-call | flops 46000001024 | bytes 161000000 | tf_op jit(solution)/shard_map/mlp/pallas_call | solution.py:75
  287.7 3.0 add_convert_fusion.7
  292.4 2.6 add_convert_fusion.6
  295.3 45.7 %mlp.7 = (f32[2560,1024]{1,0:T(8,128)}, f32[2560,1024]{1,0:T(8,128)}, bf16[512,1024]{1,0:T(8,128)(2,1)}, bf16[512,1024]{1,0:T(8,128)(2,1)}, bf16[512,1024]{1,0:T(8,128)(2,1)}, /*index=5*/bf16[512,1024]{1,0:T(8,128)(2,1)}) custom-call(bf16[2560,1024]{1,0:T(8,128)(2,1)} %get-tuple-element.153.refs_0_.refs_5_, ...), custom_call_target="tpu_custom_call", output_to_operand_aliasing={{0}: (4, {}), {1}: (5, {})} | custom-call | flops 46000001024 | bytes 161000000 | tf_op jit(solution)/shard_map/mlp/pallas_call | solution.py:75
  341.0 3.1 add_convert_fusion.3
  345.8 2.6 add_convert_fusion.2
  348.4 3.2 add_convert_fusion.5.refs_8_
  351.6 3.1 add_convert_fusion.4.refs_9_
  354.8 24.7 %middle_back.1 = (bf16[2560,1024]{1,0:T(8,128)(2,1)}, f32[2560,1024]{1,0:T(8,128)}, bf16[2560,1024]{1,0:T(8,128)(2,1)}, f32[8,4,1024]{2,1,0:T(4,128)}) custom-call(bf16[2560,1024]{1,0:T(8,128)(2,1)} %bitcast.60, bf16[2560,1024]{1,0:T(8,128)(2,1)} %bitcast.57, f32[2560,1024]{1,0:T(8,128)} %get-tuple-element.152.refs_2_, ...), custom_call_target="tpu_custom_call" | custom-call | flops 24000000000 | bytes 84000000 | tf_op jit(solution)/shard_map/middle_back/pallas_call | solution.py:75
  381.0 5.4 convolution_convert_fusion.5
  389.1 3.2 add_convert_fusion.1.refs_8_
  392.2 29.0 %attend_back.4 = (bf16[3,2560,256]{2,1,0:T(8,128)(2,1)}, f32[4,9,64,64]{3,2,1,0:T(8,128)}, bf16[3,1024,256]{2,1,0:T(8,128)(2,1)}) custom-call(bf16[2560,1024]{1,0:T(8,128)(2,1)} %get-tuple-element.202.refs_0_.refs_8_, bf16[256,1024]{1,0:T(8,128)(2,1)} %collective-permute-done.10.refs_7_.refs_1_, bf16[3,2560,256]{2,1,0:T(8,128)(2,1)} %get-tuple-element.207.refs_2_, ...), custom_call_target="tpu_custom_call" | custom-call | flops 30000001024 | bytes 105000000 | tf_op jit(solution)/shard_map/attend_back/pallas_call | solution.py:75
  421.9 3.5 add_convert_fusion.refs_9_
  425.4 29.1 %attend_back.5 = (bf16[3,2560,256]{2,1,0:T(8,128)(2,1)}, f32[4,9,64,64]{3,2,1,0:T(8,128)}, bf16[3,1024,256]{2,1,0:T(8,128)(2,1)}) custom-call(bf16[2560,1024]{1,0:T(8,128)(2,1)} %get-tuple-element.202.refs_0_.refs_8_, bf16[256,1024]{1,0:T(8,128)(2,1)} %collective-permute-done.8.refs_3_.refs_6_.refs_1_, bf16[3,2560,256]{2,1,0:T(8,128)(2,1)} %get-tuple-element.215.refs_2_, ...), custom_call_target="tpu_custom_call" | custom-call | flops 30000001024 | bytes 105000000 | tf_op jit(solution)/shard_map/attend_back/pallas_call | solution.py:75
  457.7 4.5 fusion.15
  462.8 1.8 collective-permute-start.33
  464.6 11.8 %collective-permute-done.34.refs_8_ = bf16[256,1024]{1,0:T(8,128)(2,1)S(1)} collective-permute-done((bf16[256,1024]{1,0:T(8,128)(2,1)S(1)}, bf16[256,1024]{1,0:T(8,128)(2,1)S(1)}, u32[]{:S(2)}, u32[]{:S(2)}) %collective-permute-start.34) | collective-permute-done | bytes 524320 | tf_op jit(solution)/shard_map/ppermute | solution.py:97
  477.1 5.0 fusion.12.refs_10_
  482.2 3.5 fusion.2
  486.1 29.3 %attend_back.6 = (bf16[3,2560,256]{2,1,0:T(8,128)(2,1)}, f32[4,9,64,64]{3,2,1,0:T(8,128)}, bf16[3,1024,256]{2,1,0:T(8,128)(2,1)}) custom-call(bf16[2560,1024]{1,0:T(8,128)(2,1)} %get-tuple-element.202.refs_0_.refs_8_, bf16[256,1024]{1,0:T(8,128)(2,1)} %collective-permute-done.9.refs_5_.refs_1_, bf16[3,2560,256]{2,1,0:T(8,128)(2,1)} %get-tuple-element.229.refs_2_, ...), custom_call_target="tpu_custom_call" | custom-call | flops 30000001024 | bytes 105000000 | tf_op jit(solution)/shard_map/attend_back/pallas_call | solution.py:75
  515.5 1.9 collective-permute-start.37
  517.4 4.4 collective-permute-done.36.refs_8_.refs_0_
  521.8 29.4 %attend_back.7 = (bf16[3,2560,256]{2,1,0:T(8,128)(2,1)}, f32[4,9,64,64]{3,2,1,0:T(8,128)}, bf16[3,1024,256]{2,1,0:T(8,128)(2,1)}) custom-call(bf16[2560,1024]{1,0:T(8,128)(2,1)} %get-tuple-element.202.refs_0_.refs_8_, bf16[256,1024]{1,0:T(8,128)(2,1)} %refs_1_.3, bf16[3,2560,256]{2,1,0:T(8,128)(2,1)} %get-tuple-element.203.refs_2_, ...), custom_call_target="tpu_custom_call" | custom-call | flops 30000001024 | bytes 105000000 | tf_op jit(solution)/shard_map/attend_back/pallas_call | solution.py:75
  552.8 4.0 split.2
  556.9 27.7 %last.1 = (bf16[2560,1024]{1,0:T(8,128)(2,1)}, f32[8,2,1024]{2,1,0:T(2,128)}) custom-call(bf16[3,2560,256]{2,1,0:T(8,128)(2,1)} %get-tuple-element.239.refs_0_, bf16[3,2560,256]{2,1,0:T(8,128)(2,1)} %get-tuple-element.240.refs_1_, bf16[3,2560,256]{2,1,0:T(8,128)(2,1)} %get-tuple-element.241.refs_2_, bf16[3,2560,256]{2,1,0:T(8,128)(2,1)} %get-tuple-element.242.refs_3_, ...), custom_call_target="tpu_custom_call" | custom-call | flops 28000000000 | bytes 98000000 | tf_op jit(solution)/shard_map/last/pallas_call | solution.py:75
  584.6 5.6 pad_maximum_fusion
  590.2 5.4 reshape.219
  595.6 4.1 fusion
  600.5 4.0 maximum_convert_fusion
  604.5 64.6 %all-reduce.8.cloned.1.call-done = (bf16[512,1024]{1,0:T(8,128)(2,1)}, bf16[512,1024]{1,0:T(8,128)(2,1)}) async-done(((bf16[512,1024]{1,0:T(8,128)(2,1)}, bf16[512,1024]{1,0:T(8,128)(2,1)}), (bf16[512,1024]{1,0:T(8,128)(2,1)}, bf16[512,1024]{1,0:T(8,128)(2,1)})) %all-reduce.8.cloned.1.call-update) | async-done | bytes 2097168 | tf_op jit(solution)/shard_map/psum | solution.py:280
  672.0 4.0 maximum_convert_fusion.1
  677.5 68.8 %all-reduce.6.cloned.1.call-done = bf16[256,1024]{1,0:T(8,128)(2,1)} async-done(((bf16[256,1024]{1,0:T(8,128)(2,1)}), bf16[256,1024]{1,0:T(8,128)(2,1)}) %all-reduce.6.cloned.1.call-update) | async-done | bytes 524304 | tf_op jit(solution)/shard_map/psum | solution.py:280
  746.3 2.1 convert_element_type.401
  753.0 2.0 collective-permute-done.53
  761.6 2.0 collective-permute-done.55
  765.9 3.5 collective-permute-done.59
  770.6 2.4 split.3
  773.0 2.0 collective-permute-start.42
  777.3 1.9 collective-permute-done.60
  779.3 2.5 collective-permute-done.42
  781.8 7.4 collective-permute-done.41
  794.1 2.2 collective-permute-start.45
  796.8 3.1 collective-permute-start.47
  800.0 2.0 collective-permute-start.48
  806.1 3.7 convolution_bitcast_fusion
  809.9 11.1 %collective-permute-done.46.refs_4_ = bf16[384,256]{1,0:T(8,128)(2,1)} collective-permute-done((bf16[384,256]{1,0:T(8,128)(2,1)S(1)}, bf16[384,256]{1,0:T(8,128)(2,1)}, u32[]{:S(2)}, u32[]{:S(2)}) %collective-permute-start.46) | collective-permute-done | bytes 196640 | tf_op jit(solution)/shard_map/ppermute | solution.py:97
  820.9 4.4 collective-permute-done.47.refs_5_
  825.4 4.8 assemble.1
  (220 shorter events, 69.0 us)
Async XLA Ops:
  7.2 7.8 collective-permute-start.3
  10.2 6.2 collective-permute-start.2
  13.8 8.5 %collective-permute-start = (f32[2,8,6144]{2,1,0:T(8,128)S(1)}, f32[2,8,6144]{2,1,0:T(8,128)}, u32[]{:S(2)}, u32[]{:S(2)}) collective-permute-start(f32[2,8,6144]{2,1,0:T(8,128)S(1)} %fusion.5), channel_id=1, source_target_pairs={{0,1},{1,0},{2,3},{3,2},{4,5},{5,4},{6,7},{7,6},{8,9},{9,8},{10,11... | collective-permute-start | bytes 1179656 | tf_op jit(solution)/shard_map/ppermute | solution.py:97
  24.1 12.1 %collective-permute-start.1 = (f32[2,8,6144]{2,1,0:T(8,128)}, f32[2,8,6144]{2,1,0:T(8,128)S(1)}, u32[]{:S(2)}, u32[]{:S(2)}) collective-permute-start(f32[2,8,6144]{2,1,0:T(8,128)} %add.236), channel_id=1, source_target_pairs={{0,2},{1,3},{2,0},{3,1},{4,6},{5,7},{6,4},{7,5},{8,10},{9,11},{10,... | collective-permute-start | bytes 1179656 | tf_op jit(solution)/shard_map/ppermute | solution.py:97
  37.2 32.0 %collective-permute-start.5 = (bf16[3,1024,256]{2,1,0:T(8,128)(2,1)}, bf16[3,1024,256]{2,1,0:T(8,128)(2,1)}, u32[]{:S(2)}, u32[]{:S(2)}) collective-permute-start(bf16[3,1024,256]{2,1,0:T(8,128)(2,1)} %refs_4_.3), channel_id=1, source_target_pairs={{0,1},{1,0},{2,3},{3,2},{4,5},{5,4},{6,7},{7,6},{8,9},{9,8},{10,11... | collective-permute-start | bytes 4718600 | tf_op jit(solution)/shard_map/ppermute | solution.py:97
  37.5 52.7 %collective-permute-start.6 = (bf16[3,1024,256]{2,1,0:T(8,128)(2,1)}, bf16[3,1024,256]{2,1,0:T(8,128)(2,1)}, u32[]{:S(2)}, u32[]{:S(2)}) collective-permute-start(bf16[3,1024,256]{2,1,0:T(8,128)(2,1)} %refs_4_.3), channel_id=1, source_target_pairs={{0,2},{1,3},{2,0},{3,1},{4,6},{5,7},{6,4},{7,5},{8,10},{9,11},{10,... | collective-permute-start | bytes 4718600 | tf_op jit(solution)/shard_map/ppermute | solution.py:97
  49.1 60.4 %collective-permute-start.8 = (bf16[256,1024]{1,0:T(8,128)(2,1)S(1)}, bf16[256,1024]{1,0:T(8,128)(2,1)}, u32[]{:S(2)}, u32[]{:S(2)}) collective-permute-start(bf16[256,1024]{1,0:T(8,128)(2,1)S(1)} %copy-done.23), channel_id=1, source_target_pairs={{0,2},{1,3},{2,0},{3,1},{4,6},{5,7},{6,4},{7,5},{8,10},{9,11},{10,... | collective-permute-start | bytes 1572872 | tf_op jit(solution)/shard_map/ppermute | solution.py:97
  49.4 80.0 %collective-permute-start.9 = (bf16[256,1024]{1,0:T(8,128)(2,1)S(1)}, bf16[256,1024]{1,0:T(8,128)(2,1)}, u32[]{:S(2)}, u32[]{:S(2)}) collective-permute-start(bf16[256,1024]{1,0:T(8,128)(2,1)S(1)} %copy-done.23), channel_id=1, source_target_pairs={{0,1},{1,0},{2,3},{3,2},{4,5},{5,4},{6,7},{7,6},{8,9},{9,8},{10,11... | collective-permute-start | bytes 1572872 | tf_op jit(solution)/shard_map/ppermute | solution.py:97
  68.7 77.9 %collective-permute-start.13 = (bf16[1024,1024]{1,0:T(8,128)(2,1)}, bf16[1024,1024]{1,0:T(8,128)(2,1)}, u32[]{:S(2)}, u32[]{:S(2)}) collective-permute-start(bf16[1024,1024]{1,0:T(8,128)(2,1)} %refs_3_.1), channel_id=1, source_target_pairs={{0,1},{1,0},{2,3},{3,2},{4,5},{5,4},{6,7},{7,6},{8,9},{9,8},{10,11... | collective-permute-start | bytes 6291464 | tf_op jit(solution)/shard_map/ppermute | solution.py:97
  69.2 77.2 %collective-permute-start.14 = (bf16[1024,1024]{1,0:T(8,128)(2,1)}, bf16[1024,1024]{1,0:T(8,128)(2,1)}, u32[]{:S(2)}, u32[]{:S(2)}) collective-permute-start(bf16[1024,1024]{1,0:T(8,128)(2,1)} %refs_3_.1), channel_id=1, source_target_pairs={{0,2},{1,3},{2,0},{3,1},{4,6},{5,7},{6,4},{7,5},{8,10},{9,11},{10,... | collective-permute-start | bytes 6291464 | tf_op jit(solution)/shard_map/ppermute | solution.py:97
  90.2 19.9 %collective-permute-start.7 = (bf16[3,1024,256]{2,1,0:T(8,128)(2,1)}, bf16[3,1024,256]{2,1,0:T(8,128)(2,1)}, u32[]{:S(2)}, u32[]{:S(2)}) collective-permute-start(bf16[3,1024,256]{2,1,0:T(8,128)(2,1)} %collective-permute-done.6.refs_1_.refs_3_.refs_6_), channel_id=1, source_target_pairs={{0,1},{1,0},{2,3},{3,2},{4,5},{5,4},{6,7},{7,6},{8,9},{9,8},{10,11... | collective-permute-start | bytes 4718600 | tf_op jit(solution)/shard_map/ppermute | solution.py:97
  109.5 20.3 %collective-permute-start.10 = (bf16[256,1024]{1,0:T(8,128)(2,1)}, bf16[256,1024]{1,0:T(8,128)(2,1)}, u32[]{:S(2)}, u32[]{:S(2)}) collective-permute-start(bf16[256,1024]{1,0:T(8,128)(2,1)} %collective-permute-done.8.refs_3_.refs_6_.refs_1_), channel_id=1, source_target_pairs={{0,1},{1,0},{2,3},{3,2},{4,5},{5,4},{6,7},{7,6},{8,9},{9,8},{10,11... | collective-permute-start | bytes 1572872 | tf_op jit(solution)/shard_map/ppermute | solution.py:97
  110.1 36.5 %collective-permute-start.12 = (bf16[1024,1024]{1,0:T(8,128)(2,1)}, bf16[1024,1024]{1,0:T(8,128)(2,1)}, u32[]{:S(2)}, u32[]{:S(2)}) collective-permute-start(bf16[1024,1024]{1,0:T(8,128)(2,1)} %refs_2_.1), channel_id=1, source_target_pairs={{0,1},{1,0},{2,3},{3,2},{4,5},{5,4},{6,7},{7,6},{8,9},{9,8},{10,11... | collective-permute-start | bytes 6291464 | tf_op jit(solution)/shard_map/ppermute | solution.py:97
  129.5 61.0 %collective-permute-start.11 = (bf16[1024,1024]{1,0:T(8,128)(2,1)}, bf16[1024,1024]{1,0:T(8,128)(2,1)}, u32[]{:S(2)}, u32[]{:S(2)}) collective-permute-start(bf16[1024,1024]{1,0:T(8,128)(2,1)} %refs_2_.1), channel_id=1, source_target_pairs={{0,2},{1,3},{2,0},{3,1},{4,6},{5,7},{6,4},{7,5},{8,10},{9,11},{10,... | collective-permute-start | bytes 6291464 | tf_op jit(solution)/shard_map/ppermute | solution.py:97
  146.4 45.2 %collective-permute-start.16 = (bf16[1024,1024]{1,0:T(8,128)(2,1)}, bf16[1024,1024]{1,0:T(8,128)(2,1)}, u32[]{:S(2)}, u32[]{:S(2)}) collective-permute-start(bf16[1024,1024]{1,0:T(8,128)(2,1)} %collective-permute-done.14.refs_4_.refs_3_), channel_id=1, source_target_pairs={{0,1},{1,0},{2,3},{3,2},{4,5},{5,4},{6,7},{7,6},{8,9},{9,8},{10,11... | collective-permute-start | bytes 6291464 | tf_op jit(solution)/shard_map/ppermute | solution.py:97
  190.5 4.6 collective-permute-start.15
  190.9 50.0 %collective-permute-start.17 = (bf16[512,1024]{1,0:T(8,128)(2,1)}, bf16[512,1024]{1,0:T(8,128)(2,1)}, u32[]{:S(2)}, u32[]{:S(2)}) collective-permute-start(bf16[512,1024]{1,0:T(8,128)(2,1)} %get-tuple-element.166.refs_7_), channel_id=1, source_target_pairs={{0,1},{1,0},{2,3},{3,2},{4,5},{5,4},{6,7},{7,6},{8,9},{9,8},{10,11... | collective-permute-start | bytes 3145736 | tf_op jit(solution)/shard_map/ppermute | solution.py:97
  191.0 49.8 %collective-permute-start.18 = (bf16[512,1024]{1,0:T(8,128)(2,1)}, bf16[512,1024]{1,0:T(8,128)(2,1)}, u32[]{:S(2)}, u32[]{:S(2)}) collective-permute-start(bf16[512,1024]{1,0:T(8,128)(2,1)} %get-tuple-element.170), channel_id=1, source_target_pairs={{0,1},{1,0},{2,3},{3,2},{4,5},{5,4},{6,7},{7,6},{8,9},{9,8},{10,11... | collective-permute-start | bytes 3145736 | tf_op jit(solution)/shard_map/ppermute | solution.py:97
  191.4 49.5 %collective-permute-start.19 = (bf16[512,1024]{1,0:T(8,128)(2,1)}, bf16[512,1024]{1,0:T(8,128)(2,1)}, u32[]{:S(2)}, u32[]{:S(2)}) collective-permute-start(bf16[512,1024]{1,0:T(8,128)(2,1)} %get-tuple-element.173), channel_id=1, source_target_pairs={{0,1},{1,0},{2,3},{3,2},{4,5},{5,4},{6,7},{7,6},{8,9},{9,8},{10,11... | collective-permute-start | bytes 3145736 | tf_op jit(solution)/shard_map/ppermute | solution.py:97
  191.6 49.3 %collective-permute-start.20 = (bf16[512,1024]{1,0:T(8,128)(2,1)}, bf16[512,1024]{1,0:T(8,128)(2,1)}, u32[]{:S(2)}, u32[]{:S(2)}) collective-permute-start(bf16[512,1024]{1,0:T(8,128)(2,1)} %get-tuple-element.176), channel_id=1, source_target_pairs={{0,1},{1,0},{2,3},{3,2},{4,5},{5,4},{6,7},{7,6},{8,9},{9,8},{10,11... | collective-permute-start | bytes 3145736 | tf_op jit(solution)/shard_map/ppermute | solution.py:97
  240.9 46.8 %collective-permute-start.21 = (bf16[512,1024]{1,0:T(8,128)(2,1)}, bf16[512,1024]{1,0:T(8,128)(2,1)}, u32[]{:S(2)}, u32[]{:S(2)}) collective-permute-start(bf16[512,1024]{1,0:T(8,128)(2,1)} %get-tuple-element.180.refs_10_), channel_id=1, source_target_pairs={{0,1},{1,0},{2,3},{3,2},{4,5},{5,4},{6,7},{7,6},{8,9},{9,8},{10,11... | collective-permute-start | bytes 3145736 | tf_op jit(solution)/shard_map/ppermute | solution.py:97
  241.3 46.4 %collective-permute-start.22 = (bf16[512,1024]{1,0:T(8,128)(2,1)}, bf16[512,1024]{1,0:T(8,128)(2,1)}, u32[]{:S(2)}, u32[]{:S(2)}) collective-permute-start(bf16[512,1024]{1,0:T(8,128)(2,1)} %get-tuple-element.184), channel_id=1, source_target_pairs={{0,1},{1,0},{2,3},{3,2},{4,5},{5,4},{6,7},{7,6},{8,9},{9,8},{10,11... | collective-permute-start | bytes 3145736 | tf_op jit(solution)/shard_map/ppermute | solution.py:97
  241.5 46.2 %collective-permute-start.23 = (bf16[512,1024]{1,0:T(8,128)(2,1)}, bf16[512,1024]{1,0:T(8,128)(2,1)}, u32[]{:S(2)}, u32[]{:S(2)}) collective-permute-start(bf16[512,1024]{1,0:T(8,128)(2,1)} %get-tuple-element.187), channel_id=1, source_target_pairs={{0,1},{1,0},{2,3},{3,2},{4,5},{5,4},{6,7},{7,6},{8,9},{9,8},{10,11... | collective-permute-start | bytes 3145736 | tf_op jit(solution)/shard_map/ppermute | solution.py:97
  241.8 45.9 %collective-permute-start.24 = (bf16[512,1024]{1,0:T(8,128)(2,1)}, bf16[512,1024]{1,0:T(8,128)(2,1)}, u32[]{:S(2)}, u32[]{:S(2)}) collective-permute-start(bf16[512,1024]{1,0:T(8,128)(2,1)} %get-tuple-element.190), channel_id=1, source_target_pairs={{0,1},{1,0},{2,3},{3,2},{4,5},{5,4},{6,7},{7,6},{8,9},{9,8},{10,11... | collective-permute-start | bytes 3145736 | tf_op jit(solution)/shard_map/ppermute | solution.py:97
  290.7 57.7 %collective-permute-start.25 = (bf16[512,1024]{1,0:T(8,128)(2,1)}, bf16[512,1024]{1,0:T(8,128)(2,1)}, u32[]{:S(2)}, u32[]{:S(2)}) collective-permute-start(bf16[512,1024]{1,0:T(8,128)(2,1)} %add_convert_fusion.7), channel_id=1, source_target_pairs={{0,2},{1,3},{2,0},{3,1},{4,6},{5,7},{6,4},{7,5},{8,10},{9,11},{10,... | collective-permute-start | bytes 3145736 | tf_op jit(solution)/shard_map/ppermute | solution.py:97
  295.0 53.4 %collective-permute-start.26 = (bf16[512,1024]{1,0:T(8,128)(2,1)}, bf16[512,1024]{1,0:T(8,128)(2,1)}, u32[]{:S(2)}, u32[]{:S(2)}) collective-permute-start(bf16[512,1024]{1,0:T(8,128)(2,1)} %add_convert_fusion.6), channel_id=1, source_target_pairs={{0,2},{1,3},{2,0},{3,1},{4,6},{5,7},{6,4},{7,5},{8,10},{9,11},{10,... | collective-permute-start | bytes 3145736 | tf_op jit(solution)/shard_map/ppermute | solution.py:97
  344.1 43.9 %collective-permute-start.28 = (bf16[512,1024]{1,0:T(8,128)(2,1)}, bf16[512,1024]{1,0:T(8,128)(2,1)}, u32[]{:S(2)}, u32[]{:S(2)}) collective-permute-start(bf16[512,1024]{1,0:T(8,128)(2,1)} %add_convert_fusion.3), channel_id=1, source_target_pairs={{0,2},{1,3},{2,0},{3,1},{4,6},{5,7},{6,4},{7,5},{8,10},{9,11},{10,... | collective-permute-start | bytes 3145736 | tf_op jit(solution)/shard_map/ppermute | solution.py:97
  380.9 40.3 %collective-permute-start.27 = (bf16[2,8,4096]{2,1,0:T(8,128)(2,1)S(1)}, bf16[2,8,4096]{2,1,0:T(8,128)(2,1)S(1)}, u32[]{:S(2)}, u32[]{:S(2)}) collective-permute-start(bf16[2,8,4096]{2,1,0:T(8,128)(2,1)S(1)} %convolution_convert_fusion), channel_id=1, source_target_pairs={{0,1},{1,0},{2,3},{3,2},{4,5},{5,4},{6,7},{7,6},{8,9},{9,8},{10,11... | collective-permute-start | bytes 393224 | tf_op jit(solution)/shard_map/ppermute | solution.py:97
  387.9 34.0 %collective-permute-start.30 = (bf16[512,1024]{1,0:T(8,128)(2,1)}, bf16[512,1024]{1,0:T(8,128)(2,1)}, u32[]{:S(2)}, u32[]{:S(2)}) collective-permute-start(bf16[512,1024]{1,0:T(8,128)(2,1)} %add_convert_fusion.2), channel_id=1, source_target_pairs={{0,2},{1,3},{2,0},{3,1},{4,6},{5,7},{6,4},{7,5},{8,10},{9,11},{10,... | collective-permute-start | bytes 3145736 | tf_op jit(solution)/shard_map/ppermute | solution.py:97
  388.3 33.6 %collective-permute-start.31 = (bf16[256,1024]{1,0:T(8,128)(2,1)}, bf16[256,1024]{1,0:T(8,128)(2,1)}, u32[]{:S(2)}, u32[]{:S(2)}) collective-permute-start(bf16[256,1024]{1,0:T(8,128)(2,1)} %convolution_convert_fusion.5), channel_id=1, source_target_pairs={{0,1},{1,0},{2,3},{3,2},{4,5},{5,4},{6,7},{7,6},{8,9},{9,8},{10,11... | collective-permute-start | bytes 1572872 | tf_op jit(solution)/shard_map/ppermute | solution.py:97
  389.0 32.9 %collective-permute-start.32 = (bf16[256,1024]{1,0:T(8,128)(2,1)S(1)}, bf16[256,1024]{1,0:T(8,128)(2,1)}, u32[]{:S(2)}, u32[]{:S(2)}) collective-permute-start(bf16[256,1024]{1,0:T(8,128)(2,1)S(1)} %convolution_convert_fusion.4), channel_id=1, source_target_pairs={{0,1},{1,0},{2,3},{3,2},{4,5},{5,4},{6,7},{7,6},{8,9},{9,8},{10,11... | collective-permute-start | bytes 1572872 | tf_op jit(solution)/shard_map/ppermute | solution.py:97
  454.5 130.1 %all-reduce.10.cloned.1.call-start = ((), (), s32[]{:S(2)}) async-start(), calls=%async_computation.2 | async-start | bytes 4194304 | tf_op jit(solution)/shard_map/psum | solution.py:280
  455.3 213.9 %all-reduce.8.cloned.1.call-start = ((), (), s32[]{:S(2)}) async-start(), calls=%async_computation.1 | async-start | bytes 4194304 | tf_op jit(solution)/shard_map/psum | solution.py:280
  455.3 26.8 %collective-permute-start.35 = (bf16[3072,256]{1,0:T(8,128)(2,1)}, bf16[3072,256]{1,0:T(8,128)(2,1)}, u32[]{:S(2)}, u32[]{:S(2)}) collective-permute-start(bf16[3072,256]{1,0:T(8,128)(2,1)} %bitcast.62), channel_id=1, source_target_pairs={{0,1},{1,0},{2,3},{3,2},{4,5},{5,4},{6,7},{7,6},{8,9},{9,8},{10,11... | collective-permute-start | bytes 4718600 | tf_op jit(solution)/shard_map/ppermute | solution.py:97
  456.0 6.7 collective-permute-start.29
  462.2 14.1 %collective-permute-start.34 = (bf16[256,1024]{1,0:T(8,128)(2,1)S(1)}, bf16[256,1024]{1,0:T(8,128)(2,1)S(1)}, u32[]{:S(2)}, u32[]{:S(2)}) collective-permute-start(bf16[256,1024]{1,0:T(8,128)(2,1)S(1)} %fusion.15), channel_id=1, source_target_pairs={{0,2},{1,3},{2,0},{3,1},{4,6},{5,7},{6,4},{7,5},{8,10},{9,11},{10,... | collective-permute-start | bytes 1572872 | tf_op jit(solution)/shard_map/ppermute | solution.py:97
  462.8 52.7 %collective-permute-start.33 = (bf16[2,8,4096]{2,1,0:T(8,128)(2,1)S(1)}, bf16[2,8,4096]{2,1,0:T(8,128)(2,1)S(1)}, u32[]{:S(2)}, u32[]{:S(2)}) collective-permute-start(bf16[2,8,4096]{2,1,0:T(8,128)(2,1)S(1)} %add_convert_fusion.12.refs_7_), channel_id=1, source_target_pairs={{0,4},{4,0},{8,12},{12,8},{16,20},{20,16},{24,28},{28,24},{1,5},{5... | collective-permute-start | bytes 393224 | tf_op jit(solution)/shard_map/ppermute | solution.py:97
  485.6 36.2 %collective-permute-start.36 = (bf16[3072,256]{1,0:T(8,128)(2,1)}, bf16[3072,256]{1,0:T(8,128)(2,1)}, u32[]{:S(2)}, u32[]{:S(2)}) collective-permute-start(bf16[3072,256]{1,0:T(8,128)(2,1)} %fusion.2), channel_id=1, source_target_pairs={{0,2},{1,3},{2,0},{3,1},{4,6},{5,7},{6,4},{7,5},{8,10},{9,11},{10,... | collective-permute-start | bytes 4718600 | tf_op jit(solution)/shard_map/ppermute | solution.py:97
  515.4 230.9 %all-reduce.6.cloned.1.call-start = ((), (), s32[]{:S(2)}) async-start(), calls=%async_computation | async-start | bytes 1048576 | tf_op jit(solution)/shard_map/psum | solution.py:280
  515.5 35.7 %collective-permute-start.37 = (bf16[2,8,4096]{2,1,0:T(8,128)(2,1)S(1)}, bf16[2,8,4096]{2,1,0:T(8,128)(2,1)S(1)}, u32[]{:S(2)}, u32[]{:S(2)}) collective-permute-start(bf16[2,8,4096]{2,1,0:T(8,128)(2,1)S(1)} %add_convert_fusion.11.refs_7_), channel_id=1, source_target_pairs={{0,8},{4,12},{8,0},{12,4},{16,24},{20,28},{24,16},{28,20},{1,9},{5... | collective-permute-start | bytes 393224 | tf_op jit(solution)/shard_map/ppermute | solution.py:97
  517.4 35.4 %collective-permute-start.38 = (bf16[3072,256]{1,0:T(8,128)(2,1)}, bf16[3072,256]{1,0:T(8,128)(2,1)}, u32[]{:S(2)}, u32[]{:S(2)}) collective-permute-start(bf16[3072,256]{1,0:T(8,128)(2,1)} %bitcast.63), channel_id=1, source_target_pairs={{0,1},{1,0},{2,3},{3,2},{4,5},{5,4},{6,7},{7,6},{8,9},{9,8},{10,11... | collective-permute-start | bytes 4718600 | tf_op jit(solution)/shard_map/ppermute | solution.py:97
  600.4 69.5 %collective-permute-start.51 = (bf16[4,2025]{1,0:T(4,128)(2,1)S(1)}, bf16[4,2025]{1,0:T(4,128)(2,1)S(1)}, u32[]{:S(2)}, u32[]{:S(2)}) collective-permute-start(bf16[4,2025]{1,0:T(4,128)(2,1)S(1)} %slice.60), channel_id=1, source_target_pairs={{0,1},{1,0},{2,3},{3,2},{4,5},{5,4},{6,7},{7,6},{8,9},{9,8},{10,11... | collective-permute-start | bytes 48608 | tf_op jit(solution)/shard_map/ppermute | solution.py:97
  669.9 81.2 %collective-permute-start.50 = (bf16[4,2025]{1,0:T(4,128)(2,1)}, bf16[4,2025]{1,0:T(4,128)(2,1)S(1)}, u32[]{:S(2)}, u32[]{:S(2)}) collective-permute-start(bf16[4,2025]{1,0:T(4,128)(2,1)} %slice.57), channel_id=1, source_target_pairs={{0,1},{1,0},{2,3},{3,2},{4,5},{5,4},{6,7},{7,6},{8,9},{9,8},{10,11... | collective-permute-start | bytes 48608 | tf_op jit(solution)/shard_map/ppermute | solution.py:97
  670.6 80.6 %collective-permute-start.52 = (bf16[4,2025]{1,0:T(4,128)(2,1)}, bf16[4,2025]{1,0:T(4,128)(2,1)S(1)}, u32[]{:S(2)}, u32[]{:S(2)}) collective-permute-start(bf16[4,2025]{1,0:T(4,128)(2,1)} %add_convert_fusion.23), channel_id=1, source_target_pairs={{0,2},{1,3},{2,0},{3,1},{4,6},{5,7},{6,4},{7,5},{8,10},{9,11},{10,... | collective-permute-start | bytes 48608 | tf_op jit(solution)/shard_map/ppermute | solution.py:97
  676.0 94.6 %collective-permute-start.39 = (bf16[1536,256]{1,0:T(8,128)(2,1)}, bf16[1536,256]{1,0:T(8,128)(2,1)}, u32[]{:S(2)}, u32[]{:S(2)}) collective-permute-start(bf16[1536,256]{1,0:T(8,128)(2,1)} %get-tuple-element.252.refs_13_), channel_id=1, source_target_pairs={{0,4},{4,0},{8,12},{12,8},{16,20},{20,16},{24,28},{28,24},{1,5},{5... | collective-permute-start | bytes 2359304 | tf_op jit(solution)/shard_map/ppermute | solution.py:97
  748.5 15.6 %collective-permute-start.61 = (bf16[2,8,4096]{2,1,0:T(8,128)(2,1)S(1)}, bf16[2,8,4096]{2,1,0:T(8,128)(2,1)S(1)}, u32[]{:S(2)}, u32[]{:S(2)}) collective-permute-start(bf16[2,8,4096]{2,1,0:T(8,128)(2,1)S(1)} %copy-done.8), channel_id=1, source_target_pairs={{0,16},{4,20},{8,24},{12,28},{16,0},{20,4},{24,8},{28,12},{1,17},{... | collective-permute-start | bytes 393224 | tf_op jit(solution)/shard_map/ppermute | solution.py:97
  751.2 3.8 collective-permute-start.53
  752.9 3.4 collective-permute-start.56
  755.0 3.8 collective-permute-start.54
  756.3 4.3 collective-permute-start.57
  758.8 4.7 collective-permute-start.55
  760.7 4.3 collective-permute-start.58
  765.0 4.3 collective-permute-start.59
  769.4 9.8 %collective-permute-start.60 = (bf16[2,8,2048]{2,1,0:T(8,128)(2,1)S(1)}, bf16[2,8,2048]{2,1,0:T(8,128)(2,1)S(1)}, u32[]{:S(2)}, u32[]{:S(2)}) collective-permute-start(bf16[2,8,2048]{2,1,0:T(8,128)(2,1)S(1)} %add_convert_fusion.15), channel_id=1, source_target_pairs={{0,16},{4,20},{8,24},{12,28},{16,0},{20,4},{24,8},{28,12},{1,17},{... | collective-permute-start | bytes 196616 | tf_op jit(solution)/shard_map/ppermute | solution.py:97
  773.0 8.8 %collective-permute-start.42 = (bf16[384,256]{1,0:T(8,128)(2,1)}, bf16[384,256]{1,0:T(8,128)(2,1)S(1)}, u32[]{:S(2)}, u32[]{:S(2)}) collective-permute-start(bf16[384,256]{1,0:T(8,128)(2,1)} %get-tuple-element.260), channel_id=1, source_target_pairs={{0,24},{4,28},{8,16},{12,20},{16,8},{20,12},{24,0},{28,4},{1,25},{... | collective-permute-start | bytes 589832 | tf_op jit(solution)/shard_map/ppermute | solution.py:97
  774.9 14.2 %collective-permute-start.41 = (bf16[384,256]{1,0:T(8,128)(2,1)}, bf16[384,256]{1,0:T(8,128)(2,1)S(1)}, u32[]{:S(2)}, u32[]{:S(2)}) collective-permute-start(bf16[384,256]{1,0:T(8,128)(2,1)} %get-tuple-element.258), channel_id=1, source_target_pairs={{0,16},{4,20},{8,24},{12,28},{16,0},{20,4},{24,8},{28,12},{1,17},{... | collective-permute-start | bytes 589832 | tf_op jit(solution)/shard_map/ppermute | solution.py:97
  775.7 13.4 %collective-permute-start.40 = (bf16[384,256]{1,0:T(8,128)(2,1)}, bf16[384,256]{1,0:T(8,128)(2,1)S(1)}, u32[]{:S(2)}, u32[]{:S(2)}) collective-permute-start(bf16[384,256]{1,0:T(8,128)(2,1)} %get-tuple-element.256), channel_id=1, source_target_pairs={{0,8},{4,12},{8,0},{12,4},{16,24},{20,28},{24,16},{28,20},{1,9},{5... | collective-permute-start | bytes 589832 | tf_op jit(solution)/shard_map/ppermute | solution.py:97
  790.2 9.7 %collective-permute-start.43 = (bf16[384,256]{1,0:T(8,128)(2,1)S(1)}, bf16[384,256]{1,0:T(8,128)(2,1)S(1)}, u32[]{:S(2)}, u32[]{:S(2)}) collective-permute-start(bf16[384,256]{1,0:T(8,128)(2,1)S(1)} %add_convert_fusion.8.refs_0_), channel_id=1, source_target_pairs={{0,4},{4,0},{8,12},{12,8},{16,20},{20,16},{24,28},{28,24},{1,5},{5... | collective-permute-start | bytes 589832 | tf_op jit(solution)/shard_map/ppermute | solution.py:97
  791.5 11.1 %collective-permute-start.44 = (bf16[384,256]{1,0:T(8,128)(2,1)S(1)}, bf16[384,256]{1,0:T(8,128)(2,1)S(1)}, u32[]{:S(2)}, u32[]{:S(2)}) collective-permute-start(bf16[384,256]{1,0:T(8,128)(2,1)S(1)} %add_convert_fusion.8.refs_0_), channel_id=1, source_target_pairs={{0,8},{4,12},{8,0},{12,4},{16,24},{20,28},{24,16},{28,20},{1,9},{5... | collective-permute-start | bytes 589832 | tf_op jit(solution)/shard_map/ppermute | solution.py:97
  794.1 15.8 %collective-permute-start.45 = (bf16[384,256]{1,0:T(8,128)(2,1)S(1)}, bf16[384,256]{1,0:T(8,128)(2,1)}, u32[]{:S(2)}, u32[]{:S(2)}) collective-permute-start(bf16[384,256]{1,0:T(8,128)(2,1)S(1)} %add_convert_fusion.8.refs_0_), channel_id=1, source_target_pairs={{0,12},{4,8},{8,4},{12,0},{16,28},{20,24},{24,20},{28,16},{1,13},{... | collective-permute-start | bytes 589832 | tf_op jit(solution)/shard_map/ppermute | solution.py:97
  796.3 24.6 %collective-permute-start.46 = (bf16[384,256]{1,0:T(8,128)(2,1)S(1)}, bf16[384,256]{1,0:T(8,128)(2,1)}, u32[]{:S(2)}, u32[]{:S(2)}) collective-permute-start(bf16[384,256]{1,0:T(8,128)(2,1)S(1)} %add_convert_fusion.8.refs_0_), channel_id=1, source_target_pairs={{0,16},{4,20},{8,24},{12,28},{16,0},{20,4},{24,8},{28,12},{1,17},{... | collective-permute-start | bytes 589832 | tf_op jit(solution)/shard_map/ppermute | solution.py:97
  796.8 28.5 %collective-permute-start.47 = (bf16[384,256]{1,0:T(8,128)(2,1)S(1)}, bf16[384,256]{1,0:T(8,128)(2,1)}, u32[]{:S(2)}, u32[]{:S(2)}) collective-permute-start(bf16[384,256]{1,0:T(8,128)(2,1)S(1)} %add_convert_fusion.8.refs_0_), channel_id=1, source_target_pairs={{0,20},{4,16},{8,28},{12,24},{16,4},{20,0},{24,12},{28,8},{1,21},{... | collective-permute-start | bytes 589832 | tf_op jit(solution)/shard_map/ppermute | solution.py:97
  800.0 25.4 %collective-permute-start.48 = (bf16[384,256]{1,0:T(8,128)(2,1)S(1)}, bf16[384,256]{1,0:T(8,128)(2,1)}, u32[]{:S(2)}, u32[]{:S(2)}) collective-permute-start(bf16[384,256]{1,0:T(8,128)(2,1)S(1)} %add_convert_fusion.8.refs_0_), channel_id=1, source_target_pairs={{0,24},{4,28},{8,16},{12,20},{16,8},{20,12},{24,0},{28,4},{1,25},{... | collective-permute-start | bytes 589832 | tf_op jit(solution)/shard_map/ppermute | solution.py:97
  802.6 22.8 %collective-permute-start.49 = (bf16[384,256]{1,0:T(8,128)(2,1)S(1)}, bf16[384,256]{1,0:T(8,128)(2,1)}, u32[]{:S(2)}, u32[]{:S(2)}) collective-permute-start(bf16[384,256]{1,0:T(8,128)(2,1)S(1)} %add_convert_fusion.8.refs_0_), channel_id=1, source_target_pairs={{0,28},{4,24},{8,20},{12,16},{16,12},{20,8},{24,4},{28,0},{1,29},{... | collective-permute-start | bytes 589832 | tf_op jit(solution)/shard_map/ppermute | solution.py:97
  (30 other events, 367.4 us)
Sparse Core Ops, SparseCore 0:
  459.0 104.1 all-reduce.9
  567.5 101.6 all-reduce.7
  672.5 73.7 all-reduce.5

commit v3 on v2

--- a/solution.py
+++ b/solution.py
@@ -56,9 +56,9 @@
     return pl.BlockSpec((None, count, cols), lambda i: (i, 0, 0))
 
 
-def cost(micros, scale=1.0):
+def cost(micros):
     return pl.CostEstimate(
-        flops=int(micros * scale * 1e9), bytes_accessed=int(micros * scale * 3.5e6), transcendentals=0
+        flops=int(micros * 1e9), bytes_accessed=int(micros * 3.5e6), transcendentals=0
     )
 
 
@@ -127,24 +127,41 @@
     return terms[0]
 
 
+def sum_kernel(*refs):
+    total = refs[0][...].astype(F32)
+    for ref in refs[1:-1]:
+        total = total + ref[...].astype(F32)
+    refs[-1][...] = total.astype(BF)
+
+
 def add_parts(parts):
     if len(parts) == 1:
         return parts[0]
-    total = parts[0].astype(F32)
-    for part in parts[1:]:
-        total = total + part.astype(F32)
-    return total.astype(BF)
+    rows, cols = parts[0].shape
+    block = rows // 4 if rows % 64 == 0 and rows >= 512 else rows
+    return pl.pallas_call(
+        sum_kernel,
+        grid=(rows // block,),
+        in_specs=[row_spec(block, cols)] * len(parts),
+        out_specs=row_spec(block, cols),
+        out_shape=shaped((rows, cols), BF),
+        compiler_params=params(),
+        cost_estimate=cost(0.001),
+        name="add",
+    )(*parts)
 
 
 def split_kernel(index_ref, *refs, count, terms):
     ins, outs = refs[:terms], refs[terms:]
-    size = outs[0].shape[0]
+    total = ins[0][...].astype(F32)
+    for ref in ins[1:]:
+        total = total + ref[...].astype(F32)
+    total = total.astype(BF)
     for k in range(count):
-        start = pl.multiple_of((index_ref[0] ^ k) * size, size)
-        total = ins[0][pl.ds(start, size), :].astype(F32)
-        for ref in ins[1:]:
-            total = total + ref[pl.ds(start, size), :].astype(F32)
-        outs[k][...] = total.astype(BF)
+
+        @pl.when(pl.program_id(0) == k)
+        def _():
+            outs[k][...] = total
 
 
 def split_call(parts, index, count):
@@ -152,16 +169,16 @@
     piece = (rows // count, cols)
     spec = pltpu.PrefetchScalarGridSpec(
         num_scalar_prefetch=1,
-        grid=(1,),
-        in_specs=[pl.BlockSpec((rows, cols), lambda i, f: (0, 0))] * len(parts),
-        out_specs=[pl.BlockSpec(piece, lambda i, f: (0, 0))] * count,
+        grid=(count,),
+        in_specs=[pl.BlockSpec(piece, lambda k, f: (f[0] ^ k, 0))] * len(parts),
+        out_specs=[pl.BlockSpec(piece, lambda k, f: (0, 0))] * count,
     )
     return pl.pallas_call(
         functools.partial(split_kernel, count=count, terms=len(parts)),
         grid_spec=spec,
         out_shape=[shaped(piece, BF)] * count,
         compiler_params=params(),
-        cost_estimate=cost(3),
+        cost_estimate=cost(0.001),
         name="split",
     )(jnp.reshape(index, (1,)).astype(jnp.int32), *parts)
 
@@ -171,30 +188,24 @@
 
         @pl.when(pl.program_id(0) == k)
         def _():
-            refs[-1][...] = ref[...].astype(F32)
-
-
-def assemble_call(pieces, index):
+            refs[-1][...] = ref[...].astype(refs[-1].dtype)
+
+
+def assemble_call(pieces, index, dtype):
     count = len(pieces)
     rows, cols = pieces[0].shape
-    far = count // 2
-
-    def place(k, f):
-        device = f[0] ^ k
-        return ((device % 2) * far + device // 2, 0)
-
     spec = pltpu.PrefetchScalarGridSpec(
         num_scalar_prefetch=1,
         grid=(count,),
         in_specs=[pl.BlockSpec((rows, cols), lambda k, f: (0, 0))] * count,
-        out_specs=pl.BlockSpec((rows, cols), place),
+        out_specs=pl.BlockSpec((rows, cols), lambda k, f: (f[0] ^ k, 0)),
     )
     return pl.pallas_call(
         assemble_kernel,
         grid_spec=spec,
-        out_shape=shaped((rows * count, cols), F32),
-        compiler_params=params(),
-        cost_estimate=cost(4),
+        out_shape=shaped((rows * count, cols), dtype),
+        compiler_params=params(),
+        cost_estimate=cost(0.001),
         name="assemble",
     )(jnp.reshape(index, (1,)).astype(jnp.int32), *pieces)
 
@@ -272,14 +283,14 @@
         yield [other]
 
 
-def psum_job(sums, n_dp, turn, out, name):
-    while not all(part.full(0) for part in sums):
+def psum_job(sums, earlier, out, name):
+    while not sums.full(0):
         yield []
-    values = [add_parts(part.parts[0]) for part in sums]
-    group = [(place + turn) % n_dp for place in range(n_dp)]
-    totals = lax.psum(values, "dp", axis_index_groups=[group])
-    out[name] = totals
-    yield values
+    value = add_parts(sums.parts[0])
+    yield [value]
+    while earlier not in out:
+        yield []
+    out[name] = lax.psum(after(value, out[earlier]), "dp")
 
 
 def all_job(steps, value, n_mp, n_dp, out, name):
@@ -294,23 +305,32 @@
     yield ready
 
 
-def spread_job(steps, sums, n_dp, out, name):
+def spread_job(steps, sums, n_dp, offload, out, name):
     while not sums.full(0):
         yield []
     index = lax.axis_index("dp")
+    count = n_dp // 2
     keep, send = split_call(sums.parts[0], index % 2, 2)
     other = steps.swap(send, "dp", n_dp, 1)
     yield [send]
-    other = steps.arrive(other)
-    pieces = split_call([keep, other], index // 2, n_dp // 2)
-    others = [steps.swap(pieces[k], "dp", n_dp, 2 * k) for k in range(1, n_dp // 2)]
-    yield [other]
-    total = add_parts([pieces[0]] + others)
-    whole = [total] + [steps.swap(total, "dp", n_dp, k) for k in range(1, n_dp)]
-    yield others
-    yield []
-    out[name] = assemble_call(whole, index)
-    yield whole
+    pieces = split_call([keep, steps.arrive(other)], index // 2, count)
+    others = [steps.swap(pieces[k], "dp", n_dp, 2 * k) for k in range(1, count)]
+    yield [other, *pieces]
+    total = add_parts([pieces[0]] + [steps.arrive(part) for part in others])
+    if offload:
+        whole = lax.all_gather(total, "dp", axis=0)
+        yield [total]
+        yield []
+        whole = steps.arrive(whole)
+        out[name] = whole.reshape(count, 2, *total.shape)
+        yield [whole]
+        return
+    others = [steps.swap(total, "dp", n_dp, 2 * k) for k in range(1, count)]
+    yield [total]
+    half = assemble_call([total] + [steps.arrive(part) for part in others], index // 2, BF)
+    other = steps.swap(half, "dp", n_dp, 1)
+    yield [half]
+    out[name] = assemble_call([half, steps.arrive(other)], index % 2, F32)
 
 
 def place_hot():
@@ -333,6 +353,10 @@
     flat = block_grad.reshape(heads * N_TIME, FRAME * FRAME)
     cube = lax.dot_general(flat, place_hot(), (((1,), (1,)), ((), ())), precision=highest)
     return cube[:, ::-1].reshape(heads, -1)
+
+
+def block_spec(heads, place):
+    return pl.BlockSpec((heads, N_TIME, FRAME, FRAME), lambda i: (place, 0, 0, 0))
 
 
 def frame_span(frame):
@@ -419,14 +443,14 @@
 def attend_call(attn_in, weight, blocks, deps=()):
     rows, width = attn_in.shape
     cols = weight.shape[2]
-    heads = blocks.shape[0]
+    blocks, place, heads = blocks
     windows = rows // WIN_TOK
     stat_rows = -(-heads // 8) * 8
     return call_after(
         attend_kernel,
         deps,
         grid=(windows,),
-        in_specs=[row_spec(WIN_TOK, width), whole_spec(weight.shape), whole_spec(blocks.shape)],
+        in_specs=[row_spec(WIN_TOK, width), whole_spec(weight.shape), block_spec(heads, place)],
         out_specs=[
             part_spec(WIN_TOK, cols),
             row_spec(WIN_TOK, cols),
@@ -519,7 +543,7 @@
 def attend_back_call(grad_attn, out_weight, qkv, mixed, lse, blocks, attn_in, deps=()):
     rows, width = grad_attn.shape
     cols = out_weight.shape[0]
-    heads = blocks.shape[0]
+    blocks, place, heads = blocks
     return call_after(
         attend_back_kernel,
         deps,
@@ -530,17 +554,17 @@
             part_spec(WIN_TOK, cols),
             row_spec(WIN_TOK, cols),
             mod_spec(lse.shape[1], PAD_TOK),
-            whole_spec(blocks.shape),
+            block_spec(heads, place),
             row_spec(WIN_TOK, width),
         ],
         out_specs=[
             part_spec(WIN_TOK, cols),
-            whole_spec(blocks.shape),
+            block_spec(heads, 0),
             whole_spec((3, width, cols)),
         ],
         out_shape=[
             shaped((3, rows, cols), BF),
-            shaped(blocks.shape, F32),
+            shaped((heads,) + blocks.shape[1:], F32),
             shaped((3, width, cols), BF),
         ],
         scratch_shapes=[pltpu.VMEM((heads, WIN_TOK, PAD_TOK), F32)] * 2
@@ -549,6 +573,30 @@
         cost_estimate=cost(30),
         name="attend_back",
     )(grad_attn, out_weight, qkv, mixed, lse, blocks, attn_in)
+
+
+def out_grad_kernel(grad_ref, *refs):
+    count = len(refs) // 2
+    for place in range(count):
+
+        @pl.when(pl.program_id(0) == place)
+        def _():
+            refs[count + place][...] = dot(refs[place][...], grad_ref[...], 0, 0).astype(BF)
+
+
+def out_grad_call(mixed, grad_attn):
+    rows, width = grad_attn.shape
+    cols = mixed[0].shape[1]
+    return pl.pallas_call(
+        out_grad_kernel,
+        grid=(len(mixed),),
+        in_specs=[whole_spec(grad_attn.shape)] + [whole_spec(part.shape) for part in mixed],
+        out_specs=[whole_spec((cols, width))] * len(mixed),
+        out_shape=[shaped((cols, width), BF)] * len(mixed),
+        compiler_params=params(),
+        cost_estimate=cost(0.001),
+        name="out_grad",
+    )(grad_attn, *mixed)
 
 
 def middle_kernel(*refs, count):
@@ -592,8 +640,7 @@
     x_ref, g_ref, up_ref, down_ref = refs[:4]
     rest = refs[4:] if first else refs[6:]
     out_ref, gin_ref = rest[:2]
-    ddown_refs, dup_refs = rest[2:4], rest[4:6]
-    down_total, up_total, act, ghid = rest[6:]
+    ddown_ref, dup_ref, down_total, up_total, act, ghid = rest[2:]
     step = pl.program_id(0)
     hidden_width = up_ref.shape[1]
     x = x_ref[...]
@@ -629,10 +676,8 @@
 
     @pl.when(step == pl.num_programs(0) - 1)
     def _():
-        for total, halves in ((down_total, ddown_refs), (up_total, dup_refs)):
-            size = halves[0].shape[0]
-            halves[0][...] = total[:size].astype(BF)
-            halves[1][...] = total[size:].astype(BF)
+        ddown_ref[...] = down_total[...].astype(BF)
+        dup_ref[...] = up_total[...].astype(BF)
 
 
 def mlp_call(x, g, up, down, sums, deps=()):
@@ -642,7 +687,7 @@
     row = row_spec(block, width)
     first = sums is None
     extra = () if first else tuple(sums)
-    halves = [(hidden // 2, width)] * 2 + [(width // 2, hidden)] * 2
+    halves = [down.shape, up.shape]
     out = call_after(
         functools.partial(mlp_kernel, chunk=min(512, hidden), first=first),
         deps,
@@ -793,7 +838,6 @@
     rel_tables = gather_shards(rel_bias, "mp", n_mp)
     blocks = bias_blocks(jnp.concatenate([rel_tables[m] for m in masks], axis=0))
     heads = rel_bias.shape[0]
-    blocks = {m: blocks[m * heads : (m + 1) * heads] for m in masks}
 
     def gather(own, hold):
         shards = {}
@@ -813,7 +857,7 @@
     qkv, mixed, lse = {}, {}, {}
     for m in masks:
         ties = need(qkv_w, m, ties, attn_in)
-        qkv[m], mixed[m], lse[m] = attend_call(attn_in, qkv_w[m], blocks[m], ties)
+        qkv[m], mixed[m], lse[m] = attend_call(attn_in, qkv_w[m], (blocks, m, heads), ties)
         if m == 0:
             down_w = gather(down_weight, 4)
         elif m == 2 or m == n_mp - 1 == 1:
@@ -825,10 +869,10 @@
         [mixed[m] for m in masks], [out_w[m] for m in masks], tokens_flat, cot_flat, mods, ties
     )
     ties = steps.step(mlp_in)
-    wide_sums = [Sums(steps, n_mp, lag, 1) for lag in (0, 0, 1, 2)]
+    wide_sums = [Sums(steps, n_mp, 0, 1), Sums(steps, n_mp, 1, 2)]
     grads = {}
-    steps.jobs.append(psum_job(wide_sums[:2], n_dp, 0, grads, "down"))
-    steps.jobs.append(psum_job(wide_sums[2:], n_dp, 2, grads, "up"))
+    steps.jobs.append(spread_job(steps, wide_sums[0], n_dp, True, grads, "down"))
+    steps.jobs.append(spread_job(steps, wide_sums[1], n_dp, False, grads, "up"))
     sums = None
     for m in [m for m in masks if m % 2] + [m for m in reversed(masks) if m % 2 == 0]:
         ties = need(down_w, m, need(up_w, m, ties, mlp_in), mlp_in)
@@ -845,42 +889,41 @@
         grouped = window_sums.reshape(micro, own_windows, -1)
         return jnp.einsum("mwc,mwe->mce", clip_hot, grouped, precision=highest).astype(BF)
 
-    steps.jobs.append(all_job(steps, clip_sums(late_sums), n_mp, n_dp, grads, "late"))
-
     out_sum = Sums(steps, n_mp, 0, 1)
     qkv_sum = Sums(steps, n_mp, 0, 1)
-    steps.jobs.append(psum_job([out_sum], n_dp, 4, grads, "out"))
-    steps.jobs.append(spread_job(steps, qkv_sum, n_dp, grads, "qkv"))
+    steps.jobs.append(psum_job(out_sum, "down", grads, "out"))
+    steps.jobs.append(spread_job(steps, qkv_sum, n_dp, False, grads, "qkv"))
     dqkv, block_grads = {}, {}
-    for m in masks:
-        out_sum.add(m, dot(mixed[m], grad_attn, 0, 0).astype(BF))
+    for m, out_term in zip(masks, out_grad_call([mixed[m] for m in masks], grad_attn)):
+        out_sum.add(m, out_term)
     ties = steps.step(grad_attn)
     for m in reversed(masks):
         dqkv[m], block_grads[m], qkv_term = attend_back_call(
-            grad_attn, out_w[m], qkv[m], mixed[m], lse[m], blocks[m], attn_in, ties
+            grad_attn, out_w[m], qkv[m], mixed[m], lse[m], (blocks, m, heads), attn_in, ties
         )
         qkv_sum.add(m, qkv_term.reshape(-1, qkv_term.shape[2]))
         ties = steps.step(qkv_term)
     token_grad, early_sums = last_call(
         [dqkv[m] for m in masks], [qkv_w[m] for m in masks], tokens_flat, grad_resid, mods, ties
     )
-    steps.jobs.append(all_job(steps, clip_sums(early_sums), n_mp, n_dp, grads, "early"))
+    window_sums = jnp.concatenate([early_sums, late_sums], axis=1)
+    steps.jobs.append(all_job(steps, clip_sums(window_sums), n_mp, n_dp, grads, "mod"))
     steps.step(token_grad)
     steps.finish()
-    down_grad, up_grad, out_grad = [
-        jnp.concatenate([after(part, token_grad) for part in grads[name]], axis=0).astype(F32)
-        for name in ("down", "up", "out")
-    ]
+
+    def gathered(name, shape):
+        pieces = after(grads[name], token_grad)
+        return jnp.swapaxes(pieces, 0, 1).astype(F32).reshape(shape)
+
+    down_grad = gathered("down", down_weight.shape)
+    up_grad = grads["up"]
+    out_grad = after(grads["out"], token_grad).astype(F32)
     qkv_grad = grads["qkv"].reshape(qkv_weight.shape)
     rel_grads = collect_blocks(jnp.concatenate([block_grads[m] for m in masks], axis=0)).astype(BF)
     rel_terms = {m: rel_grads[m * heads : (m + 1) * heads] for m in masks}
     rel_grad = reduce_all(reduce_shards(rel_terms, "mp", n_mp), "dp", n_dp).astype(F32)
 
-    late = grads["late"].astype(F32).reshape(micro, clips, -1, width)
-    early = grads["early"].astype(F32).reshape(micro, clips, -1, width)
-    mod_total = jnp.concatenate(
-        [early, late[:, :, 0:1], late[:, :, 1:4]], axis=2
-    ).reshape(micro, clips, 6 * width)
+    mod_total = grads["mod"].astype(F32)
     ada_bias_grad = jnp.sum(mod_total, axis=(0, 1))
     ada_weight_grad = jnp.einsum(
         "mcd,mce->de", lowered.astype(F32), mod_total, precision=highest

time: 847 us -> 709 us (0.84)
  waiting for transfers between devices: 191 us -> 41.6 us
  Pallas kernels: 464 us -> 524 us
  other arithmetic: 54.7 us -> 17.1 us
  matrix products: 32.6 us -> 19 us
    psum x3 -> x1, waiting for transfers between devices: 133 us -> 0.01 us  [psum_job(): out[name] = lax.psum(after(value, out[earlier]), 'dp')]
    convert_element_type x13 -> x1, other arithmetic: 38.9 us -> 2.14 us  [body(): out_grad = after(grads['out'], token_grad).astype(F32)]
    pallas_call x0 -> x9, Pallas kernels: none -> 35.1 us  [the longest x8 23.2 us: add_parts(): pl.pallas_call(sum_kernel, grid=(rows // block,), in_specs=[row_spec(bloc...]
    pallas_call x2 -> x6, Pallas kernels: 6.38 us -> 24.4 us  [split_call(): pl.pallas_call(functools.partial(split_kernel, count=count, terms=len(par...]
    dot_general x4 -> x0, matrix products: 16.5 us -> none  [dot(): lax.dot_general(left, right, (((left_dim,), (right_dim,)), ((), ())), pre...]
    ppermute x62 -> x60, waiting for transfers between devices: 57.1 us -> 41.6 us  [swap(): return lax.ppermute(value, axis, [(i, i ^ bit) for i in range(size)])]
    slice x5 -> x0, local copies, waits for them, and re-layouts: 11.9 us -> none  [body(): blocks = {m: blocks[m * heads:(m + 1) * heads] for m in masks}]
    ppermute x62 -> x60, starting transfers between devices: 52.1 us -> 56.3 us  [swap(): return lax.ppermute(value, axis, [(i, i ^ bit) for i in range(size)])]
  transfers between devices with their start and end apart: 65 -> 62, of which waited for: 18 -> 10; matrix products, arithmetic and copies ran while one was open for 12% -> 8% of each run, Pallas kernels for 51% -> 73%
where the time goes in v3:
time: 709 us; the launch traced here: 698 us
  Pallas kernels  524 us (74%)
  starting transfers between devices  56.4 us (8%)
  waiting for transfers between devices  41.6 us (6%)
  local copies, waits for them, and re-layouts  25.1 us (4%)
  matrix products  19 us (3%)
  other arithmetic  17.1 us (2%)
  between operations  15 us (2%)
    pallas_call x16, Pallas kernels, call_after(): return lambda *args: call(*args, *deps)  452 us
    ppermute x60, starting transfers between devices, swap(): return lax.ppermute(value, axis, [(i, i ^ bit) for i in range(size)])  56.3 us
    ppermute x60, waiting for transfers between devices, swap(): return lax.ppermute(value, axis, [(i, i ^ bit) for i in range(size)])  41.6 us
    pallas_call x6, Pallas kernels, split_call(): pl.pallas_call(functools.partial(split_kernel, count=count, terms=len(par...  24.4 us
    pallas_call x8, Pallas kernels, add_parts(): pl.pallas_call(sum_kernel, grid=(rows // block,), in_specs=[row_spec(bloc...  23.2 us
  transfers between devices with their start and end apart: 62, of which 10 were waited for; matrix products, arithmetic and copies ran while one was open for 8% of the time, Pallas kernels for 73%

profile of v3, /device:TPU:0, one launch (start us, length us, event | category | flops | bytes accessed | tf_op | source)
XLA Modules:
  0.0 697.9 jit_solution(17328679375132365449)
XLA Ops:
  7.2 3.0 collective-permute-start.3
  18.0 1.8 dot_general.32
  21.0 4.6 fusion.1
  25.7 3.7 copy.39.refs_2_.refs_5_
  29.4 2.7 collective-permute-done.1
  33.8 8.7 %norm_in.1.refs_0_.refs_3_.refs_6_ = bf16[2560,1024]{1,0:T(8,128)(2,1)} custom-call(bf16[2560,1024]{1,0:T(8,128)(2,1)} %bitcast.52, f32[8,6,1024]{2,1,0:T(8,128)} %reshape.219.refs_1_.refs_10_.refs_5_), custom_call_target="tpu_custom_call" | custom-call | flops 8000000000 | bytes 28000000 | tf_op jit(solution)/shard_map/norm_in/pallas_call | solution.py:75
  42.5 1.7 collective-permute-start.8
  44.3 19.3 %attend.4 = (bf16[3,2560,256]{2,1,0:T(8,128)(2,1)}, bf16[2560,256]{1,0:T(8,128)(2,1)}, f32[8,8,384]{2,1,0:T(8,128)}) custom-call(bf16[2560,1024]{1,0:T(8,128)(2,1)} %norm_in.1.refs_0_.refs_3_.refs_6_, bf16[3,1024,256]{2,1,0:T(8,128)(2,1)} %refs_4_.3, f32[16,9,64,64]{3,2,1,0:T(8,128)} %copy.39.refs_2_.refs_5_, bf16[2560,1024]{1,0:T(8,128)(2,1)} %norm_in.1.refs_0_.refs_3_.refs_6_), custom_call_target="tpu_custom_call" | custom-call | flops 19000000512 | bytes 66500000 | tf_op jit(solution)/shard_map/attend/pallas_call | solution.py:75
  64.3 19.2 %attend.5 = (bf16[3,2560,256]{2,1,0:T(8,128)(2,1)}, bf16[2560,256]{1,0:T(8,128)(2,1)}, f32[8,8,384]{2,1,0:T(8,128)}) custom-call(bf16[2560,1024]{1,0:T(8,128)(2,1)} %norm_in.1.refs_0_.refs_3_.refs_6_, bf16[3,1024,256]{2,1,0:T(8,128)(2,1)} %collective-permute-done.5.refs_1_.refs_5_, f32[16,9,64,64]{3,2,1,0:T(8,128)} %copy.39.refs_2_.refs_5_, ...), custom_call_target="tpu_custom_call" | custom-call | flops 19000000512 | bytes 66500000 | tf_op jit(solution)/shard_map/attend/pallas_call | solution.py:75
  83.6 19.3 %attend.6 = (bf16[3,2560,256]{2,1,0:T(8,128)(2,1)}, bf16[2560,256]{1,0:T(8,128)(2,1)}, f32[8,8,384]{2,1,0:T(8,128)}) custom-call(bf16[2560,1024]{1,0:T(8,128)(2,1)} %norm_in.1.refs_0_.refs_3_.refs_6_, bf16[3,1024,256]{2,1,0:T(8,128)(2,1)} %collective-permute-done.6.refs_1_.refs_3_.refs_6_, f32[16,9,64,64]{3,2,1,0:T(8,128)} %copy.39.refs_2_.refs_5_, ...), custom_call_target="tpu_custom_call" | custom-call | flops 19000000512 | bytes 66500000 | tf_op jit(solution)/shard_map/attend/pallas_call | solution.py:75
  103.6 19.3 %attend.7 = (bf16[3,2560,256]{2,1,0:T(8,128)(2,1)}, bf16[2560,256]{1,0:T(8,128)(2,1)}, f32[8,8,384]{2,1,0:T(8,128)}) custom-call(bf16[2560,1024]{1,0:T(8,128)(2,1)} %norm_in.1.refs_0_.refs_3_.refs_6_, bf16[3,1024,256]{2,1,0:T(8,128)(2,1)} %collective-permute-done.7.refs_1_.refs_7_, f32[16,9,64,64]{3,2,1,0:T(8,128)} %copy.39.refs_2_.refs_5_, ...), custom_call_target="tpu_custom_call" | custom-call | flops 19000000512 | bytes 66500000 | tf_op jit(solution)/shard_map/attend/pallas_call | solution.py:75
  122.8 1.8 collective-permute-start.11
  124.6 16.6 %middle.1 = (f32[2560,1024]{1,0:T(8,128)}, bf16[2560,1024]{1,0:T(8,128)(2,1)}, bf16[2560,1024]{1,0:T(8,128)(2,1)}) custom-call(bf16[2560,256]{1,0:T(8,128)(2,1)} %get-tuple-element.149.refs_3_.refs_0_, bf16[2560,256]{1,0:T(8,128)(2,1)} %get-tuple-element.151.refs_4_.refs_1_.refs_3_, bf16[2560,256]{1,0:T(8,128)(2,1)} %get-tuple-element.153.refs_4_.refs_2_.refs_3_, ...), custom_call_target="tpu_custom_call" | custom-call | flops 16000000000 | bytes 56000000 | tf_op jit(solution)/shard_map/middle/pallas_call | solution.py:75
  141.4 43.9 %mlp.4 = (f32[2560,1024]{1,0:T(8,128)}, f32[2560,1024]{1,0:T(8,128)}, bf16[1024,1024]{1,0:T(8,128)(2,1)}, bf16[1024,1024]{1,0:T(8,128)(2,1)}) custom-call(bf16[2560,1024]{1,0:T(8,128)(2,1)} %get-tuple-element.160.refs_0_.refs_5_, bf16[2560,1024]{1,0:T(8,128)(2,1)} %get-tuple-element.161.refs_1_, bf16[1024,1024]{1,0:T(8,128)(2,1)} %collective-permute-done.12.refs_2_, ...), custom_call_target="tpu_custom_call" | custom-call | flops 46000001024 | bytes 161000000 | tf_op jit(solution)/shard_map/mlp/pallas_call | solution.py:75
  186.9 3.0 collective-permute-done.15.refs_2_
  189.9 45.7 %mlp.5 = (f32[2560,1024]{1,0:T(8,128)}, f32[2560,1024]{1,0:T(8,128)}, bf16[1024,1024]{1,0:T(8,128)(2,1)}, bf16[1024,1024]{1,0:T(8,128)(2,1)}) custom-call(bf16[2560,1024]{1,0:T(8,128)(2,1)} %get-tuple-element.160.refs_0_.refs_5_, bf16[2560,1024]{1,0:T(8,128)(2,1)} %get-tuple-element.161.refs_1_, ...), custom_call_target="tpu_custom_call", output_to_operand_aliasing={{0}: (4, {}), {1}: (5, {})} | custom-call | flops 46000001024 | bytes 161000000 | tf_op jit(solution)/shard_map/mlp/pallas_call | solution.py:75
  236.2 45.9 %mlp.6 = (f32[2560,1024]{1,0:T(8,128)}, f32[2560,1024]{1,0:T(8,128)}, bf16[1024,1024]{1,0:T(8,128)(2,1)}, bf16[1024,1024]{1,0:T(8,128)(2,1)}) custom-call(bf16[2560,1024]{1,0:T(8,128)(2,1)} %get-tuple-element.160.refs_0_.refs_5_, bf16[2560,1024]{1,0:T(8,128)(2,1)} %get-tuple-element.161.refs_1_, ...), custom_call_target="tpu_custom_call", output_to_operand_aliasing={{0}: (4, {}), {1}: (5, {})} | custom-call | flops 46000001024 | bytes 161000000 | tf_op jit(solution)/shard_map/mlp/pallas_call | solution.py:75
  282.1 4.3 add.236
  286.8 45.5 %mlp.7 = (f32[2560,1024]{1,0:T(8,128)}, f32[2560,1024]{1,0:T(8,128)}, bf16[1024,1024]{1,0:T(8,128)(2,1)}, bf16[1024,1024]{1,0:T(8,128)(2,1)}) custom-call(bf16[2560,1024]{1,0:T(8,128)(2,1)} %get-tuple-element.160.refs_0_.refs_5_, bf16[2560,1024]{1,0:T(8,128)(2,1)} %get-tuple-element.161.refs_1_, ...), custom_call_target="tpu_custom_call", output_to_operand_aliasing={{0}: (4, {}), {1}: (5, {})} | custom-call | flops 46000001024 | bytes 161000000 | tf_op jit(solution)/shard_map/mlp/pallas_call | solution.py:75
  332.3 4.3 add.238
  338.3 4.9 split.6
  344.8 24.3 %middle_back.1 = (bf16[2560,1024]{1,0:T(8,128)(2,1)}, f32[2560,1024]{1,0:T(8,128)}, bf16[2560,1024]{1,0:T(8,128)(2,1)}, f32[8,4,1024]{2,1,0:T(4,128)}) custom-call(bf16[2560,1024]{1,0:T(8,128)(2,1)} %bitcast.54, bf16[2560,1024]{1,0:T(8,128)(2,1)} %bitcast.51, f32[2560,1024]{1,0:T(8,128)} %get-tuple-element.159.refs_2_, ...), custom_call_target="tpu_custom_call" | custom-call | flops 24000000000 | bytes 84000000 | tf_op jit(solution)/shard_map/middle_back/pallas_call | solution.py:75
  369.0 11.9 %out_grad.1 = (bf16[256,1024]{1,0:T(8,128)(2,1)}, bf16[256,1024]{1,0:T(8,128)(2,1)}, bf16[256,1024]{1,0:T(8,128)(2,1)}, bf16[256,1024]{1,0:T(8,128)(2,1)}) custom-call(bf16[2560,1024]{1,0:T(8,128)(2,1)} %get-tuple-element.194.refs_0_.refs_12_.grad_ref, bf16[2560,256]{1,0:T(8,128)(2,1)} %get-tuple-element.149.refs_3_.refs_0_, ...), custom_call_target="tpu_custom_call" | custom-call | flops 1000000 | bytes 3500 | tf_op jit(solution)/shard_map/out_grad/pallas_call | solution.py:590
  381.4 3.5 split.7
  386.5 2.6 collective-permute-start.24
  389.3 28.9 %attend_back.4 = (bf16[3,2560,256]{2,1,0:T(8,128)(2,1)}, f32[4,9,64,64]{3,2,1,0:T(8,128)}, bf16[3,1024,256]{2,1,0:T(8,128)(2,1)}) custom-call(bf16[2560,1024]{1,0:T(8,128)(2,1)} %get-tuple-element.194.refs_0_.refs_12_.grad_ref, bf16[256,1024]{1,0:T(8,128)(2,1)} %collective-permute-done.10.refs_7_.refs_1_, bf16[3,2560,256]{2,1,0:T(8,128)(2,1)} %get-tuple-element.203.refs_2_, ...), custom_call_target="tpu_custom_call" | custom-call | flops 30000001024 | bytes 105000000 | tf_op jit(solution)/shard_map/attend_back/pallas_call | solution.py:75
  418.2 5.0 split.8
  424.7 2.1 add.239
  428.9 2.0 add.237.refs_8_
  431.0 29.4 %attend_back.5 = (bf16[3,2560,256]{2,1,0:T(8,128)(2,1)}, f32[4,9,64,64]{3,2,1,0:T(8,128)}, bf16[3,1024,256]{2,1,0:T(8,128)(2,1)}) custom-call(bf16[2560,1024]{1,0:T(8,128)(2,1)} %get-tuple-element.194.refs_0_.refs_12_.grad_ref, bf16[256,1024]{1,0:T(8,128)(2,1)} %collective-permute-done.8.refs_3_.refs_6_.refs_1_, ...), custom_call_target="tpu_custom_call" | custom-call | flops 30000001024 | bytes 105000000 | tf_op jit(solution)/shard_map/attend_back/pallas_call | solution.py:75
  460.4 2.4 add.240.refs_14_
  462.8 3.5 split.9
  466.3 3.2 collective-permute-start.33
  470.7 4.0 add.242
  475.2 29.1 %attend_back.6 = (bf16[3,2560,256]{2,1,0:T(8,128)(2,1)}, f32[4,9,64,64]{3,2,1,0:T(8,128)}, bf16[3,1024,256]{2,1,0:T(8,128)(2,1)}) custom-call(bf16[2560,1024]{1,0:T(8,128)(2,1)} %get-tuple-element.194.refs_0_.refs_12_.grad_ref, bf16[256,1024]{1,0:T(8,128)(2,1)} %collective-permute-done.9.refs_5_.refs_1_, bf16[3,2560,256]{2,1,0:T(8,128)(2,1)} %get-tuple-element.213.refs_2_, ...), custom_call_target="tpu_custom_call" | custom-call | flops 30000001024 | bytes 105000000 | tf_op jit(solution)/shard_map/attend_back/pallas_call | solution.py:75
  505.8 2.0 add.241.refs_8_.refs_0_
  508.1 3.8 collective-permute-start.37
  512.2 29.2 %attend_back.7 = (bf16[3,2560,256]{2,1,0:T(8,128)(2,1)}, f32[4,9,64,64]{3,2,1,0:T(8,128)}, bf16[3,1024,256]{2,1,0:T(8,128)(2,1)}) custom-call(bf16[2560,1024]{1,0:T(8,128)(2,1)} %get-tuple-element.194.refs_0_.refs_12_.grad_ref, bf16[256,1024]{1,0:T(8,128)(2,1)} %refs_1_.3, bf16[3,2560,256]{2,1,0:T(8,128)(2,1)} %get-tuple-element.195.refs_2_, ...), custom_call_target="tpu_custom_call" | custom-call | flops 30000001024 | bytes 105000000 | tf_op jit(solution)/shard_map/attend_back/pallas_call | solution.py:75
  541.5 4.1 split.10
  547.0 2.8 assemble.4.refs_11_.refs_0_
  550.5 27.8 %last.1 = (bf16[2560,1024]{1,0:T(8,128)(2,1)}, f32[8,2,1024]{2,1,0:T(2,128)}) custom-call(bf16[3,2560,256]{2,1,0:T(8,128)(2,1)} %get-tuple-element.252.refs_0_, bf16[3,2560,256]{2,1,0:T(8,128)(2,1)} %get-tuple-element.253.refs_1_, bf16[3,2560,256]{2,1,0:T(8,128)(2,1)} %get-tuple-element.254.refs_2_, bf16[3,2560,256]{2,1,0:T(8,128)(2,1)} %get-tuple-element.255.refs_3_, ...), custom_call_target="tpu_custom_call" | custom-call | flops 28000000000 | bytes 98000000 | tf_op jit(solution)/shard_map/last/pallas_call | solution.py:75
  578.3 2.1 convert_bitcast_fusion
  580.4 2.4 copy.47
  584.3 2.8 pad_maximum_fusion
  587.1 5.5 reshape.232
  592.6 4.1 fusion.3
  610.8 2.5 collective-permute-done.56
  614.4 5.2 collective-permute-done.57
  619.7 3.4 split.11
  623.1 2.0 collective-permute-start.41
  629.6 2.6 collective-permute-done.41.refs_1_
  632.2 2.6 collective-permute-start.54
  634.7 7.4 %collective-permute-done.42.refs_2_ = bf16[384,256]{1,0:T(8,128)(2,1)S(1)} collective-permute-done((bf16[384,256]{1,0:T(8,128)(2,1)}, bf16[384,256]{1,0:T(8,128)(2,1)S(1)}, u32[]{:S(2)}, u32[]{:S(2)}) %collective-permute-start.42) | collective-permute-done | bytes 196640 | tf_op jit(solution)/shard_map/ppermute | solution.py:97
  642.9 2.0 add.243.refs_0_
  644.9 2.6 collective-permute-start.44
  647.5 1.8 collective-permute-start.45
  650.8 3.5 collective-permute-done.44.refs_1_
  654.4 3.1 collective-permute-start.59
  657.4 11.7 %collective-permute-done.45.refs_2_ = bf16[384,256]{1,0:T(8,128)(2,1)} collective-permute-done((bf16[384,256]{1,0:T(8,128)(2,1)}, bf16[384,256]{1,0:T(8,128)(2,1)}, u32[]{:S(2)}, u32[]{:S(2)}) %collective-permute-start.45) | collective-permute-done | bytes 196640 | tf_op jit(solution)/shard_map/ppermute | solution.py:97
  669.2 2.7 assemble.5.refs_0_
  674.7 2.1 convert_element_type.147
  680.1 3.7 convolution_bitcast_fusion
  683.8 3.7 assemble.7
  687.5 3.1 assemble.6
  (193 shorter events, 59.3 us)
Async XLA Ops:
  7.2 505.0 %all-gather.3.cloned.1.call-start = ((), (), s32[]{:S(2)}) async-start(), calls=%async_computation.1 | async-start | bytes 2359296 | tf_op jit(solution)/shard_map/all_gather | solution.py:321
  7.2 7.8 %collective-permute-start.3 = (f32[4,2025]{1,0:T(4,128)}, f32[4,2025]{1,0:T(4,128)}, u32[]{:S(2)}, u32[]{:S(2)}) collective-permute-start(f32[4,2025]{1,0:T(4,128)} %param.19), channel_id=1, source_target_pairs={{0,2},{1,3},{2,0},{3,1},{4,6},{5,7},{6,4},{7,5},{8,10},{9,11},{10,... | collective-permute-start | bytes 97208 | tf_op jit(solution)/shard_map/ppermute | solution.py:97
  10.3 4.9 collective-permute-start.2
  13.8 6.0 collective-permute-start
  15.1 1.4 collective-permute-start.4
  20.8 11.2 %collective-permute-start.1 = (f32[2,8,6144]{2,1,0:T(8,128)S(1)}, f32[2,8,6144]{2,1,0:T(8,128)S(1)}, u32[]{:S(2)}, u32[]{:S(2)}) collective-permute-start(f32[2,8,6144]{2,1,0:T(8,128)S(1)} %add.169), channel_id=1, source_target_pairs={{0,2},{1,3},{2,0},{3,1},{4,6},{5,7},{6,4},{7,5},{8,10},{9,11},{10,... | collective-permute-start | bytes 1179656 | tf_op jit(solution)/shard_map/ppermute | solution.py:97
  32.1 31.9 %collective-permute-start.5 = (bf16[3,1024,256]{2,1,0:T(8,128)(2,1)}, bf16[3,1024,256]{2,1,0:T(8,128)(2,1)}, u32[]{:S(2)}, u32[]{:S(2)}) collective-permute-start(bf16[3,1024,256]{2,1,0:T(8,128)(2,1)} %refs_4_.3), channel_id=1, source_target_pairs={{0,1},{1,0},{2,3},{3,2},{4,5},{5,4},{6,7},{7,6},{8,9},{9,8},{10,11... | collective-permute-start | bytes 4718600 | tf_op jit(solution)/shard_map/ppermute | solution.py:97
  32.2 51.3 %collective-permute-start.6 = (bf16[3,1024,256]{2,1,0:T(8,128)(2,1)}, bf16[3,1024,256]{2,1,0:T(8,128)(2,1)}, u32[]{:S(2)}, u32[]{:S(2)}) collective-permute-start(bf16[3,1024,256]{2,1,0:T(8,128)(2,1)} %refs_4_.3), channel_id=1, source_target_pairs={{0,2},{1,3},{2,0},{3,1},{4,6},{5,7},{6,4},{7,5},{8,10},{9,11},{10,... | collective-permute-start | bytes 4718600 | tf_op jit(solution)/shard_map/ppermute | solution.py:97
  42.5 60.4 %collective-permute-start.8 = (bf16[256,1024]{1,0:T(8,128)(2,1)S(1)}, bf16[256,1024]{1,0:T(8,128)(2,1)}, u32[]{:S(2)}, u32[]{:S(2)}) collective-permute-start(bf16[256,1024]{1,0:T(8,128)(2,1)S(1)} %copy-done.24), channel_id=1, source_target_pairs={{0,2},{1,3},{2,0},{3,1},{4,6},{5,7},{6,4},{7,5},{8,10},{9,11},{10,... | collective-permute-start | bytes 1572872 | tf_op jit(solution)/shard_map/ppermute | solution.py:97
  44.3 78.6 %collective-permute-start.9 = (bf16[256,1024]{1,0:T(8,128)(2,1)S(1)}, bf16[256,1024]{1,0:T(8,128)(2,1)}, u32[]{:S(2)}, u32[]{:S(2)}) collective-permute-start(bf16[256,1024]{1,0:T(8,128)(2,1)S(1)} %copy-done.24), channel_id=1, source_target_pairs={{0,1},{1,0},{2,3},{3,2},{4,5},{5,4},{6,7},{7,6},{8,9},{9,8},{10,11... | collective-permute-start | bytes 1572872 | tf_op jit(solution)/shard_map/ppermute | solution.py:97
  63.5 77.9 %collective-permute-start.13 = (bf16[1024,1024]{1,0:T(8,128)(2,1)}, bf16[1024,1024]{1,0:T(8,128)(2,1)}, u32[]{:S(2)}, u32[]{:S(2)}) collective-permute-start(bf16[1024,1024]{1,0:T(8,128)(2,1)} %refs_3_.1), channel_id=1, source_target_pairs={{0,1},{1,0},{2,3},{3,2},{4,5},{5,4},{6,7},{7,6},{8,9},{9,8},{10,11... | collective-permute-start | bytes 6291464 | tf_op jit(solution)/shard_map/ppermute | solution.py:97
  64.0 77.2 %collective-permute-start.14 = (bf16[1024,1024]{1,0:T(8,128)(2,1)}, bf16[1024,1024]{1,0:T(8,128)(2,1)}, u32[]{:S(2)}, u32[]{:S(2)}) collective-permute-start(bf16[1024,1024]{1,0:T(8,128)(2,1)} %refs_3_.1), channel_id=1, source_target_pairs={{0,2},{1,3},{2,0},{3,1},{4,6},{5,7},{6,4},{7,5},{8,10},{9,11},{10,... | collective-permute-start | bytes 6291464 | tf_op jit(solution)/shard_map/ppermute | solution.py:97
  83.6 19.9 %collective-permute-start.7 = (bf16[3,1024,256]{2,1,0:T(8,128)(2,1)}, bf16[3,1024,256]{2,1,0:T(8,128)(2,1)}, u32[]{:S(2)}, u32[]{:S(2)}) collective-permute-start(bf16[3,1024,256]{2,1,0:T(8,128)(2,1)} %collective-permute-done.6.refs_1_.refs_3_.refs_6_), channel_id=1, source_target_pairs={{0,1},{1,0},{2,3},{3,2},{4,5},{5,4},{6,7},{7,6},{8,9},{9,8},{10,11... | collective-permute-start | bytes 4718600 | tf_op jit(solution)/shard_map/ppermute | solution.py:97
  102.9 21.7 %collective-permute-start.10 = (bf16[256,1024]{1,0:T(8,128)(2,1)}, bf16[256,1024]{1,0:T(8,128)(2,1)}, u32[]{:S(2)}, u32[]{:S(2)}) collective-permute-start(bf16[256,1024]{1,0:T(8,128)(2,1)} %collective-permute-done.8.refs_3_.refs_6_.refs_1_), channel_id=1, source_target_pairs={{0,1},{1,0},{2,3},{3,2},{4,5},{5,4},{6,7},{7,6},{8,9},{9,8},{10,11... | collective-permute-start | bytes 1572872 | tf_op jit(solution)/shard_map/ppermute | solution.py:97
  103.5 38.0 %collective-permute-start.12 = (bf16[1024,1024]{1,0:T(8,128)(2,1)}, bf16[1024,1024]{1,0:T(8,128)(2,1)}, u32[]{:S(2)}, u32[]{:S(2)}) collective-permute-start(bf16[1024,1024]{1,0:T(8,128)(2,1)} %refs_2_.1), channel_id=1, source_target_pairs={{0,1},{1,0},{2,3},{3,2},{4,5},{5,4},{6,7},{7,6},{8,9},{9,8},{10,11... | collective-permute-start | bytes 6291464 | tf_op jit(solution)/shard_map/ppermute | solution.py:97
  122.8 62.5 %collective-permute-start.11 = (bf16[1024,1024]{1,0:T(8,128)(2,1)}, bf16[1024,1024]{1,0:T(8,128)(2,1)}, u32[]{:S(2)}, u32[]{:S(2)}) collective-permute-start(bf16[1024,1024]{1,0:T(8,128)(2,1)} %refs_2_.1), channel_id=1, source_target_pairs={{0,2},{1,3},{2,0},{3,1},{4,6},{5,7},{6,4},{7,5},{8,10},{9,11},{10,... | collective-permute-start | bytes 6291464 | tf_op jit(solution)/shard_map/ppermute | solution.py:97
  141.2 45.7 %collective-permute-start.16 = (bf16[1024,1024]{1,0:T(8,128)(2,1)}, bf16[1024,1024]{1,0:T(8,128)(2,1)}, u32[]{:S(2)}, u32[]{:S(2)}) collective-permute-start(bf16[1024,1024]{1,0:T(8,128)(2,1)} %collective-permute-done.14.refs_4_.refs_3_), channel_id=1, source_target_pairs={{0,1},{1,0},{2,3},{3,2},{4,5},{5,4},{6,7},{7,6},{8,9},{9,8},{10,11... | collective-permute-start | bytes 6291464 | tf_op jit(solution)/shard_map/ppermute | solution.py:97
  141.4 44.3 %copy-start.6 = (s32[64,64]{1,0:T(8,128)S(1)}, s32[64,64]{1,0:T(8,128)}, u32[]{:S(2)}) copy-start(s32[64,64]{1,0:T(8,128)} %add_add_fusion.1) | copy-start | bytes 49156
  185.3 4.6 collective-permute-start.15
  186.4 49.2 %collective-permute-start.17 = (bf16[1024,1024]{1,0:T(8,128)(2,1)}, bf16[1024,1024]{1,0:T(8,128)(2,1)}, u32[]{:S(2)}, u32[]{:S(2)}) collective-permute-start(bf16[1024,1024]{1,0:T(8,128)(2,1)} %get-tuple-element.173.refs_7_), channel_id=1, source_target_pairs={{0,1},{1,0},{2,3},{3,2},{4,5},{5,4},{6,7},{7,6},{8,9},{9,8},{10,11... | collective-permute-start | bytes 6291464 | tf_op jit(solution)/shard_map/ppermute | solution.py:97
  186.6 49.0 %collective-permute-start.18 = (bf16[1024,1024]{1,0:T(8,128)(2,1)}, bf16[1024,1024]{1,0:T(8,128)(2,1)}, u32[]{:S(2)}, u32[]{:S(2)}) collective-permute-start(bf16[1024,1024]{1,0:T(8,128)(2,1)} %get-tuple-element.177), channel_id=1, source_target_pairs={{0,1},{1,0},{2,3},{3,2},{4,5},{5,4},{6,7},{7,6},{8,9},{9,8},{10,11... | collective-permute-start | bytes 6291464 | tf_op jit(solution)/shard_map/ppermute | solution.py:97
  235.6 46.5 %collective-permute-start.19 = (bf16[1024,1024]{1,0:T(8,128)(2,1)}, bf16[1024,1024]{1,0:T(8,128)(2,1)}, u32[]{:S(2)}, u32[]{:S(2)}) collective-permute-start(bf16[1024,1024]{1,0:T(8,128)(2,1)} %get-tuple-element.181.refs_8_), channel_id=1, source_target_pairs={{0,1},{1,0},{2,3},{3,2},{4,5},{5,4},{6,7},{7,6},{8,9},{9,8},{10,11... | collective-permute-start | bytes 6291464 | tf_op jit(solution)/shard_map/ppermute | solution.py:97
  236.0 46.1 %collective-permute-start.20 = (bf16[1024,1024]{1,0:T(8,128)(2,1)}, bf16[1024,1024]{1,0:T(8,128)(2,1)}, u32[]{:S(2)}, u32[]{:S(2)}) collective-permute-start(bf16[1024,1024]{1,0:T(8,128)(2,1)} %get-tuple-element.185), channel_id=1, source_target_pairs={{0,1},{1,0},{2,3},{3,2},{4,5},{5,4},{6,7},{7,6},{8,9},{9,8},{10,11... | collective-permute-start | bytes 6291464 | tf_op jit(solution)/shard_map/ppermute | solution.py:97
  286.5 51.9 %collective-permute-start.21 = (bf16[1024,1024]{1,0:T(8,128)(2,1)}, bf16[1024,1024]{1,0:T(8,128)(2,1)}, u32[]{:S(2)}, u32[]{:S(2)}) collective-permute-start(bf16[1024,1024]{1,0:T(8,128)(2,1)} %add.236), channel_id=1, source_target_pairs={{0,2},{1,3},{2,0},{3,1},{4,6},{5,7},{6,4},{7,5},{8,10},{9,11},{10,... | collective-permute-start | bytes 6291464 | tf_op jit(solution)/shard_map/ppermute | solution.py:97
  336.6 52.5 %collective-permute-start.26 = (bf16[1024,1024]{1,0:T(8,128)(2,1)}, bf16[1024,1024]{1,0:T(8,128)(2,1)}, u32[]{:S(2)}, u32[]{:S(2)}) collective-permute-start(bf16[1024,1024]{1,0:T(8,128)(2,1)} %add.238), channel_id=1, source_target_pairs={{0,2},{1,3},{2,0},{3,1},{4,6},{5,7},{6,4},{7,5},{8,10},{9,11},{10,... | collective-permute-start | bytes 6291464 | tf_op jit(solution)/shard_map/ppermute | solution.py:97
  343.3 38.1 %collective-permute-start.22 = (bf16[512,1024]{1,0:T(8,128)(2,1)}, bf16[512,1024]{1,0:T(8,128)(2,1)}, u32[]{:S(2)}, u32[]{:S(2)}) collective-permute-start(bf16[512,1024]{1,0:T(8,128)(2,1)} %get-tuple-element.198.refs_7_), channel_id=1, source_target_pairs={{0,4},{4,0},{8,12},{12,8},{16,20},{20,16},{24,28},{28,24},{1,5},{5... | collective-permute-start | bytes 3145736 | tf_op jit(solution)/shard_map/ppermute | solution.py:97
  380.9 42.3 %collective-permute-start.28 = (bf16[256,1024]{1,0:T(8,128)(2,1)}, bf16[256,1024]{1,0:T(8,128)(2,1)}, u32[]{:S(2)}, u32[]{:S(2)}) collective-permute-start(bf16[256,1024]{1,0:T(8,128)(2,1)} %get-tuple-element.225), channel_id=1, source_target_pairs={{0,1},{1,0},{2,3},{3,2},{4,5},{5,4},{6,7},{7,6},{8,9},{9,8},{10,11... | collective-permute-start | bytes 1572872 | tf_op jit(solution)/shard_map/ppermute | solution.py:97
  380.9 43.0 %collective-permute-start.29 = (bf16[256,1024]{1,0:T(8,128)(2,1)}, bf16[256,1024]{1,0:T(8,128)(2,1)S(1)}, u32[]{:S(2)}, u32[]{:S(2)}) collective-permute-start(bf16[256,1024]{1,0:T(8,128)(2,1)} %get-tuple-element.228), channel_id=1, source_target_pairs={{0,1},{1,0},{2,3},{3,2},{4,5},{5,4},{6,7},{7,6},{8,9},{9,8},{10,11... | collective-permute-start | bytes 1572872 | tf_op jit(solution)/shard_map/ppermute | solution.py:97
  384.9 43.2 %collective-permute-start.23 = (bf16[128,1024]{1,0:T(8,128)(2,1)}, bf16[128,1024]{1,0:T(8,128)(2,1)S(1)}, u32[]{:S(2)}, u32[]{:S(2)}) collective-permute-start(bf16[128,1024]{1,0:T(8,128)(2,1)} %get-tuple-element.202.refs_9_), channel_id=1, source_target_pairs={{0,8},{4,12},{8,0},{12,4},{16,24},{20,28},{24,16},{28,20},{1,9},{5... | collective-permute-start | bytes 786440 | tf_op jit(solution)/shard_map/ppermute | solution.py:97
  386.5 41.7 %collective-permute-start.24 = (bf16[128,1024]{1,0:T(8,128)(2,1)}, bf16[128,1024]{1,0:T(8,128)(2,1)}, u32[]{:S(2)}, u32[]{:S(2)}) collective-permute-start(bf16[128,1024]{1,0:T(8,128)(2,1)} %get-tuple-element.209.refs_10_), channel_id=1, source_target_pairs={{0,16},{4,20},{8,24},{12,28},{16,0},{20,4},{24,8},{28,12},{1,17},{... | collective-permute-start | bytes 786440 | tf_op jit(solution)/shard_map/ppermute | solution.py:97
  389.1 39.1 %collective-permute-start.25 = (bf16[128,1024]{1,0:T(8,128)(2,1)}, bf16[128,1024]{1,0:T(8,128)(2,1)}, u32[]{:S(2)}, u32[]{:S(2)}) collective-permute-start(bf16[128,1024]{1,0:T(8,128)(2,1)} %get-tuple-element.211.refs_11_), channel_id=1, source_target_pairs={{0,24},{4,28},{8,16},{12,20},{16,8},{20,12},{24,0},{28,4},{1,25},{... | collective-permute-start | bytes 786440 | tf_op jit(solution)/shard_map/ppermute | solution.py:97
  423.2 39.6 %collective-permute-start.27 = (bf16[512,1024]{1,0:T(8,128)(2,1)}, bf16[512,1024]{1,0:T(8,128)(2,1)}, u32[]{:S(2)}, u32[]{:S(2)}) collective-permute-start(bf16[512,1024]{1,0:T(8,128)(2,1)} %get-tuple-element.220.refs_9_), channel_id=1, source_target_pairs={{0,4},{4,0},{8,12},{12,8},{16,20},{20,16},{24,28},{28,24},{1,5},{5... | collective-permute-start | bytes 3145736 | tf_op jit(solution)/shard_map/ppermute | solution.py:97
  426.8 33.6 %collective-permute-start.30 = (bf16[256,1024]{1,0:T(8,128)(2,1)}, bf16[256,1024]{1,0:T(8,128)(2,1)}, u32[]{:S(2)}, u32[]{:S(2)}) collective-permute-start(bf16[256,1024]{1,0:T(8,128)(2,1)} %add.239), channel_id=1, source_target_pairs={{0,2},{1,3},{2,0},{3,1},{4,6},{5,7},{6,4},{7,5},{8,10},{9,11},{10,... | collective-permute-start | bytes 1572872 | tf_op jit(solution)/shard_map/ppermute | solution.py:97
  428.2 42.5 %collective-permute-start.31 = (bf16[3072,256]{1,0:T(8,128)(2,1)}, bf16[3072,256]{1,0:T(8,128)(2,1)}, u32[]{:S(2)}, u32[]{:S(2)}) collective-permute-start(bf16[3072,256]{1,0:T(8,128)(2,1)} %bitcast.56), channel_id=1, source_target_pairs={{0,1},{1,0},{2,3},{3,2},{4,5},{5,4},{6,7},{7,6},{8,9},{9,8},{10,11... | collective-permute-start | bytes 4718600 | tf_op jit(solution)/shard_map/ppermute | solution.py:97
  430.9 243.8 %all-reduce.2.cloned.1.call-start = ((), (), s32[]{:S(2)}) async-start(), calls=%async_computation | async-start | bytes 1048576 | tf_op jit(solution)/shard_map/psum | solution.py:293
  466.3 38.0 %collective-permute-start.32 = (bf16[128,1024]{1,0:T(8,128)(2,1)}, bf16[128,1024]{1,0:T(8,128)(2,1)S(1)}, u32[]{:S(2)}, u32[]{:S(2)}) collective-permute-start(bf16[128,1024]{1,0:T(8,128)(2,1)} %get-tuple-element.244.refs_9_), channel_id=1, source_target_pairs={{0,8},{4,12},{8,0},{12,4},{16,24},{20,28},{24,16},{28,20},{1,9},{5... | collective-permute-start | bytes 786440 | tf_op jit(solution)/shard_map/ppermute | solution.py:97
  466.3 38.1 %collective-permute-start.33 = (bf16[128,1024]{1,0:T(8,128)(2,1)}, bf16[128,1024]{1,0:T(8,128)(2,1)S(1)}, u32[]{:S(2)}, u32[]{:S(2)}) collective-permute-start(bf16[128,1024]{1,0:T(8,128)(2,1)} %get-tuple-element.246.refs_10_), channel_id=1, source_target_pairs={{0,16},{4,20},{8,24},{12,28},{16,0},{20,4},{24,8},{28,12},{1,17},{... | collective-permute-start | bytes 786440 | tf_op jit(solution)/shard_map/ppermute | solution.py:97
  469.5 34.8 %collective-permute-start.34 = (bf16[128,1024]{1,0:T(8,128)(2,1)}, bf16[128,1024]{1,0:T(8,128)(2,1)S(1)}, u32[]{:S(2)}, u32[]{:S(2)}) collective-permute-start(bf16[128,1024]{1,0:T(8,128)(2,1)} %get-tuple-element.248.refs_11_), channel_id=1, source_target_pairs={{0,24},{4,28},{8,16},{12,20},{16,8},{20,12},{24,0},{28,4},{1,25},{... | collective-permute-start | bytes 786440 | tf_op jit(solution)/shard_map/ppermute | solution.py:97
  474.6 37.6 %collective-permute-start.35 = (bf16[3072,256]{1,0:T(8,128)(2,1)}, bf16[3072,256]{1,0:T(8,128)(2,1)}, u32[]{:S(2)}, u32[]{:S(2)}) collective-permute-start(bf16[3072,256]{1,0:T(8,128)(2,1)} %add.242), channel_id=1, source_target_pairs={{0,2},{1,3},{2,0},{3,1},{4,6},{5,7},{6,4},{7,5},{8,10},{9,11},{10,... | collective-permute-start | bytes 4718600 | tf_op jit(solution)/shard_map/ppermute | solution.py:97
  507.8 33.6 %collective-permute-start.36 = (bf16[128,1024]{1,0:T(8,128)(2,1)}, bf16[128,1024]{1,0:T(8,128)(2,1)S(1)}, u32[]{:S(2)}, u32[]{:S(2)}) collective-permute-start(bf16[128,1024]{1,0:T(8,128)(2,1)} %add.241.refs_8_.refs_0_), channel_id=1, source_target_pairs={{0,8},{4,12},{8,0},{12,4},{16,24},{20,28},{24,16},{28,20},{1,9},{5... | collective-permute-start | bytes 786440 | tf_op jit(solution)/shard_map/ppermute | solution.py:97
  508.1 33.4 %collective-permute-start.37 = (bf16[128,1024]{1,0:T(8,128)(2,1)}, bf16[128,1024]{1,0:T(8,128)(2,1)}, u32[]{:S(2)}, u32[]{:S(2)}) collective-permute-start(bf16[128,1024]{1,0:T(8,128)(2,1)} %add.241.refs_8_.refs_0_), channel_id=1, source_target_pairs={{0,16},{4,20},{8,24},{12,28},{16,0},{20,4},{24,8},{28,12},{1,17},{... | collective-permute-start | bytes 786440 | tf_op jit(solution)/shard_map/ppermute | solution.py:97
  511.9 29.6 %collective-permute-start.38 = (bf16[128,1024]{1,0:T(8,128)(2,1)}, bf16[128,1024]{1,0:T(8,128)(2,1)}, u32[]{:S(2)}, u32[]{:S(2)}) collective-permute-start(bf16[128,1024]{1,0:T(8,128)(2,1)} %add.241.refs_8_.refs_0_), channel_id=1, source_target_pairs={{0,24},{4,28},{8,16},{12,20},{16,8},{20,12},{24,0},{28,4},{1,25},{... | collective-permute-start | bytes 786440 | tf_op jit(solution)/shard_map/ppermute | solution.py:97
  512.2 29.3 %collective-permute-start.39 = (bf16[3072,256]{1,0:T(8,128)(2,1)}, bf16[3072,256]{1,0:T(8,128)(2,1)}, u32[]{:S(2)}, u32[]{:S(2)}) collective-permute-start(bf16[3072,256]{1,0:T(8,128)(2,1)} %bitcast.57), channel_id=1, source_target_pairs={{0,1},{1,0},{2,3},{3,2},{4,5},{5,4},{6,7},{7,6},{8,9},{9,8},{10,11... | collective-permute-start | bytes 4718600 | tf_op jit(solution)/shard_map/ppermute | solution.py:97
  545.6 74.1 %collective-permute-start.40 = (bf16[1536,256]{1,0:T(8,128)(2,1)}, bf16[1536,256]{1,0:T(8,128)(2,1)}, u32[]{:S(2)}, u32[]{:S(2)}) collective-permute-start(bf16[1536,256]{1,0:T(8,128)(2,1)} %get-tuple-element.267.refs_13_), channel_id=1, source_target_pairs={{0,4},{4,0},{8,12},{12,8},{16,20},{20,16},{24,28},{28,24},{1,5},{5... | collective-permute-start | bytes 2359304 | tf_op jit(solution)/shard_map/ppermute | solution.py:97
  549.8 134.0 %collective-permute-start.48 = (bf16[512,1024]{1,0:T(8,128)(2,1)}, bf16[512,1024]{1,0:T(8,128)(2,1)}, u32[]{:S(2)}, u32[]{:S(2)}) collective-permute-start(bf16[512,1024]{1,0:T(8,128)(2,1)} %assemble.4.refs_11_.refs_0_), channel_id=1, source_target_pairs={{0,4},{4,0},{8,12},{12,8},{16,20},{20,16},{24,28},{28,24},{1,5},{5... | collective-permute-start | bytes 3145736 | tf_op jit(solution)/shard_map/ppermute | solution.py:97
  598.8 5.1 collective-permute-start.50
  600.2 6.7 collective-permute-start.49
  603.8 2.4 collective-permute-start.55
  604.6 3.8 collective-permute-start.51
  606.2 7.1 %collective-permute-start.56 = (bf16[2,8,6144]{2,1,0:T(8,128)(2,1)S(1)}, bf16[2,8,6144]{2,1,0:T(8,128)(2,1)S(1)}, u32[]{:S(2)}, u32[]{:S(2)}) collective-permute-start(bf16[2,8,6144]{2,1,0:T(8,128)(2,1)S(1)} %add_convert_fusion.4), channel_id=1, source_target_pairs={{0,2},{1,3},{2,0},{3,1},{4,6},{5,7},{6,4},{7,5},{8,10},{9,11},{10,... | collective-permute-start | bytes 589832 | tf_op jit(solution)/shard_map/ppermute | solution.py:97
  609.2 4.9 collective-permute-start.52
  613.3 6.3 collective-permute-start.57
  614.1 12.6 %collective-permute-start.53 = (bf16[4,2025]{1,0:T(4,128)(2,1)S(1)}, bf16[4,2025]{1,0:T(4,128)(2,1)}, u32[]{:S(2)}, u32[]{:S(2)}) collective-permute-start(bf16[4,2025]{1,0:T(4,128)(2,1)S(1)} %add_convert_fusion.7), channel_id=1, source_target_pairs={{0,8},{4,12},{8,0},{12,4},{16,24},{20,28},{24,16},{28,20},{1,9},{5... | collective-permute-start | bytes 48608 | tf_op jit(solution)/shard_map/ppermute | solution.py:97
  619.6 29.7 %collective-permute-start.58 = (bf16[2,8,6144]{2,1,0:T(8,128)(2,1)S(1)}, bf16[2,8,6144]{2,1,0:T(8,128)(2,1)S(1)}, u32[]{:S(2)}, u32[]{:S(2)}) collective-permute-start(bf16[2,8,6144]{2,1,0:T(8,128)(2,1)S(1)} %add_convert_fusion.2), channel_id=1, source_target_pairs={{0,8},{4,12},{8,0},{12,4},{16,24},{20,28},{24,16},{28,20},{1,9},{5... | collective-permute-start | bytes 589832 | tf_op jit(solution)/shard_map/ppermute | solution.py:97
  623.1 9.1 %collective-permute-start.41 = (bf16[384,256]{1,0:T(8,128)(2,1)}, bf16[384,256]{1,0:T(8,128)(2,1)S(1)}, u32[]{:S(2)}, u32[]{:S(2)}) collective-permute-start(bf16[384,256]{1,0:T(8,128)(2,1)} %get-tuple-element.271), channel_id=1, source_target_pairs={{0,8},{4,12},{8,0},{12,4},{16,24},{20,28},{24,16},{28,20},{1,9},{5... | collective-permute-start | bytes 589832 | tf_op jit(solution)/shard_map/ppermute | solution.py:97
  625.1 17.0 %collective-permute-start.42 = (bf16[384,256]{1,0:T(8,128)(2,1)}, bf16[384,256]{1,0:T(8,128)(2,1)S(1)}, u32[]{:S(2)}, u32[]{:S(2)}) collective-permute-start(bf16[384,256]{1,0:T(8,128)(2,1)} %get-tuple-element.273), channel_id=1, source_target_pairs={{0,16},{4,20},{8,24},{12,28},{16,0},{20,4},{24,8},{28,12},{1,17},{... | collective-permute-start | bytes 589832 | tf_op jit(solution)/shard_map/ppermute | solution.py:97
  626.7 15.4 %collective-permute-start.43 = (bf16[384,256]{1,0:T(8,128)(2,1)}, bf16[384,256]{1,0:T(8,128)(2,1)S(1)}, u32[]{:S(2)}, u32[]{:S(2)}) collective-permute-start(bf16[384,256]{1,0:T(8,128)(2,1)} %get-tuple-element.275), channel_id=1, source_target_pairs={{0,24},{4,28},{8,16},{12,20},{16,8},{20,12},{24,0},{28,4},{1,25},{... | collective-permute-start | bytes 589832 | tf_op jit(solution)/shard_map/ppermute | solution.py:97
  632.2 41.1 %collective-permute-start.54 = (bf16[4,2025]{1,0:T(4,128)(2,1)}, bf16[4,2025]{1,0:T(4,128)(2,1)}, u32[]{:S(2)}, u32[]{:S(2)}) collective-permute-start(bf16[4,2025]{1,0:T(4,128)(2,1)} %add_convert_fusion.6), channel_id=1, source_target_pairs={{0,16},{4,20},{8,24},{12,28},{16,0},{20,4},{24,8},{28,12},{1,17},{... | collective-permute-start | bytes 48608 | tf_op jit(solution)/shard_map/ppermute | solution.py:97
  644.9 9.5 %collective-permute-start.44 = (bf16[384,256]{1,0:T(8,128)(2,1)}, bf16[384,256]{1,0:T(8,128)(2,1)}, u32[]{:S(2)}, u32[]{:S(2)}) collective-permute-start(bf16[384,256]{1,0:T(8,128)(2,1)} %add.243.refs_0_), channel_id=1, source_target_pairs={{0,8},{4,12},{8,0},{12,4},{16,24},{20,28},{24,16},{28,20},{1,9},{5... | collective-permute-start | bytes 589832 | tf_op jit(solution)/shard_map/ppermute | solution.py:97
  647.5 21.7 %collective-permute-start.45 = (bf16[384,256]{1,0:T(8,128)(2,1)}, bf16[384,256]{1,0:T(8,128)(2,1)}, u32[]{:S(2)}, u32[]{:S(2)}) collective-permute-start(bf16[384,256]{1,0:T(8,128)(2,1)} %add.243.refs_0_), channel_id=1, source_target_pairs={{0,16},{4,20},{8,24},{12,28},{16,0},{20,4},{24,8},{28,12},{1,17},{... | collective-permute-start | bytes 589832 | tf_op jit(solution)/shard_map/ppermute | solution.py:97
  649.3 19.9 %collective-permute-start.46 = (bf16[384,256]{1,0:T(8,128)(2,1)}, bf16[384,256]{1,0:T(8,128)(2,1)}, u32[]{:S(2)}, u32[]{:S(2)}) collective-permute-start(bf16[384,256]{1,0:T(8,128)(2,1)} %add.243.refs_0_), channel_id=1, source_target_pairs={{0,24},{4,28},{8,16},{12,20},{16,8},{20,12},{24,0},{28,4},{1,25},{... | collective-permute-start | bytes 589832 | tf_op jit(solution)/shard_map/ppermute | solution.py:97
  650.8 26.9 %copy-start.8 = (f32[2,8,256]{2,1,0:T(8,128)S(1)}, f32[2,8,256]{2,1,0:T(8,128)}, u32[]{:S(2)}) copy-start(f32[2,8,256]{2,1,0:T(8,128)} %copy-done.7) | copy-start | bytes 49156
  654.4 22.5 %collective-permute-start.59 = (bf16[2,8,6144]{2,1,0:T(8,128)(2,1)S(1)}, bf16[2,8,6144]{2,1,0:T(8,128)(2,1)S(1)}, u32[]{:S(2)}, u32[]{:S(2)}) collective-permute-start(bf16[2,8,6144]{2,1,0:T(8,128)(2,1)S(1)} %add_convert_fusion.1), channel_id=1, source_target_pairs={{0,16},{4,20},{8,24},{12,28},{16,0},{20,4},{24,8},{28,12},{1,17},{... | collective-permute-start | bytes 589832 | tf_op jit(solution)/shard_map/ppermute | solution.py:97
  671.9 15.7 %collective-permute-start.47 = (bf16[1536,256]{1,0:T(8,128)(2,1)}, bf16[1536,256]{1,0:T(8,128)(2,1)}, u32[]{:S(2)}, u32[]{:S(2)}) collective-permute-start(bf16[1536,256]{1,0:T(8,128)(2,1)} %assemble.5.refs_0_), channel_id=1, source_target_pairs={{0,4},{4,0},{8,12},{12,8},{16,20},{20,16},{24,28},{28,24},{1,5},{5... | collective-permute-start | bytes 2359304 | tf_op jit(solution)/shard_map/ppermute | solution.py:97
  (23 other events, 109.4 us)
Sparse Core Ops, SparseCore 0:
  431.0 62.0 all-gather.2
  547.1 74.4 all-reduce.1

commit v4 on v3

v4 whole, which is shorter than its diff:
```python
import functools
import math

import jax
import jax.numpy as jnp
from jax import lax
from jax.experimental import pallas as pl
from jax.experimental.pallas import tpu as pltpu
from jax.sharding import PartitionSpec as P

WIN_T = 5
WIN_H = 8
WIN_W = 8
WIN_TOK = WIN_T * WIN_H * WIN_W
FRAME = WIN_H * WIN_W
PAD_TOK = 384
HEAD_DIM = 64
N_TIME, N_ROW, N_COL = 2 * WIN_T - 1, 2 * WIN_H - 1, 2 * WIN_W - 1

BF = jnp.bfloat16
F32 = jnp.float32
epsilon = 1e-06
highest = lax.Precision.HIGHEST
GELU_A = 0.7978845608028654
GELU_B = GELU_A * 0.044715
VMEM_LIMIT = 63 * 1024 * 1024


def dot(left, right, left_dim=1, right_dim=0):
    return lax.dot_general(
        left, right, (((left_dim,), (right_dim,)), ((), ())), preferred_element_type=F32
    )


def params():
    return pltpu.CompilerParams(vmem_limit_bytes=VMEM_LIMIT)


def shaped(shape, dtype):
    return jax.ShapeDtypeStruct(shape, dtype)


def row_spec(rows, cols):
    return pl.BlockSpec((rows, cols), lambda i: (i, 0))


def part_spec(rows, cols):
    return pl.BlockSpec((3, rows, cols), lambda i: (0, i, 0))


def per_step(rows):
    return 2 if rows % (2 * WIN_TOK) == 0 else 1


def window_span(window):
    return slice(window * WIN_TOK, (window + 1) * WIN_TOK)


def whole_spec(shape):
    return pl.BlockSpec(shape, lambda i: (0,) * len(shape))


def mod_spec(per, count, cols):
    return pl.BlockSpec((per, count, cols), lambda i: (i, 0, 0))


def cost(micros):
    return pl.CostEstimate(
        flops=int(micros * 1e9), bytes_accessed=int(micros * 3.5e6), transcendentals=0
    )


def call_after(kernel, deps, *, in_specs, **rest):
    deps = tuple(deps)
    count = len(in_specs)

    def run(*refs):
        kernel(*refs[:count], *refs[count + len(deps) :])

    call = pl.pallas_call(
        run, in_specs=list(in_specs) + [pl.BlockSpec(memory_space=pl.ANY)] * len(deps), **rest
    )
    return lambda *args: call(*args, *deps)


def after(value, *deps):
    return lax.optimization_barrier((value, *deps))[0]


def normalise(values):
    centred = values - jnp.mean(values, axis=-1, keepdims=True)
    inverse = lax.rsqrt(jnp.mean(centred * centred, axis=-1, keepdims=True) + epsilon)
    return centred * inverse, inverse


def normalise_back(normed, inverse, grad_in):
    return inverse * (
        grad_in
        - jnp.mean(grad_in, axis=-1, keepdims=True)
        - normed * jnp.mean(grad_in * normed, axis=-1, keepdims=True)
    )


def swap(value, axis, size, bit):
    return lax.ppermute(value, axis, [(i, i ^ bit) for i in range(size)])


def bits_of(size):
    return [1 << b for b in range(size.bit_length() - 1)]


def add_low(left, right):
    return (left.astype(F32) + right.astype(F32)).astype(left.dtype)


def gather_shards(own, axis, size):
    shards = {0: own}
    for bit in reversed(bits_of(size)):
        for mask in list(shards):
            shards[mask ^ bit] = swap(shards[mask], axis, size, bit)
    return shards


def reduce_all(value, axis, size):
    for bit in bits_of(size):
        value = add_low(value, swap(value, axis, size, bit))
    return value


def reduce_shards(terms, axis, size):
    terms = dict(terms)
    for bit in bits_of(size):
        for mask in [m for m in terms if m & bit]:
            terms[mask ^ bit] = add_low(terms[mask ^ bit], swap(terms.pop(mask), axis, size, bit))
    return terms[0]


def sum_kernel(*refs, groups):
    outs = refs[sum(groups) :]
    for out, group in zip(outs, groups):
        total = refs[0][...].astype(F32)
        for ref in refs[1:group]:
            total = total + ref[...].astype(F32)
        out[...] = total.astype(BF)
        refs = refs[group:]


def add_groups(groups):
    if all(len(group) == 1 for group in groups):
        return [group[0] for group in groups]
    shapes = [group[0].shape for group in groups]
    turns = 4 if all(shape[0] % 64 == 0 and shape[0] >= 512 for shape in shapes) else 1
    spec = lambda shape: row_spec(shape[0] // turns, shape[1])
    return pl.pallas_call(
        functools.partial(sum_kernel, groups=[len(group) for group in groups]),
        grid=(turns,),
        in_specs=[spec(array.shape) for group in groups for array in group],
        out_specs=[spec(shape) for shape in shapes],
        out_shape=[shaped(shape, BF) for shape in shapes],
        compiler_params=params(),
        cost_estimate=cost(0.001),
        name="add",
    )(*[array for group in groups for array in group])


def split_kernel(index_ref, *refs, count, groups, deps):
    outs = refs[sum(groups) + deps :]
    totals = []
    for group in groups:
        total = refs[0][...].astype(F32)
        for ref in refs[1:group]:
            total = total + ref[...].astype(F32)
        totals.append(total.astype(BF))
        refs = refs[group:]
    size = totals[0].shape[0]
    for k in range(count):

        @pl.when(pl.program_id(0) == k)
        def _():
            for place, total in enumerate(totals):
                outs[k][place * size : (place + 1) * size, :] = total


def split_call(groups, index, count, deps=()):
    rows, cols = groups[0][0].shape
    part = (rows // count, cols)
    piece = (len(groups) * part[0], cols)
    parts = [array for group in groups for array in group]
    spec = pltpu.PrefetchScalarGridSpec(
        num_scalar_prefetch=1,
        grid=(count,),
        in_specs=[pl.BlockSpec(part, lambda k, f: (f[0] ^ k, 0))] * len(parts)
        + [pl.BlockSpec(memory_space=pl.ANY)] * len(deps),
        out_specs=[pl.BlockSpec(piece, lambda k, f: (0, 0))] * count,
    )
    return pl.pallas_call(
        functools.partial(
            split_kernel, count=count, groups=[len(group) for group in groups], deps=len(deps)
        ),
        grid_spec=spec,
        out_shape=[shaped(piece, BF)] * count,
        compiler_params=params(),
        cost_estimate=cost(0.001),
        name="split",
    )(jnp.reshape(index, (1,)).astype(jnp.int32), *parts, *deps)


def assemble_kernel(index_ref, *refs, groups):
    step = pl.program_id(0)
    size = refs[-1].shape[0]
    rows = pl.ds(pl.multiple_of(step % groups * size, size), size)
    for k, ref in enumerate(refs[:-1]):

        @pl.when(step // groups == k)
        def _():
            refs[-1][...] = ref[rows, :].astype(refs[-1].dtype)


def assemble_call(pieces, index, dtype, groups=1):
    count = len(pieces)
    rows, cols = pieces[0].shape
    spec = pltpu.PrefetchScalarGridSpec(
        num_scalar_prefetch=1,
        grid=(count * groups,),
        in_specs=[pl.BlockSpec((rows, cols), lambda i, f: (0, 0))] * count,
        out_specs=pl.BlockSpec(
            (rows // groups, cols), lambda i, f: (i % groups * count + (f[0] ^ (i // groups)), 0)
        ),
    )
    return pl.pallas_call(
        functools.partial(assemble_kernel, groups=groups),
        grid_spec=spec,
        out_shape=shaped((rows * count, cols), dtype),
        compiler_params=params(),
        cost_estimate=cost(0.001),
        name="assemble",
    )(jnp.reshape(index, (1,)).astype(jnp.int32), *pieces)


def unfold_kernel(part_ref, out_ref):
    out_ref[...] = part_ref[...].astype(F32)


def unfold_call(parts, groups, deps):
    count, rows, cols = parts.shape
    far = count // 2
    own = far // groups

    def place(i):
        group, near, piece = i // (2 * own), i // own % 2, i % own
        return (2 * (group * own + piece) + near, 0, 0)

    return call_after(
        unfold_kernel,
        deps,
        grid=(count,),
        in_specs=[pl.BlockSpec((None, rows, cols), place)],
        out_specs=row_spec(rows, cols),
        out_shape=shaped((count * rows, cols), F32),
        compiler_params=params(),
        cost_estimate=cost(0.001),
        name="unfold",
    )(parts)


class Steps:
    def __init__(self):
        self.jobs, self.token, self.ties = [], None, []

    def swap(self, value, axis, size, bit):
        if self.token is not None:
            value = after(value, self.token)
        return swap(value, axis, size, bit)

    def arrive(self, value):
        return value if self.token is None else after(value, self.token)

    def step(self, token=None):
        self.token = token
        self.ties, jobs = [], []
        for job in self.jobs:
            try:
                self.ties = self.ties + next(job)
            except StopIteration:
                continue
            jobs.append(job)
        self.jobs = jobs
        return self.ties if token is None else self.ties + [token]

    def finish(self):
        while self.jobs:
            self.step()


def gather_job(steps, own, shards, axis, size, hold):
    shards[0] = own
    even = {0: own}
    shards[1] = steps.swap(own, axis, size, 1)
    for bit in reversed(bits_of(size)[1:]):
        new = {mask ^ bit: steps.swap(part, axis, size, bit) for mask, part in even.items()}
        for _ in range(hold):
            yield []
        new = {mask: steps.arrive(part) for mask, part in new.items()}
        even.update(new)
        for mask, part in new.items():
            shards[mask] = part
            shards[mask ^ 1] = steps.swap(part, axis, size, 1)
        yield list(new.values())


class Sums:
    def __init__(self, steps, size, lags):
        self.steps, self.size, self.lags = steps, size, lags
        self.parts = {mask: [[] for _ in lags] for mask in range(size)}
        nearest_first = sorted(range(1, size), key=lambda mask: (mask & -mask, mask))
        steps.jobs += [self.send(mask) for mask in nearest_first]

    def full(self, mask, places):
        low = mask & -mask if mask else self.size
        return all(len(self.parts[mask][i]) == low.bit_length() for i in places)

    def add(self, mask, terms):
        for part, term in zip(self.parts[mask], terms):
            part.append(term)

    def send(self, mask):
        every = range(len(self.lags))
        while not self.full(mask, every):
            yield []
        bit = mask & -mask
        values = list(add_groups(self.parts[mask]))
        lags = self.lags if bit > 1 else [0] * len(values)
        flying, ready = {}, values if bit > 1 else []
        for turn in range(max(lags) + 2):
            for i in every:
                if turn == lags[i] + 1:
                    other = self.steps.arrive(flying[i])
                    self.parts[mask ^ bit][i].append(other)
                    ready = ready + [other]
                if turn == lags[i]:
                    flying[i] = self.steps.swap(values[i], "mp", self.size, bit)
            yield ready
            ready = []


def sum_everywhere(shared, by_shard, n_mp, n_dp):
    rows = shared.shape[0]
    for axis, size in (("mp", n_mp), ("dp", n_dp)):
        for bit in bits_of(size):
            sent = by_shard
            if axis == "mp":
                pairs = (size // (2 * bit), 2, bit * by_shard.shape[1], by_shard.shape[2])
                sent = by_shard.reshape(pairs)[:, ::-1]
            sent = jnp.concatenate([shared, sent.reshape(-1, shared.shape[1])], axis=0)
            other = swap(sent, axis, size, bit)
            shared = add_low(shared, other[:rows])
            by_shard = add_low(by_shard, other[rows:].reshape(by_shard.shape))
    return shared, by_shard[0]


def spread_job(steps, sums, places, n_dp, offload, out, name):
    while not sums.full(0, places):
        yield []
    index = lax.axis_index("dp")
    count = n_dp // 2
    keep, send = split_call([sums.parts[0][i] for i in places], index % 2, 2)
    other = steps.swap(send, "dp", n_dp, 1)
    yield [send]
    pieces = split_call([[keep, steps.arrive(other)]], index // 2, count, steps.ties)
    others = [steps.swap(pieces[k], "dp", n_dp, 2 * k) for k in range(1, count)]
    yield [other, *pieces]
    (total,) = add_groups([[pieces[0]] + [steps.arrive(part) for part in others]])
    if offload:
        whole = lax.all_gather(total, "dp", axis=0)
        yield [total]
        yield []
        out[name] = steps.arrive(whole)
        yield [whole]
        return
    others = [steps.swap(total, "dp", n_dp, 2 * k) for k in range(1, count)]
    yield others[:1] if steps.token is None else [total]
    half = assemble_call([total] + [steps.arrive(part) for part in others], index // 2, BF)
    other = steps.swap(half, "dp", n_dp, 1)
    yield [half]
    other = steps.arrive(other)
    out[name] = assemble_call([half, other], index % 2, F32, len(places))
    yield [other]


def place_hot():
    place = jnp.arange(FRAME)
    row, col = place // WIN_W, place % WIN_W
    offset = (row[:, None] - row[None, :] + WIN_H - 1) * N_COL + (
        col[:, None] - col[None, :] + WIN_W - 1
    )
    return (offset.reshape(1, -1) == jnp.arange(N_ROW * N_COL)[:, None]).astype(F32)


def bias_blocks(rel_table):
    heads = rel_table.shape[0]
    cube = rel_table.reshape(heads * N_TIME, N_ROW * N_COL)
    return lax.dot(cube, place_hot(), precision=highest).reshape(heads, N_TIME, FRAME, FRAME)


def collect_blocks(block_grad):
    heads = block_grad.shape[0]
    flat = block_grad.reshape(heads * N_TIME, FRAME * FRAME)
    cube = lax.dot_general(flat, place_hot(), (((1,), (1,)), ((), ())), precision=highest)
    return cube[:, ::-1].reshape(heads, -1)


def block_spec(heads, place):
    return pl.BlockSpec((heads, N_TIME, FRAME, FRAME), lambda i: (place, 0, 0, 0))


def frame_span(frame):
    return slice(frame * FRAME, (frame + 1) * FRAME)


def spread_blocks(blocks_ref, table, fill, transposed):
    for head in range(table.shape[0]):
        for offset in range(N_TIME):
            block = blocks_ref[head, offset]
            if transposed:
                block = block.T
            for query in range(WIN_T):
                key = query - (offset - WIN_T + 1)
                if 0 <= key < WIN_T:
                    row, col = (key, query) if transposed else (query, key)
                    table[head, frame_span(row), frame_span(col)] = block
        table[head, :, WIN_TOK:] = jnp.full((WIN_TOK, PAD_TOK - WIN_TOK), fill, F32)


def norm_kernel(tokens_ref, mod_ref, attn_in_ref):
    normed, _ = normalise(tokens_ref[...].astype(F32))
    attn_in_ref[...] = (normed * (1.0 + mod_ref[0, 1:2]) + mod_ref[0, 0:1]).astype(BF)


def norm_call(tokens, mods, deps=()):
    rows, width = tokens.shape
    return call_after(
        norm_kernel,
        deps,
        grid=(rows // WIN_TOK,),
        in_specs=[row_spec(WIN_TOK, width), mod_spec(1, mods.shape[1], width)],
        out_specs=row_spec(WIN_TOK, width),
        out_shape=shaped((rows, width), BF),
        compiler_params=params(),
        cost_estimate=cost(8),
        name="norm_in",
    )(tokens, mods)


def head_copies(value, heads):
    if heads == 1:
        return [value]
    lane = lax.broadcasted_iota(jnp.int32, value.shape, 1) // HEAD_DIM
    return [jnp.where(lane == head, value, jnp.zeros_like(value)) for head in range(heads)]


def pad_rows(value):
    return jnp.concatenate(
        [value, jnp.zeros((PAD_TOK - WIN_TOK, value.shape[1]), value.dtype)], axis=0
    )


def attend_kernel(x_ref, w_ref, blocks_ref, qkv_ref, mixed_ref, lse_ref, table, columns):
    heads = blocks_ref.shape[0]

    @pl.when(pl.program_id(0) == 0)
    def _():
        spread_blocks(blocks_ref, table, -1e30, False)
        columns[...] = jnp.zeros_like(columns)

    x = x_ref[...]
    queries = dot(x, w_ref[0]).astype(BF)
    keys = dot(x, w_ref[1]).astype(BF)
    values = dot(x, w_ref[2]).astype(BF)
    qkv_ref[0] = queries
    qkv_ref[1] = keys
    qkv_ref[2] = values
    scaled = queries * jnp.asarray(HEAD_DIM**-0.5, BF)
    for window in range(x.shape[0] // WIN_TOK):
        span = window_span(window)
        scores = dot(
            jnp.concatenate(head_copies(scaled[span], heads), axis=0), pad_rows(keys[span]), 1, 1
        )
        probs = []
        for head in range(heads):
            score = scores[window_span(head)] + table[head]
            top = jnp.max(score, axis=1, keepdims=True)
            exponent = jnp.exp(score - top)
            total = jnp.sum(exponent, axis=1, keepdims=True)
            probs.append((exponent * (1.0 / total)).astype(BF))
            columns[window, :WIN_TOK, head : head + 1] = top + jnp.log(total)
        value = jnp.concatenate([pad_rows(part) for part in head_copies(values[span], heads)], axis=0)
        mixed_ref[span, :] = dot(jnp.concatenate(probs, axis=1), value).astype(BF)
        lse_ref[window] = columns[window].T[: lse_ref.shape[1]]


def attend_call(attn_in, weight, blocks, deps=()):
    rows, width = attn_in.shape
    cols = weight.shape[2]
    blocks, place, heads = blocks
    windows = rows // WIN_TOK
    per = per_step(rows)
    block = per * WIN_TOK
    stat_rows = -(-heads // 8) * 8
    return call_after(
        attend_kernel,
        deps,
        grid=(windows // per,),
        in_specs=[row_spec(block, width), whole_spec(weight.shape), block_spec(heads, place)],
        out_specs=[
            part_spec(block, cols),
            row_spec(block, cols),
            mod_spec(per, stat_rows, PAD_TOK),
        ],
        out_shape=[
            shaped((3, rows, cols), BF),
            shaped((rows, cols), BF),
            shaped((windows, stat_rows, PAD_TOK), F32),
        ],
        scratch_shapes=[
            pltpu.VMEM((heads, WIN_TOK, PAD_TOK), F32),
            pltpu.VMEM((per, PAD_TOK, 128), F32),
        ],
        compiler_params=params(),
        cost_estimate=cost(19),
        name="attend",
    )(attn_in, weight, blocks)


def attend_back_kernel(
    grad_ref, out_w_ref, qkv_ref, mixed_ref, lse_ref, blocks_ref, x_ref, dqkv_ref, dblocks_ref, dw_ref, table, total, x_all, grad_all, d_all
):
    heads = blocks_ref.shape[0]
    cols = out_w_ref.shape[0]
    step = pl.program_id(0)

    @pl.when(step == 0)
    def _():
        spread_blocks(blocks_ref, table, 0.0, True)
        total[...] = jnp.zeros_like(total)

    grads_mixed = dot(grad_ref[...], out_w_ref[...], 1, 1).astype(BF)
    scale = jnp.asarray(HEAD_DIM**-0.5, BF)
    head_rows = (lse_ref.shape[1], cols)
    head_hot = (
        lax.broadcasted_iota(jnp.int32, head_rows, 1) // HEAD_DIM
        == lax.broadcasted_iota(jnp.int32, head_rows, 0)
    ).astype(BF)
    block = grad_ref.shape[0]
    rows = pl.ds(pl.multiple_of(step * block, block), block)
    x_all[rows, :] = x_ref[...]
    grad_all[rows, :] = grad_ref[...]
    d_all[3, rows, :] = mixed_ref[...]
    for window in range(block // WIN_TOK):
        place = window_span(window)
        grad_mixed = grads_mixed[place]
        query = qkv_ref[0, place, :]
        key = qkv_ref[1, place, :]
        value = qkv_ref[2, place, :]
        product = grad_mixed.astype(F32) * mixed_ref[place, :].astype(F32)
        upper = product.astype(BF)
        lower = (product - upper.astype(F32)).astype(BF)
        inner = dot(head_hot, pad_rows(upper), 1, 1) + dot(head_hot, pad_rows(lower), 1, 1)
        keys = jnp.concatenate(head_copies(key * scale, heads), axis=0)
        values = jnp.concatenate(head_copies(value, heads), axis=0)
        query_pad = pad_rows(query)
        grad_pad = pad_rows(grad_mixed)
        scores = dot(keys, query_pad, 1, 1)
        grad_probs = dot(values, grad_pad, 1, 1)
        probs = []
        grad_scores = []
        for head in range(heads):
            span = window_span(head)
            prob = jnp.exp(scores[span] + table[head] - lse_ref[window, head : head + 1, :])
            grad_score = (prob * (grad_probs[span] - inner[head : head + 1, :])).astype(BF)
            probs.append(prob.astype(BF))
            grad_scores.append(grad_score)
            total[head] += grad_score.astype(F32)
        wide = jnp.concatenate(grad_scores, axis=1)
        grad_value = dot(
            jnp.concatenate(probs, axis=1), jnp.concatenate(head_copies(grad_pad, heads), axis=0)
        )
        grad_key = dot(wide, jnp.concatenate(head_copies(query_pad * scale, heads), axis=0))
        grad_query = dot(jnp.concatenate(grad_scores, axis=0), keys, 0, 0)[:WIN_TOK]
        own = pl.ds(pl.multiple_of(step * block + window * WIN_TOK, WIN_TOK), WIN_TOK)
        for part, grad in enumerate((grad_query, grad_key, grad_value)):
            grad = grad.astype(BF)
            dqkv_ref[part, place, :] = grad
            d_all[part, own, :] = grad

    @pl.when(step == pl.num_programs(0) - 1)
    def _():
        for part in range(4):
            left = grad_all if part == 3 else x_all
            dw_ref[part] = dot(left[...], d_all[part], 0, 0).astype(BF)
        for head in range(heads):
            for offset in range(N_TIME):
                block = None
                for query in range(WIN_T):
                    key = query - (offset - WIN_T + 1)
                    if 0 <= key < WIN_T:
                        part = total[head, frame_span(key), frame_span(query)]
                        block = part if block is None else block + part
                dblocks_ref[head, offset] = block


def attend_back_call(grad_attn, out_weight, qkv, mixed, lse, blocks, attn_in, deps=()):
    rows, width = grad_attn.shape
    cols = out_weight.shape[0]
    blocks, place, heads = blocks
    per = per_step(rows)
    block = per * WIN_TOK
    return call_after(
        attend_back_kernel,
        deps,
        grid=(rows // block,),
        in_specs=[
            row_spec(block, width),
            whole_spec(out_weight.shape),
            part_spec(block, cols),
            row_spec(block, cols),
            mod_spec(per, lse.shape[1], PAD_TOK),
            block_spec(heads, place),
            row_spec(block, width),
        ],
        out_specs=[
            part_spec(block, cols),
            block_spec(heads, 0),
            whole_spec((4, width, cols)),
        ],
        out_shape=[
            shaped((3, rows, cols), BF),
            shaped((heads,) + blocks.shape[1:], F32),
            shaped((4, width, cols), BF),
        ],
        scratch_shapes=[pltpu.VMEM((heads, WIN_TOK, PAD_TOK), F32)] * 2
        + [pltpu.VMEM((rows, width), BF)] * 2
        + [pltpu.VMEM((4, rows, cols), BF)],
        compiler_params=params(),
        cost_estimate=cost(30),
        name="attend_back",
    )(grad_attn, out_weight, qkv, mixed, lse, blocks, attn_in)


def middle_kernel(*refs, count):
    mixed_refs = refs[:count]
    weight_refs = refs[count : 2 * count]
    tokens_ref, cot_ref, mod_ref, attn_out_ref, mlp_in_ref, grad_mlp_ref = refs[2 * count :]
    attn_out = dot(mixed_refs[0][...], weight_refs[0][...])
    for mixed_ref, weight_ref in zip(mixed_refs[1:], weight_refs[1:]):
        attn_out = attn_out + dot(mixed_ref[...], weight_ref[...])
    attn_out_ref[...] = attn_out.astype(BF)
    for window in range(attn_out.shape[0] // WIN_TOK):
        span = window_span(window)
        mod = mod_ref[window]
        resid = tokens_ref[span, :].astype(F32) + mod[2:3] * attn_out[span]
        normed, _ = normalise(resid)
        mlp_in_ref[span, :] = (normed * (1.0 + mod[4:5]) + mod[3:4]).astype(BF)
        grad_mlp_ref[span, :] = (mod[5:6] * cot_ref[span, :].astype(F32)).astype(BF)


def middle_call(mixed, weights, tokens, cotangent, mods, deps=()):
    rows, width = tokens.shape
    count = len(mixed)
    per = per_step(rows)
    block = per * WIN_TOK
    row = row_spec(block, width)
    return call_after(
        functools.partial(middle_kernel, count=count),
        deps,
        grid=(rows // block,),
        in_specs=[row_spec(block, part.shape[1]) for part in mixed]
        + [whole_spec(part.shape) for part in weights]
        + [row, row, mod_spec(per, mods.shape[1], width)],
        out_specs=[row, row, row],
        out_shape=[
            shaped((rows, width), BF),
            shaped((rows, width), BF),
            shaped((rows, width), BF),
        ],
        compiler_params=params(),
        cost_estimate=cost(16),
        name="middle",
    )(*mixed, *weights, tokens, cotangent, mods)


def mlp_kernel(
    x_ref, g_ref, up_ref, down_ref, act_ref, ghid_ref, *rest, chunk
):
    down_total, up_total = rest[4:]
    step = pl.program_id(0)
    x = x_ref[...]
    g = g_ref[...]
    for start in range(0, up_ref.shape[1], chunk):
        span = slice(start, start + chunk)
        hidden = dot(x, up_ref[:, span])
        grad_act = dot(g, down_ref[span, :], 1, 1)
        cubic = GELU_B * (hidden * hidden)
        gate = 0.5 + 0.5 * jnp.tanh(hidden * (GELU_A + cubic))
        act_ref[:, span] = (hidden * gate).astype(BF)
        slope = gate + gate * ((1.0 - gate) * (hidden * (2.0 * GELU_A + 6.0 * cubic)))
        ghid_ref[:, span] = (grad_act * slope).astype(BF)

    @pl.when(step == 0)
    def _():
        down_total[...] = dot(act_ref[...], g, 0, 0)
        up_total[...] = dot(x, ghid_ref[...], 0, 0)

    @pl.when(step > 0)
    def _():
        down_total[...] += dot(act_ref[...], g, 0, 0)
        up_total[...] += dot(x, ghid_ref[...], 0, 0)

    @pl.when(step == pl.num_programs(0) - 1)
    def _():
        for place, total in enumerate((down_total, up_total)):
            size = total.shape[0] // 2
            rest[2 * place][...] = total[:size].astype(BF)
            rest[2 * place + 1][...] = total[size:].astype(BF)


MLP_BLOCK = 1280
MLP_CHUNK = 512


def mlp_call(x, g, up, down, deps=()):
    rows, width = x.shape
    hidden = up.shape[1]
    block = MLP_BLOCK if rows % MLP_BLOCK == 0 else WIN_TOK
    row = row_spec(block, width)
    wide = row_spec(block, hidden)
    halves = [(hidden // 2, width)] * 2 + [(width // 2, hidden)] * 2
    return call_after(
        functools.partial(mlp_kernel, chunk=min(MLP_CHUNK, hidden)),
        deps,
        grid=(rows // block,),
        in_specs=[row, row, whole_spec(up.shape), whole_spec(down.shape)],
        out_specs=[wide, wide] + [whole_spec(shape) for shape in halves],
        out_shape=[
            shaped((rows, hidden), BF),
            shaped((rows, hidden), BF),
        ]
        + [shaped(shape, BF) for shape in halves],
        scratch_shapes=[pltpu.VMEM(down.shape, F32), pltpu.VMEM(up.shape, F32)],
        compiler_params=params(),
        cost_estimate=cost(30),
        name="mlp",
    )(x, g, up, down)


def mlp_out_kernel(*refs, count):
    act_refs, ghid_refs, down_refs, up_refs = [
        refs[place * count : (place + 1) * count] for place in range(4)
    ]
    tokens_ref, cot_ref, attn_out_ref, mod_ref, out_ref, gres_ref, gattn_ref, sums_ref = refs[
        4 * count :
    ]
    join = lambda parts, axis: jnp.concatenate([part[...] for part in parts], axis=axis)
    mlp_outs = dot(join(act_refs, 1), join(down_refs, 0))
    gins = dot(join(ghid_refs, 1), join(up_refs, 1), 1, 1)
    for window in range(gins.shape[0] // WIN_TOK):
        span = window_span(window)
        mod = mod_ref[window]
        mlp_out, gin = mlp_outs[span], gins[span]
        cot = cot_ref[span, :].astype(F32)
        attn_out = attn_out_ref[span, :].astype(F32)
        resid = tokens_ref[span, :].astype(F32) + mod[2:3] * attn_out
        out_ref[span, :] = (resid + mod[5:6] * mlp_out).astype(BF)
        normed, inverse = normalise(resid)
        gres = cot + normalise_back(normed, inverse, gin * (1.0 + mod[4:5]))
        gres_ref[span, :] = gres.astype(BF)
        gattn_ref[span, :] = (mod[2:3] * gres).astype(BF)
        sums_ref[window, 0:1] = jnp.sum(gres * attn_out, axis=0, keepdims=True)
        sums_ref[window, 1:2] = jnp.sum(gin, axis=0, keepdims=True)
        sums_ref[window, 2:3] = jnp.sum(gin * normed, axis=0, keepdims=True)
        sums_ref[window, 3:4] = jnp.sum(cot * mlp_out, axis=0, keepdims=True)


def kept_spec(shape):
    return pl.BlockSpec(shape, lambda i: (0,) * len(shape), pipeline_mode=pl.Buffered(1))


def mlp_out_call(act, ghid, down, up, tokens, cotangent, attn_out, mods, deps=()):
    rows, width = tokens.shape
    per = 1
    block = per * WIN_TOK
    row = row_spec(block, width)
    windows = rows // WIN_TOK
    return call_after(
        functools.partial(mlp_out_kernel, count=len(act)),
        deps,
        grid=(windows // per,),
        in_specs=[row_spec(block, part.shape[1]) for part in act + ghid]
        + [kept_spec(part.shape) for part in down + up]
        + [row, row, row, mod_spec(per, mods.shape[1], width)],
        out_specs=[row, row, row, mod_spec(per, 4, width)],
        out_shape=[
            shaped((rows, width), BF),
            shaped((rows, width), BF),
            shaped((rows, width), BF),
            shaped((windows, 4, width), F32),
        ],
        compiler_params=params(),
        cost_estimate=cost(55),
        name="mlp_out",
    )(*act, *ghid, *down, *up, tokens, cotangent, attn_out, mods)


def last_kernel(*refs, count):
    dqkv_refs = refs[:count]
    weight_refs = refs[count : 2 * count]
    tokens_ref, gres_ref, mod_ref, out_ref, sums_ref = refs[2 * count :]
    join = lambda refs: jnp.concatenate([ref[part] for ref in refs for part in range(3)], axis=1)
    gin = dot(join(dqkv_refs), join(weight_refs), 1, 1)
    for window in range(gin.shape[0] // WIN_TOK):
        span = window_span(window)
        normed, inverse = normalise(tokens_ref[span, :].astype(F32))
        grad = gin[span]
        out_ref[span, :] = (
            gres_ref[span, :].astype(F32) + normalise_back(normed, inverse, grad * (1.0 + mod_ref[window, 1:2]))
        ).astype(BF)
        sums_ref[window, 0:1] = jnp.sum(grad, axis=0, keepdims=True)
        sums_ref[window, 1:2] = jnp.sum(grad * normed, axis=0, keepdims=True)


def last_call(dqkv, weights, tokens, gres, mods, deps=()):
    rows, width = tokens.shape
    count = len(dqkv)
    per = 1
    block = per * WIN_TOK
    row = row_spec(block, width)
    windows = rows // WIN_TOK
    return call_after(
        functools.partial(last_kernel, count=count),
        deps,
        grid=(windows // per,),
        in_specs=[part_spec(block, part.shape[2]) for part in dqkv]
        + [kept_spec(part.shape) for part in weights]
        + [row, row, mod_spec(per, mods.shape[1], width)],
        out_specs=[row, mod_spec(per, 2, width)],
        out_shape=[shaped((rows, width), BF), shaped((windows, 2, width), F32)],
        compiler_params=params(),
        cost_estimate=cost(28),
        name="last",
    )(*dqkv, *weights, tokens, gres, mods)


def body(
    n_dp,
    n_mp,
    tokens,
    cotangent,
    qkv_weight,
    out_weight,
    up_weight,
    down_weight,
    rel_bias,
    ada_weight,
    ada_bias,
    class_embed,
    window_clip,
    timesteps,
    class_ids,
):
    mp_index = lax.axis_index("mp")
    micro, local_rows, width = tokens.shape
    local_cols = class_embed.shape[1]
    clips = timesteps.shape[1]
    own_windows = local_rows // WIN_TOK
    rows = micro * local_rows
    tokens_flat = tokens.reshape(rows, width)
    cot_flat = cotangent.reshape(rows, width)
    masks = range(n_mp)

    columns = mp_index * local_cols + jnp.arange(local_cols)
    half_width = width // 2
    freq_index = (columns % half_width).astype(F32)
    frequency = jnp.exp(-math.log(10000.0) * freq_index / half_width)
    angle = timesteps.astype(F32)[..., None] * frequency
    step_embed = jnp.where(columns < half_width, jnp.sin(angle), jnp.cos(angle))
    class_hot = (class_ids[..., None] == jnp.arange(class_embed.shape[0])).astype(F32)
    condition = step_embed + jnp.einsum("mck,kd->mcd", class_hot, class_embed, precision=highest)
    lowered = jax.nn.silu(condition).astype(BF)
    mod_terms = jnp.einsum("mcd,de->mce", lowered, ada_weight, preferred_element_type=F32)
    near_terms = add_low(mod_terms, swap(mod_terms, "mp", n_mp, 1))
    modulation = near_terms
    for bit in bits_of(n_mp)[1:]:
        modulation = add_low(modulation, swap(modulation, "mp", n_mp, bit))
    modulation = modulation + ada_bias
    own_clip = lax.dynamic_slice_in_dim(window_clip, mp_index * own_windows, own_windows, 1)
    clip_hot = (own_clip[..., None] == jnp.arange(clips)).astype(F32)
    mods = jnp.einsum("mwc,mce->mwe", clip_hot, modulation, precision=highest)
    mods = mods.reshape(micro * own_windows, 6, width)

    steps = Steps()
    rel_tables = gather_shards(rel_bias, "mp", n_mp)
    blocks = bias_blocks(jnp.concatenate([rel_tables[m] for m in masks], axis=0))
    heads = rel_bias.shape[0]

    def gather(own, hold):
        shards = {}
        steps.jobs.append(gather_job(steps, own, shards, "mp", n_mp, hold))
        return shards

    def need(shards, mask, ties, token):
        while mask not in shards:
            ties = ties + steps.step(token)
        return ties

    qkv_w = gather(qkv_weight, 3)
    steps.step(modulation)
    attn_in = norm_call(tokens_flat, mods)
    out_w = gather(out_weight, 3)
    ties = steps.step(attn_in)
    qkv, mixed, lse = {}, {}, {}
    for m in masks:
        ties = need(qkv_w, m, ties, attn_in)
        qkv[m], mixed[m], lse[m] = attend_call(attn_in, qkv_w[m], (blocks, m, heads), ties)
        if m == 0:
            down_w = gather(down_weight, 4)
        elif m == 2 or m == n_mp - 1 == 1:
            up_w = gather(up_weight, 3)
        ties = steps.step(mixed[m])
    for m in masks:
        ties = need(out_w, m, ties, mixed[0])
    attn_out, mlp_in, grad_mlp = middle_call(
        [mixed[m] for m in masks], [out_w[m] for m in masks], tokens_flat, cot_flat, mods, ties
    )
    ties = steps.step(mlp_in)
    wide_sums = Sums(steps, n_mp, [0, 1, 1, 2])
    grads = {}
    steps.jobs.append(spread_job(steps, wide_sums, [0, 1], n_dp, True, grads, "down"))
    steps.jobs.append(spread_job(steps, wide_sums, [2, 3], n_dp, False, grads, "up"))
    act, grad_hidden = {}, {}
    for m in [m for m in masks if m % 2] + [m for m in reversed(masks) if m % 2 == 0]:
        ties = need(down_w, m, need(up_w, m, ties, mlp_in), mlp_in)
        act[m], grad_hidden[m], *wide_terms = mlp_call(mlp_in, grad_mlp, up_w[m], down_w[m], ties)
        wide_sums.add(m, wide_terms)
        ties = steps.step(wide_terms[0])
    block_out, grad_resid, grad_attn, late_sums = mlp_out_call(
        *[[part[m] for m in masks] for part in (act, grad_hidden, down_w, up_w)],
        tokens_flat,
        cot_flat,
        attn_out,
        mods,
        ties,
    )

    def clip_sums(window_sums):
        grouped = window_sums.reshape(micro, own_windows, -1)
        return jnp.einsum("mwc,mwe->mce", clip_hot, grouped, precision=highest).astype(BF)

    attn_sums = Sums(steps, n_mp, [0])
    steps.jobs.append(spread_job(steps, attn_sums, [0], n_dp, False, grads, "qkv"))
    dqkv, block_grads = {}, {}
    ties = steps.step(grad_attn)
    for m in reversed(masks):
        dqkv[m], block_grads[m], qkv_term = attend_back_call(
            grad_attn, out_w[m], qkv[m], mixed[m], lse[m], (blocks, m, heads), attn_in, ties
        )
        attn_sums.add(m, [qkv_term.reshape(-1, qkv_term.shape[2])])
        ties = steps.step(qkv_term)
    token_grad, early_sums = last_call(
        [dqkv[m] for m in masks], [qkv_w[m] for m in masks], tokens_flat, grad_resid, mods, ties
    )
    ties = steps.step(token_grad)
    window_sums = after(jnp.concatenate([early_sums, late_sums], axis=1), *ties)
    rel_sums = after(jnp.concatenate([block_grads[m] for m in masks], axis=0), *ties)
    rel_sums = collect_blocks(rel_sums).astype(BF).reshape(n_mp, -1)
    table_size = rel_sums.shape[1]
    rel_sums = jnp.pad(rel_sums, ((0, 0), (0, -table_size % width))).reshape(n_mp, -1, width)
    clip_terms = clip_sums(window_sums).reshape(-1, width)
    ties = steps.step()
    mod_total, rel_total = sum_everywhere(
        after(clip_terms, *ties), after(rel_sums, *ties), n_mp, n_dp
    )
    rel_grad = rel_total.reshape(-1)[:table_size].reshape(rel_bias.shape).astype(F32)
    steps.finish()

    down_grad = unfold_call(grads["down"], 2, ties)
    up_grad = grads["up"]
    qkv_grad = grads["qkv"][: 3 * width].reshape(qkv_weight.shape)
    out_grad = grads["qkv"][3 * width :].T
    mod_total = mod_total.astype(F32).reshape(micro, clips, 6 * width)
    ada_bias_grad = jnp.sum(mod_total, axis=(0, 1))
    ada_weight_grad = jnp.einsum(
        "mcd,mce->de", lowered.astype(F32), mod_total, precision=highest
    )
    grad_lowered = jnp.einsum(
        "mce,de->mcd", mod_total, ada_weight.astype(F32), precision=highest
    )
    grad_condition = jax.vjp(jax.nn.silu, condition)[1](grad_lowered)[0]
    class_grad = jnp.einsum("mck,mcd->kd", class_hot, grad_condition, precision=highest)
    return (
        block_out.reshape(tokens.shape),
        token_grad.reshape(tokens.shape),
        qkv_grad,
        out_grad,
        up_grad,
        down_grad,
        rel_grad,
        ada_weight_grad,
        ada_bias_grad,
        class_grad,
    )


def solution(mesh):
    rows = P(None, ("dp", "mp"), None)
    in_specs = (
        rows,
        rows,
        P(None, None, "mp"),
        P("mp", None),
        P(None, "mp"),
        P("mp", None),
        P("mp", None),
        P("mp", None),
        P(),
        P(None, "mp"),
        P(None, "dp"),
        P(),
        P(),
    )
    out_specs = (
        rows,
        rows,
        P(None, None, "mp"),
        P("mp", None),
        P(None, "mp"),
        P("mp", None),
        P("mp", None),
        P("mp", None),
        P(),
        P(None, "mp"),
    )
    step = functools.partial(body, mesh.shape["dp"], mesh.shape["mp"])
    return jax.shard_map(step, mesh=mesh, in_specs=in_specs, out_specs=out_specs, check_vma=False)
```

time: 709 us -> 707 us (level)
  waiting for transfers between devices: 41.6 us -> 62 us
  Pallas kernels: 524 us -> 512 us
  starting transfers between devices: 56.4 us -> 46.1 us
    ppermute x60 -> x57, waiting for transfers between devices: 41.6 us -> 62 us  [swap(): return lax.ppermute(value, axis, [(i, i ^ bit) for i in range(size)])]
    pallas_call x19 -> x15, Pallas kernels: 71.7 us -> 56.4 us  [the longest x6 25.7 us: split_call(): pl.pallas_call(functools.partial(split_kernel, count=count, groups=[len(g...]
    ppermute x60 -> x57, starting transfers between devices: 56.3 us -> 46.1 us  [swap(): return lax.ppermute(value, axis, [(i, i ^ bit) for i in range(size)])]
    pallas_call x16 -> x17, Pallas kernels: 452 us -> 456 us  [call_after(): return lambda *args: call(*args, *deps)]
  transfers between devices with their start and end apart: 62 -> 58, of which waited for: 10 -> 12; matrix products, arithmetic and copies ran while one was open for 8% -> 7% of each run, Pallas kernels for 73% -> 71%
where the time goes in v4:
time: 707 us; the launch traced here: 700 us
  Pallas kernels  512 us (72%)
  waiting for transfers between devices  62 us (9%)
  starting transfers between devices  46.1 us (7%)
  local copies, waits for them, and re-layouts  29.8 us (4%)
  matrix products  19 us (3%)
  other arithmetic  16.2 us (2%)
  between operations  14.9 us (2%)
    pallas_call x17, Pallas kernels, call_after(): return lambda *args: call(*args, *deps)  456 us
    ppermute x57, waiting for transfers between devices, swap(): return lax.ppermute(value, axis, [(i, i ^ bit) for i in range(size)])  62 us
    ppermute x57, starting transfers between devices, swap(): return lax.ppermute(value, axis, [(i, i ^ bit) for i in range(size)])  46.1 us
    pallas_call x6, Pallas kernels, split_call(): pl.pallas_call(functools.partial(split_kernel, count=count, groups=[len(g...  25.7 us
    pallas_call x5, Pallas kernels, add_groups(): pl.pallas_call(functools.partial(sum_kernel, groups=[len(group) for group...  17.4 us
  transfers between devices with their start and end apart: 58, of which 12 were waited for; matrix products, arithmetic and copies ran while one was open for 7% of the time, Pallas kernels for 71%

profile of v4, /device:TPU:0, one launch (start us, length us, event | category | flops | bytes accessed | tf_op | source)
XLA Modules:
  0.0 700.1 jit_solution(3696103498035383869)
XLA Ops:
  7.8 2.6 collective-permute-start.3
  11.1 1.7 convolution_add_fusion
  12.8 2.4 fusion.6
  17.5 3.7 fusion.1
  21.1 3.6 copy.33.refs_2_.refs_5_
  24.7 3.8 collective-permute-done.1
  30.2 8.9 %norm_in.1.refs_0_.refs_3_.refs_6_ = bf16[2560,1024]{1,0:T(8,128)(2,1)} custom-call(bf16[2560,1024]{1,0:T(8,128)(2,1)} %bitcast.130, f32[8,6,1024]{2,1,0:T(8,128)} %reshape.254.refs_1_.refs_10_.refs_19_), custom_call_target="tpu_custom_call" | custom-call | flops 8000000000 | bytes 28000000 | tf_op jit(solution)/shard_map/norm_in/pallas_call | solution.py:83
  39.6 1.7 collective-permute-start.8
  41.3 16.7 %attend.4 = (bf16[3,2560,256]{2,1,0:T(8,128)(2,1)}, bf16[2560,256]{1,0:T(8,128)(2,1)}, f32[8,8,384]{2,1,0:T(8,128)}) custom-call(bf16[2560,1024]{1,0:T(8,128)(2,1)} %norm_in.1.refs_0_.refs_3_.refs_6_, bf16[3,1024,256]{2,1,0:T(8,128)(2,1)} %refs_4_.3, f32[16,9,64,64]{3,2,1,0:T(8,128)} %copy.33.refs_2_.refs_5_, bf16[2560,1024]{1,0:T(8,128)(2,1)} %norm_in.1.refs_0_.refs_3_.refs_6_), custom_call_target="tpu_custom_call" | custom-call | flops 19000000512 | bytes 66500000 | tf_op jit(solution)/shard_map/attend/pallas_call | solution.py:83
  58.3 16.7 %attend.5 = (bf16[3,2560,256]{2,1,0:T(8,128)(2,1)}, bf16[2560,256]{1,0:T(8,128)(2,1)}, f32[8,8,384]{2,1,0:T(8,128)}) custom-call(bf16[2560,1024]{1,0:T(8,128)(2,1)} %norm_in.1.refs_0_.refs_3_.refs_6_, bf16[3,1024,256]{2,1,0:T(8,128)(2,1)} %collective-permute-done.5.refs_1_.refs_5_, f32[16,9,64,64]{3,2,1,0:T(8,128)} %copy.33.refs_2_.refs_5_, ...), custom_call_target="tpu_custom_call" | custom-call | flops 19000000512 | bytes 66500000 | tf_op jit(solution)/shard_map/attend/pallas_call | solution.py:83
  75.5 16.7 %attend.6 = (bf16[3,2560,256]{2,1,0:T(8,128)(2,1)}, bf16[2560,256]{1,0:T(8,128)(2,1)}, f32[8,8,384]{2,1,0:T(8,128)}) custom-call(bf16[2560,1024]{1,0:T(8,128)(2,1)} %norm_in.1.refs_0_.refs_3_.refs_6_, bf16[3,1024,256]{2,1,0:T(8,128)(2,1)} %collective-permute-done.6.refs_1_.refs_3_.refs_6_, f32[16,9,64,64]{3,2,1,0:T(8,128)} %copy.33.refs_2_.refs_5_, ...), custom_call_target="tpu_custom_call" | custom-call | flops 19000000512 | bytes 66500000 | tf_op jit(solution)/shard_map/attend/pallas_call | solution.py:83
  92.8 30.3 %attend.7 = (bf16[3,2560,256]{2,1,0:T(8,128)(2,1)}, bf16[2560,256]{1,0:T(8,128)(2,1)}, f32[8,8,384]{2,1,0:T(8,128)}) custom-call(bf16[2560,1024]{1,0:T(8,128)(2,1)} %norm_in.1.refs_0_.refs_3_.refs_6_, bf16[3,1024,256]{2,1,0:T(8,128)(2,1)} %collective-permute-done.7.refs_1_.refs_7_, f32[16,9,64,64]{3,2,1,0:T(8,128)} %copy.33.refs_2_.refs_5_, ...), custom_call_target="tpu_custom_call" | custom-call | flops 19000000512 | bytes 66500000 | tf_op jit(solution)/shard_map/attend/pallas_call | solution.py:83
  123.1 1.8 collective-permute-start.11
  124.9 15.6 %middle.1 = (bf16[2560,1024]{1,0:T(8,128)(2,1)}, bf16[2560,1024]{1,0:T(8,128)(2,1)}, bf16[2560,1024]{1,0:T(8,128)(2,1)}) custom-call(bf16[2560,256]{1,0:T(8,128)(2,1)} %get-tuple-element.163.refs_3_.refs_0_, bf16[2560,256]{1,0:T(8,128)(2,1)} %get-tuple-element.165.refs_4_.refs_1_.refs_3_, bf16[2560,256]{1,0:T(8,128)(2,1)} %get-tuple-element.167.refs_4_.refs_2_.refs_3_, ...), custom_call_target="tpu_custom_call" | custom-call | flops 16000000000 | bytes 56000000 | tf_op jit(solution)/shard_map/middle/pallas_call | solution.py:83
  140.7 32.3 %mlp.4 = (bf16[2560,1024]{1,0:T(8,128)(2,1)}, bf16[2560,1024]{1,0:T(8,128)(2,1)}, bf16[512,1024]{1,0:T(8,128)(2,1)}, bf16[512,1024]{1,0:T(8,128)(2,1)}, bf16[512...) custom-call(bf16[2560,1024]{1,0:T(8,128)(2,1)} %get-tuple-element.173.refs_0_.refs_5_, ...), custom_call_target="tpu_custom_call" | custom-call | flops 30000001024 | bytes 105000000 | tf_op jit(solution)/shard_map/mlp/pallas_call | solution.py:83
  175.2 2.4 collective-permute-done.15.refs_2_.refs_15_
  177.7 32.6 %mlp.5 = (bf16[2560,1024]{1,0:T(8,128)(2,1)}, bf16[2560,1024]{1,0:T(8,128)(2,1)}, bf16[512,1024]{1,0:T(8,128)(2,1)}, bf16[512,1024]{1,0:T(8,128)(2,1)}, bf16[512...) custom-call(bf16[2560,1024]{1,0:T(8,128)(2,1)} %get-tuple-element.173.refs_0_.refs_5_, ...), custom_call_target="tpu_custom_call" | custom-call | flops 30000001024 | bytes 105000000 | tf_op jit(solution)/shard_map/mlp/pallas_call | solution.py:83
  211.4 32.4 %mlp.6 = (bf16[2560,1024]{1,0:T(8,128)(2,1)}, bf16[2560,1024]{1,0:T(8,128)(2,1)}, bf16[512,1024]{1,0:T(8,128)(2,1)}, bf16[512,1024]{1,0:T(8,128)(2,1)}, bf16[512...) custom-call(bf16[2560,1024]{1,0:T(8,128)(2,1)} %get-tuple-element.173.refs_0_.refs_5_, ...), custom_call_target="tpu_custom_call" | custom-call | flops 30000001024 | bytes 105000000 | tf_op jit(solution)/shard_map/mlp/pallas_call | solution.py:83
  243.9 5.8 add.257
  250.1 32.9 %mlp.7 = (bf16[2560,1024]{1,0:T(8,128)(2,1)}, bf16[2560,1024]{1,0:T(8,128)(2,1)}, bf16[512,1024]{1,0:T(8,128)(2,1)}, bf16[512,1024]{1,0:T(8,128)(2,1)}, bf16[512...) custom-call(bf16[2560,1024]{1,0:T(8,128)(2,1)} %get-tuple-element.173.refs_0_.refs_5_, ...), custom_call_target="tpu_custom_call" | custom-call | flops 30000001024 | bytes 105000000 | tf_op jit(solution)/shard_map/mlp/pallas_call | solution.py:83
  283.0 1.8 collective-permute-start.26
  285.1 62.7 %mlp_out.1 = (bf16[2560,1024]{1,0:T(8,128)(2,1)}, bf16[2560,1024]{1,0:T(8,128)(2,1)}, bf16[2560,1024]{1,0:T(8,128)(2,1)}, f32[8,4,1024]{2,1,0:T(4,128)}) custom-call(bf16[2560,1024]{1,0:T(8,128)(2,1)} %get-tuple-element.213.refs_0_, bf16[2560,1024]{1,0:T(8,128)(2,1)} %get-tuple-element.214.refs_1_, bf16[2560,1024]{1,0:T(8,128)(2,1)} %get-tuple-element.215.refs_2_, ...), custom_call_target="tpu_custom_call" | custom-call | flops 54999998464 | bytes 192500000 | tf_op jit(solution)/shard_map/mlp_out/pallas_call | solution.py:83
  347.8 1.8 collective-permute-start.27
  349.6 4.9 split.6
  355.9 31.1 %attend_back.4 = (bf16[3,2560,256]{2,1,0:T(8,128)(2,1)}, f32[4,9,64,64]{3,2,1,0:T(8,128)}, bf16[4,1024,256]{2,1,0:T(8,128)(2,1)}) custom-call(bf16[2560,1024]{1,0:T(8,128)(2,1)} %get-tuple-element.226.refs_0_.refs_10_, bf16[256,1024]{1,0:T(8,128)(2,1)} %collective-permute-done.10.refs_7_.refs_1_, bf16[3,2560,256]{2,1,0:T(8,128)(2,1)} %get-tuple-element.234.refs_2_, ...), custom_call_target="tpu_custom_call" | custom-call | flops 30000001024 | bytes 105000000 | tf_op jit(solution)/shard_map/attend_back/pallas_call | solution.py:83
  387.1 5.0 split.7
  392.6 3.5 split.8
  396.1 3.6 collective-permute-start.33
  400.5 31.5 %attend_back.5 = (bf16[3,2560,256]{2,1,0:T(8,128)(2,1)}, f32[4,9,64,64]{3,2,1,0:T(8,128)}, bf16[4,1024,256]{2,1,0:T(8,128)(2,1)}) custom-call(bf16[2560,1024]{1,0:T(8,128)(2,1)} %get-tuple-element.226.refs_0_.refs_10_, bf16[256,1024]{1,0:T(8,128)(2,1)} %collective-permute-done.8.refs_3_.refs_6_.refs_1_, bf16[3,2560,256]{2,1,0:T(8,128)(2,1)} %get-tuple-element.245.refs_2_, ...), custom_call_target="tpu_custom_call" | custom-call | flops 30000001024 | bytes 105000000 | tf_op jit(solution)/shard_map/attend_back/pallas_call | solution.py:83
  433.5 2.0 add.258.refs_2_.refs_7_
  435.6 3.5 split.9
  439.1 3.6 collective-permute-start.37
  443.5 4.3 add.259.refs_14_
  448.2 31.2 %attend_back.6 = (bf16[3,2560,256]{2,1,0:T(8,128)(2,1)}, f32[4,9,64,64]{3,2,1,0:T(8,128)}, bf16[4,1024,256]{2,1,0:T(8,128)(2,1)}) custom-call(bf16[2560,1024]{1,0:T(8,128)(2,1)} %get-tuple-element.226.refs_0_.refs_10_, bf16[256,1024]{1,0:T(8,128)(2,1)} %collective-permute-done.9.refs_5_.refs_1_, bf16[3,2560,256]{2,1,0:T(8,128)(2,1)} %get-tuple-element.265.refs_2_, ...), custom_call_target="tpu_custom_call" | custom-call | flops 30000001024 | bytes 105000000 | tf_op jit(solution)/shard_map/attend_back/pallas_call | solution.py:83
  481.0 2.0 add.260.refs_7_.refs_0_
  483.0 3.8 collective-permute-start.41
  487.4 6.9 collective-permute-done.38.refs_8_.refs_0_
  494.3 31.3 %attend_back.7 = (bf16[3,2560,256]{2,1,0:T(8,128)(2,1)}, f32[4,9,64,64]{3,2,1,0:T(8,128)}, bf16[4,1024,256]{2,1,0:T(8,128)(2,1)}) custom-call(bf16[2560,1024]{1,0:T(8,128)(2,1)} %get-tuple-element.226.refs_0_.refs_10_, bf16[256,1024]{1,0:T(8,128)(2,1)} %refs_1_.3, bf16[3,2560,256]{2,1,0:T(8,128)(2,1)} %get-tuple-element.227.refs_2_, ...), custom_call_target="tpu_custom_call" | custom-call | flops 30000001024 | bytes 105000000 | tf_op jit(solution)/shard_map/attend_back/pallas_call | solution.py:83
  527.1 2.7 assemble.4.refs_12_.refs_0_
  531.3 5.3 split.10
  537.2 5.5 pad_maximum_fusion
  542.7 26.8 %last.1 = (bf16[2560,1024]{1,0:T(8,128)(2,1)}, f32[8,2,1024]{2,1,0:T(2,128)}) custom-call(bf16[3,2560,256]{2,1,0:T(8,128)(2,1)} %get-tuple-element.279.refs_0_, bf16[3,2560,256]{2,1,0:T(8,128)(2,1)} %get-tuple-element.280.refs_1_, bf16[3,2560,256]{2,1,0:T(8,128)(2,1)} %get-tuple-element.281.refs_2_, bf16[3,2560,256]{2,1,0:T(8,128)(2,1)} %get-tuple-element.282.refs_3_, ...), custom_call_target="tpu_custom_call" | custom-call | flops 28000000000 | bytes 98000000 | tf_op jit(solution)/shard_map/last/pallas_call | solution.py:83
  569.5 5.9 collective-permute-done.43.refs_1_
  575.4 3.5 split.11
  578.9 3.5 collective-permute-start.47
  585.0 5.3 reshape.265
  590.3 11.8 %collective-permute-done.46.refs_2_ = bf16[512,256]{1,0:T(8,128)(2,1)S(1)} collective-permute-done((bf16[512,256]{1,0:T(8,128)(2,1)}, bf16[512,256]{1,0:T(8,128)(2,1)S(1)}, u32[]{:S(2)}, u32[]{:S(2)}) %collective-permute-start.46) | collective-permute-done | bytes 262176 | tf_op jit(solution)/shard_map/ppermute | solution.py:105
  602.8 3.2 add.261.refs_0_
  606.1 4.1 fusion.3
  611.0 2.8 collective-permute-done.48.refs_1_
  617.6 6.3 collective-permute-done.53
  624.1 1.7 collective-permute-start.54
  627.6 13.2 %collective-permute-done.49.refs_2_ = bf16[512,256]{1,0:T(8,128)(2,1)} collective-permute-done((bf16[512,256]{1,0:T(8,128)(2,1)S(1)}, bf16[512,256]{1,0:T(8,128)(2,1)}, u32[]{:S(2)}, u32[]{:S(2)}) %collective-permute-start.49) | collective-permute-done | bytes 262176 | tf_op jit(solution)/shard_map/ppermute | solution.py:105
  640.8 2.7 assemble.5.refs_0_
  643.5 1.7 collective-permute-start.51
  647.9 4.0 assemble.7
  651.9 6.0 unfold.1
  661.3 1.7 collective-permute-start.56
  663.0 5.1 collective-permute-done.51.refs_1_
  668.1 3.8 assemble.6
  671.9 2.3 slice_bitcast_fusion
  674.2 3.9 slice.56
  678.1 2.5 copy.41
  686.1 3.7 convolution_bitcast_fusion
  (204 shorter events, 46.8 us)
Async XLA Ops:
  7.2 535.5 %all-gather.3.cloned.1.call-start = ((), (), s32[]{:S(2)}) async-start(), calls=%async_computation | async-start | bytes 2359296 | tf_op jit(solution)/shard_map/all_gather | solution.py:374
  7.2 8.7 %collective-permute-start.2 = (f32[4,2025]{1,0:T(4,128)}, f32[4,2025]{1,0:T(4,128)S(1)}, u32[]{:S(2)}, u32[]{:S(2)}) collective-permute-start(f32[4,2025]{1,0:T(4,128)} %param.19), channel_id=1, source_target_pairs={{0,1},{1,0},{2,3},{3,2},{4,5},{5,4},{6,7},{7,6},{8,9},{9,8},{10,11... | collective-permute-start | bytes 97208 | tf_op jit(solution)/shard_map/ppermute | solution.py:105
  7.8 7.7 %collective-permute-start.3 = (f32[4,2025]{1,0:T(4,128)}, f32[4,2025]{1,0:T(4,128)S(1)}, u32[]{:S(2)}, u32[]{:S(2)}) collective-permute-start(f32[4,2025]{1,0:T(4,128)} %param.19), channel_id=1, source_target_pairs={{0,2},{1,3},{2,0},{3,1},{4,6},{5,7},{6,4},{7,5},{8,10},{9,11},{10,... | collective-permute-start | bytes 97208 | tf_op jit(solution)/shard_map/ppermute | solution.py:105
  15.2 2.1 collective-permute-start
  15.5 1.5 collective-permute-start.4
  16.0 13.0 %copy-start.26 = (s32[2,4]{1,0:T(2,128)}, s32[2,4]{1,0:T(2,128)S(1)}, u32[]{:S(2)}) copy-start(s32[2,4]{1,0:T(2,128)S(1)} %constant_dynamic-slice_fusion) | copy-start | bytes 100
  17.3 11.3 %collective-permute-start.1 = (f32[2,8,6144]{2,1,0:T(8,128)S(1)}, f32[2,8,6144]{2,1,0:T(8,128)S(1)}, u32[]{:S(2)}, u32[]{:S(2)}) collective-permute-start(f32[2,8,6144]{2,1,0:T(8,128)S(1)} %add.163), channel_id=1, source_target_pairs={{0,2},{1,3},{2,0},{3,1},{4,6},{5,7},{6,4},{7,5},{8,10},{9,11},{10,... | collective-permute-start | bytes 1179656 | tf_op jit(solution)/shard_map/ppermute | solution.py:105
  28.6 46.4 %collective-permute-start.6 = (bf16[3,1024,256]{2,1,0:T(8,128)(2,1)}, bf16[3,1024,256]{2,1,0:T(8,128)(2,1)}, u32[]{:S(2)}, u32[]{:S(2)}) collective-permute-start(bf16[3,1024,256]{2,1,0:T(8,128)(2,1)} %refs_4_.3), channel_id=1, source_target_pairs={{0,2},{1,3},{2,0},{3,1},{4,6},{5,7},{6,4},{7,5},{8,10},{9,11},{10,... | collective-permute-start | bytes 4718600 | tf_op jit(solution)/shard_map/ppermute | solution.py:105
  29.0 29.3 %collective-permute-start.5 = (bf16[3,1024,256]{2,1,0:T(8,128)(2,1)}, bf16[3,1024,256]{2,1,0:T(8,128)(2,1)}, u32[]{:S(2)}, u32[]{:S(2)}) collective-permute-start(bf16[3,1024,256]{2,1,0:T(8,128)(2,1)} %refs_4_.3), channel_id=1, source_target_pairs={{0,1},{1,0},{2,3},{3,2},{4,5},{5,4},{6,7},{7,6},{8,9},{9,8},{10,11... | collective-permute-start | bytes 4718600 | tf_op jit(solution)/shard_map/ppermute | solution.py:105
  39.1 84.0 %collective-permute-start.9 = (bf16[256,1024]{1,0:T(8,128)(2,1)S(1)}, bf16[256,1024]{1,0:T(8,128)(2,1)}, u32[]{:S(2)}, u32[]{:S(2)}) collective-permute-start(bf16[256,1024]{1,0:T(8,128)(2,1)S(1)} %copy-done.29), channel_id=1, source_target_pairs={{0,1},{1,0},{2,3},{3,2},{4,5},{5,4},{6,7},{7,6},{8,9},{9,8},{10,11... | collective-permute-start | bytes 1572872 | tf_op jit(solution)/shard_map/ppermute | solution.py:105
  39.6 52.7 %collective-permute-start.8 = (bf16[256,1024]{1,0:T(8,128)(2,1)S(1)}, bf16[256,1024]{1,0:T(8,128)(2,1)}, u32[]{:S(2)}, u32[]{:S(2)}) collective-permute-start(bf16[256,1024]{1,0:T(8,128)(2,1)S(1)} %copy-done.29), channel_id=1, source_target_pairs={{0,2},{1,3},{2,0},{3,1},{4,6},{5,7},{6,4},{7,5},{8,10},{9,11},{10,... | collective-permute-start | bytes 1572872 | tf_op jit(solution)/shard_map/ppermute | solution.py:105
  58.0 82.5 %collective-permute-start.14 = (bf16[1024,1024]{1,0:T(8,128)(2,1)}, bf16[1024,1024]{1,0:T(8,128)(2,1)}, u32[]{:S(2)}, u32[]{:S(2)}) collective-permute-start(bf16[1024,1024]{1,0:T(8,128)(2,1)} %refs_8_.1), channel_id=1, source_target_pairs={{0,2},{1,3},{2,0},{3,1},{4,6},{5,7},{6,4},{7,5},{8,10},{9,11},{10,... | collective-permute-start | bytes 6291464 | tf_op jit(solution)/shard_map/ppermute | solution.py:105
  58.3 82.4 %collective-permute-start.13 = (bf16[1024,1024]{1,0:T(8,128)(2,1)}, bf16[1024,1024]{1,0:T(8,128)(2,1)}, u32[]{:S(2)}, u32[]{:S(2)}) collective-permute-start(bf16[1024,1024]{1,0:T(8,128)(2,1)} %refs_8_.1), channel_id=1, source_target_pairs={{0,1},{1,0},{2,3},{3,2},{4,5},{5,4},{6,7},{7,6},{8,9},{9,8},{10,11... | collective-permute-start | bytes 6291464 | tf_op jit(solution)/shard_map/ppermute | solution.py:105
  75.0 17.4 %collective-permute-start.7 = (bf16[3,1024,256]{2,1,0:T(8,128)(2,1)}, bf16[3,1024,256]{2,1,0:T(8,128)(2,1)}, u32[]{:S(2)}, u32[]{:S(2)}) collective-permute-start(bf16[3,1024,256]{2,1,0:T(8,128)(2,1)} %collective-permute-done.6.refs_1_.refs_3_.refs_6_), channel_id=1, source_target_pairs={{0,1},{1,0},{2,3},{3,2},{4,5},{5,4},{6,7},{7,6},{8,9},{9,8},{10,11... | collective-permute-start | bytes 4718600 | tf_op jit(solution)/shard_map/ppermute | solution.py:105
  92.3 32.7 %collective-permute-start.10 = (bf16[256,1024]{1,0:T(8,128)(2,1)}, bf16[256,1024]{1,0:T(8,128)(2,1)}, u32[]{:S(2)}, u32[]{:S(2)}) collective-permute-start(bf16[256,1024]{1,0:T(8,128)(2,1)} %collective-permute-done.8.refs_3_.refs_6_.refs_1_), channel_id=1, source_target_pairs={{0,1},{1,0},{2,3},{3,2},{4,5},{5,4},{6,7},{7,6},{8,9},{9,8},{10,11... | collective-permute-start | bytes 1572872 | tf_op jit(solution)/shard_map/ppermute | solution.py:105
  92.4 48.3 %collective-permute-start.12 = (bf16[1024,1024]{1,0:T(8,128)(2,1)}, bf16[1024,1024]{1,0:T(8,128)(2,1)}, u32[]{:S(2)}, u32[]{:S(2)}) collective-permute-start(bf16[1024,1024]{1,0:T(8,128)(2,1)} %refs_12_.1), channel_id=1, source_target_pairs={{0,1},{1,0},{2,3},{3,2},{4,5},{5,4},{6,7},{7,6},{8,9},{9,8},{10,11... | collective-permute-start | bytes 6291464 | tf_op jit(solution)/shard_map/ppermute | solution.py:105
  123.1 49.9 %collective-permute-start.11 = (bf16[1024,1024]{1,0:T(8,128)(2,1)}, bf16[1024,1024]{1,0:T(8,128)(2,1)}, u32[]{:S(2)}, u32[]{:S(2)}) collective-permute-start(bf16[1024,1024]{1,0:T(8,128)(2,1)} %refs_12_.1), channel_id=1, source_target_pairs={{0,2},{1,3},{2,0},{3,1},{4,6},{5,7},{6,4},{7,5},{8,10},{9,11},{10,... | collective-permute-start | bytes 6291464 | tf_op jit(solution)/shard_map/ppermute | solution.py:105
  140.6 34.2 %collective-permute-start.16 = (bf16[1024,1024]{1,0:T(8,128)(2,1)}, bf16[1024,1024]{1,0:T(8,128)(2,1)}, u32[]{:S(2)}, u32[]{:S(2)}) collective-permute-start(bf16[1024,1024]{1,0:T(8,128)(2,1)} %collective-permute-done.14.refs_4_.refs_3_.refs_10_), channel_id=1, source_target_pairs={{0,1},{1,0},{2,3},{3,2},{4,5},{5,4},{6,7},{7,6},{8,9},{9,8},{10,11... | collective-permute-start | bytes 6291464 | tf_op jit(solution)/shard_map/ppermute | solution.py:105
  173.0 4.6 collective-permute-start.15
  174.2 36.1 %collective-permute-start.18 = (bf16[512,1024]{1,0:T(8,128)(2,1)}, bf16[512,1024]{1,0:T(8,128)(2,1)}, u32[]{:S(2)}, u32[]{:S(2)}) collective-permute-start(bf16[512,1024]{1,0:T(8,128)(2,1)} %get-tuple-element.184.refs_5_), channel_id=1, source_target_pairs={{0,1},{1,0},{2,3},{3,2},{4,5},{5,4},{6,7},{7,6},{8,9},{9,8},{10,11... | collective-permute-start | bytes 3145736 | tf_op jit(solution)/shard_map/ppermute | solution.py:105
  174.3 36.0 %collective-permute-start.21 = (bf16[512,1024]{1,0:T(8,128)(2,1)}, bf16[512,1024]{1,0:T(8,128)(2,1)}, u32[]{:S(2)}, u32[]{:S(2)}) collective-permute-start(bf16[512,1024]{1,0:T(8,128)(2,1)} %get-tuple-element.193), channel_id=1, source_target_pairs={{0,1},{1,0},{2,3},{3,2},{4,5},{5,4},{6,7},{7,6},{8,9},{9,8},{10,11... | collective-permute-start | bytes 3145736 | tf_op jit(solution)/shard_map/ppermute | solution.py:105
  174.7 35.6 %collective-permute-start.20 = (bf16[512,1024]{1,0:T(8,128)(2,1)}, bf16[512,1024]{1,0:T(8,128)(2,1)}, u32[]{:S(2)}, u32[]{:S(2)}) collective-permute-start(bf16[512,1024]{1,0:T(8,128)(2,1)} %get-tuple-element.190), channel_id=1, source_target_pairs={{0,1},{1,0},{2,3},{3,2},{4,5},{5,4},{6,7},{7,6},{8,9},{9,8},{10,11... | collective-permute-start | bytes 3145736 | tf_op jit(solution)/shard_map/ppermute | solution.py:105
  174.8 35.5 %collective-permute-start.19 = (bf16[512,1024]{1,0:T(8,128)(2,1)}, bf16[512,1024]{1,0:T(8,128)(2,1)}, u32[]{:S(2)}, u32[]{:S(2)}) collective-permute-start(bf16[512,1024]{1,0:T(8,128)(2,1)} %get-tuple-element.187), channel_id=1, source_target_pairs={{0,1},{1,0},{2,3},{3,2},{4,5},{5,4},{6,7},{7,6},{8,9},{9,8},{10,11... | collective-permute-start | bytes 3145736 | tf_op jit(solution)/shard_map/ppermute | solution.py:105
  210.4 33.5 %collective-permute-start.17 = (bf16[512,1024]{1,0:T(8,128)(2,1)}, bf16[512,1024]{1,0:T(8,128)(2,1)}, u32[]{:S(2)}, u32[]{:S(2)}) collective-permute-start(bf16[512,1024]{1,0:T(8,128)(2,1)} %get-tuple-element.183.refs_8_), channel_id=1, source_target_pairs={{0,1},{1,0},{2,3},{3,2},{4,5},{5,4},{6,7},{7,6},{8,9},{9,8},{10,11... | collective-permute-start | bytes 3145736 | tf_op jit(solution)/shard_map/ppermute | solution.py:105
  210.8 33.1 %collective-permute-start.24 = (bf16[512,1024]{1,0:T(8,128)(2,1)}, bf16[512,1024]{1,0:T(8,128)(2,1)}, u32[]{:S(2)}, u32[]{:S(2)}) collective-permute-start(bf16[512,1024]{1,0:T(8,128)(2,1)} %get-tuple-element.204), channel_id=1, source_target_pairs={{0,1},{1,0},{2,3},{3,2},{4,5},{5,4},{6,7},{7,6},{8,9},{9,8},{10,11... | collective-permute-start | bytes 3145736 | tf_op jit(solution)/shard_map/ppermute | solution.py:105
  210.9 32.9 %collective-permute-start.23 = (bf16[512,1024]{1,0:T(8,128)(2,1)}, bf16[512,1024]{1,0:T(8,128)(2,1)}, u32[]{:S(2)}, u32[]{:S(2)}) collective-permute-start(bf16[512,1024]{1,0:T(8,128)(2,1)} %get-tuple-element.201), channel_id=1, source_target_pairs={{0,1},{1,0},{2,3},{3,2},{4,5},{5,4},{6,7},{7,6},{8,9},{9,8},{10,11... | collective-permute-start | bytes 3145736 | tf_op jit(solution)/shard_map/ppermute | solution.py:105
  211.3 32.6 %collective-permute-start.22 = (bf16[512,1024]{1,0:T(8,128)(2,1)}, bf16[512,1024]{1,0:T(8,128)(2,1)}, u32[]{:S(2)}, u32[]{:S(2)}) collective-permute-start(bf16[512,1024]{1,0:T(8,128)(2,1)} %get-tuple-element.198), channel_id=1, source_target_pairs={{0,1},{1,0},{2,3},{3,2},{4,5},{5,4},{6,7},{7,6},{8,9},{9,8},{10,11... | collective-permute-start | bytes 3145736 | tf_op jit(solution)/shard_map/ppermute | solution.py:105
  249.7 35.3 %collective-permute-start.25 = (bf16[512,1024]{1,0:T(8,128)(2,1)}, bf16[512,1024]{1,0:T(8,128)(2,1)}, u32[]{:S(2)}, u32[]{:S(2)}) collective-permute-start(bf16[512,1024]{1,0:T(8,128)(2,1)} %get-tuple-element.222.refs_8_), channel_id=1, source_target_pairs={{0,2},{1,3},{2,0},{3,1},{4,6},{5,7},{6,4},{7,5},{8,10},{9,11},{10,... | collective-permute-start | bytes 3145736 | tf_op jit(solution)/shard_map/ppermute | solution.py:105
  283.0 66.6 %collective-permute-start.26 = (bf16[512,1024]{1,0:T(8,128)(2,1)}, bf16[512,1024]{1,0:T(8,128)(2,1)}, u32[]{:S(2)}, u32[]{:S(2)}) collective-permute-start(bf16[512,1024]{1,0:T(8,128)(2,1)} %get-tuple-element.230.refs_10_), channel_id=1, source_target_pairs={{0,2},{1,3},{2,0},{3,1},{4,6},{5,7},{6,4},{7,5},{8,10},{9,11},{10,... | collective-permute-start | bytes 3145736 | tf_op jit(solution)/shard_map/ppermute | solution.py:105
  284.8 64.8 %collective-permute-start.28 = (bf16[512,1024]{1,0:T(8,128)(2,1)}, bf16[512,1024]{1,0:T(8,128)(2,1)}, u32[]{:S(2)}, u32[]{:S(2)}) collective-permute-start(bf16[512,1024]{1,0:T(8,128)(2,1)} %get-tuple-element.236.refs_9_), channel_id=1, source_target_pairs={{0,2},{1,3},{2,0},{3,1},{4,6},{5,7},{6,4},{7,5},{8,10},{9,11},{10,... | collective-permute-start | bytes 3145736 | tf_op jit(solution)/shard_map/ppermute | solution.py:105
  347.8 39.3 %collective-permute-start.27 = (bf16[512,1024]{1,0:T(8,128)(2,1)}, bf16[512,1024]{1,0:T(8,128)(2,1)}, u32[]{:S(2)}, u32[]{:S(2)}) collective-permute-start(bf16[512,1024]{1,0:T(8,128)(2,1)} %get-tuple-element.233.refs_11_), channel_id=1, source_target_pairs={{0,2},{1,3},{2,0},{3,1},{4,6},{5,7},{6,4},{7,5},{8,10},{9,11},{10,... | collective-permute-start | bytes 3145736 | tf_op jit(solution)/shard_map/ppermute | solution.py:105
  354.4 38.2 %collective-permute-start.30 = (bf16[512,1024]{1,0:T(8,128)(2,1)}, bf16[512,1024]{1,0:T(8,128)(2,1)}, u32[]{:S(2)}, u32[]{:S(2)}) collective-permute-start(bf16[512,1024]{1,0:T(8,128)(2,1)} %get-tuple-element.247.refs_9_), channel_id=1, source_target_pairs={{0,4},{4,0},{8,12},{12,8},{16,20},{20,16},{24,28},{28,24},{1,5},{5... | collective-permute-start | bytes 3145736 | tf_op jit(solution)/shard_map/ppermute | solution.py:105
  387.0 56.5 %collective-permute-start.35 = (bf16[4096,256]{1,0:T(8,128)(2,1)}, bf16[4096,256]{1,0:T(8,128)(2,1)}, u32[]{:S(2)}, u32[]{:S(2)}) collective-permute-start(bf16[4096,256]{1,0:T(8,128)(2,1)} %bitcast.134), channel_id=1, source_target_pairs={{0,1},{1,0},{2,3},{3,2},{4,5},{5,4},{6,7},{7,6},{8,9},{9,8},{10,11... | collective-permute-start | bytes 6291464 | tf_op jit(solution)/shard_map/ppermute | solution.py:105
  392.1 43.5 %collective-permute-start.29 = (bf16[512,1024]{1,0:T(8,128)(2,1)}, bf16[512,1024]{1,0:T(8,128)(2,1)}, u32[]{:S(2)}, u32[]{:S(2)}) collective-permute-start(bf16[512,1024]{1,0:T(8,128)(2,1)} %get-tuple-element.244.refs_13_), channel_id=1, source_target_pairs={{0,4},{4,0},{8,12},{12,8},{16,20},{20,16},{24,28},{28,24},{1,5},{5... | collective-permute-start | bytes 3145736 | tf_op jit(solution)/shard_map/ppermute | solution.py:105
  396.1 35.9 %collective-permute-start.33 = (bf16[128,1024]{1,0:T(8,128)(2,1)}, bf16[128,1024]{1,0:T(8,128)(2,1)S(1)}, u32[]{:S(2)}, u32[]{:S(2)}) collective-permute-start(bf16[128,1024]{1,0:T(8,128)(2,1)} %get-tuple-element.260.refs_12_), channel_id=1, source_target_pairs={{0,24},{4,28},{8,16},{12,20},{16,8},{20,12},{24,0},{28,4},{1,25},{... | collective-permute-start | bytes 786440 | tf_op jit(solution)/shard_map/ppermute | solution.py:105
  399.7 32.3 %collective-permute-start.32 = (bf16[128,1024]{1,0:T(8,128)(2,1)}, bf16[128,1024]{1,0:T(8,128)(2,1)S(1)}, u32[]{:S(2)}, u32[]{:S(2)}) collective-permute-start(bf16[128,1024]{1,0:T(8,128)(2,1)} %get-tuple-element.258.refs_11_), channel_id=1, source_target_pairs={{0,16},{4,20},{8,24},{12,28},{16,0},{20,4},{24,8},{28,12},{1,17},{... | collective-permute-start | bytes 786440 | tf_op jit(solution)/shard_map/ppermute | solution.py:105
  399.7 32.3 %collective-permute-start.31 = (bf16[128,1024]{1,0:T(8,128)(2,1)}, bf16[128,1024]{1,0:T(8,128)(2,1)S(1)}, u32[]{:S(2)}, u32[]{:S(2)}) collective-permute-start(bf16[128,1024]{1,0:T(8,128)(2,1)} %get-tuple-element.256.refs_10_), channel_id=1, source_target_pairs={{0,8},{4,12},{8,0},{12,4},{16,24},{20,28},{24,16},{28,20},{1,9},{5... | collective-permute-start | bytes 786440 | tf_op jit(solution)/shard_map/ppermute | solution.py:105
  439.1 40.4 %collective-permute-start.37 = (bf16[128,1024]{1,0:T(8,128)(2,1)}, bf16[128,1024]{1,0:T(8,128)(2,1)S(1)}, u32[]{:S(2)}, u32[]{:S(2)}) collective-permute-start(bf16[128,1024]{1,0:T(8,128)(2,1)} %get-tuple-element.275.refs_12_), channel_id=1, source_target_pairs={{0,24},{4,28},{8,16},{12,20},{16,8},{20,12},{24,0},{28,4},{1,25},{... | collective-permute-start | bytes 786440 | tf_op jit(solution)/shard_map/ppermute | solution.py:105
  442.7 36.8 %collective-permute-start.36 = (bf16[128,1024]{1,0:T(8,128)(2,1)}, bf16[128,1024]{1,0:T(8,128)(2,1)S(1)}, u32[]{:S(2)}, u32[]{:S(2)}) collective-permute-start(bf16[128,1024]{1,0:T(8,128)(2,1)} %get-tuple-element.273.refs_11_), channel_id=1, source_target_pairs={{0,16},{4,20},{8,24},{12,28},{16,0},{20,4},{24,8},{28,12},{1,17},{... | collective-permute-start | bytes 786440 | tf_op jit(solution)/shard_map/ppermute | solution.py:105
  442.7 36.8 %collective-permute-start.34 = (bf16[128,1024]{1,0:T(8,128)(2,1)}, bf16[128,1024]{1,0:T(8,128)(2,1)S(1)}, u32[]{:S(2)}, u32[]{:S(2)}) collective-permute-start(bf16[128,1024]{1,0:T(8,128)(2,1)} %get-tuple-element.264.refs_10_), channel_id=1, source_target_pairs={{0,8},{4,12},{8,0},{12,4},{16,24},{20,28},{24,16},{28,20},{1,9},{5... | collective-permute-start | bytes 786440 | tf_op jit(solution)/shard_map/ppermute | solution.py:105
  447.8 46.5 %collective-permute-start.38 = (bf16[4096,256]{1,0:T(8,128)(2,1)}, bf16[4096,256]{1,0:T(8,128)(2,1)}, u32[]{:S(2)}, u32[]{:S(2)}) collective-permute-start(bf16[4096,256]{1,0:T(8,128)(2,1)} %add.259.refs_14_), channel_id=1, source_target_pairs={{0,2},{1,3},{2,0},{3,1},{4,6},{5,7},{6,4},{7,5},{8,10},{9,11},{10,... | collective-permute-start | bytes 6291464 | tf_op jit(solution)/shard_map/ppermute | solution.py:105
  479.4 51.9 %collective-permute-start.42 = (bf16[4096,256]{1,0:T(8,128)(2,1)}, bf16[4096,256]{1,0:T(8,128)(2,1)}, u32[]{:S(2)}, u32[]{:S(2)}) collective-permute-start(bf16[4096,256]{1,0:T(8,128)(2,1)} %bitcast.135), channel_id=1, source_target_pairs={{0,1},{1,0},{2,3},{3,2},{4,5},{5,4},{6,7},{7,6},{8,9},{9,8},{10,11... | collective-permute-start | bytes 6291464 | tf_op jit(solution)/shard_map/ppermute | solution.py:105
  483.0 42.6 %collective-permute-start.41 = (bf16[128,1024]{1,0:T(8,128)(2,1)}, bf16[128,1024]{1,0:T(8,128)(2,1)S(1)}, u32[]{:S(2)}, u32[]{:S(2)}) collective-permute-start(bf16[128,1024]{1,0:T(8,128)(2,1)} %add.260.refs_7_.refs_0_), channel_id=1, source_target_pairs={{0,24},{4,28},{8,16},{12,20},{16,8},{20,12},{24,0},{28,4},{1,25},{... | collective-permute-start | bytes 786440 | tf_op jit(solution)/shard_map/ppermute | solution.py:105
  486.8 38.8 %collective-permute-start.40 = (bf16[128,1024]{1,0:T(8,128)(2,1)}, bf16[128,1024]{1,0:T(8,128)(2,1)S(1)}, u32[]{:S(2)}, u32[]{:S(2)}) collective-permute-start(bf16[128,1024]{1,0:T(8,128)(2,1)} %add.260.refs_7_.refs_0_), channel_id=1, source_target_pairs={{0,16},{4,20},{8,24},{12,28},{16,0},{20,4},{24,8},{28,12},{1,17},{... | collective-permute-start | bytes 786440 | tf_op jit(solution)/shard_map/ppermute | solution.py:105
  486.8 38.8 %collective-permute-start.39 = (bf16[128,1024]{1,0:T(8,128)(2,1)}, bf16[128,1024]{1,0:T(8,128)(2,1)S(1)}, u32[]{:S(2)}, u32[]{:S(2)}) collective-permute-start(bf16[128,1024]{1,0:T(8,128)(2,1)} %add.260.refs_7_.refs_0_), channel_id=1, source_target_pairs={{0,8},{4,12},{8,0},{12,4},{16,24},{20,28},{24,16},{28,20},{1,9},{5... | collective-permute-start | bytes 786440 | tf_op jit(solution)/shard_map/ppermute | solution.py:105
  529.8 39.6 %collective-permute-start.44 = (bf16[512,1024]{1,0:T(8,128)(2,1)}, bf16[512,1024]{1,0:T(8,128)(2,1)}, u32[]{:S(2)}, u32[]{:S(2)}) collective-permute-start(bf16[512,1024]{1,0:T(8,128)(2,1)} %assemble.4.refs_12_.refs_0_), channel_id=1, source_target_pairs={{0,4},{4,0},{8,12},{12,8},{16,20},{20,16},{24,28},{28,24},{1,5},{5... | collective-permute-start | bytes 3145736 | tf_op jit(solution)/shard_map/ppermute | solution.py:105
  536.6 38.7 %collective-permute-start.43 = (bf16[2048,256]{1,0:T(8,128)(2,1)}, bf16[2048,256]{1,0:T(8,128)(2,1)}, u32[]{:S(2)}, u32[]{:S(2)}) collective-permute-start(bf16[2048,256]{1,0:T(8,128)(2,1)} %get-tuple-element.294.refs_14_), channel_id=1, source_target_pairs={{0,4},{4,0},{8,12},{12,8},{16,20},{20,16},{24,28},{28,24},{1,5},{5... | collective-permute-start | bytes 3145736 | tf_op jit(solution)/shard_map/ppermute | solution.py:105
  542.7 40.6 %copy-start.22 = (f32[8,4,1024]{2,1,0:T(4,128)S(1)}, f32[8,4,1024]{2,1,0:T(4,128)}, u32[]{:S(2)}) copy-start(f32[8,4,1024]{2,1,0:T(4,128)} %get-tuple-element.313) | copy-start | bytes 393220
  569.4 14.9 %copy-start.27 = (s32[2,4]{1,0:T(2,128)S(1)}, s32[2,4]{1,0:T(2,128)}, u32[]{:S(2)}) copy-start(s32[2,4]{1,0:T(2,128)} %copy-done.26) | copy-start | bytes 100
  578.9 11.4 %collective-permute-start.47 = (bf16[512,256]{1,0:T(8,128)(2,1)}, bf16[512,256]{1,0:T(8,128)(2,1)S(1)}, u32[]{:S(2)}, u32[]{:S(2)}) collective-permute-start(bf16[512,256]{1,0:T(8,128)(2,1)} %get-tuple-element.304), channel_id=1, source_target_pairs={{0,24},{4,28},{8,16},{12,20},{16,8},{20,12},{24,0},{28,4},{1,25},{... | collective-permute-start | bytes 786440 | tf_op jit(solution)/shard_map/ppermute | solution.py:105
  582.3 19.8 %collective-permute-start.46 = (bf16[512,256]{1,0:T(8,128)(2,1)}, bf16[512,256]{1,0:T(8,128)(2,1)S(1)}, u32[]{:S(2)}, u32[]{:S(2)}) collective-permute-start(bf16[512,256]{1,0:T(8,128)(2,1)} %get-tuple-element.302), channel_id=1, source_target_pairs={{0,16},{4,20},{8,24},{12,28},{16,0},{20,4},{24,8},{28,12},{1,17},{... | collective-permute-start | bytes 786440 | tf_op jit(solution)/shard_map/ppermute | solution.py:105
  582.3 19.8 %collective-permute-start.45 = (bf16[512,256]{1,0:T(8,128)(2,1)}, bf16[512,256]{1,0:T(8,128)(2,1)}, u32[]{:S(2)}, u32[]{:S(2)}) collective-permute-start(bf16[512,256]{1,0:T(8,128)(2,1)} %get-tuple-element.300), channel_id=1, source_target_pairs={{0,8},{4,12},{8,0},{12,4},{16,24},{20,28},{24,16},{28,20},{1,9},{5... | collective-permute-start | bytes 786440 | tf_op jit(solution)/shard_map/ppermute | solution.py:105
  585.0 21.1 %copy-start.23 = (s32[4096]{0:T(1024)S(1)}, s32[4096]{0:T(1024)}, u32[]{:S(2)}) copy-start(s32[4096]{0:T(1024)} %add.170) | copy-start | bytes 49156
  590.3 11.8 %copy-start.13 = (bf16[512,256]{1,0:T(8,128)(2,1)}, bf16[512,256]{1,0:T(8,128)(2,1)S(1)}, u32[]{:S(2)}) copy-start(bf16[512,256]{1,0:T(8,128)(2,1)S(1)} %collective-permute-done.47.refs_3_) | copy-start | bytes 786436
  606.0 7.7 %collective-permute-start.48 = (bf16[512,256]{1,0:T(8,128)(2,1)}, bf16[512,256]{1,0:T(8,128)(2,1)S(1)}, u32[]{:S(2)}, u32[]{:S(2)}) collective-permute-start(bf16[512,256]{1,0:T(8,128)(2,1)} %add.261.refs_0_), channel_id=1, source_target_pairs={{0,8},{4,12},{8,0},{12,4},{16,24},{20,28},{24,16},{28,20},{1,9},{5... | collective-permute-start | bytes 786440 | tf_op jit(solution)/shard_map/ppermute | solution.py:105
  613.8 27.0 %copy-start.3 = (bf16[512,256]{1,0:T(8,128)(2,1)}, bf16[512,256]{1,0:T(8,128)(2,1)S(1)}, u32[]{:S(2)}) copy-start(bf16[512,256]{1,0:T(8,128)(2,1)S(1)} %collective-permute-done.48.refs_1_) | copy-start | bytes 786436
  613.8 1.6 collective-permute-start.52
  615.6 8.4 %collective-permute-start.53 = (bf16[128,1024]{1,0:T(8,128)(2,1)S(1)}, bf16[128,1024]{1,0:T(8,128)(2,1)S(1)}, u32[]{:S(2)}, u32[]{:S(2)}) collective-permute-start(bf16[128,1024]{1,0:T(8,128)(2,1)S(1)} %pad_maximum_fusion.3), channel_id=1, source_target_pairs={{0,2},{1,3},{2,0},{3,1},{4,6},{5,7},{6,4},{7,5},{8,10},{9,11},{10,... | collective-permute-start | bytes 786440 | tf_op jit(solution)/shard_map/ppermute | solution.py:105
  615.8 11.1 %collective-permute-start.50 = (bf16[512,256]{1,0:T(8,128)(2,1)S(1)}, bf16[512,256]{1,0:T(8,128)(2,1)S(1)}, u32[]{:S(2)}, u32[]{:S(2)}) collective-permute-start(bf16[512,256]{1,0:T(8,128)(2,1)S(1)} %copy-done.4), channel_id=1, source_target_pairs={{0,24},{4,28},{8,16},{12,20},{16,8},{20,12},{24,0},{28,4},{1,25},{... | collective-permute-start | bytes 786440 | tf_op jit(solution)/shard_map/ppermute | solution.py:105
  617.4 23.4 %collective-permute-start.49 = (bf16[512,256]{1,0:T(8,128)(2,1)S(1)}, bf16[512,256]{1,0:T(8,128)(2,1)}, u32[]{:S(2)}, u32[]{:S(2)}) collective-permute-start(bf16[512,256]{1,0:T(8,128)(2,1)S(1)} %copy-done.4), channel_id=1, source_target_pairs={{0,16},{4,20},{8,24},{12,28},{16,0},{20,4},{24,8},{28,12},{1,17},{... | collective-permute-start | bytes 786440 | tf_op jit(solution)/shard_map/ppermute | solution.py:105
  624.1 21.2 %collective-permute-start.54 = (bf16[128,1024]{1,0:T(8,128)(2,1)S(1)}, bf16[128,1024]{1,0:T(8,128)(2,1)}, u32[]{:S(2)}, u32[]{:S(2)}) collective-permute-start(bf16[128,1024]{1,0:T(8,128)(2,1)S(1)} %pad_maximum_fusion.4), channel_id=1, source_target_pairs={{0,4},{4,0},{8,12},{12,8},{16,20},{20,16},{24,28},{28,24},{1,5},{5... | collective-permute-start | bytes 786440 | tf_op jit(solution)/shard_map/ppermute | solution.py:105
  643.5 24.6 %collective-permute-start.51 = (bf16[2048,256]{1,0:T(8,128)(2,1)}, bf16[2048,256]{1,0:T(8,128)(2,1)}, u32[]{:S(2)}, u32[]{:S(2)}) collective-permute-start(bf16[2048,256]{1,0:T(8,128)(2,1)} %assemble.5.refs_0_), channel_id=1, source_target_pairs={{0,4},{4,0},{8,12},{12,8},{16,20},{20,16},{24,28},{28,24},{1,5},{5... | collective-permute-start | bytes 3145736 | tf_op jit(solution)/shard_map/ppermute | solution.py:105
  647.9 10.0 %collective-permute-start.55 = (bf16[128,1024]{1,0:T(8,128)(2,1)}, bf16[128,1024]{1,0:T(8,128)(2,1)S(1)}, u32[]{:S(2)}, u32[]{:S(2)}) collective-permute-start(bf16[128,1024]{1,0:T(8,128)(2,1)} %pad_maximum_fusion.5), channel_id=1, source_target_pairs={{0,8},{4,12},{8,0},{12,4},{16,24},{20,28},{24,16},{28,20},{1,9},{5... | collective-permute-start | bytes 786440 | tf_op jit(solution)/shard_map/ppermute | solution.py:105
  661.3 20.4 %collective-permute-start.56 = (bf16[128,1024]{1,0:T(8,128)(2,1)}, bf16[128,1024]{1,0:T(8,128)(2,1)}, u32[]{:S(2)}, u32[]{:S(2)}) collective-permute-start(bf16[128,1024]{1,0:T(8,128)(2,1)} %pad_maximum_fusion.6), channel_id=1, source_target_pairs={{0,16},{4,20},{8,24},{12,28},{16,0},{20,4},{24,8},{28,12},{1,17},{... | collective-permute-start | bytes 786440 | tf_op jit(solution)/shard_map/ppermute | solution.py:105
  (24 other events, 102.2 us)
Sparse Core Ops, SparseCore 0:
  435.7 74.2 all-gather.2

commit v5 on v4

--- a/solution.py
+++ b/solution.py
@@ -235,6 +235,45 @@
         cost_estimate=cost(0.001),
         name="assemble",
     )(jnp.reshape(index, (1,)).astype(jnp.int32), *pieces)
+
+
+def attention_grads_kernel(index_ref, own_ref, other_ref, qkv_ref, out_ref):
+    step = pl.program_id(0)
+    place = 2 * (index_ref[0] ^ (step // 2)) + step % 2
+    size = qkv_ref.shape[0]
+    rows = pl.ds(pl.multiple_of(step % 2 * size, size), size)
+    for k, ref in enumerate((own_ref, other_ref)):
+
+        @pl.when((step // 2 == k) & (place < 3))
+        def _():
+            qkv_ref[...] = ref[rows, :].astype(F32)
+
+        @pl.when((step // 2 == k) & (place == 3))
+        def _():
+            out_ref[...] = ref[rows, :].astype(F32).T
+
+
+def attention_grads_call(halves, index, dtype, groups):
+    rows, cols = halves[0].shape
+    size = rows // 2
+    place = lambda i, f: (jnp.minimum(2 * (f[0] ^ (i // 2)) + i % 2, 2), 0)
+    spec = pltpu.PrefetchScalarGridSpec(
+        num_scalar_prefetch=1,
+        grid=(4,),
+        in_specs=[pl.BlockSpec((rows, cols), lambda i, f: (0, 0))] * 2,
+        out_specs=[
+            pl.BlockSpec((size, cols), place),
+            pl.BlockSpec((cols, size), lambda i, f: (0, 0)),
+        ],
+    )
+    return pl.pallas_call(
+        attention_grads_kernel,
+        grid_spec=spec,
+        out_shape=[shaped((3 * size, cols), dtype), shaped((cols, size), dtype)],
+        compiler_params=params(),
+        cost_estimate=cost(0.001),
+        name="attention_grads",
+    )(jnp.reshape(index, (1,)).astype(jnp.int32), *halves)
 
 
 def unfold_kernel(part_ref, out_ref):
@@ -378,12 +417,13 @@
         yield [whole]
         return
     others = [steps.swap(total, "dp", n_dp, 2 * k) for k in range(1, count)]
-    yield others[:1] if steps.token is None else [total]
+    yield [total]
     half = assemble_call([total] + [steps.arrive(part) for part in others], index // 2, BF)
     other = steps.swap(half, "dp", n_dp, 1)
     yield [half]
     other = steps.arrive(other)
-    out[name] = assemble_call([half, other], index % 2, F32, len(places))
+    finish = attention_grads_call if name == "attention" else assemble_call
+    out[name] = finish([half, other], index % 2, F32, len(places))
     yield [other]
 
 
@@ -531,9 +571,9 @@
     )(attn_in, weight, blocks)
 
 
-def attend_back_kernel(
-    grad_ref, out_w_ref, qkv_ref, mixed_ref, lse_ref, blocks_ref, x_ref, dqkv_ref, dblocks_ref, dw_ref, table, total, x_all, grad_all, d_all
-):
+def attend_back_kernel(*refs, held):
+    grad_ref, out_w_ref, qkv_ref, mixed_ref, lse_ref, blocks_ref, x_ref = refs[:7]
+    dqkv_ref, dblocks_ref, dw_ref, table, total, x_all, grad_all, d_all = refs[7 + held :]
     heads = blocks_ref.shape[0]
     cols = out_w_ref.shape[0]
     step = pl.program_id(0)
@@ -608,14 +648,15 @@
                 dblocks_ref[head, offset] = block
 
 
-def attend_back_call(grad_attn, out_weight, qkv, mixed, lse, blocks, attn_in, deps=()):
+def attend_back_call(grad_attn, out_weight, qkv, mixed, lse, blocks, attn_in, block_grads, deps=()):
     rows, width = grad_attn.shape
     cols = out_weight.shape[0]
     blocks, place, heads = blocks
     per = per_step(rows)
     block = per * WIN_TOK
+    held = () if block_grads is None else (block_grads,)
     return call_after(
-        attend_back_kernel,
+        functools.partial(attend_back_kernel, held=len(held)),
         deps,
         grid=(rows // block,),
         in_specs=[
@@ -626,24 +667,26 @@
             mod_spec(per, lse.shape[1], PAD_TOK),
             block_spec(heads, place),
             row_spec(block, width),
-        ],
+        ]
+        + [pl.BlockSpec(memory_space=pl.ANY)] * len(held),
         out_specs=[
             part_spec(block, cols),
-            block_spec(heads, 0),
+            block_spec(heads, place),
             whole_spec((4, width, cols)),
         ],
         out_shape=[
             shaped((3, rows, cols), BF),
-            shaped((heads,) + blocks.shape[1:], F32),
+            shaped(blocks.shape, F32),
             shaped((4, width, cols), BF),
         ],
         scratch_shapes=[pltpu.VMEM((heads, WIN_TOK, PAD_TOK), F32)] * 2
         + [pltpu.VMEM((rows, width), BF)] * 2
         + [pltpu.VMEM((4, rows, cols), BF)],
+        input_output_aliases={7: 1} if held else {},
         compiler_params=params(),
         cost_estimate=cost(30),
         name="attend_back",
-    )(grad_attn, out_weight, qkv, mixed, lse, blocks, attn_in)
+    )(grad_attn, out_weight, qkv, mixed, lse, blocks, attn_in, *held)
 
 
 def middle_kernel(*refs, count):
@@ -955,12 +998,12 @@
         return jnp.einsum("mwc,mwe->mce", clip_hot, grouped, precision=highest).astype(BF)
 
     attn_sums = Sums(steps, n_mp, [0])
-    steps.jobs.append(spread_job(steps, attn_sums, [0], n_dp, False, grads, "qkv"))
-    dqkv, block_grads = {}, {}
+    steps.jobs.append(spread_job(steps, attn_sums, [0], n_dp, False, grads, "attention"))
+    dqkv, block_grads = {}, None
     ties = steps.step(grad_attn)
     for m in reversed(masks):
-        dqkv[m], block_grads[m], qkv_term = attend_back_call(
-            grad_attn, out_w[m], qkv[m], mixed[m], lse[m], (blocks, m, heads), attn_in, ties
+        dqkv[m], block_grads, qkv_term = attend_back_call(
+            grad_attn, out_w[m], qkv[m], mixed[m], lse[m], (blocks, m, heads), attn_in, block_grads, ties
         )
         attn_sums.add(m, [qkv_term.reshape(-1, qkv_term.shape[2])])
         ties = steps.step(qkv_term)
@@ -969,11 +1012,12 @@
     )
     ties = steps.step(token_grad)
     window_sums = after(jnp.concatenate([early_sums, late_sums], axis=1), *ties)
-    rel_sums = after(jnp.concatenate([block_grads[m] for m in masks], axis=0), *ties)
+    rel_sums = after(block_grads, *ties)
     rel_sums = collect_blocks(rel_sums).astype(BF).reshape(n_mp, -1)
     table_size = rel_sums.shape[1]
     rel_sums = jnp.pad(rel_sums, ((0, 0), (0, -table_size % width))).reshape(n_mp, -1, width)
     clip_terms = clip_sums(window_sums).reshape(-1, width)
+    summed = steps.step()
     ties = steps.step()
     mod_total, rel_total = sum_everywhere(
         after(clip_terms, *ties), after(rel_sums, *ties), n_mp, n_dp
@@ -981,10 +1025,10 @@
     rel_grad = rel_total.reshape(-1)[:table_size].reshape(rel_bias.shape).astype(F32)
     steps.finish()
 
-    down_grad = unfold_call(grads["down"], 2, ties)
+    down_grad = unfold_call(grads["down"], 2, summed)
     up_grad = grads["up"]
-    qkv_grad = grads["qkv"][: 3 * width].reshape(qkv_weight.shape)
-    out_grad = grads["qkv"][3 * width :].T
+    qkv_grad, out_grad = grads["attention"]
+    qkv_grad = qkv_grad.reshape(qkv_weight.shape)
     mod_total = mod_total.astype(F32).reshape(micro, clips, 6 * width)
     ada_bias_grad = jnp.sum(mod_total, axis=(0, 1))
     ada_weight_grad = jnp.einsum(

time: 707 us -> 704 us (level)
  waiting for transfers between devices: 62 us -> 75.8 us
  other arithmetic: 16.2 us -> 5.57 us
  local copies, waits for them, and re-layouts: 29.8 us -> 20.1 us
    ppermute x57, waiting for transfers between devices: 62 us -> 75.7 us  [swap(): return lax.ppermute(value, axis, [(i, i ^ bit) for i in range(size)])]
  transfers between devices with their start and end apart: 58 -> 58, of which waited for: 12 -> 13; matrix products, arithmetic and copies ran while one was open for 7% -> 4% of each run, Pallas kernels for 71% -> 71%
where the time goes in v5:
time: 704 us; the launch traced here: 697 us
  Pallas kernels  513 us (73%)
  waiting for transfers between devices  75.8 us (11%)
  starting transfers between devices  46.8 us (7%)
  matrix products  20.8 us (3%)
  local copies, waits for them, and re-layouts  20.1 us (3%)
  between operations  15.2 us (2%)
    pallas_call x17, Pallas kernels, call_after(): return lambda *args: call(*args, *deps)  456 us
    ppermute x57, waiting for transfers between devices, swap(): return lax.ppermute(value, axis, [(i, i ^ bit) for i in range(size)])  75.7 us
    ppermute x57, starting transfers between devices, swap(): return lax.ppermute(value, axis, [(i, i ^ bit) for i in range(size)])  46.8 us
    pallas_call x6, Pallas kernels, split_call(): pl.pallas_call(functools.partial(split_kernel, count=count, groups=[len(g...  25.7 us
    pallas_call x5, Pallas kernels, add_groups(): pl.pallas_call(functools.partial(sum_kernel, groups=[len(group) for group...  17.4 us
  transfers between devices with their start and end apart: 58, of which 13 were waited for; matrix products, arithmetic and copies ran while one was open for 4% of the time, Pallas kernels for 71%

profile of v5, /device:TPU:0, one launch (start us, length us, event | category | flops | bytes accessed | tf_op | source)
XLA Modules:
  0.0 697.3 jit_solution(12809059503108238964)
XLA Ops:
  7.8 2.6 collective-permute-start.3
  11.1 1.7 convolution_add_fusion
  12.8 2.4 fusion.6
  17.5 3.7 fusion.1
  21.1 3.6 copy.35.refs_2_.refs_5_
  24.7 3.8 collective-permute-done.1
  30.2 8.8 %norm_in.1.refs_0_.refs_3_.refs_6_ = bf16[2560,1024]{1,0:T(8,128)(2,1)} custom-call(bf16[2560,1024]{1,0:T(8,128)(2,1)} %bitcast.127, f32[8,6,1024]{2,1,0:T(8,128)} %reshape.254.refs_1_.refs_10_.refs_19_), custom_call_target="tpu_custom_call" | custom-call | flops 8000000000 | bytes 28000000 | tf_op jit(solution)/shard_map/norm_in/pallas_call | solution.py:83
  39.5 1.7 collective-permute-start.8
  41.2 16.7 %attend.4 = (bf16[3,2560,256]{2,1,0:T(8,128)(2,1)}, bf16[2560,256]{1,0:T(8,128)(2,1)}, f32[8,8,384]{2,1,0:T(8,128)}) custom-call(bf16[2560,1024]{1,0:T(8,128)(2,1)} %norm_in.1.refs_0_.refs_3_.refs_6_, bf16[3,1024,256]{2,1,0:T(8,128)(2,1)} %refs_4_.3, f32[16,9,64,64]{3,2,1,0:T(8,128)} %copy.35.refs_2_.refs_5_, bf16[2560,1024]{1,0:T(8,128)(2,1)} %norm_in.1.refs_0_.refs_3_.refs_6_), custom_call_target="tpu_custom_call" | custom-call | flops 19000000512 | bytes 66500000 | tf_op jit(solution)/shard_map/attend/pallas_call | solution.py:83
  58.2 16.7 %attend.5 = (bf16[3,2560,256]{2,1,0:T(8,128)(2,1)}, bf16[2560,256]{1,0:T(8,128)(2,1)}, f32[8,8,384]{2,1,0:T(8,128)}) custom-call(bf16[2560,1024]{1,0:T(8,128)(2,1)} %norm_in.1.refs_0_.refs_3_.refs_6_, bf16[3,1024,256]{2,1,0:T(8,128)(2,1)} %collective-permute-done.5.refs_1_.refs_5_, f32[16,9,64,64]{3,2,1,0:T(8,128)} %copy.35.refs_2_.refs_5_, ...), custom_call_target="tpu_custom_call" | custom-call | flops 19000000512 | bytes 66500000 | tf_op jit(solution)/shard_map/attend/pallas_call | solution.py:83
  75.4 16.7 %attend.6 = (bf16[3,2560,256]{2,1,0:T(8,128)(2,1)}, bf16[2560,256]{1,0:T(8,128)(2,1)}, f32[8,8,384]{2,1,0:T(8,128)}) custom-call(bf16[2560,1024]{1,0:T(8,128)(2,1)} %norm_in.1.refs_0_.refs_3_.refs_6_, bf16[3,1024,256]{2,1,0:T(8,128)(2,1)} %collective-permute-done.6.refs_1_.refs_3_.refs_6_, f32[16,9,64,64]{3,2,1,0:T(8,128)} %copy.35.refs_2_.refs_5_, ...), custom_call_target="tpu_custom_call" | custom-call | flops 19000000512 | bytes 66500000 | tf_op jit(solution)/shard_map/attend/pallas_call | solution.py:83
  92.7 30.3 %attend.7 = (bf16[3,2560,256]{2,1,0:T(8,128)(2,1)}, bf16[2560,256]{1,0:T(8,128)(2,1)}, f32[8,8,384]{2,1,0:T(8,128)}) custom-call(bf16[2560,1024]{1,0:T(8,128)(2,1)} %norm_in.1.refs_0_.refs_3_.refs_6_, bf16[3,1024,256]{2,1,0:T(8,128)(2,1)} %collective-permute-done.7.refs_1_.refs_7_, f32[16,9,64,64]{3,2,1,0:T(8,128)} %copy.35.refs_2_.refs_5_, ...), custom_call_target="tpu_custom_call" | custom-call | flops 19000000512 | bytes 66500000 | tf_op jit(solution)/shard_map/attend/pallas_call | solution.py:83
  123.1 1.8 collective-permute-start.11
  124.9 15.6 %middle.1 = (bf16[2560,1024]{1,0:T(8,128)(2,1)}, bf16[2560,1024]{1,0:T(8,128)(2,1)}, bf16[2560,1024]{1,0:T(8,128)(2,1)}) custom-call(bf16[2560,256]{1,0:T(8,128)(2,1)} %get-tuple-element.165.refs_3_.refs_0_, bf16[2560,256]{1,0:T(8,128)(2,1)} %get-tuple-element.167.refs_4_.refs_1_.refs_3_, bf16[2560,256]{1,0:T(8,128)(2,1)} %get-tuple-element.169.refs_4_.refs_2_.refs_3_, ...), custom_call_target="tpu_custom_call" | custom-call | flops 16000000000 | bytes 56000000 | tf_op jit(solution)/shard_map/middle/pallas_call | solution.py:83
  140.6 32.4 %mlp.4 = (bf16[2560,1024]{1,0:T(8,128)(2,1)}, bf16[2560,1024]{1,0:T(8,128)(2,1)}, bf16[512,1024]{1,0:T(8,128)(2,1)}, bf16[512,1024]{1,0:T(8,128)(2,1)}, bf16[512...) custom-call(bf16[2560,1024]{1,0:T(8,128)(2,1)} %get-tuple-element.175.refs_0_.refs_5_, ...), custom_call_target="tpu_custom_call" | custom-call | flops 30000001024 | bytes 105000000 | tf_op jit(solution)/shard_map/mlp/pallas_call | solution.py:83
  175.2 2.4 collective-permute-done.15.refs_2_.refs_15_
  177.6 32.6 %mlp.5 = (bf16[2560,1024]{1,0:T(8,128)(2,1)}, bf16[2560,1024]{1,0:T(8,128)(2,1)}, bf16[512,1024]{1,0:T(8,128)(2,1)}, bf16[512,1024]{1,0:T(8,128)(2,1)}, bf16[512...) custom-call(bf16[2560,1024]{1,0:T(8,128)(2,1)} %get-tuple-element.175.refs_0_.refs_5_, ...), custom_call_target="tpu_custom_call" | custom-call | flops 30000001024 | bytes 105000000 | tf_op jit(solution)/shard_map/mlp/pallas_call | solution.py:83
  211.4 32.4 %mlp.6 = (bf16[2560,1024]{1,0:T(8,128)(2,1)}, bf16[2560,1024]{1,0:T(8,128)(2,1)}, bf16[512,1024]{1,0:T(8,128)(2,1)}, bf16[512,1024]{1,0:T(8,128)(2,1)}, bf16[512...) custom-call(bf16[2560,1024]{1,0:T(8,128)(2,1)} %get-tuple-element.175.refs_0_.refs_5_, ...), custom_call_target="tpu_custom_call" | custom-call | flops 30000001024 | bytes 105000000 | tf_op jit(solution)/shard_map/mlp/pallas_call | solution.py:83
  243.8 5.8 add.257
  250.0 32.8 %mlp.7 = (bf16[2560,1024]{1,0:T(8,128)(2,1)}, bf16[2560,1024]{1,0:T(8,128)(2,1)}, bf16[512,1024]{1,0:T(8,128)(2,1)}, bf16[512,1024]{1,0:T(8,128)(2,1)}, bf16[512...) custom-call(bf16[2560,1024]{1,0:T(8,128)(2,1)} %get-tuple-element.175.refs_0_.refs_5_, ...), custom_call_target="tpu_custom_call" | custom-call | flops 30000001024 | bytes 105000000 | tf_op jit(solution)/shard_map/mlp/pallas_call | solution.py:83
  282.9 1.8 collective-permute-start.26
  285.0 62.7 %mlp_out.1 = (bf16[2560,1024]{1,0:T(8,128)(2,1)}, bf16[2560,1024]{1,0:T(8,128)(2,1)}, bf16[2560,1024]{1,0:T(8,128)(2,1)}, f32[8,4,1024]{2,1,0:T(4,128)}) custom-call(bf16[2560,1024]{1,0:T(8,128)(2,1)} %get-tuple-element.215.refs_0_, bf16[2560,1024]{1,0:T(8,128)(2,1)} %get-tuple-element.216.refs_1_, bf16[2560,1024]{1,0:T(8,128)(2,1)} %get-tuple-element.217.refs_2_, ...), custom_call_target="tpu_custom_call" | custom-call | flops 54999998464 | bytes 192500000 | tf_op jit(solution)/shard_map/mlp_out/pallas_call | solution.py:83
  347.7 1.8 collective-permute-start.28
  349.5 4.9 split.6
  355.9 31.1 %attend_back.4 = (bf16[3,2560,256]{2,1,0:T(8,128)(2,1)}, f32[16,9,64,64]{3,2,1,0:T(8,128)}, bf16[4,1024,256]{2,1,0:T(8,128)(2,1)}) custom-call(bf16[2560,1024]{1,0:T(8,128)(2,1)} %get-tuple-element.228.refs_0_.refs_10_, bf16[256,1024]{1,0:T(8,128)(2,1)} %collective-permute-done.10.refs_7_.refs_1_, bf16[3,2560,256]{2,1,0:T(8,128)(2,1)} %get-tuple-element.235.refs_2_, ...), custom_call_target="tpu_custom_call" | custom-call | flops 30000001024 | bytes 105000000 | tf_op jit(solution)/shard_map/attend_back/pallas_call | solution.py:83
  387.1 3.6 split.7
  390.6 4.9 split.8
  395.6 3.6 collective-permute-start.32
  400.5 31.6 %attend_back.5 = (bf16[3,2560,256]{2,1,0:T(8,128)(2,1)}, f32[16,9,64,64]{3,2,1,0:T(8,128)}, bf16[4,1024,256]{2,1,0:T(8,128)(2,1)}) custom-call(bf16[2560,1024]{1,0:T(8,128)(2,1)} %get-tuple-element.228.refs_0_.refs_10_, bf16[256,1024]{1,0:T(8,128)(2,1)} %collective-permute-done.8.refs_3_.refs_6_.refs_1_, ...), custom_call_target="tpu_custom_call", output_to_operand_aliasing={{1}: (7, {})} | custom-call | flops 30000001024 | bytes 105000000 | tf_op jit(solution)/shard_map/attend_back/pallas_call | solution.py:83
  433.6 2.0 add.258.refs_2_.refs_8_
  435.7 3.5 split.9
  439.2 3.6 collective-permute-start.37
  443.6 4.3 add.259.refs_15_
  448.4 31.2 %attend_back.6 = (bf16[3,2560,256]{2,1,0:T(8,128)(2,1)}, f32[16,9,64,64]{3,2,1,0:T(8,128)}, bf16[4,1024,256]{2,1,0:T(8,128)(2,1)}) custom-call(bf16[2560,1024]{1,0:T(8,128)(2,1)} %get-tuple-element.228.refs_0_.refs_10_, bf16[256,1024]{1,0:T(8,128)(2,1)} %collective-permute-done.9.refs_5_.refs_1_, ...), custom_call_target="tpu_custom_call", output_to_operand_aliasing={{1}: (7, {})} | custom-call | flops 30000001024 | bytes 105000000 | tf_op jit(solution)/shard_map/attend_back/pallas_call | solution.py:83
  481.2 2.0 add.260.refs_8_.refs_0_
  483.2 3.7 collective-permute-start.41
  487.6 6.9 collective-permute-done.38.refs_9_.refs_0_
  494.5 31.3 %attend_back.7 = (bf16[3,2560,256]{2,1,0:T(8,128)(2,1)}, f32[16,9,64,64]{3,2,1,0:T(8,128)}, bf16[4,1024,256]{2,1,0:T(8,128)(2,1)}) custom-call(bf16[2560,1024]{1,0:T(8,128)(2,1)} %get-tuple-element.228.refs_0_.refs_10_, bf16[256,1024]{1,0:T(8,128)(2,1)} %refs_1_.3, ...), custom_call_target="tpu_custom_call", output_to_operand_aliasing={{1}: (7, {})} | custom-call | flops 30000001024 | bytes 105000000 | tf_op jit(solution)/shard_map/attend_back/pallas_call | solution.py:83
  527.3 2.7 assemble.3.refs_12_.refs_0_
  531.5 5.2 split.10
  537.3 26.8 %last.1 = (bf16[2560,1024]{1,0:T(8,128)(2,1)}, f32[8,2,1024]{2,1,0:T(2,128)}) custom-call(bf16[3,2560,256]{2,1,0:T(8,128)(2,1)} %get-tuple-element.284.refs_0_, bf16[3,2560,256]{2,1,0:T(8,128)(2,1)} %get-tuple-element.285.refs_1_, bf16[3,2560,256]{2,1,0:T(8,128)(2,1)} %get-tuple-element.286.refs_2_, bf16[3,2560,256]{2,1,0:T(8,128)(2,1)} %get-tuple-element.287.refs_3_, ...), custom_call_target="tpu_custom_call" | custom-call | flops 28000000000 | bytes 98000000 | tf_op jit(solution)/shard_map/last/pallas_call | solution.py:83
  564.1 11.6 %collective-permute-done.43.refs_1_ = bf16[2048,256]{1,0:T(8,128)(2,1)} collective-permute-done((bf16[2048,256]{1,0:T(8,128)(2,1)}, bf16[2048,256]{1,0:T(8,128)(2,1)}, u32[]{:S(2)}, u32[]{:S(2)}) %collective-permute-start.43) | collective-permute-done | bytes 1048608 | tf_op jit(solution)/shard_map/ppermute | solution.py:105
  575.7 3.5 split.11
  579.2 3.3 collective-permute-start.47
  585.3 5.3 reshape.265
  590.6 11.6 %collective-permute-done.46.refs_2_ = bf16[512,256]{1,0:T(8,128)(2,1)S(1)} collective-permute-done((bf16[512,256]{1,0:T(8,128)(2,1)}, bf16[512,256]{1,0:T(8,128)(2,1)S(1)}, u32[]{:S(2)}, u32[]{:S(2)}) %collective-permute-start.46) | collective-permute-done | bytes 262176 | tf_op jit(solution)/shard_map/ppermute | solution.py:105
  602.9 3.2 add.261.refs_0_.refs_1_
  606.1 2.4 collective-permute-start.50
  608.5 2.0 collective-permute-start.48
  610.5 4.1 fusion.3
  615.4 2.0 collective-permute-done.50.refs_3_
  617.5 11.3 %collective-permute-done.49.refs_2_ = bf16[512,256]{1,0:T(8,128)(2,1)S(1)} collective-permute-done((bf16[512,256]{1,0:T(8,128)(2,1)}, bf16[512,256]{1,0:T(8,128)(2,1)S(1)}, u32[]{:S(2)}, u32[]{:S(2)}) %collective-permute-start.49) | collective-permute-done | bytes 262176 | tf_op jit(solution)/shard_map/ppermute | solution.py:105
  629.4 2.7 assemble.4.own_ref
  634.5 7.9 %collective-permute-done.53 = bf16[128,1024]{1,0:T(8,128)(2,1)S(1)} collective-permute-done((bf16[128,1024]{1,0:T(8,128)(2,1)S(1)}, bf16[128,1024]{1,0:T(8,128)(2,1)S(1)}, u32[]{:S(2)}, u32[]{:S(2)}) %collective-permute-start.53) | collective-permute-done | bytes 262176 | tf_op jit(solution)/shard_map/ppermute | solution.py:105
  642.5 1.6 collective-permute-start.54
  644.6 7.2 %collective-permute-done.54 = bf16[128,1024]{1,0:T(8,128)(2,1)S(1)} collective-permute-done((bf16[128,1024]{1,0:T(8,128)(2,1)S(1)}, bf16[128,1024]{1,0:T(8,128)(2,1)S(1)}, u32[]{:S(2)}, u32[]{:S(2)}) %collective-permute-start.54) | collective-permute-done | bytes 262176 | tf_op jit(solution)/shard_map/ppermute | solution.py:105
  652.0 6.4 collective-permute-done.55
  660.6 4.0 assemble.5
  664.6 6.0 unfold.1
  670.6 2.0 collective-permute-done.51.other_ref
  672.6 4.7 attention_grads.1
  679.5 2.8 fusion.4
  683.0 3.7 convolution_bitcast_fusion
  688.3 1.6 convolution_bitcast_fusion.1
  (194 shorter events, 37.2 us)
Async XLA Ops:
  7.2 530.1 %all-gather.3.cloned.1.call-start = ((), (), s32[]{:S(2)}) async-start(), calls=%async_computation | async-start | bytes 2359296 | tf_op jit(solution)/shard_map/all_gather | solution.py:413
  7.2 8.7 %collective-permute-start.2 = (f32[4,2025]{1,0:T(4,128)}, f32[4,2025]{1,0:T(4,128)S(1)}, u32[]{:S(2)}, u32[]{:S(2)}) collective-permute-start(f32[4,2025]{1,0:T(4,128)} %param.19), channel_id=1, source_target_pairs={{0,1},{1,0},{2,3},{3,2},{4,5},{5,4},{6,7},{7,6},{8,9},{9,8},{10,11... | collective-permute-start | bytes 97208 | tf_op jit(solution)/shard_map/ppermute | solution.py:105
  7.8 7.7 %collective-permute-start.3 = (f32[4,2025]{1,0:T(4,128)}, f32[4,2025]{1,0:T(4,128)S(1)}, u32[]{:S(2)}, u32[]{:S(2)}) collective-permute-start(f32[4,2025]{1,0:T(4,128)} %param.19), channel_id=1, source_target_pairs={{0,2},{1,3},{2,0},{3,1},{4,6},{5,7},{6,4},{7,5},{8,10},{9,11},{10,... | collective-permute-start | bytes 97208 | tf_op jit(solution)/shard_map/ppermute | solution.py:105
  15.2 2.1 collective-permute-start
  15.5 1.5 collective-permute-start.4
  16.0 13.0 %copy-start.23 = (s32[2,4]{1,0:T(2,128)}, s32[2,4]{1,0:T(2,128)S(1)}, u32[]{:S(2)}) copy-start(s32[2,4]{1,0:T(2,128)S(1)} %constant_dynamic-slice_fusion) | copy-start | bytes 100
  17.3 11.3 %collective-permute-start.1 = (f32[2,8,6144]{2,1,0:T(8,128)S(1)}, f32[2,8,6144]{2,1,0:T(8,128)S(1)}, u32[]{:S(2)}, u32[]{:S(2)}) collective-permute-start(f32[2,8,6144]{2,1,0:T(8,128)S(1)} %add.163), channel_id=1, source_target_pairs={{0,2},{1,3},{2,0},{3,1},{4,6},{5,7},{6,4},{7,5},{8,10},{9,11},{10,... | collective-permute-start | bytes 1179656 | tf_op jit(solution)/shard_map/ppermute | solution.py:105
  28.6 46.3 %collective-permute-start.6 = (bf16[3,1024,256]{2,1,0:T(8,128)(2,1)}, bf16[3,1024,256]{2,1,0:T(8,128)(2,1)}, u32[]{:S(2)}, u32[]{:S(2)}) collective-permute-start(bf16[3,1024,256]{2,1,0:T(8,128)(2,1)} %refs_4_.3), channel_id=1, source_target_pairs={{0,2},{1,3},{2,0},{3,1},{4,6},{5,7},{6,4},{7,5},{8,10},{9,11},{10,... | collective-permute-start | bytes 4718600 | tf_op jit(solution)/shard_map/ppermute | solution.py:105
  29.0 29.2 %collective-permute-start.5 = (bf16[3,1024,256]{2,1,0:T(8,128)(2,1)}, bf16[3,1024,256]{2,1,0:T(8,128)(2,1)}, u32[]{:S(2)}, u32[]{:S(2)}) collective-permute-start(bf16[3,1024,256]{2,1,0:T(8,128)(2,1)} %refs_4_.3), channel_id=1, source_target_pairs={{0,1},{1,0},{2,3},{3,2},{4,5},{5,4},{6,7},{7,6},{8,9},{9,8},{10,11... | collective-permute-start | bytes 4718600 | tf_op jit(solution)/shard_map/ppermute | solution.py:105
  39.0 84.1 %collective-permute-start.9 = (bf16[256,1024]{1,0:T(8,128)(2,1)S(1)}, bf16[256,1024]{1,0:T(8,128)(2,1)}, u32[]{:S(2)}, u32[]{:S(2)}) collective-permute-start(bf16[256,1024]{1,0:T(8,128)(2,1)S(1)} %copy-done.26), channel_id=1, source_target_pairs={{0,1},{1,0},{2,3},{3,2},{4,5},{5,4},{6,7},{7,6},{8,9},{9,8},{10,11... | collective-permute-start | bytes 1572872 | tf_op jit(solution)/shard_map/ppermute | solution.py:105
  39.5 52.7 %collective-permute-start.8 = (bf16[256,1024]{1,0:T(8,128)(2,1)S(1)}, bf16[256,1024]{1,0:T(8,128)(2,1)}, u32[]{:S(2)}, u32[]{:S(2)}) collective-permute-start(bf16[256,1024]{1,0:T(8,128)(2,1)S(1)} %copy-done.26), channel_id=1, source_target_pairs={{0,2},{1,3},{2,0},{3,1},{4,6},{5,7},{6,4},{7,5},{8,10},{9,11},{10,... | collective-permute-start | bytes 1572872 | tf_op jit(solution)/shard_map/ppermute | solution.py:105
  57.9 82.6 %collective-permute-start.14 = (bf16[1024,1024]{1,0:T(8,128)(2,1)}, bf16[1024,1024]{1,0:T(8,128)(2,1)}, u32[]{:S(2)}, u32[]{:S(2)}) collective-permute-start(bf16[1024,1024]{1,0:T(8,128)(2,1)} %refs_8_.1), channel_id=1, source_target_pairs={{0,2},{1,3},{2,0},{3,1},{4,6},{5,7},{6,4},{7,5},{8,10},{9,11},{10,... | collective-permute-start | bytes 6291464 | tf_op jit(solution)/shard_map/ppermute | solution.py:105
  58.2 82.4 %collective-permute-start.13 = (bf16[1024,1024]{1,0:T(8,128)(2,1)}, bf16[1024,1024]{1,0:T(8,128)(2,1)}, u32[]{:S(2)}, u32[]{:S(2)}) collective-permute-start(bf16[1024,1024]{1,0:T(8,128)(2,1)} %refs_8_.1), channel_id=1, source_target_pairs={{0,1},{1,0},{2,3},{3,2},{4,5},{5,4},{6,7},{7,6},{8,9},{9,8},{10,11... | collective-permute-start | bytes 6291464 | tf_op jit(solution)/shard_map/ppermute | solution.py:105
  74.9 17.4 %collective-permute-start.7 = (bf16[3,1024,256]{2,1,0:T(8,128)(2,1)}, bf16[3,1024,256]{2,1,0:T(8,128)(2,1)}, u32[]{:S(2)}, u32[]{:S(2)}) collective-permute-start(bf16[3,1024,256]{2,1,0:T(8,128)(2,1)} %collective-permute-done.6.refs_1_.refs_3_.refs_6_), channel_id=1, source_target_pairs={{0,1},{1,0},{2,3},{3,2},{4,5},{5,4},{6,7},{7,6},{8,9},{9,8},{10,11... | collective-permute-start | bytes 4718600 | tf_op jit(solution)/shard_map/ppermute | solution.py:105
  92.2 32.7 %collective-permute-start.10 = (bf16[256,1024]{1,0:T(8,128)(2,1)}, bf16[256,1024]{1,0:T(8,128)(2,1)}, u32[]{:S(2)}, u32[]{:S(2)}) collective-permute-start(bf16[256,1024]{1,0:T(8,128)(2,1)} %collective-permute-done.8.refs_3_.refs_6_.refs_1_), channel_id=1, source_target_pairs={{0,1},{1,0},{2,3},{3,2},{4,5},{5,4},{6,7},{7,6},{8,9},{9,8},{10,11... | collective-permute-start | bytes 1572872 | tf_op jit(solution)/shard_map/ppermute | solution.py:105
  92.3 48.3 %collective-permute-start.12 = (bf16[1024,1024]{1,0:T(8,128)(2,1)}, bf16[1024,1024]{1,0:T(8,128)(2,1)}, u32[]{:S(2)}, u32[]{:S(2)}) collective-permute-start(bf16[1024,1024]{1,0:T(8,128)(2,1)} %refs_12_.1), channel_id=1, source_target_pairs={{0,1},{1,0},{2,3},{3,2},{4,5},{5,4},{6,7},{7,6},{8,9},{9,8},{10,11... | collective-permute-start | bytes 6291464 | tf_op jit(solution)/shard_map/ppermute | solution.py:105
  123.1 49.9 %collective-permute-start.11 = (bf16[1024,1024]{1,0:T(8,128)(2,1)}, bf16[1024,1024]{1,0:T(8,128)(2,1)}, u32[]{:S(2)}, u32[]{:S(2)}) collective-permute-start(bf16[1024,1024]{1,0:T(8,128)(2,1)} %refs_12_.1), channel_id=1, source_target_pairs={{0,2},{1,3},{2,0},{3,1},{4,6},{5,7},{6,4},{7,5},{8,10},{9,11},{10,... | collective-permute-start | bytes 6291464 | tf_op jit(solution)/shard_map/ppermute | solution.py:105
  140.5 34.2 %collective-permute-start.16 = (bf16[1024,1024]{1,0:T(8,128)(2,1)}, bf16[1024,1024]{1,0:T(8,128)(2,1)}, u32[]{:S(2)}, u32[]{:S(2)}) collective-permute-start(bf16[1024,1024]{1,0:T(8,128)(2,1)} %collective-permute-done.14.refs_4_.refs_3_.refs_10_), channel_id=1, source_target_pairs={{0,1},{1,0},{2,3},{3,2},{4,5},{5,4},{6,7},{7,6},{8,9},{9,8},{10,11... | collective-permute-start | bytes 6291464 | tf_op jit(solution)/shard_map/ppermute | solution.py:105
  173.0 4.7 collective-permute-start.15
  174.2 36.1 %collective-permute-start.18 = (bf16[512,1024]{1,0:T(8,128)(2,1)}, bf16[512,1024]{1,0:T(8,128)(2,1)}, u32[]{:S(2)}, u32[]{:S(2)}) collective-permute-start(bf16[512,1024]{1,0:T(8,128)(2,1)} %get-tuple-element.186.refs_5_), channel_id=1, source_target_pairs={{0,1},{1,0},{2,3},{3,2},{4,5},{5,4},{6,7},{7,6},{8,9},{9,8},{10,11... | collective-permute-start | bytes 3145736 | tf_op jit(solution)/shard_map/ppermute | solution.py:105
  174.2 36.1 %collective-permute-start.21 = (bf16[512,1024]{1,0:T(8,128)(2,1)}, bf16[512,1024]{1,0:T(8,128)(2,1)}, u32[]{:S(2)}, u32[]{:S(2)}) collective-permute-start(bf16[512,1024]{1,0:T(8,128)(2,1)} %get-tuple-element.195), channel_id=1, source_target_pairs={{0,1},{1,0},{2,3},{3,2},{4,5},{5,4},{6,7},{7,6},{8,9},{9,8},{10,11... | collective-permute-start | bytes 3145736 | tf_op jit(solution)/shard_map/ppermute | solution.py:105
  174.7 35.6 %collective-permute-start.20 = (bf16[512,1024]{1,0:T(8,128)(2,1)}, bf16[512,1024]{1,0:T(8,128)(2,1)}, u32[]{:S(2)}, u32[]{:S(2)}) collective-permute-start(bf16[512,1024]{1,0:T(8,128)(2,1)} %get-tuple-element.192), channel_id=1, source_target_pairs={{0,1},{1,0},{2,3},{3,2},{4,5},{5,4},{6,7},{7,6},{8,9},{9,8},{10,11... | collective-permute-start | bytes 3145736 | tf_op jit(solution)/shard_map/ppermute | solution.py:105
  174.7 35.6 %collective-permute-start.19 = (bf16[512,1024]{1,0:T(8,128)(2,1)}, bf16[512,1024]{1,0:T(8,128)(2,1)}, u32[]{:S(2)}, u32[]{:S(2)}) collective-permute-start(bf16[512,1024]{1,0:T(8,128)(2,1)} %get-tuple-element.189), channel_id=1, source_target_pairs={{0,1},{1,0},{2,3},{3,2},{4,5},{5,4},{6,7},{7,6},{8,9},{9,8},{10,11... | collective-permute-start | bytes 3145736 | tf_op jit(solution)/shard_map/ppermute | solution.py:105
  210.3 33.5 %collective-permute-start.17 = (bf16[512,1024]{1,0:T(8,128)(2,1)}, bf16[512,1024]{1,0:T(8,128)(2,1)}, u32[]{:S(2)}, u32[]{:S(2)}) collective-permute-start(bf16[512,1024]{1,0:T(8,128)(2,1)} %get-tuple-element.185.refs_8_), channel_id=1, source_target_pairs={{0,1},{1,0},{2,3},{3,2},{4,5},{5,4},{6,7},{7,6},{8,9},{9,8},{10,11... | collective-permute-start | bytes 3145736 | tf_op jit(solution)/shard_map/ppermute | solution.py:105
  210.7 33.1 %collective-permute-start.24 = (bf16[512,1024]{1,0:T(8,128)(2,1)}, bf16[512,1024]{1,0:T(8,128)(2,1)}, u32[]{:S(2)}, u32[]{:S(2)}) collective-permute-start(bf16[512,1024]{1,0:T(8,128)(2,1)} %get-tuple-element.206), channel_id=1, source_target_pairs={{0,1},{1,0},{2,3},{3,2},{4,5},{5,4},{6,7},{7,6},{8,9},{9,8},{10,11... | collective-permute-start | bytes 3145736 | tf_op jit(solution)/shard_map/ppermute | solution.py:105
  210.9 32.9 %collective-permute-start.23 = (bf16[512,1024]{1,0:T(8,128)(2,1)}, bf16[512,1024]{1,0:T(8,128)(2,1)}, u32[]{:S(2)}, u32[]{:S(2)}) collective-permute-start(bf16[512,1024]{1,0:T(8,128)(2,1)} %get-tuple-element.203), channel_id=1, source_target_pairs={{0,1},{1,0},{2,3},{3,2},{4,5},{5,4},{6,7},{7,6},{8,9},{9,8},{10,11... | collective-permute-start | bytes 3145736 | tf_op jit(solution)/shard_map/ppermute | solution.py:105
  211.3 32.6 %collective-permute-start.22 = (bf16[512,1024]{1,0:T(8,128)(2,1)}, bf16[512,1024]{1,0:T(8,128)(2,1)}, u32[]{:S(2)}, u32[]{:S(2)}) collective-permute-start(bf16[512,1024]{1,0:T(8,128)(2,1)} %get-tuple-element.200), channel_id=1, source_target_pairs={{0,1},{1,0},{2,3},{3,2},{4,5},{5,4},{6,7},{7,6},{8,9},{9,8},{10,11... | collective-permute-start | bytes 3145736 | tf_op jit(solution)/shard_map/ppermute | solution.py:105
  249.7 35.3 %collective-permute-start.25 = (bf16[512,1024]{1,0:T(8,128)(2,1)}, bf16[512,1024]{1,0:T(8,128)(2,1)}, u32[]{:S(2)}, u32[]{:S(2)}) collective-permute-start(bf16[512,1024]{1,0:T(8,128)(2,1)} %get-tuple-element.224.refs_8_), channel_id=1, source_target_pairs={{0,2},{1,3},{2,0},{3,1},{4,6},{5,7},{6,4},{7,5},{8,10},{9,11},{10,... | collective-permute-start | bytes 3145736 | tf_op jit(solution)/shard_map/ppermute | solution.py:105
  282.9 66.6 %collective-permute-start.26 = (bf16[512,1024]{1,0:T(8,128)(2,1)}, bf16[512,1024]{1,0:T(8,128)(2,1)}, u32[]{:S(2)}, u32[]{:S(2)}) collective-permute-start(bf16[512,1024]{1,0:T(8,128)(2,1)} %get-tuple-element.237.refs_9_), channel_id=1, source_target_pairs={{0,2},{1,3},{2,0},{3,1},{4,6},{5,7},{6,4},{7,5},{8,10},{9,11},{10,... | collective-permute-start | bytes 3145736 | tf_op jit(solution)/shard_map/ppermute | solution.py:105
  284.7 71.2 %collective-permute-start.27 = (bf16[512,1024]{1,0:T(8,128)(2,1)}, bf16[512,1024]{1,0:T(8,128)(2,1)}, u32[]{:S(2)}, u32[]{:S(2)}) collective-permute-start(bf16[512,1024]{1,0:T(8,128)(2,1)} %get-tuple-element.239.refs_10_), channel_id=1, source_target_pairs={{0,2},{1,3},{2,0},{3,1},{4,6},{5,7},{6,4},{7,5},{8,10},{9,11},{10,... | collective-permute-start | bytes 3145736 | tf_op jit(solution)/shard_map/ppermute | solution.py:105
  347.7 39.4 %collective-permute-start.28 = (bf16[512,1024]{1,0:T(8,128)(2,1)}, bf16[512,1024]{1,0:T(8,128)(2,1)}, u32[]{:S(2)}, u32[]{:S(2)}) collective-permute-start(bf16[512,1024]{1,0:T(8,128)(2,1)} %get-tuple-element.244.refs_11_), channel_id=1, source_target_pairs={{0,2},{1,3},{2,0},{3,1},{4,6},{5,7},{6,4},{7,5},{8,10},{9,11},{10,... | collective-permute-start | bytes 3145736 | tf_op jit(solution)/shard_map/ppermute | solution.py:105
  354.4 32.7 %collective-permute-start.29 = (bf16[512,1024]{1,0:T(8,128)(2,1)}, bf16[512,1024]{1,0:T(8,128)(2,1)}, u32[]{:S(2)}, u32[]{:S(2)}) collective-permute-start(bf16[512,1024]{1,0:T(8,128)(2,1)} %get-tuple-element.247.refs_9_), channel_id=1, source_target_pairs={{0,4},{4,0},{8,12},{12,8},{16,20},{20,16},{24,28},{28,24},{1,5},{5... | collective-permute-start | bytes 3145736 | tf_op jit(solution)/shard_map/ppermute | solution.py:105
  387.0 56.6 %collective-permute-start.34 = (bf16[4096,256]{1,0:T(8,128)(2,1)}, bf16[4096,256]{1,0:T(8,128)(2,1)}, u32[]{:S(2)}, u32[]{:S(2)}) collective-permute-start(bf16[4096,256]{1,0:T(8,128)(2,1)} %bitcast.132), channel_id=1, source_target_pairs={{0,1},{1,0},{2,3},{3,2},{4,5},{5,4},{6,7},{7,6},{8,9},{9,8},{10,11... | collective-permute-start | bytes 6291464 | tf_op jit(solution)/shard_map/ppermute | solution.py:105
  395.6 36.5 %collective-permute-start.32 = (bf16[128,1024]{1,0:T(8,128)(2,1)}, bf16[128,1024]{1,0:T(8,128)(2,1)S(1)}, u32[]{:S(2)}, u32[]{:S(2)}) collective-permute-start(bf16[128,1024]{1,0:T(8,128)(2,1)} %get-tuple-element.263.refs_13_), channel_id=1, source_target_pairs={{0,24},{4,28},{8,16},{12,20},{16,8},{20,12},{24,0},{28,4},{1,25},{... | collective-permute-start | bytes 786440 | tf_op jit(solution)/shard_map/ppermute | solution.py:105
  399.2 32.9 %collective-permute-start.31 = (bf16[128,1024]{1,0:T(8,128)(2,1)}, bf16[128,1024]{1,0:T(8,128)(2,1)S(1)}, u32[]{:S(2)}, u32[]{:S(2)}) collective-permute-start(bf16[128,1024]{1,0:T(8,128)(2,1)} %get-tuple-element.261.refs_12_), channel_id=1, source_target_pairs={{0,16},{4,20},{8,24},{12,28},{16,0},{20,4},{24,8},{28,12},{1,17},{... | collective-permute-start | bytes 786440 | tf_op jit(solution)/shard_map/ppermute | solution.py:105
  399.2 32.9 %collective-permute-start.30 = (bf16[128,1024]{1,0:T(8,128)(2,1)}, bf16[128,1024]{1,0:T(8,128)(2,1)S(1)}, u32[]{:S(2)}, u32[]{:S(2)}) collective-permute-start(bf16[128,1024]{1,0:T(8,128)(2,1)} %get-tuple-element.258.refs_11_), channel_id=1, source_target_pairs={{0,8},{4,12},{8,0},{12,4},{16,24},{20,28},{24,16},{28,20},{1,9},{5... | collective-permute-start | bytes 786440 | tf_op jit(solution)/shard_map/ppermute | solution.py:105
  400.0 35.7 %collective-permute-start.33 = (bf16[512,1024]{1,0:T(8,128)(2,1)}, bf16[512,1024]{1,0:T(8,128)(2,1)}, u32[]{:S(2)}, u32[]{:S(2)}) collective-permute-start(bf16[512,1024]{1,0:T(8,128)(2,1)} %get-tuple-element.265.refs_14_), channel_id=1, source_target_pairs={{0,4},{4,0},{8,12},{12,8},{16,20},{20,16},{24,28},{28,24},{1,5},{5... | collective-permute-start | bytes 3145736 | tf_op jit(solution)/shard_map/ppermute | solution.py:105
  439.2 40.5 %collective-permute-start.37 = (bf16[128,1024]{1,0:T(8,128)(2,1)}, bf16[128,1024]{1,0:T(8,128)(2,1)S(1)}, u32[]{:S(2)}, u32[]{:S(2)}) collective-permute-start(bf16[128,1024]{1,0:T(8,128)(2,1)} %get-tuple-element.280.refs_13_), channel_id=1, source_target_pairs={{0,24},{4,28},{8,16},{12,20},{16,8},{20,12},{24,0},{28,4},{1,25},{... | collective-permute-start | bytes 786440 | tf_op jit(solution)/shard_map/ppermute | solution.py:105
  442.8 36.9 %collective-permute-start.36 = (bf16[128,1024]{1,0:T(8,128)(2,1)}, bf16[128,1024]{1,0:T(8,128)(2,1)S(1)}, u32[]{:S(2)}, u32[]{:S(2)}) collective-permute-start(bf16[128,1024]{1,0:T(8,128)(2,1)} %get-tuple-element.278.refs_12_), channel_id=1, source_target_pairs={{0,16},{4,20},{8,24},{12,28},{16,0},{20,4},{24,8},{28,12},{1,17},{... | collective-permute-start | bytes 786440 | tf_op jit(solution)/shard_map/ppermute | solution.py:105
  442.8 36.9 %collective-permute-start.35 = (bf16[128,1024]{1,0:T(8,128)(2,1)}, bf16[128,1024]{1,0:T(8,128)(2,1)S(1)}, u32[]{:S(2)}, u32[]{:S(2)}) collective-permute-start(bf16[128,1024]{1,0:T(8,128)(2,1)} %get-tuple-element.275.refs_11_), channel_id=1, source_target_pairs={{0,8},{4,12},{8,0},{12,4},{16,24},{20,28},{24,16},{28,20},{1,9},{5... | collective-permute-start | bytes 786440 | tf_op jit(solution)/shard_map/ppermute | solution.py:105
  447.9 46.5 %collective-permute-start.38 = (bf16[4096,256]{1,0:T(8,128)(2,1)}, bf16[4096,256]{1,0:T(8,128)(2,1)}, u32[]{:S(2)}, u32[]{:S(2)}) collective-permute-start(bf16[4096,256]{1,0:T(8,128)(2,1)} %add.259.refs_15_), channel_id=1, source_target_pairs={{0,2},{1,3},{2,0},{3,1},{4,6},{5,7},{6,4},{7,5},{8,10},{9,11},{10,... | collective-permute-start | bytes 6291464 | tf_op jit(solution)/shard_map/ppermute | solution.py:105
  479.6 51.9 %collective-permute-start.42 = (bf16[4096,256]{1,0:T(8,128)(2,1)}, bf16[4096,256]{1,0:T(8,128)(2,1)}, u32[]{:S(2)}, u32[]{:S(2)}) collective-permute-start(bf16[4096,256]{1,0:T(8,128)(2,1)} %bitcast.133), channel_id=1, source_target_pairs={{0,1},{1,0},{2,3},{3,2},{4,5},{5,4},{6,7},{7,6},{8,9},{9,8},{10,11... | collective-permute-start | bytes 6291464 | tf_op jit(solution)/shard_map/ppermute | solution.py:105
  483.2 42.6 %collective-permute-start.41 = (bf16[128,1024]{1,0:T(8,128)(2,1)}, bf16[128,1024]{1,0:T(8,128)(2,1)S(1)}, u32[]{:S(2)}, u32[]{:S(2)}) collective-permute-start(bf16[128,1024]{1,0:T(8,128)(2,1)} %add.260.refs_8_.refs_0_), channel_id=1, source_target_pairs={{0,24},{4,28},{8,16},{12,20},{16,8},{20,12},{24,0},{28,4},{1,25},{... | collective-permute-start | bytes 786440 | tf_op jit(solution)/shard_map/ppermute | solution.py:105
  486.9 38.9 %collective-permute-start.40 = (bf16[128,1024]{1,0:T(8,128)(2,1)}, bf16[128,1024]{1,0:T(8,128)(2,1)S(1)}, u32[]{:S(2)}, u32[]{:S(2)}) collective-permute-start(bf16[128,1024]{1,0:T(8,128)(2,1)} %add.260.refs_8_.refs_0_), channel_id=1, source_target_pairs={{0,16},{4,20},{8,24},{12,28},{16,0},{20,4},{24,8},{28,12},{1,17},{... | collective-permute-start | bytes 786440 | tf_op jit(solution)/shard_map/ppermute | solution.py:105
  486.9 38.9 %collective-permute-start.39 = (bf16[128,1024]{1,0:T(8,128)(2,1)}, bf16[128,1024]{1,0:T(8,128)(2,1)S(1)}, u32[]{:S(2)}, u32[]{:S(2)}) collective-permute-start(bf16[128,1024]{1,0:T(8,128)(2,1)} %add.260.refs_8_.refs_0_), channel_id=1, source_target_pairs={{0,8},{4,12},{8,0},{12,4},{16,24},{20,28},{24,16},{28,20},{1,9},{5... | collective-permute-start | bytes 786440 | tf_op jit(solution)/shard_map/ppermute | solution.py:105
  530.0 34.0 %collective-permute-start.44 = (bf16[512,1024]{1,0:T(8,128)(2,1)}, bf16[512,1024]{1,0:T(8,128)(2,1)}, u32[]{:S(2)}, u32[]{:S(2)}) collective-permute-start(bf16[512,1024]{1,0:T(8,128)(2,1)} %assemble.3.refs_12_.refs_0_), channel_id=1, source_target_pairs={{0,4},{4,0},{8,12},{12,8},{16,20},{20,16},{24,28},{28,24},{1,5},{5... | collective-permute-start | bytes 3145736 | tf_op jit(solution)/shard_map/ppermute | solution.py:105
  536.7 39.0 %collective-permute-start.43 = (bf16[2048,256]{1,0:T(8,128)(2,1)}, bf16[2048,256]{1,0:T(8,128)(2,1)}, u32[]{:S(2)}, u32[]{:S(2)}) collective-permute-start(bf16[2048,256]{1,0:T(8,128)(2,1)} %get-tuple-element.299.refs_14_), channel_id=1, source_target_pairs={{0,4},{4,0},{8,12},{12,8},{16,20},{20,16},{24,28},{28,24},{1,5},{5... | collective-permute-start | bytes 3145736 | tf_op jit(solution)/shard_map/ppermute | solution.py:105
  537.3 46.3 %copy-start.19 = (f32[8,4,1024]{2,1,0:T(4,128)S(1)}, f32[8,4,1024]{2,1,0:T(4,128)}, u32[]{:S(2)}) copy-start(f32[8,4,1024]{2,1,0:T(4,128)} %get-tuple-element.317) | copy-start | bytes 393220
  564.1 20.5 %copy-start.24 = (s32[2,4]{1,0:T(2,128)S(1)}, s32[2,4]{1,0:T(2,128)}, u32[]{:S(2)}) copy-start(s32[2,4]{1,0:T(2,128)} %copy-done.23) | copy-start | bytes 100
  579.2 11.4 %collective-permute-start.47 = (bf16[512,256]{1,0:T(8,128)(2,1)}, bf16[512,256]{1,0:T(8,128)(2,1)S(1)}, u32[]{:S(2)}, u32[]{:S(2)}) collective-permute-start(bf16[512,256]{1,0:T(8,128)(2,1)} %get-tuple-element.309), channel_id=1, source_target_pairs={{0,24},{4,28},{8,16},{12,20},{16,8},{20,12},{24,0},{28,4},{1,25},{... | collective-permute-start | bytes 786440 | tf_op jit(solution)/shard_map/ppermute | solution.py:105
  582.5 19.7 %collective-permute-start.46 = (bf16[512,256]{1,0:T(8,128)(2,1)}, bf16[512,256]{1,0:T(8,128)(2,1)S(1)}, u32[]{:S(2)}, u32[]{:S(2)}) collective-permute-start(bf16[512,256]{1,0:T(8,128)(2,1)} %get-tuple-element.307), channel_id=1, source_target_pairs={{0,16},{4,20},{8,24},{12,28},{16,0},{20,4},{24,8},{28,12},{1,17},{... | collective-permute-start | bytes 786440 | tf_op jit(solution)/shard_map/ppermute | solution.py:105
  582.5 19.7 %collective-permute-start.45 = (bf16[512,256]{1,0:T(8,128)(2,1)}, bf16[512,256]{1,0:T(8,128)(2,1)}, u32[]{:S(2)}, u32[]{:S(2)}) collective-permute-start(bf16[512,256]{1,0:T(8,128)(2,1)} %get-tuple-element.305), channel_id=1, source_target_pairs={{0,8},{4,12},{8,0},{12,4},{16,24},{20,28},{24,16},{28,20},{1,9},{5... | collective-permute-start | bytes 786440 | tf_op jit(solution)/shard_map/ppermute | solution.py:105
  585.3 25.2 %copy-start.20 = (s32[4096]{0:T(1024)S(1)}, s32[4096]{0:T(1024)}, u32[]{:S(2)}) copy-start(s32[4096]{0:T(1024)} %add.170) | copy-start | bytes 49156
  590.6 11.7 %copy-start.10 = (bf16[512,256]{1,0:T(8,128)(2,1)}, bf16[512,256]{1,0:T(8,128)(2,1)S(1)}, u32[]{:S(2)}) copy-start(bf16[512,256]{1,0:T(8,128)(2,1)S(1)} %collective-permute-done.47.refs_3_) | copy-start | bytes 786436
  606.1 11.4 %collective-permute-start.50 = (bf16[512,256]{1,0:T(8,128)(2,1)}, bf16[512,256]{1,0:T(8,128)(2,1)S(1)}, u32[]{:S(2)}, u32[]{:S(2)}) collective-permute-start(bf16[512,256]{1,0:T(8,128)(2,1)} %add.261.refs_0_.refs_1_), channel_id=1, source_target_pairs={{0,24},{4,28},{8,16},{12,20},{16,8},{20,12},{24,0},{28,4},{1,25},{... | collective-permute-start | bytes 786440 | tf_op jit(solution)/shard_map/ppermute | solution.py:105
  608.5 20.3 %collective-permute-start.49 = (bf16[512,256]{1,0:T(8,128)(2,1)}, bf16[512,256]{1,0:T(8,128)(2,1)S(1)}, u32[]{:S(2)}, u32[]{:S(2)}) collective-permute-start(bf16[512,256]{1,0:T(8,128)(2,1)} %add.261.refs_0_.refs_1_), channel_id=1, source_target_pairs={{0,16},{4,20},{8,24},{12,28},{16,0},{20,4},{24,8},{28,12},{1,17},{... | collective-permute-start | bytes 786440 | tf_op jit(solution)/shard_map/ppermute | solution.py:105
  608.5 20.3 %collective-permute-start.48 = (bf16[512,256]{1,0:T(8,128)(2,1)}, bf16[512,256]{1,0:T(8,128)(2,1)}, u32[]{:S(2)}, u32[]{:S(2)}) collective-permute-start(bf16[512,256]{1,0:T(8,128)(2,1)} %add.261.refs_0_.refs_1_), channel_id=1, source_target_pairs={{0,8},{4,12},{8,0},{12,4},{16,24},{20,28},{24,16},{28,20},{1,9},{5... | collective-permute-start | bytes 786440 | tf_op jit(solution)/shard_map/ppermute | solution.py:105
  632.2 1.6 collective-permute-start.52
  633.9 8.4 %collective-permute-start.53 = (bf16[128,1024]{1,0:T(8,128)(2,1)S(1)}, bf16[128,1024]{1,0:T(8,128)(2,1)S(1)}, u32[]{:S(2)}, u32[]{:S(2)}) collective-permute-start(bf16[128,1024]{1,0:T(8,128)(2,1)S(1)} %pad_maximum_fusion.2), channel_id=1, source_target_pairs={{0,2},{1,3},{2,0},{3,1},{4,6},{5,7},{6,4},{7,5},{8,10},{9,11},{10,... | collective-permute-start | bytes 786440 | tf_op jit(solution)/shard_map/ppermute | solution.py:105
  642.5 9.3 %collective-permute-start.54 = (bf16[128,1024]{1,0:T(8,128)(2,1)S(1)}, bf16[128,1024]{1,0:T(8,128)(2,1)S(1)}, u32[]{:S(2)}, u32[]{:S(2)}) collective-permute-start(bf16[128,1024]{1,0:T(8,128)(2,1)S(1)} %pad_maximum_fusion.3), channel_id=1, source_target_pairs={{0,4},{4,0},{8,12},{12,8},{16,20},{20,16},{24,28},{28,24},{1,5},{5... | collective-permute-start | bytes 786440 | tf_op jit(solution)/shard_map/ppermute | solution.py:105
  644.0 28.6 %collective-permute-start.51 = (bf16[2048,256]{1,0:T(8,128)(2,1)}, bf16[2048,256]{1,0:T(8,128)(2,1)}, u32[]{:S(2)}, u32[]{:S(2)}) collective-permute-start(bf16[2048,256]{1,0:T(8,128)(2,1)} %assemble.4.own_ref), channel_id=1, source_target_pairs={{0,4},{4,0},{8,12},{12,8},{16,20},{20,16},{24,28},{28,24},{1,5},{5... | collective-permute-start | bytes 3145736 | tf_op jit(solution)/shard_map/ppermute | solution.py:105
  651.9 6.4 collective-permute-start.55
  659.8 18.5 %collective-permute-start.56 = (bf16[128,1024]{1,0:T(8,128)(2,1)}, bf16[128,1024]{1,0:T(8,128)(2,1)}, u32[]{:S(2)}, u32[]{:S(2)}) collective-permute-start(bf16[128,1024]{1,0:T(8,128)(2,1)} %pad_maximum_fusion.5), channel_id=1, source_target_pairs={{0,16},{4,20},{8,24},{12,28},{16,0},{20,4},{24,8},{28,12},{1,17},{... | collective-permute-start | bytes 786440 | tf_op jit(solution)/shard_map/ppermute | solution.py:105
  670.6 12.4 %copy-start.5 = (f32[2,8,256]{2,1,0:T(8,128)S(1)}, f32[2,8,256]{2,1,0:T(8,128)}, u32[]{:S(2)}) copy-start(f32[2,8,256]{2,1,0:T(8,128)} %copy-done.4) | copy-start | bytes 49156
  (21 other events, 78.3 us)
Sparse Core Ops, SparseCore 0:
  435.8 74.2 all-gather.2

commit v6 on v5

--- a/solution.py
+++ b/solution.py
@@ -205,36 +205,37 @@
     )(jnp.reshape(index, (1,)).astype(jnp.int32), *parts, *deps)
 
 
-def assemble_kernel(index_ref, *refs, groups):
+def assemble_kernel(index_ref, *refs, count, groups):
     step = pl.program_id(0)
     size = refs[-1].shape[0]
     rows = pl.ds(pl.multiple_of(step % groups * size, size), size)
-    for k, ref in enumerate(refs[:-1]):
+    for k, ref in enumerate(refs[:count]):
 
         @pl.when(step // groups == k)
         def _():
             refs[-1][...] = ref[rows, :].astype(refs[-1].dtype)
 
 
-def assemble_call(pieces, index, dtype, groups=1):
+def assemble_call(pieces, index, dtype, groups=1, deps=()):
     count = len(pieces)
     rows, cols = pieces[0].shape
     spec = pltpu.PrefetchScalarGridSpec(
         num_scalar_prefetch=1,
         grid=(count * groups,),
-        in_specs=[pl.BlockSpec((rows, cols), lambda i, f: (0, 0))] * count,
+        in_specs=[pl.BlockSpec((rows, cols), lambda i, f: (0, 0))] * count
+        + [pl.BlockSpec(memory_space=pl.ANY)] * len(deps),
         out_specs=pl.BlockSpec(
             (rows // groups, cols), lambda i, f: (i % groups * count + (f[0] ^ (i // groups)), 0)
         ),
     )
     return pl.pallas_call(
-        functools.partial(assemble_kernel, groups=groups),
+        functools.partial(assemble_kernel, count=count, groups=groups),
         grid_spec=spec,
         out_shape=shaped((rows * count, cols), dtype),
         compiler_params=params(),
         cost_estimate=cost(0.001),
         name="assemble",
-    )(jnp.reshape(index, (1,)).astype(jnp.int32), *pieces)
+    )(jnp.reshape(index, (1,)).astype(jnp.int32), *pieces, *deps)
 
 
 def attention_grads_kernel(index_ref, own_ref, other_ref, qkv_ref, out_ref):
@@ -304,7 +305,7 @@
 
 class Steps:
     def __init__(self):
-        self.jobs, self.token, self.ties = [], None, []
+        self.jobs, self.token, self.ties, self.first = [], None, [], []
 
     def swap(self, value, axis, size, bit):
         if self.token is not None:
@@ -397,7 +398,7 @@
     return shared, by_shard[0]
 
 
-def spread_job(steps, sums, places, n_dp, offload, out, name):
+def spread_job(steps, sums, places, n_dp, offload, late, out, name):
     while not sums.full(0, places):
         yield []
     index = lax.axis_index("dp")
@@ -418,13 +419,16 @@
         return
     others = [steps.swap(total, "dp", n_dp, 2 * k) for k in range(1, count)]
     yield [total]
-    half = assemble_call([total] + [steps.arrive(part) for part in others], index // 2, BF)
+    others = [steps.arrive(part) for part in others]
+    half = assemble_call([total] + others, index // 2, BF, deps=steps.first)
+    if late:
+        yield [half]
     other = steps.swap(half, "dp", n_dp, 1)
-    yield [half]
+    yield [] if late else [half]
     other = steps.arrive(other)
     finish = attention_grads_call if name == "attention" else assemble_call
     out[name] = finish([half, other], index % 2, F32, len(places))
-    yield [other]
+    yield [] if late else [other]
 
 
 def place_hot():
@@ -976,8 +980,8 @@
     ties = steps.step(mlp_in)
     wide_sums = Sums(steps, n_mp, [0, 1, 1, 2])
     grads = {}
-    steps.jobs.append(spread_job(steps, wide_sums, [0, 1], n_dp, True, grads, "down"))
-    steps.jobs.append(spread_job(steps, wide_sums, [2, 3], n_dp, False, grads, "up"))
+    steps.jobs.append(spread_job(steps, wide_sums, [0, 1], n_dp, True, False, grads, "down"))
+    steps.jobs.append(spread_job(steps, wide_sums, [2, 3], n_dp, False, True, grads, "up"))
     act, grad_hidden = {}, {}
     for m in [m for m in masks if m % 2] + [m for m in reversed(masks) if m % 2 == 0]:
         ties = need(down_w, m, need(up_w, m, ties, mlp_in), mlp_in)
@@ -998,7 +1002,7 @@
         return jnp.einsum("mwc,mwe->mce", clip_hot, grouped, precision=highest).astype(BF)
 
     attn_sums = Sums(steps, n_mp, [0])
-    steps.jobs.append(spread_job(steps, attn_sums, [0], n_dp, False, grads, "attention"))
+    steps.jobs.append(spread_job(steps, attn_sums, [0], n_dp, False, False, grads, "attention"))
     dqkv, block_grads = {}, None
     ties = steps.step(grad_attn)
     for m in reversed(masks):
@@ -1018,6 +1022,8 @@
     rel_sums = jnp.pad(rel_sums, ((0, 0), (0, -table_size % width))).reshape(n_mp, -1, width)
     clip_terms = clip_sums(window_sums).reshape(-1, width)
     summed = steps.step()
+    down_grad = unfold_call(grads["down"], 2, summed)
+    steps.first = [down_grad, grads["up"]]
     ties = steps.step()
     mod_total, rel_total = sum_everywhere(
         after(clip_terms, *ties), after(rel_sums, *ties), n_mp, n_dp
@@ -1025,7 +1031,6 @@
     rel_grad = rel_total.reshape(-1)[:table_size].reshape(rel_bias.shape).astype(F32)
     steps.finish()
 
-    down_grad = unfold_call(grads["down"], 2, summed)
     up_grad = grads["up"]
     qkv_grad, out_grad = grads["attention"]
     qkv_grad = qkv_grad.reshape(qkv_weight.shape)

time: 704 us -> 692 us (0.983)
  waiting for transfers between devices: 75.8 us -> 65 us
    ppermute x57, waiting for transfers between devices: 75.7 us -> 65 us  [swap(): return lax.ppermute(value, axis, [(i, i ^ bit) for i in range(size)])]
  transfers between devices with their start and end apart: 58 -> 58, of which waited for: 13 -> 11; matrix products, arithmetic and copies ran while one was open for 4% -> 4% of each run, Pallas kernels for 71% -> 74%
where the time goes in v6:
time: 692 us; the launch traced here: 685 us
  Pallas kernels  513 us (74%)
  waiting for transfers between devices  65 us (9%)
  starting transfers between devices  46.9 us (7%)
  matrix products  20.8 us (3%)
  local copies, waits for them, and re-layouts  18.1 us (3%)
  between operations  15.3 us (2%)
    pallas_call x17, Pallas kernels, call_after(): return lambda *args: call(*args, *deps)  456 us
    ppermute x57, waiting for transfers between devices, swap(): return lax.ppermute(value, axis, [(i, i ^ bit) for i in range(size)])  65 us
    ppermute x57, starting transfers between devices, swap(): return lax.ppermute(value, axis, [(i, i ^ bit) for i in range(size)])  46.9 us
    pallas_call x6, Pallas kernels, split_call(): pl.pallas_call(functools.partial(split_kernel, count=count, groups=[len(g...  25.6 us
    pallas_call x5, Pallas kernels, add_groups(): pl.pallas_call(functools.partial(sum_kernel, groups=[len(group) for group...  17.4 us
  transfers between devices with their start and end apart: 58, of which 11 were waited for; matrix products, arithmetic and copies ran while one was open for 4% of the time, Pallas kernels for 74%

profile of v6, /device:TPU:0, one launch (start us, length us, event | category | flops | bytes accessed | tf_op | source)
XLA Modules:
  0.0 684.5 jit_solution(12347437928059558728)
XLA Ops:
  7.8 2.6 collective-permute-start.3
  11.1 1.7 convolution_add_fusion
  12.8 2.4 fusion.6
  17.4 3.7 fusion.1
  21.2 3.6 copy.35.refs_2_.refs_5_
  24.7 3.8 collective-permute-done.1
  30.2 8.8 %norm_in.1.refs_0_.refs_3_.refs_6_ = bf16[2560,1024]{1,0:T(8,128)(2,1)} custom-call(bf16[2560,1024]{1,0:T(8,128)(2,1)} %bitcast.127, f32[8,6,1024]{2,1,0:T(8,128)} %reshape.254.refs_1_.refs_10_.refs_19_), custom_call_target="tpu_custom_call" | custom-call | flops 8000000000 | bytes 28000000 | tf_op jit(solution)/shard_map/norm_in/pallas_call | solution.py:83
  39.5 1.7 collective-permute-start.8
  41.2 16.7 %attend.4 = (bf16[3,2560,256]{2,1,0:T(8,128)(2,1)}, bf16[2560,256]{1,0:T(8,128)(2,1)}, f32[8,8,384]{2,1,0:T(8,128)}) custom-call(bf16[2560,1024]{1,0:T(8,128)(2,1)} %norm_in.1.refs_0_.refs_3_.refs_6_, bf16[3,1024,256]{2,1,0:T(8,128)(2,1)} %refs_4_.3, f32[16,9,64,64]{3,2,1,0:T(8,128)} %copy.35.refs_2_.refs_5_, bf16[2560,1024]{1,0:T(8,128)(2,1)} %norm_in.1.refs_0_.refs_3_.refs_6_), custom_call_target="tpu_custom_call" | custom-call | flops 19000000512 | bytes 66500000 | tf_op jit(solution)/shard_map/attend/pallas_call | solution.py:83
  58.2 16.7 %attend.5 = (bf16[3,2560,256]{2,1,0:T(8,128)(2,1)}, bf16[2560,256]{1,0:T(8,128)(2,1)}, f32[8,8,384]{2,1,0:T(8,128)}) custom-call(bf16[2560,1024]{1,0:T(8,128)(2,1)} %norm_in.1.refs_0_.refs_3_.refs_6_, bf16[3,1024,256]{2,1,0:T(8,128)(2,1)} %collective-permute-done.5.refs_1_.refs_5_, f32[16,9,64,64]{3,2,1,0:T(8,128)} %copy.35.refs_2_.refs_5_, ...), custom_call_target="tpu_custom_call" | custom-call | flops 19000000512 | bytes 66500000 | tf_op jit(solution)/shard_map/attend/pallas_call | solution.py:83
  75.4 16.7 %attend.6 = (bf16[3,2560,256]{2,1,0:T(8,128)(2,1)}, bf16[2560,256]{1,0:T(8,128)(2,1)}, f32[8,8,384]{2,1,0:T(8,128)}) custom-call(bf16[2560,1024]{1,0:T(8,128)(2,1)} %norm_in.1.refs_0_.refs_3_.refs_6_, bf16[3,1024,256]{2,1,0:T(8,128)(2,1)} %collective-permute-done.6.refs_1_.refs_3_.refs_6_, f32[16,9,64,64]{3,2,1,0:T(8,128)} %copy.35.refs_2_.refs_5_, ...), custom_call_target="tpu_custom_call" | custom-call | flops 19000000512 | bytes 66500000 | tf_op jit(solution)/shard_map/attend/pallas_call | solution.py:83
  92.7 30.2 %attend.7 = (bf16[3,2560,256]{2,1,0:T(8,128)(2,1)}, bf16[2560,256]{1,0:T(8,128)(2,1)}, f32[8,8,384]{2,1,0:T(8,128)}) custom-call(bf16[2560,1024]{1,0:T(8,128)(2,1)} %norm_in.1.refs_0_.refs_3_.refs_6_, bf16[3,1024,256]{2,1,0:T(8,128)(2,1)} %collective-permute-done.7.refs_1_.refs_7_, f32[16,9,64,64]{3,2,1,0:T(8,128)} %copy.35.refs_2_.refs_5_, ...), custom_call_target="tpu_custom_call" | custom-call | flops 19000000512 | bytes 66500000 | tf_op jit(solution)/shard_map/attend/pallas_call | solution.py:83
  122.9 1.8 collective-permute-start.11
  124.8 15.6 %middle.1 = (bf16[2560,1024]{1,0:T(8,128)(2,1)}, bf16[2560,1024]{1,0:T(8,128)(2,1)}, bf16[2560,1024]{1,0:T(8,128)(2,1)}) custom-call(bf16[2560,256]{1,0:T(8,128)(2,1)} %get-tuple-element.164.refs_3_.refs_0_, bf16[2560,256]{1,0:T(8,128)(2,1)} %get-tuple-element.166.refs_4_.refs_1_.refs_3_, bf16[2560,256]{1,0:T(8,128)(2,1)} %get-tuple-element.168.refs_4_.refs_2_.refs_3_, ...), custom_call_target="tpu_custom_call" | custom-call | flops 16000000000 | bytes 56000000 | tf_op jit(solution)/shard_map/middle/pallas_call | solution.py:83
  140.5 32.4 %mlp.4 = (bf16[2560,1024]{1,0:T(8,128)(2,1)}, bf16[2560,1024]{1,0:T(8,128)(2,1)}, bf16[512,1024]{1,0:T(8,128)(2,1)}, bf16[512,1024]{1,0:T(8,128)(2,1)}, bf16[512...) custom-call(bf16[2560,1024]{1,0:T(8,128)(2,1)} %get-tuple-element.174.refs_0_.refs_5_, ...), custom_call_target="tpu_custom_call" | custom-call | flops 30000001024 | bytes 105000000 | tf_op jit(solution)/shard_map/mlp/pallas_call | solution.py:83
  174.4 3.1 collective-permute-done.15.refs_2_.refs_15_
  177.5 32.6 %mlp.5 = (bf16[2560,1024]{1,0:T(8,128)(2,1)}, bf16[2560,1024]{1,0:T(8,128)(2,1)}, bf16[512,1024]{1,0:T(8,128)(2,1)}, bf16[512,1024]{1,0:T(8,128)(2,1)}, bf16[512...) custom-call(bf16[2560,1024]{1,0:T(8,128)(2,1)} %get-tuple-element.174.refs_0_.refs_5_, ...), custom_call_target="tpu_custom_call" | custom-call | flops 30000001024 | bytes 105000000 | tf_op jit(solution)/shard_map/mlp/pallas_call | solution.py:83
  211.3 32.4 %mlp.6 = (bf16[2560,1024]{1,0:T(8,128)(2,1)}, bf16[2560,1024]{1,0:T(8,128)(2,1)}, bf16[512,1024]{1,0:T(8,128)(2,1)}, bf16[512,1024]{1,0:T(8,128)(2,1)}, bf16[512...) custom-call(bf16[2560,1024]{1,0:T(8,128)(2,1)} %get-tuple-element.174.refs_0_.refs_5_, ...), custom_call_target="tpu_custom_call" | custom-call | flops 30000001024 | bytes 105000000 | tf_op jit(solution)/shard_map/mlp/pallas_call | solution.py:83
  243.7 5.8 add.257
  249.9 32.8 %mlp.7 = (bf16[2560,1024]{1,0:T(8,128)(2,1)}, bf16[2560,1024]{1,0:T(8,128)(2,1)}, bf16[512,1024]{1,0:T(8,128)(2,1)}, bf16[512,1024]{1,0:T(8,128)(2,1)}, bf16[512...) custom-call(bf16[2560,1024]{1,0:T(8,128)(2,1)} %get-tuple-element.174.refs_0_.refs_5_, ...), custom_call_target="tpu_custom_call" | custom-call | flops 30000001024 | bytes 105000000 | tf_op jit(solution)/shard_map/mlp/pallas_call | solution.py:83
  282.7 1.8 collective-permute-start.26
  284.8 62.7 %mlp_out.1 = (bf16[2560,1024]{1,0:T(8,128)(2,1)}, bf16[2560,1024]{1,0:T(8,128)(2,1)}, bf16[2560,1024]{1,0:T(8,128)(2,1)}, f32[8,4,1024]{2,1,0:T(4,128)}) custom-call(bf16[2560,1024]{1,0:T(8,128)(2,1)} %get-tuple-element.214.refs_0_, bf16[2560,1024]{1,0:T(8,128)(2,1)} %get-tuple-element.215.refs_1_, bf16[2560,1024]{1,0:T(8,128)(2,1)} %get-tuple-element.216.refs_2_, ...), custom_call_target="tpu_custom_call" | custom-call | flops 54999998464 | bytes 192500000 | tf_op jit(solution)/shard_map/mlp_out/pallas_call | solution.py:83
  347.5 1.8 collective-permute-start.28
  349.3 4.9 split.6
  354.2 1.5 collective-permute-start.29
  355.7 31.1 %attend_back.4 = (bf16[3,2560,256]{2,1,0:T(8,128)(2,1)}, f32[16,9,64,64]{3,2,1,0:T(8,128)}, bf16[4,1024,256]{2,1,0:T(8,128)(2,1)}) custom-call(bf16[2560,1024]{1,0:T(8,128)(2,1)} %get-tuple-element.227.refs_0_.refs_10_, bf16[256,1024]{1,0:T(8,128)(2,1)} %collective-permute-done.10.refs_7_.refs_1_, bf16[3,2560,256]{2,1,0:T(8,128)(2,1)} %get-tuple-element.234.refs_2_, ...), custom_call_target="tpu_custom_call" | custom-call | flops 30000001024 | bytes 105000000 | tf_op jit(solution)/shard_map/attend_back/pallas_call | solution.py:83
  386.9 3.6 split.7
  390.4 4.9 split.8
  395.4 3.6 collective-permute-start.32
  400.3 31.6 %attend_back.5 = (bf16[3,2560,256]{2,1,0:T(8,128)(2,1)}, f32[16,9,64,64]{3,2,1,0:T(8,128)}, bf16[4,1024,256]{2,1,0:T(8,128)(2,1)}) custom-call(bf16[2560,1024]{1,0:T(8,128)(2,1)} %get-tuple-element.227.refs_0_.refs_10_, bf16[256,1024]{1,0:T(8,128)(2,1)} %collective-permute-done.8.refs_3_.refs_6_.refs_1_, ...), custom_call_target="tpu_custom_call", output_to_operand_aliasing={{1}: (7, {})} | custom-call | flops 30000001024 | bytes 105000000 | tf_op jit(solution)/shard_map/attend_back/pallas_call | solution.py:83
  433.4 2.0 add.258.refs_2_.refs_8_
  435.5 3.5 split.9
  439.0 3.6 collective-permute-start.37
  443.4 4.3 add.259.refs_15_
  448.1 31.2 %attend_back.6 = (bf16[3,2560,256]{2,1,0:T(8,128)(2,1)}, f32[16,9,64,64]{3,2,1,0:T(8,128)}, bf16[4,1024,256]{2,1,0:T(8,128)(2,1)}) custom-call(bf16[2560,1024]{1,0:T(8,128)(2,1)} %get-tuple-element.227.refs_0_.refs_10_, bf16[256,1024]{1,0:T(8,128)(2,1)} %collective-permute-done.9.refs_5_.refs_1_, ...), custom_call_target="tpu_custom_call", output_to_operand_aliasing={{1}: (7, {})} | custom-call | flops 30000001024 | bytes 105000000 | tf_op jit(solution)/shard_map/attend_back/pallas_call | solution.py:83
  480.9 2.0 add.260.refs_8_.refs_0_
  483.0 3.7 collective-permute-start.41
  487.4 6.9 %collective-permute-done.38.refs_9_.refs_0_ = bf16[4096,256]{1,0:T(8,128)(2,1)} collective-permute-done((bf16[4096,256]{1,0:T(8,128)(2,1)}, bf16[4096,256]{1,0:T(8,128)(2,1)}, u32[]{:S(2)}, u32[]{:S(2)}) %collective-permute-start.38) | collective-permute-done | bytes 2097184 | tf_op jit(solution)/shard_map/ppermute | solution.py:105
  494.2 31.3 %attend_back.7 = (bf16[3,2560,256]{2,1,0:T(8,128)(2,1)}, f32[16,9,64,64]{3,2,1,0:T(8,128)}, bf16[4,1024,256]{2,1,0:T(8,128)(2,1)}) custom-call(bf16[2560,1024]{1,0:T(8,128)(2,1)} %get-tuple-element.227.refs_0_.refs_10_, bf16[256,1024]{1,0:T(8,128)(2,1)} %refs_1_.3, ...), custom_call_target="tpu_custom_call", output_to_operand_aliasing={{1}: (7, {})} | custom-call | flops 30000001024 | bytes 105000000 | tf_op jit(solution)/shard_map/attend_back/pallas_call | solution.py:83
  525.6 5.2 split.10
  532.3 2.8 assemble.3.refs_12_.refs_0_
  535.1 26.8 %last.1 = (bf16[2560,1024]{1,0:T(8,128)(2,1)}, f32[8,2,1024]{2,1,0:T(2,128)}) custom-call(bf16[3,2560,256]{2,1,0:T(8,128)(2,1)} %get-tuple-element.283.refs_0_, bf16[3,2560,256]{2,1,0:T(8,128)(2,1)} %get-tuple-element.284.refs_1_, bf16[3,2560,256]{2,1,0:T(8,128)(2,1)} %get-tuple-element.285.refs_2_, bf16[3,2560,256]{2,1,0:T(8,128)(2,1)} %get-tuple-element.286.refs_3_, ...), custom_call_target="tpu_custom_call" | custom-call | flops 28000000000 | bytes 98000000 | tf_op jit(solution)/shard_map/last/pallas_call | solution.py:83
  562.6 3.5 split.11
  566.1 3.5 collective-permute-start.46
  572.2 5.3 reshape.265
  577.5 12.0 %collective-permute-done.45.refs_2_ = bf16[512,256]{1,0:T(8,128)(2,1)S(1)} collective-permute-done((bf16[512,256]{1,0:T(8,128)(2,1)}, bf16[512,256]{1,0:T(8,128)(2,1)S(1)}, u32[]{:S(2)}, u32[]{:S(2)}) %collective-permute-start.45) | collective-permute-done | bytes 262176 | tf_op jit(solution)/shard_map/ppermute | solution.py:105
  590.1 3.2 add.261.refs_1_.refs_0_
  593.3 2.4 collective-permute-start.49
  595.7 2.0 collective-permute-start.47
  597.7 4.1 fusion.3
  602.6 6.0 unfold.1.refs_4_
  608.7 4.0 assemble.4.refs_5_
  612.7 3.2 collective-permute-done.48.refs_2_
  616.6 2.7 assemble.5.own_ref
  619.5 1.5 collective-permute-done.52
  621.7 7.8 %collective-permute-done.53 = bf16[128,1024]{1,0:T(8,128)(2,1)S(1)} collective-permute-done((bf16[128,1024]{1,0:T(8,128)(2,1)S(1)}, bf16[128,1024]{1,0:T(8,128)(2,1)S(1)}, u32[]{:S(2)}, u32[]{:S(2)}) %collective-permute-start.53) | collective-permute-done | bytes 262176 | tf_op jit(solution)/shard_map/ppermute | solution.py:105
  629.6 1.6 collective-permute-start.54
  631.7 7.2 %collective-permute-done.54 = bf16[128,1024]{1,0:T(8,128)(2,1)S(1)} collective-permute-done((bf16[128,1024]{1,0:T(8,128)(2,1)S(1)}, bf16[128,1024]{1,0:T(8,128)(2,1)S(1)}, u32[]{:S(2)}, u32[]{:S(2)}) %collective-permute-start.54) | collective-permute-done | bytes 262176 | tf_op jit(solution)/shard_map/ppermute | solution.py:105
  639.2 6.4 collective-permute-done.55
  647.8 12.0 %collective-permute-done.51.other_ref = bf16[2048,256]{1,0:T(8,128)(2,1)} collective-permute-done((bf16[2048,256]{1,0:T(8,128)(2,1)}, bf16[2048,256]{1,0:T(8,128)(2,1)}, u32[]{:S(2)}, u32[]{:S(2)}) %collective-permute-start.51) | collective-permute-done | bytes 1048608 | tf_op jit(solution)/shard_map/ppermute | solution.py:105
  659.8 4.7 attention_grads.1
  666.7 2.8 fusion.4
  670.2 3.7 convolution_bitcast_fusion
  675.5 1.6 convolution_bitcast_fusion.1
  (196 shorter events, 32.0 us)
Async XLA Ops:
  7.2 527.8 %all-gather.3.cloned.1.call-start = ((), (), s32[]{:S(2)}) async-start(), calls=%async_computation | async-start | bytes 2359296 | tf_op jit(solution)/shard_map/all_gather | solution.py:414
  7.2 8.7 %collective-permute-start.2 = (f32[4,2025]{1,0:T(4,128)}, f32[4,2025]{1,0:T(4,128)S(1)}, u32[]{:S(2)}, u32[]{:S(2)}) collective-permute-start(f32[4,2025]{1,0:T(4,128)} %param.19), channel_id=1, source_target_pairs={{0,1},{1,0},{2,3},{3,2},{4,5},{5,4},{6,7},{7,6},{8,9},{9,8},{10,11... | collective-permute-start | bytes 97208 | tf_op jit(solution)/shard_map/ppermute | solution.py:105
  7.8 7.7 %collective-permute-start.3 = (f32[4,2025]{1,0:T(4,128)}, f32[4,2025]{1,0:T(4,128)S(1)}, u32[]{:S(2)}, u32[]{:S(2)}) collective-permute-start(f32[4,2025]{1,0:T(4,128)} %param.19), channel_id=1, source_target_pairs={{0,2},{1,3},{2,0},{3,1},{4,6},{5,7},{6,4},{7,5},{8,10},{9,11},{10,... | collective-permute-start | bytes 97208 | tf_op jit(solution)/shard_map/ppermute | solution.py:105
  15.2 2.1 collective-permute-start
  15.5 1.5 collective-permute-start.4
  16.0 13.0 %copy-start.24 = (s32[2,4]{1,0:T(2,128)}, s32[2,4]{1,0:T(2,128)S(1)}, u32[]{:S(2)}) copy-start(s32[2,4]{1,0:T(2,128)S(1)} %constant_dynamic-slice_fusion) | copy-start | bytes 100
  17.3 11.3 %collective-permute-start.1 = (f32[2,8,6144]{2,1,0:T(8,128)S(1)}, f32[2,8,6144]{2,1,0:T(8,128)S(1)}, u32[]{:S(2)}, u32[]{:S(2)}) collective-permute-start(f32[2,8,6144]{2,1,0:T(8,128)S(1)} %add.163), channel_id=1, source_target_pairs={{0,2},{1,3},{2,0},{3,1},{4,6},{5,7},{6,4},{7,5},{8,10},{9,11},{10,... | collective-permute-start | bytes 1179656 | tf_op jit(solution)/shard_map/ppermute | solution.py:105
  28.6 46.2 %collective-permute-start.6 = (bf16[3,1024,256]{2,1,0:T(8,128)(2,1)}, bf16[3,1024,256]{2,1,0:T(8,128)(2,1)}, u32[]{:S(2)}, u32[]{:S(2)}) collective-permute-start(bf16[3,1024,256]{2,1,0:T(8,128)(2,1)} %refs_4_.3), channel_id=1, source_target_pairs={{0,2},{1,3},{2,0},{3,1},{4,6},{5,7},{6,4},{7,5},{8,10},{9,11},{10,... | collective-permute-start | bytes 4718600 | tf_op jit(solution)/shard_map/ppermute | solution.py:105
  29.0 29.2 %collective-permute-start.5 = (bf16[3,1024,256]{2,1,0:T(8,128)(2,1)}, bf16[3,1024,256]{2,1,0:T(8,128)(2,1)}, u32[]{:S(2)}, u32[]{:S(2)}) collective-permute-start(bf16[3,1024,256]{2,1,0:T(8,128)(2,1)} %refs_4_.3), channel_id=1, source_target_pairs={{0,1},{1,0},{2,3},{3,2},{4,5},{5,4},{6,7},{7,6},{8,9},{9,8},{10,11... | collective-permute-start | bytes 4718600 | tf_op jit(solution)/shard_map/ppermute | solution.py:105
  39.0 84.0 %collective-permute-start.9 = (bf16[256,1024]{1,0:T(8,128)(2,1)S(1)}, bf16[256,1024]{1,0:T(8,128)(2,1)}, u32[]{:S(2)}, u32[]{:S(2)}) collective-permute-start(bf16[256,1024]{1,0:T(8,128)(2,1)S(1)} %copy-done.27), channel_id=1, source_target_pairs={{0,1},{1,0},{2,3},{3,2},{4,5},{5,4},{6,7},{7,6},{8,9},{9,8},{10,11... | collective-permute-start | bytes 1572872 | tf_op jit(solution)/shard_map/ppermute | solution.py:105
  39.5 52.7 %collective-permute-start.8 = (bf16[256,1024]{1,0:T(8,128)(2,1)S(1)}, bf16[256,1024]{1,0:T(8,128)(2,1)}, u32[]{:S(2)}, u32[]{:S(2)}) collective-permute-start(bf16[256,1024]{1,0:T(8,128)(2,1)S(1)} %copy-done.27), channel_id=1, source_target_pairs={{0,2},{1,3},{2,0},{3,1},{4,6},{5,7},{6,4},{7,5},{8,10},{9,11},{10,... | collective-permute-start | bytes 1572872 | tf_op jit(solution)/shard_map/ppermute | solution.py:105
  57.9 82.5 %collective-permute-start.14 = (bf16[1024,1024]{1,0:T(8,128)(2,1)}, bf16[1024,1024]{1,0:T(8,128)(2,1)}, u32[]{:S(2)}, u32[]{:S(2)}) collective-permute-start(bf16[1024,1024]{1,0:T(8,128)(2,1)} %refs_8_.1), channel_id=1, source_target_pairs={{0,2},{1,3},{2,0},{3,1},{4,6},{5,7},{6,4},{7,5},{8,10},{9,11},{10,... | collective-permute-start | bytes 6291464 | tf_op jit(solution)/shard_map/ppermute | solution.py:105
  58.2 82.3 %collective-permute-start.13 = (bf16[1024,1024]{1,0:T(8,128)(2,1)}, bf16[1024,1024]{1,0:T(8,128)(2,1)}, u32[]{:S(2)}, u32[]{:S(2)}) collective-permute-start(bf16[1024,1024]{1,0:T(8,128)(2,1)} %refs_8_.1), channel_id=1, source_target_pairs={{0,1},{1,0},{2,3},{3,2},{4,5},{5,4},{6,7},{7,6},{8,9},{9,8},{10,11... | collective-permute-start | bytes 6291464 | tf_op jit(solution)/shard_map/ppermute | solution.py:105
  74.9 17.4 %collective-permute-start.7 = (bf16[3,1024,256]{2,1,0:T(8,128)(2,1)}, bf16[3,1024,256]{2,1,0:T(8,128)(2,1)}, u32[]{:S(2)}, u32[]{:S(2)}) collective-permute-start(bf16[3,1024,256]{2,1,0:T(8,128)(2,1)} %collective-permute-done.6.refs_1_.refs_3_.refs_6_), channel_id=1, source_target_pairs={{0,1},{1,0},{2,3},{3,2},{4,5},{5,4},{6,7},{7,6},{8,9},{9,8},{10,11... | collective-permute-start | bytes 4718600 | tf_op jit(solution)/shard_map/ppermute | solution.py:105
  92.1 32.6 %collective-permute-start.10 = (bf16[256,1024]{1,0:T(8,128)(2,1)}, bf16[256,1024]{1,0:T(8,128)(2,1)}, u32[]{:S(2)}, u32[]{:S(2)}) collective-permute-start(bf16[256,1024]{1,0:T(8,128)(2,1)} %collective-permute-done.8.refs_3_.refs_6_.refs_1_), channel_id=1, source_target_pairs={{0,1},{1,0},{2,3},{3,2},{4,5},{5,4},{6,7},{7,6},{8,9},{9,8},{10,11... | collective-permute-start | bytes 1572872 | tf_op jit(solution)/shard_map/ppermute | solution.py:105
  92.2 48.2 %collective-permute-start.12 = (bf16[1024,1024]{1,0:T(8,128)(2,1)}, bf16[1024,1024]{1,0:T(8,128)(2,1)}, u32[]{:S(2)}, u32[]{:S(2)}) collective-permute-start(bf16[1024,1024]{1,0:T(8,128)(2,1)} %refs_12_.1), channel_id=1, source_target_pairs={{0,1},{1,0},{2,3},{3,2},{4,5},{5,4},{6,7},{7,6},{8,9},{9,8},{10,11... | collective-permute-start | bytes 6291464 | tf_op jit(solution)/shard_map/ppermute | solution.py:105
  122.9 49.9 %collective-permute-start.11 = (bf16[1024,1024]{1,0:T(8,128)(2,1)}, bf16[1024,1024]{1,0:T(8,128)(2,1)}, u32[]{:S(2)}, u32[]{:S(2)}) collective-permute-start(bf16[1024,1024]{1,0:T(8,128)(2,1)} %refs_12_.1), channel_id=1, source_target_pairs={{0,2},{1,3},{2,0},{3,1},{4,6},{5,7},{6,4},{7,5},{8,10},{9,11},{10,... | collective-permute-start | bytes 6291464 | tf_op jit(solution)/shard_map/ppermute | solution.py:105
  140.4 33.6 %collective-permute-start.16 = (bf16[1024,1024]{1,0:T(8,128)(2,1)}, bf16[1024,1024]{1,0:T(8,128)(2,1)}, u32[]{:S(2)}, u32[]{:S(2)}) collective-permute-start(bf16[1024,1024]{1,0:T(8,128)(2,1)} %collective-permute-done.14.refs_4_.refs_3_.refs_10_), channel_id=1, source_target_pairs={{0,1},{1,0},{2,3},{3,2},{4,5},{5,4},{6,7},{7,6},{8,9},{9,8},{10,11... | collective-permute-start | bytes 6291464 | tf_op jit(solution)/shard_map/ppermute | solution.py:105
  172.8 4.7 collective-permute-start.15
  173.4 36.8 %collective-permute-start.18 = (bf16[512,1024]{1,0:T(8,128)(2,1)}, bf16[512,1024]{1,0:T(8,128)(2,1)}, u32[]{:S(2)}, u32[]{:S(2)}) collective-permute-start(bf16[512,1024]{1,0:T(8,128)(2,1)} %get-tuple-element.185.refs_5_), channel_id=1, source_target_pairs={{0,1},{1,0},{2,3},{3,2},{4,5},{5,4},{6,7},{7,6},{8,9},{9,8},{10,11... | collective-permute-start | bytes 3145736 | tf_op jit(solution)/shard_map/ppermute | solution.py:105
  173.5 36.7 %collective-permute-start.21 = (bf16[512,1024]{1,0:T(8,128)(2,1)}, bf16[512,1024]{1,0:T(8,128)(2,1)}, u32[]{:S(2)}, u32[]{:S(2)}) collective-permute-start(bf16[512,1024]{1,0:T(8,128)(2,1)} %get-tuple-element.194), channel_id=1, source_target_pairs={{0,1},{1,0},{2,3},{3,2},{4,5},{5,4},{6,7},{7,6},{8,9},{9,8},{10,11... | collective-permute-start | bytes 3145736 | tf_op jit(solution)/shard_map/ppermute | solution.py:105
  173.9 36.3 %collective-permute-start.20 = (bf16[512,1024]{1,0:T(8,128)(2,1)}, bf16[512,1024]{1,0:T(8,128)(2,1)}, u32[]{:S(2)}, u32[]{:S(2)}) collective-permute-start(bf16[512,1024]{1,0:T(8,128)(2,1)} %get-tuple-element.191), channel_id=1, source_target_pairs={{0,1},{1,0},{2,3},{3,2},{4,5},{5,4},{6,7},{7,6},{8,9},{9,8},{10,11... | collective-permute-start | bytes 3145736 | tf_op jit(solution)/shard_map/ppermute | solution.py:105
  174.0 36.2 %collective-permute-start.19 = (bf16[512,1024]{1,0:T(8,128)(2,1)}, bf16[512,1024]{1,0:T(8,128)(2,1)}, u32[]{:S(2)}, u32[]{:S(2)}) collective-permute-start(bf16[512,1024]{1,0:T(8,128)(2,1)} %get-tuple-element.188), channel_id=1, source_target_pairs={{0,1},{1,0},{2,3},{3,2},{4,5},{5,4},{6,7},{7,6},{8,9},{9,8},{10,11... | collective-permute-start | bytes 3145736 | tf_op jit(solution)/shard_map/ppermute | solution.py:105
  210.2 33.5 %collective-permute-start.17 = (bf16[512,1024]{1,0:T(8,128)(2,1)}, bf16[512,1024]{1,0:T(8,128)(2,1)}, u32[]{:S(2)}, u32[]{:S(2)}) collective-permute-start(bf16[512,1024]{1,0:T(8,128)(2,1)} %get-tuple-element.184.refs_8_), channel_id=1, source_target_pairs={{0,1},{1,0},{2,3},{3,2},{4,5},{5,4},{6,7},{7,6},{8,9},{9,8},{10,11... | collective-permute-start | bytes 3145736 | tf_op jit(solution)/shard_map/ppermute | solution.py:105
  210.6 33.1 %collective-permute-start.24 = (bf16[512,1024]{1,0:T(8,128)(2,1)}, bf16[512,1024]{1,0:T(8,128)(2,1)}, u32[]{:S(2)}, u32[]{:S(2)}) collective-permute-start(bf16[512,1024]{1,0:T(8,128)(2,1)} %get-tuple-element.205), channel_id=1, source_target_pairs={{0,1},{1,0},{2,3},{3,2},{4,5},{5,4},{6,7},{7,6},{8,9},{9,8},{10,11... | collective-permute-start | bytes 3145736 | tf_op jit(solution)/shard_map/ppermute | solution.py:105
  210.8 32.9 %collective-permute-start.23 = (bf16[512,1024]{1,0:T(8,128)(2,1)}, bf16[512,1024]{1,0:T(8,128)(2,1)}, u32[]{:S(2)}, u32[]{:S(2)}) collective-permute-start(bf16[512,1024]{1,0:T(8,128)(2,1)} %get-tuple-element.202), channel_id=1, source_target_pairs={{0,1},{1,0},{2,3},{3,2},{4,5},{5,4},{6,7},{7,6},{8,9},{9,8},{10,11... | collective-permute-start | bytes 3145736 | tf_op jit(solution)/shard_map/ppermute | solution.py:105
  211.1 32.6 %collective-permute-start.22 = (bf16[512,1024]{1,0:T(8,128)(2,1)}, bf16[512,1024]{1,0:T(8,128)(2,1)}, u32[]{:S(2)}, u32[]{:S(2)}) collective-permute-start(bf16[512,1024]{1,0:T(8,128)(2,1)} %get-tuple-element.199), channel_id=1, source_target_pairs={{0,1},{1,0},{2,3},{3,2},{4,5},{5,4},{6,7},{7,6},{8,9},{9,8},{10,11... | collective-permute-start | bytes 3145736 | tf_op jit(solution)/shard_map/ppermute | solution.py:105
  249.6 35.3 %collective-permute-start.25 = (bf16[512,1024]{1,0:T(8,128)(2,1)}, bf16[512,1024]{1,0:T(8,128)(2,1)}, u32[]{:S(2)}, u32[]{:S(2)}) collective-permute-start(bf16[512,1024]{1,0:T(8,128)(2,1)} %get-tuple-element.223.refs_8_), channel_id=1, source_target_pairs={{0,2},{1,3},{2,0},{3,1},{4,6},{5,7},{6,4},{7,5},{8,10},{9,11},{10,... | collective-permute-start | bytes 3145736 | tf_op jit(solution)/shard_map/ppermute | solution.py:105
  282.7 66.6 %collective-permute-start.26 = (bf16[512,1024]{1,0:T(8,128)(2,1)}, bf16[512,1024]{1,0:T(8,128)(2,1)}, u32[]{:S(2)}, u32[]{:S(2)}) collective-permute-start(bf16[512,1024]{1,0:T(8,128)(2,1)} %get-tuple-element.236.refs_9_), channel_id=1, source_target_pairs={{0,2},{1,3},{2,0},{3,1},{4,6},{5,7},{6,4},{7,5},{8,10},{9,11},{10,... | collective-permute-start | bytes 3145736 | tf_op jit(solution)/shard_map/ppermute | solution.py:105
  284.5 71.1 %collective-permute-start.27 = (bf16[512,1024]{1,0:T(8,128)(2,1)}, bf16[512,1024]{1,0:T(8,128)(2,1)}, u32[]{:S(2)}, u32[]{:S(2)}) collective-permute-start(bf16[512,1024]{1,0:T(8,128)(2,1)} %get-tuple-element.238.refs_10_), channel_id=1, source_target_pairs={{0,2},{1,3},{2,0},{3,1},{4,6},{5,7},{6,4},{7,5},{8,10},{9,11},{10,... | collective-permute-start | bytes 3145736 | tf_op jit(solution)/shard_map/ppermute | solution.py:105
  347.5 39.4 %collective-permute-start.28 = (bf16[512,1024]{1,0:T(8,128)(2,1)}, bf16[512,1024]{1,0:T(8,128)(2,1)}, u32[]{:S(2)}, u32[]{:S(2)}) collective-permute-start(bf16[512,1024]{1,0:T(8,128)(2,1)} %get-tuple-element.243.refs_11_), channel_id=1, source_target_pairs={{0,2},{1,3},{2,0},{3,1},{4,6},{5,7},{6,4},{7,5},{8,10},{9,11},{10,... | collective-permute-start | bytes 3145736 | tf_op jit(solution)/shard_map/ppermute | solution.py:105
  354.2 32.7 %collective-permute-start.29 = (bf16[512,1024]{1,0:T(8,128)(2,1)}, bf16[512,1024]{1,0:T(8,128)(2,1)}, u32[]{:S(2)}, u32[]{:S(2)}) collective-permute-start(bf16[512,1024]{1,0:T(8,128)(2,1)} %get-tuple-element.246.refs_9_), channel_id=1, source_target_pairs={{0,4},{4,0},{8,12},{12,8},{16,20},{20,16},{24,28},{28,24},{1,5},{5... | collective-permute-start | bytes 3145736 | tf_op jit(solution)/shard_map/ppermute | solution.py:105
  386.8 56.6 %collective-permute-start.34 = (bf16[4096,256]{1,0:T(8,128)(2,1)}, bf16[4096,256]{1,0:T(8,128)(2,1)}, u32[]{:S(2)}, u32[]{:S(2)}) collective-permute-start(bf16[4096,256]{1,0:T(8,128)(2,1)} %bitcast.132), channel_id=1, source_target_pairs={{0,1},{1,0},{2,3},{3,2},{4,5},{5,4},{6,7},{7,6},{8,9},{9,8},{10,11... | collective-permute-start | bytes 6291464 | tf_op jit(solution)/shard_map/ppermute | solution.py:105
  395.4 36.5 %collective-permute-start.32 = (bf16[128,1024]{1,0:T(8,128)(2,1)}, bf16[128,1024]{1,0:T(8,128)(2,1)S(1)}, u32[]{:S(2)}, u32[]{:S(2)}) collective-permute-start(bf16[128,1024]{1,0:T(8,128)(2,1)} %get-tuple-element.262.refs_13_), channel_id=1, source_target_pairs={{0,24},{4,28},{8,16},{12,20},{16,8},{20,12},{24,0},{28,4},{1,25},{... | collective-permute-start | bytes 786440 | tf_op jit(solution)/shard_map/ppermute | solution.py:105
  399.0 32.9 %collective-permute-start.31 = (bf16[128,1024]{1,0:T(8,128)(2,1)}, bf16[128,1024]{1,0:T(8,128)(2,1)S(1)}, u32[]{:S(2)}, u32[]{:S(2)}) collective-permute-start(bf16[128,1024]{1,0:T(8,128)(2,1)} %get-tuple-element.260.refs_12_), channel_id=1, source_target_pairs={{0,16},{4,20},{8,24},{12,28},{16,0},{20,4},{24,8},{28,12},{1,17},{... | collective-permute-start | bytes 786440 | tf_op jit(solution)/shard_map/ppermute | solution.py:105
  399.0 32.9 %collective-permute-start.30 = (bf16[128,1024]{1,0:T(8,128)(2,1)}, bf16[128,1024]{1,0:T(8,128)(2,1)S(1)}, u32[]{:S(2)}, u32[]{:S(2)}) collective-permute-start(bf16[128,1024]{1,0:T(8,128)(2,1)} %get-tuple-element.257.refs_11_), channel_id=1, source_target_pairs={{0,8},{4,12},{8,0},{12,4},{16,24},{20,28},{24,16},{28,20},{1,9},{5... | collective-permute-start | bytes 786440 | tf_op jit(solution)/shard_map/ppermute | solution.py:105
  399.8 35.7 %collective-permute-start.33 = (bf16[512,1024]{1,0:T(8,128)(2,1)}, bf16[512,1024]{1,0:T(8,128)(2,1)}, u32[]{:S(2)}, u32[]{:S(2)}) collective-permute-start(bf16[512,1024]{1,0:T(8,128)(2,1)} %get-tuple-element.264.refs_14_), channel_id=1, source_target_pairs={{0,4},{4,0},{8,12},{12,8},{16,20},{20,16},{24,28},{28,24},{1,5},{5... | collective-permute-start | bytes 3145736 | tf_op jit(solution)/shard_map/ppermute | solution.py:105
  439.0 40.5 %collective-permute-start.37 = (bf16[128,1024]{1,0:T(8,128)(2,1)}, bf16[128,1024]{1,0:T(8,128)(2,1)S(1)}, u32[]{:S(2)}, u32[]{:S(2)}) collective-permute-start(bf16[128,1024]{1,0:T(8,128)(2,1)} %get-tuple-element.279.refs_13_), channel_id=1, source_target_pairs={{0,24},{4,28},{8,16},{12,20},{16,8},{20,12},{24,0},{28,4},{1,25},{... | collective-permute-start | bytes 786440 | tf_op jit(solution)/shard_map/ppermute | solution.py:105
  442.6 36.9 %collective-permute-start.36 = (bf16[128,1024]{1,0:T(8,128)(2,1)}, bf16[128,1024]{1,0:T(8,128)(2,1)S(1)}, u32[]{:S(2)}, u32[]{:S(2)}) collective-permute-start(bf16[128,1024]{1,0:T(8,128)(2,1)} %get-tuple-element.277.refs_12_), channel_id=1, source_target_pairs={{0,16},{4,20},{8,24},{12,28},{16,0},{20,4},{24,8},{28,12},{1,17},{... | collective-permute-start | bytes 786440 | tf_op jit(solution)/shard_map/ppermute | solution.py:105
  442.6 36.9 %collective-permute-start.35 = (bf16[128,1024]{1,0:T(8,128)(2,1)}, bf16[128,1024]{1,0:T(8,128)(2,1)S(1)}, u32[]{:S(2)}, u32[]{:S(2)}) collective-permute-start(bf16[128,1024]{1,0:T(8,128)(2,1)} %get-tuple-element.274.refs_11_), channel_id=1, source_target_pairs={{0,8},{4,12},{8,0},{12,4},{16,24},{20,28},{24,16},{28,20},{1,9},{5... | collective-permute-start | bytes 786440 | tf_op jit(solution)/shard_map/ppermute | solution.py:105
  447.7 46.5 %collective-permute-start.38 = (bf16[4096,256]{1,0:T(8,128)(2,1)}, bf16[4096,256]{1,0:T(8,128)(2,1)}, u32[]{:S(2)}, u32[]{:S(2)}) collective-permute-start(bf16[4096,256]{1,0:T(8,128)(2,1)} %add.259.refs_15_), channel_id=1, source_target_pairs={{0,2},{1,3},{2,0},{3,1},{4,6},{5,7},{6,4},{7,5},{8,10},{9,11},{10,... | collective-permute-start | bytes 6291464 | tf_op jit(solution)/shard_map/ppermute | solution.py:105
  479.4 46.3 %collective-permute-start.42 = (bf16[4096,256]{1,0:T(8,128)(2,1)}, bf16[4096,256]{1,0:T(8,128)(2,1)}, u32[]{:S(2)}, u32[]{:S(2)}) collective-permute-start(bf16[4096,256]{1,0:T(8,128)(2,1)} %bitcast.133), channel_id=1, source_target_pairs={{0,1},{1,0},{2,3},{3,2},{4,5},{5,4},{6,7},{7,6},{8,9},{9,8},{10,11... | collective-permute-start | bytes 6291464 | tf_op jit(solution)/shard_map/ppermute | solution.py:105
  483.0 42.6 %collective-permute-start.41 = (bf16[128,1024]{1,0:T(8,128)(2,1)}, bf16[128,1024]{1,0:T(8,128)(2,1)S(1)}, u32[]{:S(2)}, u32[]{:S(2)}) collective-permute-start(bf16[128,1024]{1,0:T(8,128)(2,1)} %add.260.refs_8_.refs_0_), channel_id=1, source_target_pairs={{0,24},{4,28},{8,16},{12,20},{16,8},{20,12},{24,0},{28,4},{1,25},{... | collective-permute-start | bytes 786440 | tf_op jit(solution)/shard_map/ppermute | solution.py:105
  486.7 38.9 %collective-permute-start.40 = (bf16[128,1024]{1,0:T(8,128)(2,1)}, bf16[128,1024]{1,0:T(8,128)(2,1)S(1)}, u32[]{:S(2)}, u32[]{:S(2)}) collective-permute-start(bf16[128,1024]{1,0:T(8,128)(2,1)} %add.260.refs_8_.refs_0_), channel_id=1, source_target_pairs={{0,16},{4,20},{8,24},{12,28},{16,0},{20,4},{24,8},{28,12},{1,17},{... | collective-permute-start | bytes 786440 | tf_op jit(solution)/shard_map/ppermute | solution.py:105
  486.7 38.9 %collective-permute-start.39 = (bf16[128,1024]{1,0:T(8,128)(2,1)}, bf16[128,1024]{1,0:T(8,128)(2,1)S(1)}, u32[]{:S(2)}, u32[]{:S(2)}) collective-permute-start(bf16[128,1024]{1,0:T(8,128)(2,1)} %add.260.refs_8_.refs_0_), channel_id=1, source_target_pairs={{0,8},{4,12},{8,0},{12,4},{16,24},{20,28},{24,16},{28,20},{1,9},{5... | collective-permute-start | bytes 786440 | tf_op jit(solution)/shard_map/ppermute | solution.py:105
  530.8 31.7 %collective-permute-start.43 = (bf16[2048,256]{1,0:T(8,128)(2,1)}, bf16[2048,256]{1,0:T(8,128)(2,1)}, u32[]{:S(2)}, u32[]{:S(2)}) collective-permute-start(bf16[2048,256]{1,0:T(8,128)(2,1)} %get-tuple-element.298.refs_14_), channel_id=1, source_target_pairs={{0,4},{4,0},{8,12},{12,8},{16,20},{20,16},{24,28},{28,24},{1,5},{5... | collective-permute-start | bytes 3145736 | tf_op jit(solution)/shard_map/ppermute | solution.py:105
  535.0 27.4 %copy-start.5 = (s32[64,64]{1,0:T(8,128)S(1)}, s32[64,64]{1,0:T(8,128)}, u32[]{:S(2)}) copy-start(s32[64,64]{1,0:T(8,128)} %copy-done.4) | copy-start | bytes 49156
  535.0 35.4 %copy-start.21 = (f32[8,4,1024]{2,1,0:T(4,128)S(1)}, f32[8,4,1024]{2,1,0:T(4,128)}, u32[]{:S(2)}) copy-start(f32[8,4,1024]{2,1,0:T(4,128)} %get-tuple-element.315) | copy-start | bytes 393220
  535.1 36.5 %copy-start.25 = (s32[2,4]{1,0:T(2,128)S(1)}, s32[2,4]{1,0:T(2,128)}, u32[]{:S(2)}) copy-start(s32[2,4]{1,0:T(2,128)} %copy-done.24) | copy-start | bytes 100
  561.8 46.8 %collective-permute-start.50 = (bf16[512,1024]{1,0:T(8,128)(2,1)}, bf16[512,1024]{1,0:T(8,128)(2,1)}, u32[]{:S(2)}, u32[]{:S(2)}) collective-permute-start(bf16[512,1024]{1,0:T(8,128)(2,1)} %assemble.3.refs_12_.refs_0_), channel_id=1, source_target_pairs={{0,4},{4,0},{8,12},{12,8},{16,20},{20,16},{24,28},{28,24},{1,5},{5... | collective-permute-start | bytes 3145736 | tf_op jit(solution)/shard_map/ppermute | solution.py:105
  566.1 11.4 %collective-permute-start.46 = (bf16[512,256]{1,0:T(8,128)(2,1)}, bf16[512,256]{1,0:T(8,128)(2,1)S(1)}, u32[]{:S(2)}, u32[]{:S(2)}) collective-permute-start(bf16[512,256]{1,0:T(8,128)(2,1)} %get-tuple-element.306), channel_id=1, source_target_pairs={{0,24},{4,28},{8,16},{12,20},{16,8},{20,12},{24,0},{28,4},{1,25},{... | collective-permute-start | bytes 786440 | tf_op jit(solution)/shard_map/ppermute | solution.py:105
  569.5 19.9 %collective-permute-start.45 = (bf16[512,256]{1,0:T(8,128)(2,1)}, bf16[512,256]{1,0:T(8,128)(2,1)S(1)}, u32[]{:S(2)}, u32[]{:S(2)}) collective-permute-start(bf16[512,256]{1,0:T(8,128)(2,1)} %get-tuple-element.304), channel_id=1, source_target_pairs={{0,16},{4,20},{8,24},{12,28},{16,0},{20,4},{24,8},{28,12},{1,17},{... | collective-permute-start | bytes 786440 | tf_op jit(solution)/shard_map/ppermute | solution.py:105
  569.5 19.9 %collective-permute-start.44 = (bf16[512,256]{1,0:T(8,128)(2,1)}, bf16[512,256]{1,0:T(8,128)(2,1)}, u32[]{:S(2)}, u32[]{:S(2)}) collective-permute-start(bf16[512,256]{1,0:T(8,128)(2,1)} %get-tuple-element.302), channel_id=1, source_target_pairs={{0,8},{4,12},{8,0},{12,4},{16,24},{20,28},{24,16},{28,20},{1,9},{5... | collective-permute-start | bytes 786440 | tf_op jit(solution)/shard_map/ppermute | solution.py:105
  577.5 12.0 %copy-start.15 = (bf16[512,256]{1,0:T(8,128)(2,1)}, bf16[512,256]{1,0:T(8,128)(2,1)S(1)}, u32[]{:S(2)}) copy-start(bf16[512,256]{1,0:T(8,128)(2,1)S(1)} %collective-permute-done.46.refs_3_) | copy-start | bytes 786436
  593.3 19.3 %collective-permute-start.49 = (bf16[512,256]{1,0:T(8,128)(2,1)}, bf16[512,256]{1,0:T(8,128)(2,1)S(1)}, u32[]{:S(2)}, u32[]{:S(2)}) collective-permute-start(bf16[512,256]{1,0:T(8,128)(2,1)} %add.261.refs_1_.refs_0_), channel_id=1, source_target_pairs={{0,24},{4,28},{8,16},{12,20},{16,8},{20,12},{24,0},{28,4},{1,25},{... | collective-permute-start | bytes 786440 | tf_op jit(solution)/shard_map/ppermute | solution.py:105
  595.7 20.2 %collective-permute-start.48 = (bf16[512,256]{1,0:T(8,128)(2,1)}, bf16[512,256]{1,0:T(8,128)(2,1)S(1)}, u32[]{:S(2)}, u32[]{:S(2)}) collective-permute-start(bf16[512,256]{1,0:T(8,128)(2,1)} %add.261.refs_1_.refs_0_), channel_id=1, source_target_pairs={{0,16},{4,20},{8,24},{12,28},{16,0},{20,4},{24,8},{28,12},{1,17},{... | collective-permute-start | bytes 786440 | tf_op jit(solution)/shard_map/ppermute | solution.py:105
  595.7 20.2 %collective-permute-start.47 = (bf16[512,256]{1,0:T(8,128)(2,1)}, bf16[512,256]{1,0:T(8,128)(2,1)}, u32[]{:S(2)}, u32[]{:S(2)}) collective-permute-start(bf16[512,256]{1,0:T(8,128)(2,1)} %add.261.refs_1_.refs_0_), channel_id=1, source_target_pairs={{0,8},{4,12},{8,0},{12,4},{16,24},{20,28},{24,16},{28,20},{1,9},{5... | collective-permute-start | bytes 786440 | tf_op jit(solution)/shard_map/ppermute | solution.py:105
  619.4 1.6 collective-permute-start.52
  621.1 8.4 %collective-permute-start.53 = (bf16[128,1024]{1,0:T(8,128)(2,1)S(1)}, bf16[128,1024]{1,0:T(8,128)(2,1)S(1)}, u32[]{:S(2)}, u32[]{:S(2)}) collective-permute-start(bf16[128,1024]{1,0:T(8,128)(2,1)S(1)} %pad_maximum_fusion.2), channel_id=1, source_target_pairs={{0,2},{1,3},{2,0},{3,1},{4,6},{5,7},{6,4},{7,5},{8,10},{9,11},{10,... | collective-permute-start | bytes 786440 | tf_op jit(solution)/shard_map/ppermute | solution.py:105
  629.6 9.3 %collective-permute-start.54 = (bf16[128,1024]{1,0:T(8,128)(2,1)S(1)}, bf16[128,1024]{1,0:T(8,128)(2,1)S(1)}, u32[]{:S(2)}, u32[]{:S(2)}) collective-permute-start(bf16[128,1024]{1,0:T(8,128)(2,1)S(1)} %pad_maximum_fusion.3), channel_id=1, source_target_pairs={{0,4},{4,0},{8,12},{12,8},{16,20},{20,16},{24,28},{28,24},{1,5},{5... | collective-permute-start | bytes 786440 | tf_op jit(solution)/shard_map/ppermute | solution.py:105
  631.2 28.6 %collective-permute-start.51 = (bf16[2048,256]{1,0:T(8,128)(2,1)}, bf16[2048,256]{1,0:T(8,128)(2,1)}, u32[]{:S(2)}, u32[]{:S(2)}) collective-permute-start(bf16[2048,256]{1,0:T(8,128)(2,1)} %assemble.5.own_ref), channel_id=1, source_target_pairs={{0,4},{4,0},{8,12},{12,8},{16,20},{20,16},{24,28},{28,24},{1,5},{5... | collective-permute-start | bytes 3145736 | tf_op jit(solution)/shard_map/ppermute | solution.py:105
  639.1 6.4 collective-permute-start.55
  646.3 23.9 %copy-start.7 = (f32[2,8,256]{2,1,0:T(8,128)S(1)}, f32[2,8,256]{2,1,0:T(8,128)}, u32[]{:S(2)}) copy-start(f32[2,8,256]{2,1,0:T(8,128)} %copy-done.6) | copy-start | bytes 49156
  647.0 18.4 %collective-permute-start.56 = (bf16[128,1024]{1,0:T(8,128)(2,1)}, bf16[128,1024]{1,0:T(8,128)(2,1)}, u32[]{:S(2)}, u32[]{:S(2)}) collective-permute-start(bf16[128,1024]{1,0:T(8,128)(2,1)} %pad_maximum_fusion.5), channel_id=1, source_target_pairs={{0,16},{4,20},{8,24},{12,28},{16,0},{20,4},{24,8},{28,12},{1,17},{... | collective-permute-start | bytes 786440 | tf_op jit(solution)/shard_map/ppermute | solution.py:105
  (22 other events, 93.8 us)
Sparse Core Ops, SparseCore 0:
  435.6 74.2 all-gather.2

commit v7 on v6

--- a/solution.py
+++ b/solution.py
@@ -542,12 +542,12 @@
         lse_ref[window] = columns[window].T[: lse_ref.shape[1]]
 
 
-def attend_call(attn_in, weight, blocks, deps=()):
+def attend_call(attn_in, weight, blocks, deps=(), most=2):
     rows, width = attn_in.shape
     cols = weight.shape[2]
     blocks, place, heads = blocks
     windows = rows // WIN_TOK
-    per = per_step(rows)
+    per = min(most, per_step(rows))
     block = per * WIN_TOK
     stat_rows = -(-heads // 8) * 8
     return call_after(
@@ -770,7 +770,7 @@
             rest[2 * place + 1][...] = total[size:].astype(BF)
 
 
-MLP_BLOCK = 1280
+MLP_BLOCK = 640
 MLP_CHUNK = 512
 
 
@@ -966,7 +966,9 @@
     qkv, mixed, lse = {}, {}, {}
     for m in masks:
         ties = need(qkv_w, m, ties, attn_in)
-        qkv[m], mixed[m], lse[m] = attend_call(attn_in, qkv_w[m], (blocks, m, heads), ties)
+        qkv[m], mixed[m], lse[m] = attend_call(
+            attn_in, qkv_w[m], (blocks, m, heads), ties, 1 if m == n_mp - 1 else 2
+        )
         if m == 0:
             down_w = gather(down_weight, 4)
         elif m == 2 or m == n_mp - 1 == 1:

time: 692 us -> 686 us (level)
  Pallas kernels: 513 us -> 504 us
    pallas_call x17, Pallas kernels: 456 us -> 447 us  [call_after(): return lambda *args: call(*args, *deps)]
  transfers between devices with their start and end apart: 58 -> 58, of which waited for: 11 -> 12; matrix products, arithmetic and copies ran while one was open for 4% -> 4% of each run, Pallas kernels for 74% -> 73%
where the time goes in v7:
time: 686 us; the launch traced here: 679 us
  Pallas kernels  504 us (73%)
  waiting for transfers between devices  68.3 us (10%)
  starting transfers between devices  46.5 us (7%)
  matrix products  20.8 us (3%)
  local copies, waits for them, and re-layouts  18.1 us (3%)
  between operations  15.3 us (2%)
    pallas_call x17, Pallas kernels, call_after(): return lambda *args: call(*args, *deps)  447 us
    ppermute x57, waiting for transfers between devices, swap(): return lax.ppermute(value, axis, [(i, i ^ bit) for i in range(size)])  68.3 us
    ppermute x57, starting transfers between devices, swap(): return lax.ppermute(value, axis, [(i, i ^ bit) for i in range(size)])  46.5 us
    pallas_call x6, Pallas kernels, split_call(): pl.pallas_call(functools.partial(split_kernel, count=count, groups=[len(g...  25.6 us
    pallas_call x5, Pallas kernels, add_groups(): pl.pallas_call(functools.partial(sum_kernel, groups=[len(group) for group...  17.4 us
  transfers between devices with their start and end apart: 58, of which 12 were waited for; matrix products, arithmetic and copies ran while one was open for 4% of the time, Pallas kernels for 73%

profile of v7, /device:TPU:0, one launch (start us, length us, event | category | flops | bytes accessed | tf_op | source)
XLA Modules:
  0.0 678.9 jit_solution(16341518956319768224)
XLA Ops:
  7.8 2.6 collective-permute-start.3
  11.1 1.7 convolution_add_fusion
  12.8 2.4 fusion.6
  17.4 3.7 fusion.1
  21.2 3.6 copy.35.refs_2_.refs_5_
  24.7 3.8 collective-permute-done.1
  30.2 8.7 %norm_in.1.refs_0_.refs_3_.refs_6_ = bf16[2560,1024]{1,0:T(8,128)(2,1)} custom-call(bf16[2560,1024]{1,0:T(8,128)(2,1)} %bitcast.127, f32[8,6,1024]{2,1,0:T(8,128)} %reshape.254.refs_1_.refs_10_.refs_19_), custom_call_target="tpu_custom_call" | custom-call | flops 8000000000 | bytes 28000000 | tf_op jit(solution)/shard_map/norm_in/pallas_call | solution.py:83
  39.4 1.7 collective-permute-start.8
  41.2 16.7 %attend.4 = (bf16[3,2560,256]{2,1,0:T(8,128)(2,1)}, bf16[2560,256]{1,0:T(8,128)(2,1)}, f32[8,8,384]{2,1,0:T(8,128)}) custom-call(bf16[2560,1024]{1,0:T(8,128)(2,1)} %norm_in.1.refs_0_.refs_3_.refs_6_, bf16[3,1024,256]{2,1,0:T(8,128)(2,1)} %refs_4_.3, f32[16,9,64,64]{3,2,1,0:T(8,128)} %copy.35.refs_2_.refs_5_, bf16[2560,1024]{1,0:T(8,128)(2,1)} %norm_in.1.refs_0_.refs_3_.refs_6_), custom_call_target="tpu_custom_call" | custom-call | flops 19000000512 | bytes 66500000 | tf_op jit(solution)/shard_map/attend/pallas_call | solution.py:83
  58.1 16.7 %attend.5 = (bf16[3,2560,256]{2,1,0:T(8,128)(2,1)}, bf16[2560,256]{1,0:T(8,128)(2,1)}, f32[8,8,384]{2,1,0:T(8,128)}) custom-call(bf16[2560,1024]{1,0:T(8,128)(2,1)} %norm_in.1.refs_0_.refs_3_.refs_6_, bf16[3,1024,256]{2,1,0:T(8,128)(2,1)} %collective-permute-done.5.refs_1_.refs_5_, f32[16,9,64,64]{3,2,1,0:T(8,128)} %copy.35.refs_2_.refs_5_, ...), custom_call_target="tpu_custom_call" | custom-call | flops 19000000512 | bytes 66500000 | tf_op jit(solution)/shard_map/attend/pallas_call | solution.py:83
  75.4 16.7 %attend.6 = (bf16[3,2560,256]{2,1,0:T(8,128)(2,1)}, bf16[2560,256]{1,0:T(8,128)(2,1)}, f32[8,8,384]{2,1,0:T(8,128)}) custom-call(bf16[2560,1024]{1,0:T(8,128)(2,1)} %norm_in.1.refs_0_.refs_3_.refs_6_, bf16[3,1024,256]{2,1,0:T(8,128)(2,1)} %collective-permute-done.6.refs_1_.refs_3_.refs_6_, f32[16,9,64,64]{3,2,1,0:T(8,128)} %copy.35.refs_2_.refs_5_, ...), custom_call_target="tpu_custom_call" | custom-call | flops 19000000512 | bytes 66500000 | tf_op jit(solution)/shard_map/attend/pallas_call | solution.py:83
  92.7 19.7 %attend.7 = (bf16[3,2560,256]{2,1,0:T(8,128)(2,1)}, bf16[2560,256]{1,0:T(8,128)(2,1)}, f32[8,8,384]{2,1,0:T(8,128)}) custom-call(bf16[2560,1024]{1,0:T(8,128)(2,1)} %norm_in.1.refs_0_.refs_3_.refs_6_, bf16[3,1024,256]{2,1,0:T(8,128)(2,1)} %collective-permute-done.7.refs_1_.refs_7_, f32[16,9,64,64]{3,2,1,0:T(8,128)} %copy.35.refs_2_.refs_5_, ...), custom_call_target="tpu_custom_call" | custom-call | flops 19000000512 | bytes 66500000 | tf_op jit(solution)/shard_map/attend/pallas_call | solution.py:83
  112.3 1.8 collective-permute-start.11
  114.1 15.6 %middle.1 = (bf16[2560,1024]{1,0:T(8,128)(2,1)}, bf16[2560,1024]{1,0:T(8,128)(2,1)}, bf16[2560,1024]{1,0:T(8,128)(2,1)}) custom-call(bf16[2560,256]{1,0:T(8,128)(2,1)} %get-tuple-element.164.refs_3_.refs_0_, bf16[2560,256]{1,0:T(8,128)(2,1)} %get-tuple-element.166.refs_4_.refs_1_.refs_3_, bf16[2560,256]{1,0:T(8,128)(2,1)} %get-tuple-element.168.refs_4_.refs_2_.refs_3_, ...), custom_call_target="tpu_custom_call" | custom-call | flops 16000000000 | bytes 56000000 | tf_op jit(solution)/shard_map/middle/pallas_call | solution.py:83
  129.8 32.8 %mlp.4 = (bf16[2560,1024]{1,0:T(8,128)(2,1)}, bf16[2560,1024]{1,0:T(8,128)(2,1)}, bf16[512,1024]{1,0:T(8,128)(2,1)}, bf16[512,1024]{1,0:T(8,128)(2,1)}, bf16[512...) custom-call(bf16[2560,1024]{1,0:T(8,128)(2,1)} %get-tuple-element.174.refs_0_.refs_5_, ...), custom_call_target="tpu_custom_call" | custom-call | flops 30000001024 | bytes 105000000 | tf_op jit(solution)/shard_map/mlp/pallas_call | solution.py:83
  162.7 3.1 collective-permute-done.11.refs_4_.refs_2_.refs_14_
  166.8 3.5 collective-permute-done.15.refs_2_.refs_15_
  170.3 32.9 %mlp.5 = (bf16[2560,1024]{1,0:T(8,128)(2,1)}, bf16[2560,1024]{1,0:T(8,128)(2,1)}, bf16[512,1024]{1,0:T(8,128)(2,1)}, bf16[512,1024]{1,0:T(8,128)(2,1)}, bf16[512...) custom-call(bf16[2560,1024]{1,0:T(8,128)(2,1)} %get-tuple-element.174.refs_0_.refs_5_, ...), custom_call_target="tpu_custom_call" | custom-call | flops 30000001024 | bytes 105000000 | tf_op jit(solution)/shard_map/mlp/pallas_call | solution.py:83
  204.2 32.9 %mlp.6 = (bf16[2560,1024]{1,0:T(8,128)(2,1)}, bf16[2560,1024]{1,0:T(8,128)(2,1)}, bf16[512,1024]{1,0:T(8,128)(2,1)}, bf16[512,1024]{1,0:T(8,128)(2,1)}, bf16[512...) custom-call(bf16[2560,1024]{1,0:T(8,128)(2,1)} %get-tuple-element.174.refs_0_.refs_5_, ...), custom_call_target="tpu_custom_call" | custom-call | flops 30000001024 | bytes 105000000 | tf_op jit(solution)/shard_map/mlp/pallas_call | solution.py:83
  237.2 5.8 add.257
  243.7 33.0 %mlp.7 = (bf16[2560,1024]{1,0:T(8,128)(2,1)}, bf16[2560,1024]{1,0:T(8,128)(2,1)}, bf16[512,1024]{1,0:T(8,128)(2,1)}, bf16[512,1024]{1,0:T(8,128)(2,1)}, bf16[512...) custom-call(bf16[2560,1024]{1,0:T(8,128)(2,1)} %get-tuple-element.174.refs_0_.refs_5_, ...), custom_call_target="tpu_custom_call" | custom-call | flops 30000001024 | bytes 105000000 | tf_op jit(solution)/shard_map/mlp/pallas_call | solution.py:83
  276.7 1.5 collective-permute-start.26
  278.8 63.2 %mlp_out.1 = (bf16[2560,1024]{1,0:T(8,128)(2,1)}, bf16[2560,1024]{1,0:T(8,128)(2,1)}, bf16[2560,1024]{1,0:T(8,128)(2,1)}, f32[8,4,1024]{2,1,0:T(4,128)}) custom-call(bf16[2560,1024]{1,0:T(8,128)(2,1)} %get-tuple-element.214.refs_0_, bf16[2560,1024]{1,0:T(8,128)(2,1)} %get-tuple-element.215.refs_1_, bf16[2560,1024]{1,0:T(8,128)(2,1)} %get-tuple-element.216.refs_2_, ...), custom_call_target="tpu_custom_call" | custom-call | flops 54999998464 | bytes 192500000 | tf_op jit(solution)/shard_map/mlp_out/pallas_call | solution.py:83
  343.5 4.9 split.6
  348.3 1.5 collective-permute-start.29
  349.9 31.3 %attend_back.4 = (bf16[3,2560,256]{2,1,0:T(8,128)(2,1)}, f32[16,9,64,64]{3,2,1,0:T(8,128)}, bf16[4,1024,256]{2,1,0:T(8,128)(2,1)}) custom-call(bf16[2560,1024]{1,0:T(8,128)(2,1)} %get-tuple-element.227.refs_0_.refs_10_, bf16[256,1024]{1,0:T(8,128)(2,1)} %collective-permute-done.10.refs_7_.refs_1_, bf16[3,2560,256]{2,1,0:T(8,128)(2,1)} %get-tuple-element.234.refs_2_, ...), custom_call_target="tpu_custom_call" | custom-call | flops 30000001024 | bytes 105000000 | tf_op jit(solution)/shard_map/attend_back/pallas_call | solution.py:83
  381.3 3.6 split.7
  384.8 4.9 split.8
  389.8 3.6 collective-permute-start.32
  394.7 31.6 %attend_back.5 = (bf16[3,2560,256]{2,1,0:T(8,128)(2,1)}, f32[16,9,64,64]{3,2,1,0:T(8,128)}, bf16[4,1024,256]{2,1,0:T(8,128)(2,1)}) custom-call(bf16[2560,1024]{1,0:T(8,128)(2,1)} %get-tuple-element.227.refs_0_.refs_10_, bf16[256,1024]{1,0:T(8,128)(2,1)} %collective-permute-done.8.refs_3_.refs_6_.refs_1_, ...), custom_call_target="tpu_custom_call", output_to_operand_aliasing={{1}: (7, {})} | custom-call | flops 30000001024 | bytes 105000000 | tf_op jit(solution)/shard_map/attend_back/pallas_call | solution.py:83
  427.8 2.0 add.258.refs_2_.refs_8_
  429.8 3.5 split.9
  433.4 3.6 collective-permute-start.37
  437.7 4.3 add.259.refs_15_
  442.7 31.2 %attend_back.6 = (bf16[3,2560,256]{2,1,0:T(8,128)(2,1)}, f32[16,9,64,64]{3,2,1,0:T(8,128)}, bf16[4,1024,256]{2,1,0:T(8,128)(2,1)}) custom-call(bf16[2560,1024]{1,0:T(8,128)(2,1)} %get-tuple-element.227.refs_0_.refs_10_, bf16[256,1024]{1,0:T(8,128)(2,1)} %collective-permute-done.9.refs_5_.refs_1_, ...), custom_call_target="tpu_custom_call", output_to_operand_aliasing={{1}: (7, {})} | custom-call | flops 30000001024 | bytes 105000000 | tf_op jit(solution)/shard_map/attend_back/pallas_call | solution.py:83
  475.5 2.0 add.260.refs_8_.refs_0_
  477.5 3.6 collective-permute-start.41
  481.9 6.7 collective-permute-done.38.refs_9_.refs_0_
  488.6 31.3 %attend_back.7 = (bf16[3,2560,256]{2,1,0:T(8,128)(2,1)}, f32[16,9,64,64]{3,2,1,0:T(8,128)}, bf16[4,1024,256]{2,1,0:T(8,128)(2,1)}) custom-call(bf16[2560,1024]{1,0:T(8,128)(2,1)} %get-tuple-element.227.refs_0_.refs_10_, bf16[256,1024]{1,0:T(8,128)(2,1)} %refs_1_.3, ...), custom_call_target="tpu_custom_call", output_to_operand_aliasing={{1}: (7, {})} | custom-call | flops 30000001024 | bytes 105000000 | tf_op jit(solution)/shard_map/attend_back/pallas_call | solution.py:83
  520.0 5.2 split.10
  526.6 2.8 assemble.3.refs_12_.refs_0_
  529.4 26.8 %last.1 = (bf16[2560,1024]{1,0:T(8,128)(2,1)}, f32[8,2,1024]{2,1,0:T(2,128)}) custom-call(bf16[3,2560,256]{2,1,0:T(8,128)(2,1)} %get-tuple-element.283.refs_0_, bf16[3,2560,256]{2,1,0:T(8,128)(2,1)} %get-tuple-element.284.refs_1_, bf16[3,2560,256]{2,1,0:T(8,128)(2,1)} %get-tuple-element.285.refs_2_, bf16[3,2560,256]{2,1,0:T(8,128)(2,1)} %get-tuple-element.286.refs_3_, ...), custom_call_target="tpu_custom_call" | custom-call | flops 28000000000 | bytes 98000000 | tf_op jit(solution)/shard_map/last/pallas_call | solution.py:83
  557.0 3.5 split.11
  560.5 3.4 collective-permute-start.46
  566.6 5.3 reshape.265
  571.9 11.9 %collective-permute-done.45.refs_2_ = bf16[512,256]{1,0:T(8,128)(2,1)S(1)} collective-permute-done((bf16[512,256]{1,0:T(8,128)(2,1)}, bf16[512,256]{1,0:T(8,128)(2,1)S(1)}, u32[]{:S(2)}, u32[]{:S(2)}) %collective-permute-start.45) | collective-permute-done | bytes 262176 | tf_op jit(solution)/shard_map/ppermute | solution.py:105
  584.5 3.2 add.261.refs_1_.refs_0_
  587.7 2.4 collective-permute-start.49
  590.1 2.0 collective-permute-start.47
  592.1 4.1 fusion.3
  597.0 6.0 unfold.1.refs_4_
  603.1 4.0 assemble.4.refs_5_
  607.1 3.2 collective-permute-done.48.refs_2_
  611.0 2.7 assemble.5.own_ref
  613.8 1.5 collective-permute-done.52
  616.1 7.8 %collective-permute-done.53 = bf16[128,1024]{1,0:T(8,128)(2,1)S(1)} collective-permute-done((bf16[128,1024]{1,0:T(8,128)(2,1)S(1)}, bf16[128,1024]{1,0:T(8,128)(2,1)S(1)}, u32[]{:S(2)}, u32[]{:S(2)}) %collective-permute-start.53) | collective-permute-done | bytes 262176 | tf_op jit(solution)/shard_map/ppermute | solution.py:105
  624.0 1.5 collective-permute-start.54
  626.1 7.2 %collective-permute-done.54 = bf16[128,1024]{1,0:T(8,128)(2,1)S(1)} collective-permute-done((bf16[128,1024]{1,0:T(8,128)(2,1)S(1)}, bf16[128,1024]{1,0:T(8,128)(2,1)S(1)}, u32[]{:S(2)}, u32[]{:S(2)}) %collective-permute-start.54) | collective-permute-done | bytes 262176 | tf_op jit(solution)/shard_map/ppermute | solution.py:105
  633.5 6.4 collective-permute-done.55
  642.2 12.0 %collective-permute-done.51.other_ref = bf16[2048,256]{1,0:T(8,128)(2,1)} collective-permute-done((bf16[2048,256]{1,0:T(8,128)(2,1)}, bf16[2048,256]{1,0:T(8,128)(2,1)}, u32[]{:S(2)}, u32[]{:S(2)}) %collective-permute-start.51) | collective-permute-done | bytes 1048608 | tf_op jit(solution)/shard_map/ppermute | solution.py:105
  654.2 4.7 attention_grads.1
  661.1 2.8 fusion.4
  664.6 3.7 convolution_bitcast_fusion
  669.9 1.6 convolution_bitcast_fusion.1
  (196 shorter events, 33.9 us)
Async XLA Ops:
  7.2 522.2 %all-gather.3.cloned.1.call-start = ((), (), s32[]{:S(2)}) async-start(), calls=%async_computation | async-start | bytes 2359296 | tf_op jit(solution)/shard_map/all_gather | solution.py:414
  7.2 8.7 %collective-permute-start.2 = (f32[4,2025]{1,0:T(4,128)}, f32[4,2025]{1,0:T(4,128)S(1)}, u32[]{:S(2)}, u32[]{:S(2)}) collective-permute-start(f32[4,2025]{1,0:T(4,128)} %param.19), channel_id=1, source_target_pairs={{0,1},{1,0},{2,3},{3,2},{4,5},{5,4},{6,7},{7,6},{8,9},{9,8},{10,11... | collective-permute-start | bytes 97208 | tf_op jit(solution)/shard_map/ppermute | solution.py:105
  7.8 7.7 %collective-permute-start.3 = (f32[4,2025]{1,0:T(4,128)}, f32[4,2025]{1,0:T(4,128)S(1)}, u32[]{:S(2)}, u32[]{:S(2)}) collective-permute-start(f32[4,2025]{1,0:T(4,128)} %param.19), channel_id=1, source_target_pairs={{0,2},{1,3},{2,0},{3,1},{4,6},{5,7},{6,4},{7,5},{8,10},{9,11},{10,... | collective-permute-start | bytes 97208 | tf_op jit(solution)/shard_map/ppermute | solution.py:105
  15.2 2.1 collective-permute-start
  15.5 1.5 collective-permute-start.4
  16.0 13.0 %copy-start.24 = (s32[2,4]{1,0:T(2,128)}, s32[2,4]{1,0:T(2,128)S(1)}, u32[]{:S(2)}) copy-start(s32[2,4]{1,0:T(2,128)S(1)} %constant_dynamic-slice_fusion) | copy-start | bytes 100
  17.3 11.3 %collective-permute-start.1 = (f32[2,8,6144]{2,1,0:T(8,128)S(1)}, f32[2,8,6144]{2,1,0:T(8,128)S(1)}, u32[]{:S(2)}, u32[]{:S(2)}) collective-permute-start(f32[2,8,6144]{2,1,0:T(8,128)S(1)} %add.163), channel_id=1, source_target_pairs={{0,2},{1,3},{2,0},{3,1},{4,6},{5,7},{6,4},{7,5},{8,10},{9,11},{10,... | collective-permute-start | bytes 1179656 | tf_op jit(solution)/shard_map/ppermute | solution.py:105
  28.6 46.2 %collective-permute-start.6 = (bf16[3,1024,256]{2,1,0:T(8,128)(2,1)}, bf16[3,1024,256]{2,1,0:T(8,128)(2,1)}, u32[]{:S(2)}, u32[]{:S(2)}) collective-permute-start(bf16[3,1024,256]{2,1,0:T(8,128)(2,1)} %refs_4_.3), channel_id=1, source_target_pairs={{0,2},{1,3},{2,0},{3,1},{4,6},{5,7},{6,4},{7,5},{8,10},{9,11},{10,... | collective-permute-start | bytes 4718600 | tf_op jit(solution)/shard_map/ppermute | solution.py:105
  29.0 29.2 %collective-permute-start.5 = (bf16[3,1024,256]{2,1,0:T(8,128)(2,1)}, bf16[3,1024,256]{2,1,0:T(8,128)(2,1)}, u32[]{:S(2)}, u32[]{:S(2)}) collective-permute-start(bf16[3,1024,256]{2,1,0:T(8,128)(2,1)} %refs_4_.3), channel_id=1, source_target_pairs={{0,1},{1,0},{2,3},{3,2},{4,5},{5,4},{6,7},{7,6},{8,9},{9,8},{10,11... | collective-permute-start | bytes 4718600 | tf_op jit(solution)/shard_map/ppermute | solution.py:105
  38.9 73.4 %collective-permute-start.9 = (bf16[256,1024]{1,0:T(8,128)(2,1)S(1)}, bf16[256,1024]{1,0:T(8,128)(2,1)}, u32[]{:S(2)}, u32[]{:S(2)}) collective-permute-start(bf16[256,1024]{1,0:T(8,128)(2,1)S(1)} %copy-done.27), channel_id=1, source_target_pairs={{0,1},{1,0},{2,3},{3,2},{4,5},{5,4},{6,7},{7,6},{8,9},{9,8},{10,11... | collective-permute-start | bytes 1572872 | tf_op jit(solution)/shard_map/ppermute | solution.py:105
  39.4 52.7 %collective-permute-start.8 = (bf16[256,1024]{1,0:T(8,128)(2,1)S(1)}, bf16[256,1024]{1,0:T(8,128)(2,1)}, u32[]{:S(2)}, u32[]{:S(2)}) collective-permute-start(bf16[256,1024]{1,0:T(8,128)(2,1)S(1)} %copy-done.27), channel_id=1, source_target_pairs={{0,2},{1,3},{2,0},{3,1},{4,6},{5,7},{6,4},{7,5},{8,10},{9,11},{10,... | collective-permute-start | bytes 1572872 | tf_op jit(solution)/shard_map/ppermute | solution.py:105
  57.8 71.9 %collective-permute-start.14 = (bf16[1024,1024]{1,0:T(8,128)(2,1)}, bf16[1024,1024]{1,0:T(8,128)(2,1)}, u32[]{:S(2)}, u32[]{:S(2)}) collective-permute-start(bf16[1024,1024]{1,0:T(8,128)(2,1)} %refs_8_.1), channel_id=1, source_target_pairs={{0,2},{1,3},{2,0},{3,1},{4,6},{5,7},{6,4},{7,5},{8,10},{9,11},{10,... | collective-permute-start | bytes 6291464 | tf_op jit(solution)/shard_map/ppermute | solution.py:105
  58.1 71.7 %collective-permute-start.13 = (bf16[1024,1024]{1,0:T(8,128)(2,1)}, bf16[1024,1024]{1,0:T(8,128)(2,1)}, u32[]{:S(2)}, u32[]{:S(2)}) collective-permute-start(bf16[1024,1024]{1,0:T(8,128)(2,1)} %refs_8_.1), channel_id=1, source_target_pairs={{0,1},{1,0},{2,3},{3,2},{4,5},{5,4},{6,7},{7,6},{8,9},{9,8},{10,11... | collective-permute-start | bytes 6291464 | tf_op jit(solution)/shard_map/ppermute | solution.py:105
  74.8 17.4 %collective-permute-start.7 = (bf16[3,1024,256]{2,1,0:T(8,128)(2,1)}, bf16[3,1024,256]{2,1,0:T(8,128)(2,1)}, u32[]{:S(2)}, u32[]{:S(2)}) collective-permute-start(bf16[3,1024,256]{2,1,0:T(8,128)(2,1)} %collective-permute-done.6.refs_1_.refs_3_.refs_6_), channel_id=1, source_target_pairs={{0,1},{1,0},{2,3},{3,2},{4,5},{5,4},{6,7},{7,6},{8,9},{9,8},{10,11... | collective-permute-start | bytes 4718600 | tf_op jit(solution)/shard_map/ppermute | solution.py:105
  92.1 22.0 %collective-permute-start.10 = (bf16[256,1024]{1,0:T(8,128)(2,1)}, bf16[256,1024]{1,0:T(8,128)(2,1)}, u32[]{:S(2)}, u32[]{:S(2)}) collective-permute-start(bf16[256,1024]{1,0:T(8,128)(2,1)} %collective-permute-done.8.refs_3_.refs_6_.refs_1_), channel_id=1, source_target_pairs={{0,1},{1,0},{2,3},{3,2},{4,5},{5,4},{6,7},{7,6},{8,9},{9,8},{10,11... | collective-permute-start | bytes 1572872 | tf_op jit(solution)/shard_map/ppermute | solution.py:105
  92.2 37.6 %collective-permute-start.12 = (bf16[1024,1024]{1,0:T(8,128)(2,1)}, bf16[1024,1024]{1,0:T(8,128)(2,1)}, u32[]{:S(2)}, u32[]{:S(2)}) collective-permute-start(bf16[1024,1024]{1,0:T(8,128)(2,1)} %refs_12_.1), channel_id=1, source_target_pairs={{0,1},{1,0},{2,3},{3,2},{4,5},{5,4},{6,7},{7,6},{8,9},{9,8},{10,11... | collective-permute-start | bytes 6291464 | tf_op jit(solution)/shard_map/ppermute | solution.py:105
  112.3 53.4 %collective-permute-start.11 = (bf16[1024,1024]{1,0:T(8,128)(2,1)}, bf16[1024,1024]{1,0:T(8,128)(2,1)}, u32[]{:S(2)}, u32[]{:S(2)}) collective-permute-start(bf16[1024,1024]{1,0:T(8,128)(2,1)} %refs_12_.1), channel_id=1, source_target_pairs={{0,2},{1,3},{2,0},{3,1},{4,6},{5,7},{6,4},{7,5},{8,10},{9,11},{10,... | collective-permute-start | bytes 6291464 | tf_op jit(solution)/shard_map/ppermute | solution.py:105
  129.7 37.0 %collective-permute-start.16 = (bf16[1024,1024]{1,0:T(8,128)(2,1)}, bf16[1024,1024]{1,0:T(8,128)(2,1)}, u32[]{:S(2)}, u32[]{:S(2)}) collective-permute-start(bf16[1024,1024]{1,0:T(8,128)(2,1)} %collective-permute-done.14.refs_4_.refs_3_.refs_10_), channel_id=1, source_target_pairs={{0,1},{1,0},{2,3},{3,2},{4,5},{5,4},{6,7},{7,6},{8,9},{9,8},{10,11... | collective-permute-start | bytes 6291464 | tf_op jit(solution)/shard_map/ppermute | solution.py:105
  165.8 4.5 collective-permute-start.15
  165.8 37.4 %collective-permute-start.18 = (bf16[512,1024]{1,0:T(8,128)(2,1)}, bf16[512,1024]{1,0:T(8,128)(2,1)}, u32[]{:S(2)}, u32[]{:S(2)}) collective-permute-start(bf16[512,1024]{1,0:T(8,128)(2,1)} %get-tuple-element.185.refs_5_), channel_id=1, source_target_pairs={{0,1},{1,0},{2,3},{3,2},{4,5},{5,4},{6,7},{7,6},{8,9},{9,8},{10,11... | collective-permute-start | bytes 3145736 | tf_op jit(solution)/shard_map/ppermute | solution.py:105
  166.3 36.9 %collective-permute-start.21 = (bf16[512,1024]{1,0:T(8,128)(2,1)}, bf16[512,1024]{1,0:T(8,128)(2,1)}, u32[]{:S(2)}, u32[]{:S(2)}) collective-permute-start(bf16[512,1024]{1,0:T(8,128)(2,1)} %get-tuple-element.194), channel_id=1, source_target_pairs={{0,1},{1,0},{2,3},{3,2},{4,5},{5,4},{6,7},{7,6},{8,9},{9,8},{10,11... | collective-permute-start | bytes 3145736 | tf_op jit(solution)/shard_map/ppermute | solution.py:105
  166.3 36.9 %collective-permute-start.20 = (bf16[512,1024]{1,0:T(8,128)(2,1)}, bf16[512,1024]{1,0:T(8,128)(2,1)}, u32[]{:S(2)}, u32[]{:S(2)}) collective-permute-start(bf16[512,1024]{1,0:T(8,128)(2,1)} %get-tuple-element.191), channel_id=1, source_target_pairs={{0,1},{1,0},{2,3},{3,2},{4,5},{5,4},{6,7},{7,6},{8,9},{9,8},{10,11... | collective-permute-start | bytes 3145736 | tf_op jit(solution)/shard_map/ppermute | solution.py:105
  166.8 36.4 %collective-permute-start.19 = (bf16[512,1024]{1,0:T(8,128)(2,1)}, bf16[512,1024]{1,0:T(8,128)(2,1)}, u32[]{:S(2)}, u32[]{:S(2)}) collective-permute-start(bf16[512,1024]{1,0:T(8,128)(2,1)} %get-tuple-element.188), channel_id=1, source_target_pairs={{0,1},{1,0},{2,3},{3,2},{4,5},{5,4},{6,7},{7,6},{8,9},{9,8},{10,11... | collective-permute-start | bytes 3145736 | tf_op jit(solution)/shard_map/ppermute | solution.py:105
  203.2 34.1 %collective-permute-start.17 = (bf16[512,1024]{1,0:T(8,128)(2,1)}, bf16[512,1024]{1,0:T(8,128)(2,1)}, u32[]{:S(2)}, u32[]{:S(2)}) collective-permute-start(bf16[512,1024]{1,0:T(8,128)(2,1)} %get-tuple-element.184.refs_8_), channel_id=1, source_target_pairs={{0,1},{1,0},{2,3},{3,2},{4,5},{5,4},{6,7},{7,6},{8,9},{9,8},{10,11... | collective-permute-start | bytes 3145736 | tf_op jit(solution)/shard_map/ppermute | solution.py:105
  203.4 33.8 %collective-permute-start.24 = (bf16[512,1024]{1,0:T(8,128)(2,1)}, bf16[512,1024]{1,0:T(8,128)(2,1)}, u32[]{:S(2)}, u32[]{:S(2)}) collective-permute-start(bf16[512,1024]{1,0:T(8,128)(2,1)} %get-tuple-element.205), channel_id=1, source_target_pairs={{0,1},{1,0},{2,3},{3,2},{4,5},{5,4},{6,7},{7,6},{8,9},{9,8},{10,11... | collective-permute-start | bytes 3145736 | tf_op jit(solution)/shard_map/ppermute | solution.py:105
  203.7 33.5 %collective-permute-start.23 = (bf16[512,1024]{1,0:T(8,128)(2,1)}, bf16[512,1024]{1,0:T(8,128)(2,1)}, u32[]{:S(2)}, u32[]{:S(2)}) collective-permute-start(bf16[512,1024]{1,0:T(8,128)(2,1)} %get-tuple-element.202), channel_id=1, source_target_pairs={{0,1},{1,0},{2,3},{3,2},{4,5},{5,4},{6,7},{7,6},{8,9},{9,8},{10,11... | collective-permute-start | bytes 3145736 | tf_op jit(solution)/shard_map/ppermute | solution.py:105
  203.9 33.3 %collective-permute-start.22 = (bf16[512,1024]{1,0:T(8,128)(2,1)}, bf16[512,1024]{1,0:T(8,128)(2,1)}, u32[]{:S(2)}, u32[]{:S(2)}) collective-permute-start(bf16[512,1024]{1,0:T(8,128)(2,1)} %get-tuple-element.199), channel_id=1, source_target_pairs={{0,1},{1,0},{2,3},{3,2},{4,5},{5,4},{6,7},{7,6},{8,9},{9,8},{10,11... | collective-permute-start | bytes 3145736 | tf_op jit(solution)/shard_map/ppermute | solution.py:105
  243.1 35.8 %collective-permute-start.25 = (bf16[512,1024]{1,0:T(8,128)(2,1)}, bf16[512,1024]{1,0:T(8,128)(2,1)}, u32[]{:S(2)}, u32[]{:S(2)}) collective-permute-start(bf16[512,1024]{1,0:T(8,128)(2,1)} %get-tuple-element.223.refs_8_), channel_id=1, source_target_pairs={{0,2},{1,3},{2,0},{3,1},{4,6},{5,7},{6,4},{7,5},{8,10},{9,11},{10,... | collective-permute-start | bytes 3145736 | tf_op jit(solution)/shard_map/ppermute | solution.py:105
  276.7 66.8 %collective-permute-start.26 = (bf16[512,1024]{1,0:T(8,128)(2,1)}, bf16[512,1024]{1,0:T(8,128)(2,1)}, u32[]{:S(2)}, u32[]{:S(2)}) collective-permute-start(bf16[512,1024]{1,0:T(8,128)(2,1)} %get-tuple-element.236.refs_9_), channel_id=1, source_target_pairs={{0,2},{1,3},{2,0},{3,1},{4,6},{5,7},{6,4},{7,5},{8,10},{9,11},{10,... | collective-permute-start | bytes 3145736 | tf_op jit(solution)/shard_map/ppermute | solution.py:105
  278.2 71.7 %collective-permute-start.27 = (bf16[512,1024]{1,0:T(8,128)(2,1)}, bf16[512,1024]{1,0:T(8,128)(2,1)}, u32[]{:S(2)}, u32[]{:S(2)}) collective-permute-start(bf16[512,1024]{1,0:T(8,128)(2,1)} %get-tuple-element.238.refs_10_), channel_id=1, source_target_pairs={{0,2},{1,3},{2,0},{3,1},{4,6},{5,7},{6,4},{7,5},{8,10},{9,11},{10,... | collective-permute-start | bytes 3145736 | tf_op jit(solution)/shard_map/ppermute | solution.py:105
  342.0 39.3 %collective-permute-start.28 = (bf16[512,1024]{1,0:T(8,128)(2,1)}, bf16[512,1024]{1,0:T(8,128)(2,1)}, u32[]{:S(2)}, u32[]{:S(2)}) collective-permute-start(bf16[512,1024]{1,0:T(8,128)(2,1)} %get-tuple-element.243.refs_11_), channel_id=1, source_target_pairs={{0,2},{1,3},{2,0},{3,1},{4,6},{5,7},{6,4},{7,5},{8,10},{9,11},{10,... | collective-permute-start | bytes 3145736 | tf_op jit(solution)/shard_map/ppermute | solution.py:105
  348.3 32.9 %collective-permute-start.29 = (bf16[512,1024]{1,0:T(8,128)(2,1)}, bf16[512,1024]{1,0:T(8,128)(2,1)}, u32[]{:S(2)}, u32[]{:S(2)}) collective-permute-start(bf16[512,1024]{1,0:T(8,128)(2,1)} %get-tuple-element.246.refs_9_), channel_id=1, source_target_pairs={{0,4},{4,0},{8,12},{12,8},{16,20},{20,16},{24,28},{28,24},{1,5},{5... | collective-permute-start | bytes 3145736 | tf_op jit(solution)/shard_map/ppermute | solution.py:105
  381.2 56.6 %collective-permute-start.34 = (bf16[4096,256]{1,0:T(8,128)(2,1)}, bf16[4096,256]{1,0:T(8,128)(2,1)}, u32[]{:S(2)}, u32[]{:S(2)}) collective-permute-start(bf16[4096,256]{1,0:T(8,128)(2,1)} %bitcast.132), channel_id=1, source_target_pairs={{0,1},{1,0},{2,3},{3,2},{4,5},{5,4},{6,7},{7,6},{8,9},{9,8},{10,11... | collective-permute-start | bytes 6291464 | tf_op jit(solution)/shard_map/ppermute | solution.py:105
  389.8 36.5 %collective-permute-start.32 = (bf16[128,1024]{1,0:T(8,128)(2,1)}, bf16[128,1024]{1,0:T(8,128)(2,1)S(1)}, u32[]{:S(2)}, u32[]{:S(2)}) collective-permute-start(bf16[128,1024]{1,0:T(8,128)(2,1)} %get-tuple-element.262.refs_13_), channel_id=1, source_target_pairs={{0,24},{4,28},{8,16},{12,20},{16,8},{20,12},{24,0},{28,4},{1,25},{... | collective-permute-start | bytes 786440 | tf_op jit(solution)/shard_map/ppermute | solution.py:105
  393.3 32.9 %collective-permute-start.31 = (bf16[128,1024]{1,0:T(8,128)(2,1)}, bf16[128,1024]{1,0:T(8,128)(2,1)S(1)}, u32[]{:S(2)}, u32[]{:S(2)}) collective-permute-start(bf16[128,1024]{1,0:T(8,128)(2,1)} %get-tuple-element.260.refs_12_), channel_id=1, source_target_pairs={{0,16},{4,20},{8,24},{12,28},{16,0},{20,4},{24,8},{28,12},{1,17},{... | collective-permute-start | bytes 786440 | tf_op jit(solution)/shard_map/ppermute | solution.py:105
  393.3 32.9 %collective-permute-start.30 = (bf16[128,1024]{1,0:T(8,128)(2,1)}, bf16[128,1024]{1,0:T(8,128)(2,1)S(1)}, u32[]{:S(2)}, u32[]{:S(2)}) collective-permute-start(bf16[128,1024]{1,0:T(8,128)(2,1)} %get-tuple-element.257.refs_11_), channel_id=1, source_target_pairs={{0,8},{4,12},{8,0},{12,4},{16,24},{20,28},{24,16},{28,20},{1,9},{5... | collective-permute-start | bytes 786440 | tf_op jit(solution)/shard_map/ppermute | solution.py:105
  394.2 35.7 %collective-permute-start.33 = (bf16[512,1024]{1,0:T(8,128)(2,1)}, bf16[512,1024]{1,0:T(8,128)(2,1)}, u32[]{:S(2)}, u32[]{:S(2)}) collective-permute-start(bf16[512,1024]{1,0:T(8,128)(2,1)} %get-tuple-element.264.refs_14_), channel_id=1, source_target_pairs={{0,4},{4,0},{8,12},{12,8},{16,20},{20,16},{24,28},{28,24},{1,5},{5... | collective-permute-start | bytes 3145736 | tf_op jit(solution)/shard_map/ppermute | solution.py:105
  433.4 40.6 %collective-permute-start.37 = (bf16[128,1024]{1,0:T(8,128)(2,1)}, bf16[128,1024]{1,0:T(8,128)(2,1)S(1)}, u32[]{:S(2)}, u32[]{:S(2)}) collective-permute-start(bf16[128,1024]{1,0:T(8,128)(2,1)} %get-tuple-element.279.refs_13_), channel_id=1, source_target_pairs={{0,24},{4,28},{8,16},{12,20},{16,8},{20,12},{24,0},{28,4},{1,25},{... | collective-permute-start | bytes 786440 | tf_op jit(solution)/shard_map/ppermute | solution.py:105
  437.0 37.0 %collective-permute-start.36 = (bf16[128,1024]{1,0:T(8,128)(2,1)}, bf16[128,1024]{1,0:T(8,128)(2,1)S(1)}, u32[]{:S(2)}, u32[]{:S(2)}) collective-permute-start(bf16[128,1024]{1,0:T(8,128)(2,1)} %get-tuple-element.277.refs_12_), channel_id=1, source_target_pairs={{0,16},{4,20},{8,24},{12,28},{16,0},{20,4},{24,8},{28,12},{1,17},{... | collective-permute-start | bytes 786440 | tf_op jit(solution)/shard_map/ppermute | solution.py:105
  437.0 37.0 %collective-permute-start.35 = (bf16[128,1024]{1,0:T(8,128)(2,1)}, bf16[128,1024]{1,0:T(8,128)(2,1)S(1)}, u32[]{:S(2)}, u32[]{:S(2)}) collective-permute-start(bf16[128,1024]{1,0:T(8,128)(2,1)} %get-tuple-element.274.refs_11_), channel_id=1, source_target_pairs={{0,8},{4,12},{8,0},{12,4},{16,24},{20,28},{24,16},{28,20},{1,9},{5... | collective-permute-start | bytes 786440 | tf_op jit(solution)/shard_map/ppermute | solution.py:105
  442.1 46.6 %collective-permute-start.38 = (bf16[4096,256]{1,0:T(8,128)(2,1)}, bf16[4096,256]{1,0:T(8,128)(2,1)}, u32[]{:S(2)}, u32[]{:S(2)}) collective-permute-start(bf16[4096,256]{1,0:T(8,128)(2,1)} %add.259.refs_15_), channel_id=1, source_target_pairs={{0,2},{1,3},{2,0},{3,1},{4,6},{5,7},{6,4},{7,5},{8,10},{9,11},{10,... | collective-permute-start | bytes 6291464 | tf_op jit(solution)/shard_map/ppermute | solution.py:105
  473.9 46.1 %collective-permute-start.42 = (bf16[4096,256]{1,0:T(8,128)(2,1)}, bf16[4096,256]{1,0:T(8,128)(2,1)}, u32[]{:S(2)}, u32[]{:S(2)}) collective-permute-start(bf16[4096,256]{1,0:T(8,128)(2,1)} %bitcast.133), channel_id=1, source_target_pairs={{0,1},{1,0},{2,3},{3,2},{4,5},{5,4},{6,7},{7,6},{8,9},{9,8},{10,11... | collective-permute-start | bytes 6291464 | tf_op jit(solution)/shard_map/ppermute | solution.py:105
  477.5 42.5 %collective-permute-start.41 = (bf16[128,1024]{1,0:T(8,128)(2,1)}, bf16[128,1024]{1,0:T(8,128)(2,1)S(1)}, u32[]{:S(2)}, u32[]{:S(2)}) collective-permute-start(bf16[128,1024]{1,0:T(8,128)(2,1)} %add.260.refs_8_.refs_0_), channel_id=1, source_target_pairs={{0,24},{4,28},{8,16},{12,20},{16,8},{20,12},{24,0},{28,4},{1,25},{... | collective-permute-start | bytes 786440 | tf_op jit(solution)/shard_map/ppermute | solution.py:105
  481.1 38.9 %collective-permute-start.40 = (bf16[128,1024]{1,0:T(8,128)(2,1)}, bf16[128,1024]{1,0:T(8,128)(2,1)S(1)}, u32[]{:S(2)}, u32[]{:S(2)}) collective-permute-start(bf16[128,1024]{1,0:T(8,128)(2,1)} %add.260.refs_8_.refs_0_), channel_id=1, source_target_pairs={{0,16},{4,20},{8,24},{12,28},{16,0},{20,4},{24,8},{28,12},{1,17},{... | collective-permute-start | bytes 786440 | tf_op jit(solution)/shard_map/ppermute | solution.py:105
  481.1 38.9 %collective-permute-start.39 = (bf16[128,1024]{1,0:T(8,128)(2,1)}, bf16[128,1024]{1,0:T(8,128)(2,1)S(1)}, u32[]{:S(2)}, u32[]{:S(2)}) collective-permute-start(bf16[128,1024]{1,0:T(8,128)(2,1)} %add.260.refs_8_.refs_0_), channel_id=1, source_target_pairs={{0,8},{4,12},{8,0},{12,4},{16,24},{20,28},{24,16},{28,20},{1,9},{5... | collective-permute-start | bytes 786440 | tf_op jit(solution)/shard_map/ppermute | solution.py:105
  525.2 31.7 %collective-permute-start.43 = (bf16[2048,256]{1,0:T(8,128)(2,1)}, bf16[2048,256]{1,0:T(8,128)(2,1)}, u32[]{:S(2)}, u32[]{:S(2)}) collective-permute-start(bf16[2048,256]{1,0:T(8,128)(2,1)} %get-tuple-element.298.refs_14_), channel_id=1, source_target_pairs={{0,4},{4,0},{8,12},{12,8},{16,20},{20,16},{24,28},{28,24},{1,5},{5... | collective-permute-start | bytes 3145736 | tf_op jit(solution)/shard_map/ppermute | solution.py:105
  529.4 27.5 %copy-start.5 = (s32[64,64]{1,0:T(8,128)S(1)}, s32[64,64]{1,0:T(8,128)}, u32[]{:S(2)}) copy-start(s32[64,64]{1,0:T(8,128)} %copy-done.4) | copy-start | bytes 49156
  529.4 35.5 %copy-start.21 = (f32[8,4,1024]{2,1,0:T(4,128)S(1)}, f32[8,4,1024]{2,1,0:T(4,128)}, u32[]{:S(2)}) copy-start(f32[8,4,1024]{2,1,0:T(4,128)} %get-tuple-element.315) | copy-start | bytes 393220
  529.4 36.5 %copy-start.25 = (s32[2,4]{1,0:T(2,128)S(1)}, s32[2,4]{1,0:T(2,128)}, u32[]{:S(2)}) copy-start(s32[2,4]{1,0:T(2,128)} %copy-done.24) | copy-start | bytes 100
  556.2 46.9 %collective-permute-start.50 = (bf16[512,1024]{1,0:T(8,128)(2,1)}, bf16[512,1024]{1,0:T(8,128)(2,1)}, u32[]{:S(2)}, u32[]{:S(2)}) collective-permute-start(bf16[512,1024]{1,0:T(8,128)(2,1)} %assemble.3.refs_12_.refs_0_), channel_id=1, source_target_pairs={{0,4},{4,0},{8,12},{12,8},{16,20},{20,16},{24,28},{28,24},{1,5},{5... | collective-permute-start | bytes 3145736 | tf_op jit(solution)/shard_map/ppermute | solution.py:105
  560.5 11.4 %collective-permute-start.46 = (bf16[512,256]{1,0:T(8,128)(2,1)}, bf16[512,256]{1,0:T(8,128)(2,1)S(1)}, u32[]{:S(2)}, u32[]{:S(2)}) collective-permute-start(bf16[512,256]{1,0:T(8,128)(2,1)} %get-tuple-element.306), channel_id=1, source_target_pairs={{0,24},{4,28},{8,16},{12,20},{16,8},{20,12},{24,0},{28,4},{1,25},{... | collective-permute-start | bytes 786440 | tf_op jit(solution)/shard_map/ppermute | solution.py:105
  563.9 19.9 %collective-permute-start.45 = (bf16[512,256]{1,0:T(8,128)(2,1)}, bf16[512,256]{1,0:T(8,128)(2,1)S(1)}, u32[]{:S(2)}, u32[]{:S(2)}) collective-permute-start(bf16[512,256]{1,0:T(8,128)(2,1)} %get-tuple-element.304), channel_id=1, source_target_pairs={{0,16},{4,20},{8,24},{12,28},{16,0},{20,4},{24,8},{28,12},{1,17},{... | collective-permute-start | bytes 786440 | tf_op jit(solution)/shard_map/ppermute | solution.py:105
  563.9 19.9 %collective-permute-start.44 = (bf16[512,256]{1,0:T(8,128)(2,1)}, bf16[512,256]{1,0:T(8,128)(2,1)}, u32[]{:S(2)}, u32[]{:S(2)}) collective-permute-start(bf16[512,256]{1,0:T(8,128)(2,1)} %get-tuple-element.302), channel_id=1, source_target_pairs={{0,8},{4,12},{8,0},{12,4},{16,24},{20,28},{24,16},{28,20},{1,9},{5... | collective-permute-start | bytes 786440 | tf_op jit(solution)/shard_map/ppermute | solution.py:105
  571.9 11.9 %copy-start.15 = (bf16[512,256]{1,0:T(8,128)(2,1)}, bf16[512,256]{1,0:T(8,128)(2,1)S(1)}, u32[]{:S(2)}) copy-start(bf16[512,256]{1,0:T(8,128)(2,1)S(1)} %collective-permute-done.46.refs_3_) | copy-start | bytes 786436
  587.7 19.3 %collective-permute-start.49 = (bf16[512,256]{1,0:T(8,128)(2,1)}, bf16[512,256]{1,0:T(8,128)(2,1)S(1)}, u32[]{:S(2)}, u32[]{:S(2)}) collective-permute-start(bf16[512,256]{1,0:T(8,128)(2,1)} %add.261.refs_1_.refs_0_), channel_id=1, source_target_pairs={{0,24},{4,28},{8,16},{12,20},{16,8},{20,12},{24,0},{28,4},{1,25},{... | collective-permute-start | bytes 786440 | tf_op jit(solution)/shard_map/ppermute | solution.py:105
  590.1 20.2 %collective-permute-start.48 = (bf16[512,256]{1,0:T(8,128)(2,1)}, bf16[512,256]{1,0:T(8,128)(2,1)S(1)}, u32[]{:S(2)}, u32[]{:S(2)}) collective-permute-start(bf16[512,256]{1,0:T(8,128)(2,1)} %add.261.refs_1_.refs_0_), channel_id=1, source_target_pairs={{0,16},{4,20},{8,24},{12,28},{16,0},{20,4},{24,8},{28,12},{1,17},{... | collective-permute-start | bytes 786440 | tf_op jit(solution)/shard_map/ppermute | solution.py:105
  590.1 20.2 %collective-permute-start.47 = (bf16[512,256]{1,0:T(8,128)(2,1)}, bf16[512,256]{1,0:T(8,128)(2,1)}, u32[]{:S(2)}, u32[]{:S(2)}) collective-permute-start(bf16[512,256]{1,0:T(8,128)(2,1)} %add.261.refs_1_.refs_0_), channel_id=1, source_target_pairs={{0,8},{4,12},{8,0},{12,4},{16,24},{20,28},{24,16},{28,20},{1,9},{5... | collective-permute-start | bytes 786440 | tf_op jit(solution)/shard_map/ppermute | solution.py:105
  613.8 1.6 collective-permute-start.52
  615.5 8.4 %collective-permute-start.53 = (bf16[128,1024]{1,0:T(8,128)(2,1)S(1)}, bf16[128,1024]{1,0:T(8,128)(2,1)S(1)}, u32[]{:S(2)}, u32[]{:S(2)}) collective-permute-start(bf16[128,1024]{1,0:T(8,128)(2,1)S(1)} %pad_maximum_fusion.2), channel_id=1, source_target_pairs={{0,2},{1,3},{2,0},{3,1},{4,6},{5,7},{6,4},{7,5},{8,10},{9,11},{10,... | collective-permute-start | bytes 786440 | tf_op jit(solution)/shard_map/ppermute | solution.py:105
  624.0 9.3 %collective-permute-start.54 = (bf16[128,1024]{1,0:T(8,128)(2,1)S(1)}, bf16[128,1024]{1,0:T(8,128)(2,1)S(1)}, u32[]{:S(2)}, u32[]{:S(2)}) collective-permute-start(bf16[128,1024]{1,0:T(8,128)(2,1)S(1)} %pad_maximum_fusion.3), channel_id=1, source_target_pairs={{0,4},{4,0},{8,12},{12,8},{16,20},{20,16},{24,28},{28,24},{1,5},{5... | collective-permute-start | bytes 786440 | tf_op jit(solution)/shard_map/ppermute | solution.py:105
  625.5 28.6 %collective-permute-start.51 = (bf16[2048,256]{1,0:T(8,128)(2,1)}, bf16[2048,256]{1,0:T(8,128)(2,1)}, u32[]{:S(2)}, u32[]{:S(2)}) collective-permute-start(bf16[2048,256]{1,0:T(8,128)(2,1)} %assemble.5.own_ref), channel_id=1, source_target_pairs={{0,4},{4,0},{8,12},{12,8},{16,20},{20,16},{24,28},{28,24},{1,5},{5... | collective-permute-start | bytes 3145736 | tf_op jit(solution)/shard_map/ppermute | solution.py:105
  633.5 6.4 collective-permute-start.55
  640.7 23.9 %copy-start.7 = (f32[2,8,256]{2,1,0:T(8,128)S(1)}, f32[2,8,256]{2,1,0:T(8,128)}, u32[]{:S(2)}) copy-start(f32[2,8,256]{2,1,0:T(8,128)} %copy-done.6) | copy-start | bytes 49156
  641.4 18.4 %collective-permute-start.56 = (bf16[128,1024]{1,0:T(8,128)(2,1)}, bf16[128,1024]{1,0:T(8,128)(2,1)}, u32[]{:S(2)}, u32[]{:S(2)}) collective-permute-start(bf16[128,1024]{1,0:T(8,128)(2,1)} %pad_maximum_fusion.5), channel_id=1, source_target_pairs={{0,16},{4,20},{8,24},{12,28},{16,0},{20,4},{24,8},{28,12},{1,17},{... | collective-permute-start | bytes 786440 | tf_op jit(solution)/shard_map/ppermute | solution.py:105
  (22 other events, 93.6 us)
Sparse Core Ops, SparseCore 0:
  429.9 74.2 all-gather.2

commit v8 on v7

--- a/solution.py
+++ b/solution.py
@@ -959,7 +959,7 @@
         return ties
 
     qkv_w = gather(qkv_weight, 3)
-    steps.step(modulation)
+    steps.step(near_terms)
     attn_in = norm_call(tokens_flat, mods)
     out_w = gather(out_weight, 3)
     ties = steps.step(attn_in)

time: 686 us -> 684 us (level)
  no operation moved by 1% of the time
where the time goes in v8:
time: 684 us; the launch traced here: 677 us
  Pallas kernels  504 us (74%)
  waiting for transfers between devices  65.8 us (10%)
  starting transfers between devices  46.8 us (7%)
  matrix products  20.8 us (3%)
  local copies, waits for them, and re-layouts  18.1 us (3%)
  between operations  15.3 us (2%)
    pallas_call x17, Pallas kernels, call_after(): return lambda *args: call(*args, *deps)  447 us
    ppermute x57, waiting for transfers between devices, swap(): return lax.ppermute(value, axis, [(i, i ^ bit) for i in range(size)])  65.8 us
    ppermute x57, starting transfers between devices, swap(): return lax.ppermute(value, axis, [(i, i ^ bit) for i in range(size)])  46.7 us
    pallas_call x6, Pallas kernels, split_call(): pl.pallas_call(functools.partial(split_kernel, count=count, groups=[len(g...  25.6 us
    pallas_call x5, Pallas kernels, add_groups(): pl.pallas_call(functools.partial(sum_kernel, groups=[len(group) for group...  17.4 us
  transfers between devices with their start and end apart: 58, of which 12 were waited for; matrix products, arithmetic and copies ran while one was open for 4% of the time, Pallas kernels for 73%

profile of v8, /device:TPU:0, one launch (start us, length us, event | category | flops | bytes accessed | tf_op | source)
XLA Modules:
  0.0 676.7 jit_solution(3862552804867049387)
XLA Ops:
  7.8 2.6 collective-permute-start.3
  11.1 1.7 convolution_add_fusion
  12.8 2.4 fusion.6
  17.4 3.7 fusion.1
  21.2 3.6 copy.35.refs_2_.refs_5_
  24.7 1.9 collective-permute-start.6
  26.7 2.6 collective-permute-done.1
  30.6 8.7 %norm_in.1.refs_0_.refs_3_.refs_6_ = bf16[2560,1024]{1,0:T(8,128)(2,1)} custom-call(bf16[2560,1024]{1,0:T(8,128)(2,1)} %bitcast.126, f32[8,6,1024]{2,1,0:T(8,128)} %reshape.254.refs_1_.refs_10_.refs_19_), custom_call_target="tpu_custom_call" | custom-call | flops 8000000000 | bytes 28000000 | tf_op jit(solution)/shard_map/norm_in/pallas_call | solution.py:83
  39.4 16.7 %attend.4 = (bf16[3,2560,256]{2,1,0:T(8,128)(2,1)}, bf16[2560,256]{1,0:T(8,128)(2,1)}, f32[8,8,384]{2,1,0:T(8,128)}) custom-call(bf16[2560,1024]{1,0:T(8,128)(2,1)} %norm_in.1.refs_0_.refs_3_.refs_6_, bf16[3,1024,256]{2,1,0:T(8,128)(2,1)} %refs_4_.3, f32[16,9,64,64]{3,2,1,0:T(8,128)} %copy.35.refs_2_.refs_5_, bf16[2560,1024]{1,0:T(8,128)(2,1)} %norm_in.1.refs_0_.refs_3_.refs_6_), custom_call_target="tpu_custom_call" | custom-call | flops 19000000512 | bytes 66500000 | tf_op jit(solution)/shard_map/attend/pallas_call | solution.py:83
  56.1 2.0 collective-permute-start.14
  58.1 16.7 %attend.5 = (bf16[3,2560,256]{2,1,0:T(8,128)(2,1)}, bf16[2560,256]{1,0:T(8,128)(2,1)}, f32[8,8,384]{2,1,0:T(8,128)}) custom-call(bf16[2560,1024]{1,0:T(8,128)(2,1)} %norm_in.1.refs_0_.refs_3_.refs_6_, bf16[3,1024,256]{2,1,0:T(8,128)(2,1)} %collective-permute-done.5.refs_1_.refs_5_, f32[16,9,64,64]{3,2,1,0:T(8,128)} %copy.35.refs_2_.refs_5_, ...), custom_call_target="tpu_custom_call" | custom-call | flops 19000000512 | bytes 66500000 | tf_op jit(solution)/shard_map/attend/pallas_call | solution.py:83
  75.3 16.7 %attend.6 = (bf16[3,2560,256]{2,1,0:T(8,128)(2,1)}, bf16[2560,256]{1,0:T(8,128)(2,1)}, f32[8,8,384]{2,1,0:T(8,128)}) custom-call(bf16[2560,1024]{1,0:T(8,128)(2,1)} %norm_in.1.refs_0_.refs_3_.refs_6_, bf16[3,1024,256]{2,1,0:T(8,128)(2,1)} %collective-permute-done.6.refs_1_.refs_3_.refs_6_, f32[16,9,64,64]{3,2,1,0:T(8,128)} %copy.35.refs_2_.refs_5_, ...), custom_call_target="tpu_custom_call" | custom-call | flops 19000000512 | bytes 66500000 | tf_op jit(solution)/shard_map/attend/pallas_call | solution.py:83
  92.6 19.7 %attend.7 = (bf16[3,2560,256]{2,1,0:T(8,128)(2,1)}, bf16[2560,256]{1,0:T(8,128)(2,1)}, f32[8,8,384]{2,1,0:T(8,128)}) custom-call(bf16[2560,1024]{1,0:T(8,128)(2,1)} %norm_in.1.refs_0_.refs_3_.refs_6_, bf16[3,1024,256]{2,1,0:T(8,128)(2,1)} %collective-permute-done.7.refs_1_.refs_7_, f32[16,9,64,64]{3,2,1,0:T(8,128)} %copy.35.refs_2_.refs_5_, ...), custom_call_target="tpu_custom_call" | custom-call | flops 19000000512 | bytes 66500000 | tf_op jit(solution)/shard_map/attend/pallas_call | solution.py:83
  112.4 15.6 %middle.1 = (bf16[2560,1024]{1,0:T(8,128)(2,1)}, bf16[2560,1024]{1,0:T(8,128)(2,1)}, bf16[2560,1024]{1,0:T(8,128)(2,1)}) custom-call(bf16[2560,256]{1,0:T(8,128)(2,1)} %get-tuple-element.164.refs_3_.refs_0_, bf16[2560,256]{1,0:T(8,128)(2,1)} %get-tuple-element.166.refs_4_.refs_1_.refs_3_, bf16[2560,256]{1,0:T(8,128)(2,1)} %get-tuple-element.168.refs_4_.refs_2_.refs_3_, ...), custom_call_target="tpu_custom_call" | custom-call | flops 16000000000 | bytes 56000000 | tf_op jit(solution)/shard_map/middle/pallas_call | solution.py:83
  128.1 32.9 %mlp.4 = (bf16[2560,1024]{1,0:T(8,128)(2,1)}, bf16[2560,1024]{1,0:T(8,128)(2,1)}, bf16[512,1024]{1,0:T(8,128)(2,1)}, bf16[512,1024]{1,0:T(8,128)(2,1)}, bf16[512...) custom-call(bf16[2560,1024]{1,0:T(8,128)(2,1)} %get-tuple-element.174.refs_0_.refs_5_, ...), custom_call_target="tpu_custom_call" | custom-call | flops 30000001024 | bytes 105000000 | tf_op jit(solution)/shard_map/mlp/pallas_call | solution.py:83
  161.0 2.5 collective-permute-done.11.refs_4_.refs_2_.refs_14_
  164.5 3.5 collective-permute-done.15.refs_2_.refs_15_
  168.0 32.9 %mlp.5 = (bf16[2560,1024]{1,0:T(8,128)(2,1)}, bf16[2560,1024]{1,0:T(8,128)(2,1)}, bf16[512,1024]{1,0:T(8,128)(2,1)}, bf16[512,1024]{1,0:T(8,128)(2,1)}, bf16[512...) custom-call(bf16[2560,1024]{1,0:T(8,128)(2,1)} %get-tuple-element.174.refs_0_.refs_5_, ...), custom_call_target="tpu_custom_call" | custom-call | flops 30000001024 | bytes 105000000 | tf_op jit(solution)/shard_map/mlp/pallas_call | solution.py:83
  202.0 33.0 %mlp.6 = (bf16[2560,1024]{1,0:T(8,128)(2,1)}, bf16[2560,1024]{1,0:T(8,128)(2,1)}, bf16[512,1024]{1,0:T(8,128)(2,1)}, bf16[512,1024]{1,0:T(8,128)(2,1)}, bf16[512...) custom-call(bf16[2560,1024]{1,0:T(8,128)(2,1)} %get-tuple-element.174.refs_0_.refs_5_, ...), custom_call_target="tpu_custom_call" | custom-call | flops 30000001024 | bytes 105000000 | tf_op jit(solution)/shard_map/mlp/pallas_call | solution.py:83
  235.0 5.8 add.264
  241.7 33.0 %mlp.7 = (bf16[2560,1024]{1,0:T(8,128)(2,1)}, bf16[2560,1024]{1,0:T(8,128)(2,1)}, bf16[512,1024]{1,0:T(8,128)(2,1)}, bf16[512,1024]{1,0:T(8,128)(2,1)}, bf16[512...) custom-call(bf16[2560,1024]{1,0:T(8,128)(2,1)} %get-tuple-element.174.refs_0_.refs_5_, ...), custom_call_target="tpu_custom_call" | custom-call | flops 30000001024 | bytes 105000000 | tf_op jit(solution)/shard_map/mlp/pallas_call | solution.py:83
  276.8 63.1 %mlp_out.1 = (bf16[2560,1024]{1,0:T(8,128)(2,1)}, bf16[2560,1024]{1,0:T(8,128)(2,1)}, bf16[2560,1024]{1,0:T(8,128)(2,1)}, f32[8,4,1024]{2,1,0:T(4,128)}) custom-call(bf16[2560,1024]{1,0:T(8,128)(2,1)} %get-tuple-element.214.refs_0_, bf16[2560,1024]{1,0:T(8,128)(2,1)} %get-tuple-element.215.refs_1_, bf16[2560,1024]{1,0:T(8,128)(2,1)} %get-tuple-element.216.refs_2_, ...), custom_call_target="tpu_custom_call" | custom-call | flops 54999998464 | bytes 192500000 | tf_op jit(solution)/shard_map/mlp_out/pallas_call | solution.py:83
  341.3 4.9 split.6
  346.2 1.4 collective-permute-start.29
  347.6 31.3 %attend_back.4 = (bf16[3,2560,256]{2,1,0:T(8,128)(2,1)}, f32[16,9,64,64]{3,2,1,0:T(8,128)}, bf16[4,1024,256]{2,1,0:T(8,128)(2,1)}) custom-call(bf16[2560,1024]{1,0:T(8,128)(2,1)} %get-tuple-element.227.refs_0_.refs_10_, bf16[256,1024]{1,0:T(8,128)(2,1)} %collective-permute-done.10.refs_7_.refs_1_, bf16[3,2560,256]{2,1,0:T(8,128)(2,1)} %get-tuple-element.234.refs_2_, ...), custom_call_target="tpu_custom_call" | custom-call | flops 30000001024 | bytes 105000000 | tf_op jit(solution)/shard_map/attend_back/pallas_call | solution.py:83
  378.9 3.6 split.7
  382.5 4.9 split.8
  387.4 3.7 collective-permute-start.32
  392.5 31.6 %attend_back.5 = (bf16[3,2560,256]{2,1,0:T(8,128)(2,1)}, f32[16,9,64,64]{3,2,1,0:T(8,128)}, bf16[4,1024,256]{2,1,0:T(8,128)(2,1)}) custom-call(bf16[2560,1024]{1,0:T(8,128)(2,1)} %get-tuple-element.227.refs_0_.refs_10_, bf16[256,1024]{1,0:T(8,128)(2,1)} %collective-permute-done.8.refs_3_.refs_6_.refs_1_, ...), custom_call_target="tpu_custom_call", output_to_operand_aliasing={{1}: (7, {})} | custom-call | flops 30000001024 | bytes 105000000 | tf_op jit(solution)/shard_map/attend_back/pallas_call | solution.py:83
  425.6 2.0 add.265.refs_2_.refs_8_
  427.6 3.5 split.9
  431.2 3.5 collective-permute-start.37
  435.5 4.3 add.266.refs_15_
  440.7 31.2 %attend_back.6 = (bf16[3,2560,256]{2,1,0:T(8,128)(2,1)}, f32[16,9,64,64]{3,2,1,0:T(8,128)}, bf16[4,1024,256]{2,1,0:T(8,128)(2,1)}) custom-call(bf16[2560,1024]{1,0:T(8,128)(2,1)} %get-tuple-element.227.refs_0_.refs_10_, bf16[256,1024]{1,0:T(8,128)(2,1)} %collective-permute-done.9.refs_5_.refs_1_, ...), custom_call_target="tpu_custom_call", output_to_operand_aliasing={{1}: (7, {})} | custom-call | flops 30000001024 | bytes 105000000 | tf_op jit(solution)/shard_map/attend_back/pallas_call | solution.py:83
  473.5 2.0 add.267.refs_8_.refs_0_
  475.5 3.6 collective-permute-start.41
  479.9 6.4 collective-permute-done.38.refs_9_.refs_0_
  486.3 31.3 %attend_back.7 = (bf16[3,2560,256]{2,1,0:T(8,128)(2,1)}, f32[16,9,64,64]{3,2,1,0:T(8,128)}, bf16[4,1024,256]{2,1,0:T(8,128)(2,1)}) custom-call(bf16[2560,1024]{1,0:T(8,128)(2,1)} %get-tuple-element.227.refs_0_.refs_10_, bf16[256,1024]{1,0:T(8,128)(2,1)} %refs_1_.3, ...), custom_call_target="tpu_custom_call", output_to_operand_aliasing={{1}: (7, {})} | custom-call | flops 30000001024 | bytes 105000000 | tf_op jit(solution)/shard_map/attend_back/pallas_call | solution.py:83
  517.7 5.2 split.10
  522.8 1.6 collective-permute-start.43
  524.4 2.8 assemble.3.refs_12_.refs_0_
  527.2 26.8 %last.1 = (bf16[2560,1024]{1,0:T(8,128)(2,1)}, f32[8,2,1024]{2,1,0:T(2,128)}) custom-call(bf16[3,2560,256]{2,1,0:T(8,128)(2,1)} %get-tuple-element.283.refs_0_, bf16[3,2560,256]{2,1,0:T(8,128)(2,1)} %get-tuple-element.284.refs_1_, bf16[3,2560,256]{2,1,0:T(8,128)(2,1)} %get-tuple-element.285.refs_2_, bf16[3,2560,256]{2,1,0:T(8,128)(2,1)} %get-tuple-element.286.refs_3_, ...), custom_call_target="tpu_custom_call" | custom-call | flops 28000000000 | bytes 98000000 | tf_op jit(solution)/shard_map/last/pallas_call | solution.py:83
  554.6 3.5 split.11
  558.1 3.5 collective-permute-start.46
  564.2 5.3 reshape.265
  569.5 12.1 %collective-permute-done.45.refs_2_ = bf16[512,256]{1,0:T(8,128)(2,1)S(1)} collective-permute-done((bf16[512,256]{1,0:T(8,128)(2,1)}, bf16[512,256]{1,0:T(8,128)(2,1)S(1)}, u32[]{:S(2)}, u32[]{:S(2)}) %collective-permute-start.45) | collective-permute-done | bytes 262176 | tf_op jit(solution)/shard_map/ppermute | solution.py:105
  582.3 3.2 add.268.refs_1_.refs_0_
  585.5 2.4 collective-permute-start.49
  587.8 2.0 collective-permute-start.47
  589.9 4.1 fusion.3
  594.8 6.0 unfold.1.refs_4_
  600.8 4.0 assemble.4.refs_5_
  604.8 3.3 collective-permute-done.48.refs_2_
  608.8 2.7 assemble.5.own_ref
  611.6 1.5 collective-permute-done.52
  614.1 7.6 %collective-permute-done.53 = bf16[128,1024]{1,0:T(8,128)(2,1)S(1)} collective-permute-done((bf16[128,1024]{1,0:T(8,128)(2,1)S(1)}, bf16[128,1024]{1,0:T(8,128)(2,1)S(1)}, u32[]{:S(2)}, u32[]{:S(2)}) %collective-permute-start.53) | collective-permute-done | bytes 262176 | tf_op jit(solution)/shard_map/ppermute | solution.py:105
  621.8 1.6 collective-permute-start.54
  623.9 7.2 %collective-permute-done.54 = bf16[128,1024]{1,0:T(8,128)(2,1)S(1)} collective-permute-done((bf16[128,1024]{1,0:T(8,128)(2,1)S(1)}, bf16[128,1024]{1,0:T(8,128)(2,1)S(1)}, u32[]{:S(2)}, u32[]{:S(2)}) %collective-permute-start.54) | collective-permute-done | bytes 262176 | tf_op jit(solution)/shard_map/ppermute | solution.py:105
  631.3 6.4 collective-permute-done.55
  640.3 11.7 %collective-permute-done.51.other_ref = bf16[2048,256]{1,0:T(8,128)(2,1)} collective-permute-done((bf16[2048,256]{1,0:T(8,128)(2,1)}, bf16[2048,256]{1,0:T(8,128)(2,1)}, u32[]{:S(2)}, u32[]{:S(2)}) %collective-permute-start.51) | collective-permute-done | bytes 1048608 | tf_op jit(solution)/shard_map/ppermute | solution.py:105
  652.0 4.7 attention_grads.1
  658.8 2.8 fusion.4
  662.3 3.7 convolution_bitcast_fusion
  667.7 1.6 convolution_bitcast_fusion.1
  (195 shorter events, 33.7 us)
Async XLA Ops:
  7.2 520.0 %all-gather.3.cloned.1.call-start = ((), (), s32[]{:S(2)}) async-start(), calls=%async_computation | async-start | bytes 2359296 | tf_op jit(solution)/shard_map/all_gather | solution.py:414
  7.2 8.7 %collective-permute-start.2 = (f32[4,2025]{1,0:T(4,128)}, f32[4,2025]{1,0:T(4,128)S(1)}, u32[]{:S(2)}, u32[]{:S(2)}) collective-permute-start(f32[4,2025]{1,0:T(4,128)} %param.19), channel_id=1, source_target_pairs={{0,1},{1,0},{2,3},{3,2},{4,5},{5,4},{6,7},{7,6},{8,9},{9,8},{10,11... | collective-permute-start | bytes 97208 | tf_op jit(solution)/shard_map/ppermute | solution.py:105
  7.8 7.7 %collective-permute-start.3 = (f32[4,2025]{1,0:T(4,128)}, f32[4,2025]{1,0:T(4,128)S(1)}, u32[]{:S(2)}, u32[]{:S(2)}) collective-permute-start(f32[4,2025]{1,0:T(4,128)} %param.19), channel_id=1, source_target_pairs={{0,2},{1,3},{2,0},{3,1},{4,6},{5,7},{6,4},{7,5},{8,10},{9,11},{10,... | collective-permute-start | bytes 97208 | tf_op jit(solution)/shard_map/ppermute | solution.py:105
  15.2 2.1 collective-permute-start
  15.5 1.5 collective-permute-start.4
  16.0 13.4 %copy-start.24 = (s32[2,4]{1,0:T(2,128)}, s32[2,4]{1,0:T(2,128)S(1)}, u32[]{:S(2)}) copy-start(s32[2,4]{1,0:T(2,128)S(1)} %constant_dynamic-slice_fusion) | copy-start | bytes 100
  17.3 12.0 %collective-permute-start.1 = (f32[2,8,6144]{2,1,0:T(8,128)S(1)}, f32[2,8,6144]{2,1,0:T(8,128)S(1)}, u32[]{:S(2)}, u32[]{:S(2)}) collective-permute-start(f32[2,8,6144]{2,1,0:T(8,128)S(1)} %add.163), channel_id=1, source_target_pairs={{0,2},{1,3},{2,0},{3,1},{4,6},{5,7},{6,4},{7,5},{8,10},{9,11},{10,... | collective-permute-start | bytes 1179656 | tf_op jit(solution)/shard_map/ppermute | solution.py:105
  24.7 50.0 %collective-permute-start.6 = (bf16[3,1024,256]{2,1,0:T(8,128)(2,1)}, bf16[3,1024,256]{2,1,0:T(8,128)(2,1)}, u32[]{:S(2)}, u32[]{:S(2)}) collective-permute-start(bf16[3,1024,256]{2,1,0:T(8,128)(2,1)} %refs_4_.3), channel_id=1, source_target_pairs={{0,2},{1,3},{2,0},{3,1},{4,6},{5,7},{6,4},{7,5},{8,10},{9,11},{10,... | collective-permute-start | bytes 4718600 | tf_op jit(solution)/shard_map/ppermute | solution.py:105
  26.7 31.4 %collective-permute-start.5 = (bf16[3,1024,256]{2,1,0:T(8,128)(2,1)}, bf16[3,1024,256]{2,1,0:T(8,128)(2,1)}, u32[]{:S(2)}, u32[]{:S(2)}) collective-permute-start(bf16[3,1024,256]{2,1,0:T(8,128)(2,1)} %refs_4_.3), channel_id=1, source_target_pairs={{0,1},{1,0},{2,3},{3,2},{4,5},{5,4},{6,7},{7,6},{8,9},{9,8},{10,11... | collective-permute-start | bytes 4718600 | tf_op jit(solution)/shard_map/ppermute | solution.py:105
  39.3 73.0 %collective-permute-start.9 = (bf16[256,1024]{1,0:T(8,128)(2,1)S(1)}, bf16[256,1024]{1,0:T(8,128)(2,1)}, u32[]{:S(2)}, u32[]{:S(2)}) collective-permute-start(bf16[256,1024]{1,0:T(8,128)(2,1)S(1)} %copy-done.27), channel_id=1, source_target_pairs={{0,1},{1,0},{2,3},{3,2},{4,5},{5,4},{6,7},{7,6},{8,9},{9,8},{10,11... | collective-permute-start | bytes 1572872 | tf_op jit(solution)/shard_map/ppermute | solution.py:105
  39.3 52.7 %collective-permute-start.8 = (bf16[256,1024]{1,0:T(8,128)(2,1)S(1)}, bf16[256,1024]{1,0:T(8,128)(2,1)}, u32[]{:S(2)}, u32[]{:S(2)}) collective-permute-start(bf16[256,1024]{1,0:T(8,128)(2,1)S(1)} %copy-done.27), channel_id=1, source_target_pairs={{0,2},{1,3},{2,0},{3,1},{4,6},{5,7},{6,4},{7,5},{8,10},{9,11},{10,... | collective-permute-start | bytes 1572872 | tf_op jit(solution)/shard_map/ppermute | solution.py:105
  56.1 71.9 %collective-permute-start.14 = (bf16[1024,1024]{1,0:T(8,128)(2,1)}, bf16[1024,1024]{1,0:T(8,128)(2,1)}, u32[]{:S(2)}, u32[]{:S(2)}) collective-permute-start(bf16[1024,1024]{1,0:T(8,128)(2,1)} %refs_8_.1), channel_id=1, source_target_pairs={{0,2},{1,3},{2,0},{3,1},{4,6},{5,7},{6,4},{7,5},{8,10},{9,11},{10,... | collective-permute-start | bytes 6291464 | tf_op jit(solution)/shard_map/ppermute | solution.py:105
  58.1 70.1 %collective-permute-start.13 = (bf16[1024,1024]{1,0:T(8,128)(2,1)}, bf16[1024,1024]{1,0:T(8,128)(2,1)}, u32[]{:S(2)}, u32[]{:S(2)}) collective-permute-start(bf16[1024,1024]{1,0:T(8,128)(2,1)} %refs_8_.1), channel_id=1, source_target_pairs={{0,1},{1,0},{2,3},{3,2},{4,5},{5,4},{6,7},{7,6},{8,9},{9,8},{10,11... | collective-permute-start | bytes 6291464 | tf_op jit(solution)/shard_map/ppermute | solution.py:105
  74.8 17.4 %collective-permute-start.7 = (bf16[3,1024,256]{2,1,0:T(8,128)(2,1)}, bf16[3,1024,256]{2,1,0:T(8,128)(2,1)}, u32[]{:S(2)}, u32[]{:S(2)}) collective-permute-start(bf16[3,1024,256]{2,1,0:T(8,128)(2,1)} %collective-permute-done.6.refs_1_.refs_3_.refs_6_), channel_id=1, source_target_pairs={{0,1},{1,0},{2,3},{3,2},{4,5},{5,4},{6,7},{7,6},{8,9},{9,8},{10,11... | collective-permute-start | bytes 4718600 | tf_op jit(solution)/shard_map/ppermute | solution.py:105
  92.0 20.4 %collective-permute-start.10 = (bf16[256,1024]{1,0:T(8,128)(2,1)}, bf16[256,1024]{1,0:T(8,128)(2,1)}, u32[]{:S(2)}, u32[]{:S(2)}) collective-permute-start(bf16[256,1024]{1,0:T(8,128)(2,1)} %collective-permute-done.8.refs_3_.refs_6_.refs_1_), channel_id=1, source_target_pairs={{0,1},{1,0},{2,3},{3,2},{4,5},{5,4},{6,7},{7,6},{8,9},{9,8},{10,11... | collective-permute-start | bytes 1572872 | tf_op jit(solution)/shard_map/ppermute | solution.py:105
  92.1 36.0 %collective-permute-start.12 = (bf16[1024,1024]{1,0:T(8,128)(2,1)}, bf16[1024,1024]{1,0:T(8,128)(2,1)}, u32[]{:S(2)}, u32[]{:S(2)}) collective-permute-start(bf16[1024,1024]{1,0:T(8,128)(2,1)} %refs_12_.1), channel_id=1, source_target_pairs={{0,1},{1,0},{2,3},{3,2},{4,5},{5,4},{6,7},{7,6},{8,9},{9,8},{10,11... | collective-permute-start | bytes 6291464 | tf_op jit(solution)/shard_map/ppermute | solution.py:105
  112.3 51.2 %collective-permute-start.11 = (bf16[1024,1024]{1,0:T(8,128)(2,1)}, bf16[1024,1024]{1,0:T(8,128)(2,1)}, u32[]{:S(2)}, u32[]{:S(2)}) collective-permute-start(bf16[1024,1024]{1,0:T(8,128)(2,1)} %refs_12_.1), channel_id=1, source_target_pairs={{0,2},{1,3},{2,0},{3,1},{4,6},{5,7},{6,4},{7,5},{8,10},{9,11},{10,... | collective-permute-start | bytes 6291464 | tf_op jit(solution)/shard_map/ppermute | solution.py:105
  128.0 36.5 %collective-permute-start.16 = (bf16[1024,1024]{1,0:T(8,128)(2,1)}, bf16[1024,1024]{1,0:T(8,128)(2,1)}, u32[]{:S(2)}, u32[]{:S(2)}) collective-permute-start(bf16[1024,1024]{1,0:T(8,128)(2,1)} %collective-permute-done.14.refs_4_.refs_3_.refs_10_), channel_id=1, source_target_pairs={{0,1},{1,0},{2,3},{3,2},{4,5},{5,4},{6,7},{7,6},{8,9},{9,8},{10,11... | collective-permute-start | bytes 6291464 | tf_op jit(solution)/shard_map/ppermute | solution.py:105
  163.5 4.5 collective-permute-start.15
  163.5 37.4 %collective-permute-start.18 = (bf16[512,1024]{1,0:T(8,128)(2,1)}, bf16[512,1024]{1,0:T(8,128)(2,1)}, u32[]{:S(2)}, u32[]{:S(2)}) collective-permute-start(bf16[512,1024]{1,0:T(8,128)(2,1)} %get-tuple-element.185.refs_5_), channel_id=1, source_target_pairs={{0,1},{1,0},{2,3},{3,2},{4,5},{5,4},{6,7},{7,6},{8,9},{9,8},{10,11... | collective-permute-start | bytes 3145736 | tf_op jit(solution)/shard_map/ppermute | solution.py:105
  164.0 36.9 %collective-permute-start.21 = (bf16[512,1024]{1,0:T(8,128)(2,1)}, bf16[512,1024]{1,0:T(8,128)(2,1)}, u32[]{:S(2)}, u32[]{:S(2)}) collective-permute-start(bf16[512,1024]{1,0:T(8,128)(2,1)} %get-tuple-element.194), channel_id=1, source_target_pairs={{0,1},{1,0},{2,3},{3,2},{4,5},{5,4},{6,7},{7,6},{8,9},{9,8},{10,11... | collective-permute-start | bytes 3145736 | tf_op jit(solution)/shard_map/ppermute | solution.py:105
  164.0 36.9 %collective-permute-start.20 = (bf16[512,1024]{1,0:T(8,128)(2,1)}, bf16[512,1024]{1,0:T(8,128)(2,1)}, u32[]{:S(2)}, u32[]{:S(2)}) collective-permute-start(bf16[512,1024]{1,0:T(8,128)(2,1)} %get-tuple-element.191), channel_id=1, source_target_pairs={{0,1},{1,0},{2,3},{3,2},{4,5},{5,4},{6,7},{7,6},{8,9},{9,8},{10,11... | collective-permute-start | bytes 3145736 | tf_op jit(solution)/shard_map/ppermute | solution.py:105
  164.5 36.4 %collective-permute-start.19 = (bf16[512,1024]{1,0:T(8,128)(2,1)}, bf16[512,1024]{1,0:T(8,128)(2,1)}, u32[]{:S(2)}, u32[]{:S(2)}) collective-permute-start(bf16[512,1024]{1,0:T(8,128)(2,1)} %get-tuple-element.188), channel_id=1, source_target_pairs={{0,1},{1,0},{2,3},{3,2},{4,5},{5,4},{6,7},{7,6},{8,9},{9,8},{10,11... | collective-permute-start | bytes 3145736 | tf_op jit(solution)/shard_map/ppermute | solution.py:105
  200.9 34.1 %collective-permute-start.17 = (bf16[512,1024]{1,0:T(8,128)(2,1)}, bf16[512,1024]{1,0:T(8,128)(2,1)}, u32[]{:S(2)}, u32[]{:S(2)}) collective-permute-start(bf16[512,1024]{1,0:T(8,128)(2,1)} %get-tuple-element.184.refs_8_), channel_id=1, source_target_pairs={{0,1},{1,0},{2,3},{3,2},{4,5},{5,4},{6,7},{7,6},{8,9},{9,8},{10,11... | collective-permute-start | bytes 3145736 | tf_op jit(solution)/shard_map/ppermute | solution.py:105
  201.1 33.9 %collective-permute-start.24 = (bf16[512,1024]{1,0:T(8,128)(2,1)}, bf16[512,1024]{1,0:T(8,128)(2,1)}, u32[]{:S(2)}, u32[]{:S(2)}) collective-permute-start(bf16[512,1024]{1,0:T(8,128)(2,1)} %get-tuple-element.205), channel_id=1, source_target_pairs={{0,1},{1,0},{2,3},{3,2},{4,5},{5,4},{6,7},{7,6},{8,9},{9,8},{10,11... | collective-permute-start | bytes 3145736 | tf_op jit(solution)/shard_map/ppermute | solution.py:105
  201.5 33.5 %collective-permute-start.23 = (bf16[512,1024]{1,0:T(8,128)(2,1)}, bf16[512,1024]{1,0:T(8,128)(2,1)}, u32[]{:S(2)}, u32[]{:S(2)}) collective-permute-start(bf16[512,1024]{1,0:T(8,128)(2,1)} %get-tuple-element.202), channel_id=1, source_target_pairs={{0,1},{1,0},{2,3},{3,2},{4,5},{5,4},{6,7},{7,6},{8,9},{9,8},{10,11... | collective-permute-start | bytes 3145736 | tf_op jit(solution)/shard_map/ppermute | solution.py:105
  201.6 33.4 %collective-permute-start.22 = (bf16[512,1024]{1,0:T(8,128)(2,1)}, bf16[512,1024]{1,0:T(8,128)(2,1)}, u32[]{:S(2)}, u32[]{:S(2)}) collective-permute-start(bf16[512,1024]{1,0:T(8,128)(2,1)} %get-tuple-element.199), channel_id=1, source_target_pairs={{0,1},{1,0},{2,3},{3,2},{4,5},{5,4},{6,7},{7,6},{8,9},{9,8},{10,11... | collective-permute-start | bytes 3145736 | tf_op jit(solution)/shard_map/ppermute | solution.py:105
  240.8 36.0 %collective-permute-start.25 = (bf16[512,1024]{1,0:T(8,128)(2,1)}, bf16[512,1024]{1,0:T(8,128)(2,1)}, u32[]{:S(2)}, u32[]{:S(2)}) collective-permute-start(bf16[512,1024]{1,0:T(8,128)(2,1)} %get-tuple-element.223.refs_8_), channel_id=1, source_target_pairs={{0,2},{1,3},{2,0},{3,1},{4,6},{5,7},{6,4},{7,5},{8,10},{9,11},{10,... | collective-permute-start | bytes 3145736 | tf_op jit(solution)/shard_map/ppermute | solution.py:105
  274.7 66.6 %collective-permute-start.26 = (bf16[512,1024]{1,0:T(8,128)(2,1)}, bf16[512,1024]{1,0:T(8,128)(2,1)}, u32[]{:S(2)}, u32[]{:S(2)}) collective-permute-start(bf16[512,1024]{1,0:T(8,128)(2,1)} %get-tuple-element.236.refs_9_), channel_id=1, source_target_pairs={{0,2},{1,3},{2,0},{3,1},{4,6},{5,7},{6,4},{7,5},{8,10},{9,11},{10,... | collective-permute-start | bytes 3145736 | tf_op jit(solution)/shard_map/ppermute | solution.py:105
  276.0 71.5 %collective-permute-start.27 = (bf16[512,1024]{1,0:T(8,128)(2,1)}, bf16[512,1024]{1,0:T(8,128)(2,1)}, u32[]{:S(2)}, u32[]{:S(2)}) collective-permute-start(bf16[512,1024]{1,0:T(8,128)(2,1)} %get-tuple-element.238.refs_10_), channel_id=1, source_target_pairs={{0,2},{1,3},{2,0},{3,1},{4,6},{5,7},{6,4},{7,5},{8,10},{9,11},{10,... | collective-permute-start | bytes 3145736 | tf_op jit(solution)/shard_map/ppermute | solution.py:105
  339.9 39.0 %collective-permute-start.28 = (bf16[512,1024]{1,0:T(8,128)(2,1)}, bf16[512,1024]{1,0:T(8,128)(2,1)}, u32[]{:S(2)}, u32[]{:S(2)}) collective-permute-start(bf16[512,1024]{1,0:T(8,128)(2,1)} %get-tuple-element.243.refs_11_), channel_id=1, source_target_pairs={{0,2},{1,3},{2,0},{3,1},{4,6},{5,7},{6,4},{7,5},{8,10},{9,11},{10,... | collective-permute-start | bytes 3145736 | tf_op jit(solution)/shard_map/ppermute | solution.py:105
  346.2 32.8 %collective-permute-start.29 = (bf16[512,1024]{1,0:T(8,128)(2,1)}, bf16[512,1024]{1,0:T(8,128)(2,1)}, u32[]{:S(2)}, u32[]{:S(2)}) collective-permute-start(bf16[512,1024]{1,0:T(8,128)(2,1)} %get-tuple-element.246.refs_9_), channel_id=1, source_target_pairs={{0,4},{4,0},{8,12},{12,8},{16,20},{20,16},{24,28},{28,24},{1,5},{5... | collective-permute-start | bytes 3145736 | tf_op jit(solution)/shard_map/ppermute | solution.py:105
  378.8 56.7 %collective-permute-start.34 = (bf16[4096,256]{1,0:T(8,128)(2,1)}, bf16[4096,256]{1,0:T(8,128)(2,1)}, u32[]{:S(2)}, u32[]{:S(2)}) collective-permute-start(bf16[4096,256]{1,0:T(8,128)(2,1)} %bitcast.131), channel_id=1, source_target_pairs={{0,1},{1,0},{2,3},{3,2},{4,5},{5,4},{6,7},{7,6},{8,9},{9,8},{10,11... | collective-permute-start | bytes 6291464 | tf_op jit(solution)/shard_map/ppermute | solution.py:105
  387.4 36.6 %collective-permute-start.32 = (bf16[128,1024]{1,0:T(8,128)(2,1)}, bf16[128,1024]{1,0:T(8,128)(2,1)S(1)}, u32[]{:S(2)}, u32[]{:S(2)}) collective-permute-start(bf16[128,1024]{1,0:T(8,128)(2,1)} %get-tuple-element.262.refs_13_), channel_id=1, source_target_pairs={{0,24},{4,28},{8,16},{12,20},{16,8},{20,12},{24,0},{28,4},{1,25},{... | collective-permute-start | bytes 786440 | tf_op jit(solution)/shard_map/ppermute | solution.py:105
  391.1 33.0 %collective-permute-start.31 = (bf16[128,1024]{1,0:T(8,128)(2,1)}, bf16[128,1024]{1,0:T(8,128)(2,1)S(1)}, u32[]{:S(2)}, u32[]{:S(2)}) collective-permute-start(bf16[128,1024]{1,0:T(8,128)(2,1)} %get-tuple-element.260.refs_12_), channel_id=1, source_target_pairs={{0,16},{4,20},{8,24},{12,28},{16,0},{20,4},{24,8},{28,12},{1,17},{... | collective-permute-start | bytes 786440 | tf_op jit(solution)/shard_map/ppermute | solution.py:105
  391.1 33.0 %collective-permute-start.30 = (bf16[128,1024]{1,0:T(8,128)(2,1)}, bf16[128,1024]{1,0:T(8,128)(2,1)S(1)}, u32[]{:S(2)}, u32[]{:S(2)}) collective-permute-start(bf16[128,1024]{1,0:T(8,128)(2,1)} %get-tuple-element.257.refs_11_), channel_id=1, source_target_pairs={{0,8},{4,12},{8,0},{12,4},{16,24},{20,28},{24,16},{28,20},{1,9},{5... | collective-permute-start | bytes 786440 | tf_op jit(solution)/shard_map/ppermute | solution.py:105
  391.9 35.8 %collective-permute-start.33 = (bf16[512,1024]{1,0:T(8,128)(2,1)}, bf16[512,1024]{1,0:T(8,128)(2,1)}, u32[]{:S(2)}, u32[]{:S(2)}) collective-permute-start(bf16[512,1024]{1,0:T(8,128)(2,1)} %get-tuple-element.264.refs_14_), channel_id=1, source_target_pairs={{0,4},{4,0},{8,12},{12,8},{16,20},{20,16},{24,28},{28,24},{1,5},{5... | collective-permute-start | bytes 3145736 | tf_op jit(solution)/shard_map/ppermute | solution.py:105
  431.2 40.8 %collective-permute-start.37 = (bf16[128,1024]{1,0:T(8,128)(2,1)}, bf16[128,1024]{1,0:T(8,128)(2,1)S(1)}, u32[]{:S(2)}, u32[]{:S(2)}) collective-permute-start(bf16[128,1024]{1,0:T(8,128)(2,1)} %get-tuple-element.279.refs_13_), channel_id=1, source_target_pairs={{0,24},{4,28},{8,16},{12,20},{16,8},{20,12},{24,0},{28,4},{1,25},{... | collective-permute-start | bytes 786440 | tf_op jit(solution)/shard_map/ppermute | solution.py:105
  434.7 37.3 %collective-permute-start.36 = (bf16[128,1024]{1,0:T(8,128)(2,1)}, bf16[128,1024]{1,0:T(8,128)(2,1)S(1)}, u32[]{:S(2)}, u32[]{:S(2)}) collective-permute-start(bf16[128,1024]{1,0:T(8,128)(2,1)} %get-tuple-element.277.refs_12_), channel_id=1, source_target_pairs={{0,16},{4,20},{8,24},{12,28},{16,0},{20,4},{24,8},{28,12},{1,17},{... | collective-permute-start | bytes 786440 | tf_op jit(solution)/shard_map/ppermute | solution.py:105
  434.7 37.4 %collective-permute-start.35 = (bf16[128,1024]{1,0:T(8,128)(2,1)}, bf16[128,1024]{1,0:T(8,128)(2,1)S(1)}, u32[]{:S(2)}, u32[]{:S(2)}) collective-permute-start(bf16[128,1024]{1,0:T(8,128)(2,1)} %get-tuple-element.274.refs_11_), channel_id=1, source_target_pairs={{0,8},{4,12},{8,0},{12,4},{16,24},{20,28},{24,16},{28,20},{1,9},{5... | collective-permute-start | bytes 786440 | tf_op jit(solution)/shard_map/ppermute | solution.py:105
  439.9 46.4 %collective-permute-start.38 = (bf16[4096,256]{1,0:T(8,128)(2,1)}, bf16[4096,256]{1,0:T(8,128)(2,1)}, u32[]{:S(2)}, u32[]{:S(2)}) collective-permute-start(bf16[4096,256]{1,0:T(8,128)(2,1)} %add.266.refs_15_), channel_id=1, source_target_pairs={{0,2},{1,3},{2,0},{3,1},{4,6},{5,7},{6,4},{7,5},{8,10},{9,11},{10,... | collective-permute-start | bytes 6291464 | tf_op jit(solution)/shard_map/ppermute | solution.py:105
  471.9 45.7 %collective-permute-start.42 = (bf16[4096,256]{1,0:T(8,128)(2,1)}, bf16[4096,256]{1,0:T(8,128)(2,1)}, u32[]{:S(2)}, u32[]{:S(2)}) collective-permute-start(bf16[4096,256]{1,0:T(8,128)(2,1)} %bitcast.132), channel_id=1, source_target_pairs={{0,1},{1,0},{2,3},{3,2},{4,5},{5,4},{6,7},{7,6},{8,9},{9,8},{10,11... | collective-permute-start | bytes 6291464 | tf_op jit(solution)/shard_map/ppermute | solution.py:105
  475.5 42.1 %collective-permute-start.41 = (bf16[128,1024]{1,0:T(8,128)(2,1)}, bf16[128,1024]{1,0:T(8,128)(2,1)S(1)}, u32[]{:S(2)}, u32[]{:S(2)}) collective-permute-start(bf16[128,1024]{1,0:T(8,128)(2,1)} %add.267.refs_8_.refs_0_), channel_id=1, source_target_pairs={{0,24},{4,28},{8,16},{12,20},{16,8},{20,12},{24,0},{28,4},{1,25},{... | collective-permute-start | bytes 786440 | tf_op jit(solution)/shard_map/ppermute | solution.py:105
  479.1 38.5 %collective-permute-start.40 = (bf16[128,1024]{1,0:T(8,128)(2,1)}, bf16[128,1024]{1,0:T(8,128)(2,1)S(1)}, u32[]{:S(2)}, u32[]{:S(2)}) collective-permute-start(bf16[128,1024]{1,0:T(8,128)(2,1)} %add.267.refs_8_.refs_0_), channel_id=1, source_target_pairs={{0,16},{4,20},{8,24},{12,28},{16,0},{20,4},{24,8},{28,12},{1,17},{... | collective-permute-start | bytes 786440 | tf_op jit(solution)/shard_map/ppermute | solution.py:105
  479.1 38.5 %collective-permute-start.39 = (bf16[128,1024]{1,0:T(8,128)(2,1)}, bf16[128,1024]{1,0:T(8,128)(2,1)S(1)}, u32[]{:S(2)}, u32[]{:S(2)}) collective-permute-start(bf16[128,1024]{1,0:T(8,128)(2,1)} %add.267.refs_8_.refs_0_), channel_id=1, source_target_pairs={{0,8},{4,12},{8,0},{12,4},{16,24},{20,28},{24,16},{28,20},{1,9},{5... | collective-permute-start | bytes 786440 | tf_op jit(solution)/shard_map/ppermute | solution.py:105
  522.8 31.7 %collective-permute-start.43 = (bf16[2048,256]{1,0:T(8,128)(2,1)}, bf16[2048,256]{1,0:T(8,128)(2,1)}, u32[]{:S(2)}, u32[]{:S(2)}) collective-permute-start(bf16[2048,256]{1,0:T(8,128)(2,1)} %get-tuple-element.298.refs_14_), channel_id=1, source_target_pairs={{0,4},{4,0},{8,12},{12,8},{16,20},{20,16},{24,28},{28,24},{1,5},{5... | collective-permute-start | bytes 3145736 | tf_op jit(solution)/shard_map/ppermute | solution.py:105
  527.2 27.3 %copy-start.5 = (s32[64,64]{1,0:T(8,128)S(1)}, s32[64,64]{1,0:T(8,128)}, u32[]{:S(2)}) copy-start(s32[64,64]{1,0:T(8,128)} %copy-done.4) | copy-start | bytes 49156
  527.2 35.3 %copy-start.21 = (f32[8,4,1024]{2,1,0:T(4,128)S(1)}, f32[8,4,1024]{2,1,0:T(4,128)}, u32[]{:S(2)}) copy-start(f32[8,4,1024]{2,1,0:T(4,128)} %get-tuple-element.315) | copy-start | bytes 393220
  527.2 36.4 %copy-start.25 = (s32[2,4]{1,0:T(2,128)S(1)}, s32[2,4]{1,0:T(2,128)}, u32[]{:S(2)}) copy-start(s32[2,4]{1,0:T(2,128)} %copy-done.24) | copy-start | bytes 100
  554.0 46.8 %collective-permute-start.50 = (bf16[512,1024]{1,0:T(8,128)(2,1)}, bf16[512,1024]{1,0:T(8,128)(2,1)}, u32[]{:S(2)}, u32[]{:S(2)}) collective-permute-start(bf16[512,1024]{1,0:T(8,128)(2,1)} %assemble.3.refs_12_.refs_0_), channel_id=1, source_target_pairs={{0,4},{4,0},{8,12},{12,8},{16,20},{20,16},{24,28},{28,24},{1,5},{5... | collective-permute-start | bytes 3145736 | tf_op jit(solution)/shard_map/ppermute | solution.py:105
  558.1 11.4 %collective-permute-start.46 = (bf16[512,256]{1,0:T(8,128)(2,1)}, bf16[512,256]{1,0:T(8,128)(2,1)S(1)}, u32[]{:S(2)}, u32[]{:S(2)}) collective-permute-start(bf16[512,256]{1,0:T(8,128)(2,1)} %get-tuple-element.306), channel_id=1, source_target_pairs={{0,24},{4,28},{8,16},{12,20},{16,8},{20,12},{24,0},{28,4},{1,25},{... | collective-permute-start | bytes 786440 | tf_op jit(solution)/shard_map/ppermute | solution.py:105
  561.6 20.0 %collective-permute-start.45 = (bf16[512,256]{1,0:T(8,128)(2,1)}, bf16[512,256]{1,0:T(8,128)(2,1)S(1)}, u32[]{:S(2)}, u32[]{:S(2)}) collective-permute-start(bf16[512,256]{1,0:T(8,128)(2,1)} %get-tuple-element.304), channel_id=1, source_target_pairs={{0,16},{4,20},{8,24},{12,28},{16,0},{20,4},{24,8},{28,12},{1,17},{... | collective-permute-start | bytes 786440 | tf_op jit(solution)/shard_map/ppermute | solution.py:105
  561.6 20.0 %collective-permute-start.44 = (bf16[512,256]{1,0:T(8,128)(2,1)}, bf16[512,256]{1,0:T(8,128)(2,1)}, u32[]{:S(2)}, u32[]{:S(2)}) collective-permute-start(bf16[512,256]{1,0:T(8,128)(2,1)} %get-tuple-element.302), channel_id=1, source_target_pairs={{0,8},{4,12},{8,0},{12,4},{16,24},{20,28},{24,16},{28,20},{1,9},{5... | collective-permute-start | bytes 786440 | tf_op jit(solution)/shard_map/ppermute | solution.py:105
  569.5 12.1 %copy-start.15 = (bf16[512,256]{1,0:T(8,128)(2,1)}, bf16[512,256]{1,0:T(8,128)(2,1)S(1)}, u32[]{:S(2)}) copy-start(bf16[512,256]{1,0:T(8,128)(2,1)S(1)} %collective-permute-done.46.refs_3_) | copy-start | bytes 786436
  585.5 19.3 %collective-permute-start.49 = (bf16[512,256]{1,0:T(8,128)(2,1)}, bf16[512,256]{1,0:T(8,128)(2,1)S(1)}, u32[]{:S(2)}, u32[]{:S(2)}) collective-permute-start(bf16[512,256]{1,0:T(8,128)(2,1)} %add.268.refs_1_.refs_0_), channel_id=1, source_target_pairs={{0,24},{4,28},{8,16},{12,20},{16,8},{20,12},{24,0},{28,4},{1,25},{... | collective-permute-start | bytes 786440 | tf_op jit(solution)/shard_map/ppermute | solution.py:105
  587.8 20.2 %collective-permute-start.48 = (bf16[512,256]{1,0:T(8,128)(2,1)}, bf16[512,256]{1,0:T(8,128)(2,1)S(1)}, u32[]{:S(2)}, u32[]{:S(2)}) collective-permute-start(bf16[512,256]{1,0:T(8,128)(2,1)} %add.268.refs_1_.refs_0_), channel_id=1, source_target_pairs={{0,16},{4,20},{8,24},{12,28},{16,0},{20,4},{24,8},{28,12},{1,17},{... | collective-permute-start | bytes 786440 | tf_op jit(solution)/shard_map/ppermute | solution.py:105
  587.8 20.2 %collective-permute-start.47 = (bf16[512,256]{1,0:T(8,128)(2,1)}, bf16[512,256]{1,0:T(8,128)(2,1)}, u32[]{:S(2)}, u32[]{:S(2)}) collective-permute-start(bf16[512,256]{1,0:T(8,128)(2,1)} %add.268.refs_1_.refs_0_), channel_id=1, source_target_pairs={{0,8},{4,12},{8,0},{12,4},{16,24},{20,28},{24,16},{28,20},{1,9},{5... | collective-permute-start | bytes 786440 | tf_op jit(solution)/shard_map/ppermute | solution.py:105
  611.5 1.6 collective-permute-start.52
  613.3 8.4 %collective-permute-start.53 = (bf16[128,1024]{1,0:T(8,128)(2,1)S(1)}, bf16[128,1024]{1,0:T(8,128)(2,1)S(1)}, u32[]{:S(2)}, u32[]{:S(2)}) collective-permute-start(bf16[128,1024]{1,0:T(8,128)(2,1)S(1)} %pad_maximum_fusion.2), channel_id=1, source_target_pairs={{0,2},{1,3},{2,0},{3,1},{4,6},{5,7},{6,4},{7,5},{8,10},{9,11},{10,... | collective-permute-start | bytes 786440 | tf_op jit(solution)/shard_map/ppermute | solution.py:105
  621.8 9.3 %collective-permute-start.54 = (bf16[128,1024]{1,0:T(8,128)(2,1)S(1)}, bf16[128,1024]{1,0:T(8,128)(2,1)S(1)}, u32[]{:S(2)}, u32[]{:S(2)}) collective-permute-start(bf16[128,1024]{1,0:T(8,128)(2,1)S(1)} %pad_maximum_fusion.3), channel_id=1, source_target_pairs={{0,4},{4,0},{8,12},{12,8},{16,20},{20,16},{24,28},{28,24},{1,5},{5... | collective-permute-start | bytes 786440 | tf_op jit(solution)/shard_map/ppermute | solution.py:105
  623.4 28.6 %collective-permute-start.51 = (bf16[2048,256]{1,0:T(8,128)(2,1)}, bf16[2048,256]{1,0:T(8,128)(2,1)}, u32[]{:S(2)}, u32[]{:S(2)}) collective-permute-start(bf16[2048,256]{1,0:T(8,128)(2,1)} %assemble.5.own_ref), channel_id=1, source_target_pairs={{0,4},{4,0},{8,12},{12,8},{16,20},{20,16},{24,28},{28,24},{1,5},{5... | collective-permute-start | bytes 3145736 | tf_op jit(solution)/shard_map/ppermute | solution.py:105
  631.2 6.4 collective-permute-start.55
  638.5 23.9 %copy-start.7 = (f32[2,8,256]{2,1,0:T(8,128)S(1)}, f32[2,8,256]{2,1,0:T(8,128)}, u32[]{:S(2)}) copy-start(f32[2,8,256]{2,1,0:T(8,128)} %copy-done.6) | copy-start | bytes 49156
  639.2 18.4 %collective-permute-start.56 = (bf16[128,1024]{1,0:T(8,128)(2,1)}, bf16[128,1024]{1,0:T(8,128)(2,1)}, u32[]{:S(2)}, u32[]{:S(2)}) collective-permute-start(bf16[128,1024]{1,0:T(8,128)(2,1)} %pad_maximum_fusion.5), channel_id=1, source_target_pairs={{0,16},{4,20},{8,24},{12,28},{16,0},{20,4},{24,8},{28,12},{1,17},{... | collective-permute-start | bytes 786440 | tf_op jit(solution)/shard_map/ppermute | solution.py:105
  (22 other events, 94.9 us)
Sparse Core Ops, SparseCore 0:
  427.7 74.4 all-gather.2
